TPU v7x, 32 devices: a whole 2x2x4 slice. The times are simulated.
32 devices in a mesh: parts: 2 (over y), attn: 8 (over z, x), ffn: 2 (over core).
Axes of the slice: x: 2, y: 2, z: 4, core: 2. Of those that a mesh axis runs over, the one named last changes fastest.
Arguments:
- queries: bfloat16 [128, 64, 128], P(('parts', 'attn'), 'ffn'), parts along dimension 0, may hold values from -10 to 10
- cache_keys: bfloat16 [128, 128, 4, 128], P(('parts', 'attn'), None, 'ffn'), parts along dimension 0, may hold values from -6 to 6
- stored_value_cache: bfloat16 [128, 128, 4, 128], P(('parts', 'attn'), None, 'ffn'), parts along dimension 0, may hold values from -6 to 6
- lengths: int32 [128], P(('parts', 'attn')), parts along dimension 0, may hold values from 2 to 128, as said below
- residual: bfloat16 [128, 8192], P(('parts', 'attn'), 'ffn'), parts along dimension 0, may hold values from -6 to 6
- target: int32 [128, 1], P('parts'), parts along dimension 0, may hold values from 0 to 15; in each aligned block of 64 rows (0 to 63, 64 to 127, ...) at most 8 rows name the same one
- gate_weight: bfloat16 [8192, 26624], P('ffn', 'attn'), may hold values from -0.0625 to 0.0625
- up_weight: bfloat16 [8192, 26624], P('ffn', 'attn'), may hold values from -0.0625 to 0.0625
- down_weight: bfloat16 [26624, 8192], P('attn', 'ffn'), may hold values from -0.0390625 to 0.0390625
Outputs:
- returned: bfloat16 [256, 8192], P(('parts', 'attn'), 'ffn'), parts along dimension 0
There are 2 independent parts, one for each index of `parts`. A program takes and returns all parts, laid end to end along the dimension named above; an argument that names none is the same for every part. Nothing has to cross between parts.
Inputs may be any that keep to these rules, and one draw needn't show every extreme that they name: `lengths`: each device's requests lie in a bucket of 128, 64 or 32 positions, and one request of each device fills its bucket; some device's bucket is 128. `target`: no value is named by more than 8 requests, a bound that some block reaches.
All inputs are finite; a program needn't handle non-finite values.
Results may differ from a plain program's by a relative error of at most 0.006.
Values may be sent and summed in bfloat16 or wider, within the bound.
No kernel may reach another device: no remote copies, remote signals or barrier semaphores. Data moves between devices by JAX's collectives and lax.ppermute only.
A program may use at most 192 MiB of HBM per device.

v0:
```python
import math

import jax
import jax.numpy as jnp
from jax import lax
from jax.sharding import PartitionSpec as P


def slot_positions(column, destinations, capacity):
    onehot = (column[:, None] == jnp.arange(destinations, dtype=jnp.int32)[None, :]).astype(
        jnp.int32
    )
    before = jnp.cumsum(onehot, axis=0) - onehot
    slot_rank = jnp.sum(before * onehot, axis=1)
    return column * capacity + slot_rank


def take_rows(table, slot_owner):
    present = slot_owner >= 0
    selected_items = jnp.take(table, jnp.maximum(slot_owner, 0), axis=0)
    return jnp.where(present[:, None], selected_items, jnp.zeros_like(selected_items))


def local(
    queries,
    cache_keys,
    stored_value_cache,
    lengths,
    residual,
    target,
    gate_weight,
    up_weight,
    down_weight,
):
    rows_dev = cache_keys.shape[0]
    cache_len = cache_keys.shape[1]
    kv_local = cache_keys.shape[2]
    head_dim = cache_keys.shape[3]
    heads_per_group = queries.shape[1] // kv_local
    score_scale = 1.0 / math.sqrt(head_dim)
    grouped_heads = queries.reshape(rows_dev, kv_local, heads_per_group, head_dim)
    scores = (
        jnp.einsum("rgqd,rlgd->rgql", grouped_heads, cache_keys, preferred_element_type=jnp.float32)
        * score_scale
    )
    in_cache = (jnp.arange(cache_len, dtype=jnp.int32)[None, :] < lengths[:, None])[
        :, None, None, :
    ]
    masked = jnp.where(in_cache, scores, -1e30)
    row_peak = jnp.max(masked, axis=-1, keepdims=True)
    raw_weights = jnp.where(in_cache, jnp.exp(masked - row_peak), 0.0)
    weights_bf = (raw_weights / jnp.sum(raw_weights, axis=-1, keepdims=True)).astype(jnp.bfloat16)
    attended = jnp.einsum(
        "rgql,rlgd->rgqd", weights_bf, stored_value_cache, preferred_element_type=jnp.float32
    )
    attended = attended.reshape(rows_dev, kv_local * heads_per_group * head_dim)
    mixed_rows = (residual.astype(jnp.float32) + attended).astype(jnp.bfloat16)
    gathered = lax.all_gather(mixed_rows, "attn", axis=0, tiled=True)
    gate_part = jnp.dot(gathered, gate_weight, preferred_element_type=jnp.float32)
    up_part = jnp.dot(gathered, up_weight, preferred_element_type=jnp.float32)
    gate_sum, up_sum = lax.psum((gate_part, up_part), "ffn")
    hidden = (jax.nn.silu(gate_sum) * up_sum).astype(jnp.bfloat16)
    devices = lax.axis_size("attn")
    my_index = lax.axis_index("attn")
    total_rows = gathered.shape[0]
    slot_count = 2 * devices * rows_dev
    position = slot_positions(target[:, 0], 2 * devices, rows_dev)
    slot_owner = (
        jnp.full((slot_count,), -1, jnp.int32)
        .at[position]
        .set(jnp.arange(total_rows, dtype=jnp.int32))
    )
    my_slots = lax.dynamic_slice_in_dim(slot_owner, my_index * (2 * rows_dev), 2 * rows_dev)
    summed = lax.psum_scatter(
        jnp.dot(take_rows(hidden, slot_owner), down_weight, preferred_element_type=jnp.float32),
        "attn",
        scatter_dimension=0,
        tiled=True,
    )
    result = (take_rows(gathered, my_slots).astype(jnp.float32) + summed).astype(jnp.bfloat16)
    return result


def solution(mesh):
    return jax.shard_map(
        local,
        mesh=mesh,
        in_specs=(
            P(("parts", "attn"), "ffn", None),
            P(("parts", "attn"), None, "ffn", None),
            P(("parts", "attn"), None, "ffn", None),
            P(("parts", "attn")),
            P(("parts", "attn"), "ffn"),
            P("parts", None),
            P("ffn", "attn"),
            P("ffn", "attn"),
            P("attn", "ffn"),
        ),
        out_specs=P(("parts", "attn"), "ffn"),
        check_vma=False,
    )
```

profile of v0, /device:TPU:0, one launch (start us, length us, event | category | flops | bytes accessed | tf_op | source)
XLA Modules:
  0.0 185.3 jit_solution(15794582299999025207)
XLA Ops:
  6.5 0.8 iota_compare_fusion.1
  7.3 0.3 copy-done
  7.6 1.2 fusion.2
  8.8 0.2 fusion.25
  9.0 1.5 fusion.10
  10.6 0.9 fusion.15
  11.5 33.0 %all_gather.3 = bf16[64,4096]{1,0:T(8,128)(2,1)S(1)} all-gather(bf16[8,4096]{1,0:T(8,128)(2,1)S(1)} %fusion.15), channel_id=1, replica_groups=mesh['parts'=2,'attn'=8,'ffn'=2] {'attn'}, dimensions={0}, use_global_device_ids=true | all-gather | bytes 589824 | tf_op jit(solution)/shard_map/all_gather | solution.py:58
  44.5 12.1 %fusion.27 = f32[64,3328]{1,0:T(8,128)} fusion(bf16[64,4096]{1,0:T(8,128)(2,1)S(1)} %all_gather.3, bf16[4096,3328]{1,0:T(8,128)(2,1)} %param.16), kind=kOutput, calls=%fused_computation.48 | convolution fusion | flops 1744830464 | bytes 28639232 | tf_op jit(solution)/shard_map/dot_general | solution.py:60
  56.6 12.2 %fusion.26 = f32[64,3328]{1,0:T(8,128)} fusion(bf16[64,4096]{1,0:T(8,128)(2,1)S(1)} %all_gather.3, bf16[4096,3328]{1,0:T(8,128)(2,1)} %param.15), kind=kOutput, calls=%fused_computation.47 | convolution fusion | flops 1744830464 | bytes 28639232 | tf_op jit(solution)/shard_map/dot_general | solution.py:59
  68.8 0.0 all-reduce.3.cloned.1.call-update
  68.8 0.0 reduce-scatter.2.cloned.1.call-start
  68.9 0.1 fusion.17
  69.0 0.1 reduce_window_sum.11
  69.0 0.2 select_reduce_fusion
  69.3 0.8 scatter_custom_fusion
  70.1 20.7 %all-reduce.3.cloned.1.call-done = (f32[64,3328]{1,0:T(8,128)}, f32[64,3328]{1,0:T(8,128)}) async-done(((f32[64,3328]{1,0:T(8,128)}, f32[64,3328]{1,0:T(8,128)}), (f32[64,3328]{1,0:T(8,128)}, f32[64,3328]{1,0:T(8,128)})) %all-reduce.3.cloned.1.call-update) | async-done | bytes 1703952 | tf_op jit(solution)/shard_map/psum | solution.py:61
  90.8 1.6 multiply_convert_fusion
  92.4 1.1 gather_fusion.1
  93.5 13.9 %fusion.5 = f32[128,4096]{1,0:T(8,128)} fusion(bf16[3328,4096]{1,0:T(8,128)(2,1)} %param.17, bf16[128,3328]{1,0:T(8,128)(2,1)S(1)} %gather_fusion.1, pred[128]{0:T(512)(128)(4,1)S(1)} %get-tuple-element.11, pred[128]{0:T(512)(128)(4,1)S(1)} %get-tuple-element.10), kind=kOutput, calls=%fused_computation.9 | convolution fusion | flops 3490512896 | bytes 30212352 | tf_op jit(solution)/shard_map/dot_general | solution.py:75
  107.4 0.0 reduce-scatter.2.cloned.1.call-update
  107.5 0.1 broadcast_compare_fusion.2
  107.6 0.6 gather_fusion
  108.2 68.6 %reduce-scatter.2.cloned.1.call-done = f32[16,4096]{1,0:T(8,128)} async-done(((f32[128,4096]{1,0:T(8,128)}), f32[16,4096]{1,0:T(8,128)}) %reduce-scatter.2.cloned.1.call-update) | async-done | bytes 262160 | tf_op jit(solution)/shard_map/reduce_scatter | solution.py:74
  176.8 1.7 add_convert_fusion
  (12 shorter events, 0.0 us)
Async XLA Ops:
  6.5 1.1 copy-start
  6.5 84.2 %all-reduce.3.cloned.1.call-start = ((), (), s32[]{:S(2)}) async-start(), calls=%async_computation.2 | async-start | bytes 3407872 | tf_op jit(solution)/shard_map/psum | solution.py:61
  44.5 24.4 %copy-start.2 = (s32[64,1]{0,1:T(1,128)S(1)}, s32[64,1]{0,1:T(1,128)}, u32[]{:S(2)}) copy-start(s32[64,1]{0,1:T(1,128)} %param.14) | copy-start | bytes 772
  56.6 121.9 %copy-start.1 = (bf16[8,128,2,128]{3,2,1,0:T(2,128)(2,1)S(1)}, bf16[8,128,2,128]{3,2,1,0:T(2,128)(2,1)}, u32[]{:S(2)}) copy-start(bf16[8,128,2,128]{3,2,1,0:T(2,128)(2,1)} %param.10) | copy-start | bytes 1572868
  68.8 108.0 %reduce-scatter.2.cloned.1.call-start = ((), (), s32[]{:S(2)}) async-start(), calls=%async_computation.1 | async-start | bytes 2359296 | tf_op jit(solution)/shard_map/reduce_scatter | solution.py:74
Sparse Core Ops, SparseCore 0:
  68.9 21.7 all-reduce.2
  107.6 69.1 reduce-scatter.1
where the time goes:
time: 186 us; the launch traced here: 185 us
  waiting for transfers between devices  89.3 us (48%)
  matrix products  40.9 us (22%)
  blocking collectives  33 us (18%)
  between operations  13.5 us (7%)
  other arithmetic  5.74 us (3%)
  local copies, waits for them, and re-layouts  2.78 us (1%)
    reduce_scatter x1, waiting for transfers between devices, local(): lax.psum_scatter(jnp.dot(take_rows(hidden, slot_owner), down_weight, pref...  68.6 us
    all_gather x1, blocking collectives, local(): gathered = lax.all_gather(mixed_rows, 'attn', axis=0, tiled=True)  33 us
    psum x1, waiting for transfers between devices, local(): gate_sum, up_sum = lax.psum((gate_part, up_part), 'ffn')  20.7 us
    dot_general x1, matrix products, local(): jnp.dot(take_rows(hidden, slot_owner), down_weight, preferred_element_typ...  13.9 us
    dot_general x1, matrix products, local(): jnp.dot(gathered, gate_weight, preferred_element_type=jnp.float32)  12.2 us
    dot_general x1, matrix products, local(): up_part = jnp.dot(gathered, up_weight, preferred_element_type=jnp.float32)  12.1 us
  transfers between devices with their start and end apart: 2, of which 2 were waited for; matrix products, arithmetic and copies ran while one was open for 1% of the time, Pallas kernels for 0%

commit v1 on v0

--- a/solution.py
+++ b/solution.py
@@ -4,6 +4,8 @@
 import jax.numpy as jnp
 from jax import lax
 from jax.sharding import PartitionSpec as P
+
+AXIS = "attn"
 
 
 def slot_positions(column, destinations, capacity):
@@ -15,23 +17,42 @@
     return column * capacity + slot_rank
 
 
-def take_rows(table, slot_owner):
-    present = slot_owner >= 0
-    selected_items = jnp.take(table, jnp.maximum(slot_owner, 0), axis=0)
-    return jnp.where(present[:, None], selected_items, jnp.zeros_like(selected_items))
+def grid_of(devices):
+    nx = 1
+    while 4 * nx * nx < devices:
+        nx *= 2
+    if devices % nx:
+        nx = 1
+    return devices // nx, nx
 
 
-def local(
-    queries,
-    cache_keys,
-    stored_value_cache,
-    lengths,
-    residual,
-    target,
-    gate_weight,
-    up_weight,
-    down_weight,
-):
+def gather_rows(rows, devices):
+    nz, nx = grid_of(devices)
+    blocks = [rows]
+    for shift in range(1, nz):
+        perm = [
+            (z * nx + x, ((z + shift) % nz) * nx + x) for z in range(nz) for x in range(nx)
+        ]
+        blocks.append(lax.ppermute(rows, AXIS, perm))
+    column = jnp.stack(blocks)
+    planes = [column]
+    for shift in range(1, nx):
+        perm = [
+            (z * nx + x, z * nx + (x + shift) % nx) for z in range(nz) for x in range(nx)
+        ]
+        planes.append(lax.ppermute(column, AXIS, perm))
+    table = jnp.stack(planes).reshape((devices,) + rows.shape)
+    me = lax.axis_index(AXIS)
+    my_z, my_x = me // nx, me % nx
+    owner = jnp.arange(devices, dtype=jnp.int32)
+    dz = (my_z - owner // nx) % nz
+    dx = (my_x - owner % nx) % nx
+    return jnp.take(table, dx * nz + dz, axis=0, mode="clip").reshape(
+        (devices * rows.shape[0], rows.shape[1])
+    )
+
+
+def attend(queries, cache_keys, stored_value_cache, lengths, residual):
     rows_dev = cache_keys.shape[0]
     cache_len = cache_keys.shape[1]
     kv_local = cache_keys.shape[2]
@@ -54,31 +75,50 @@
         "rgql,rlgd->rgqd", weights_bf, stored_value_cache, preferred_element_type=jnp.float32
     )
     attended = attended.reshape(rows_dev, kv_local * heads_per_group * head_dim)
-    mixed_rows = (residual.astype(jnp.float32) + attended).astype(jnp.bfloat16)
-    gathered = lax.all_gather(mixed_rows, "attn", axis=0, tiled=True)
+    return (residual.astype(jnp.float32) + attended).astype(jnp.bfloat16)
+
+
+def local(
+    queries,
+    cache_keys,
+    stored_value_cache,
+    lengths,
+    residual,
+    target,
+    gate_weight,
+    up_weight,
+    down_weight,
+):
+    rows_dev = cache_keys.shape[0]
+    devices = lax.axis_size(AXIS)
+    me = lax.axis_index(AXIS)
+    mixed_rows = attend(queries, cache_keys, stored_value_cache, lengths, residual)
+    gathered = gather_rows(mixed_rows, devices)
+    total_rows, features = gathered.shape
     gate_part = jnp.dot(gathered, gate_weight, preferred_element_type=jnp.float32)
     up_part = jnp.dot(gathered, up_weight, preferred_element_type=jnp.float32)
-    gate_sum, up_sum = lax.psum((gate_part, up_part), "ffn")
+    mine = jnp.stack([gate_part, up_part])
+    other = lax.ppermute(mine.astype(jnp.bfloat16), "ffn", [(0, 1), (1, 0)])
+    gate_sum, up_sum = mine + other.astype(jnp.float32)
     hidden = (jax.nn.silu(gate_sum) * up_sum).astype(jnp.bfloat16)
-    devices = lax.axis_size("attn")
-    my_index = lax.axis_index("attn")
-    total_rows = gathered.shape[0]
+    down = jnp.dot(hidden, down_weight, preferred_element_type=jnp.float32)
+    share = features // devices
+    pieces = jnp.moveaxis(
+        down.astype(jnp.bfloat16).reshape(total_rows, devices, share), 1, 0
+    )
+    landed = lax.all_to_all(pieces, AXIS, split_axis=0, concat_axis=0)
+    summed = jnp.sum(landed.astype(jnp.float32), axis=0)
+    mixed_share = lax.dynamic_slice_in_dim(gathered, me * share, share, axis=1)
+    finished = (mixed_share.astype(jnp.float32) + summed).astype(jnp.bfloat16)
     slot_count = 2 * devices * rows_dev
     position = slot_positions(target[:, 0], 2 * devices, rows_dev)
-    slot_owner = (
-        jnp.full((slot_count,), -1, jnp.int32)
-        .at[position]
-        .set(jnp.arange(total_rows, dtype=jnp.int32))
+    chosen = (jnp.arange(slot_count, dtype=jnp.int32)[:, None] == position[None, :]).astype(
+        jnp.bfloat16
     )
-    my_slots = lax.dynamic_slice_in_dim(slot_owner, my_index * (2 * rows_dev), 2 * rows_dev)
-    summed = lax.psum_scatter(
-        jnp.dot(take_rows(hidden, slot_owner), down_weight, preferred_element_type=jnp.float32),
-        "attn",
-        scatter_dimension=0,
-        tiled=True,
-    )
-    result = (take_rows(gathered, my_slots).astype(jnp.float32) + summed).astype(jnp.bfloat16)
-    return result
+    slots = jnp.dot(chosen, finished, preferred_element_type=jnp.float32).astype(jnp.bfloat16)
+    slots = slots.reshape(devices, 2 * rows_dev, share)
+    mine_out = lax.all_to_all(slots, AXIS, split_axis=0, concat_axis=0)
+    return jnp.moveaxis(mine_out, 0, 1).reshape(2 * rows_dev, features)
 
 
 def solution(mesh):

time: 186 us -> 92.1 us (0.50)
  waiting for transfers between devices: 89.3 us -> 26.4 us
  blocking collectives: 33 us -> 10.8 us
  between operations: 13.5 us -> 0.11 us
  starting transfers between devices: 0.04 us -> 12.6 us
  matrix products: 40.9 us -> 36.7 us
  other arithmetic: 5.74 us -> 2.73 us
    reduce_scatter x1 -> x0, waiting for transfers between devices: 68.6 us -> none  [local(): lax.psum_scatter(jnp.dot(take_rows(hidden, slot_owner), down_weight, pref...]
    all_gather x1 -> x0, blocking collectives: 33 us -> none  [local(): gathered = lax.all_gather(mixed_rows, 'attn', axis=0, tiled=True)]
    psum x1 -> x0, waiting for transfers between devices: 20.7 us -> none  [local(): gate_sum, up_sum = lax.psum((gate_part, up_part), 'ffn')]
    all_to_all x0 -> x1, waiting for transfers between devices: none -> 14.4 us  [local(): landed = lax.all_to_all(pieces, AXIS, split_axis=0, concat_axis=0)]
    ppermute x0 -> x5, waiting for transfers between devices: none -> 12 us  [the longest x1 6.23 us: gather_rows(): planes.append(lax.ppermute(column, AXIS, perm))]
    all_to_all x0 -> x1, blocking collectives: none -> 10.8 us  [local(): mine_out = lax.all_to_all(slots, AXIS, split_axis=0, concat_axis=0)]
    ppermute x0 -> x5, starting transfers between devices: none -> 8.69 us  [the longest x3 7.01 us: gather_rows(): blocks.append(lax.ppermute(rows, AXIS, perm))]
    all_to_all x0 -> x1, starting transfers between devices: none -> 3.89 us  [local(): landed = lax.all_to_all(pieces, AXIS, split_axis=0, concat_axis=0)]
  transfers between devices with their start and end apart: 2 -> 6, of which waited for: 2 -> 6; matrix products, arithmetic and copies ran while one was open for 1% -> 0% of each run, Pallas kernels for 0% -> 0%
where the time goes in v1:
time: 92.1 us; the launch traced here: 91.7 us
  matrix products  36.7 us (40%)
  waiting for transfers between devices  26.4 us (29%)
  starting transfers between devices  12.6 us (14%)
  blocking collectives  10.8 us (12%)
  other arithmetic  2.73 us (3%)
  local copies, waits for them, and re-layouts  2.37 us (3%)
    all_to_all x1, waiting for transfers between devices, local(): landed = lax.all_to_all(pieces, AXIS, split_axis=0, concat_axis=0)  14.4 us
    dot_general x1, matrix products, local(): down = jnp.dot(hidden, down_weight, preferred_element_type=jnp.float32)  11.3 us
    dot_general x1, matrix products, local(): jnp.dot(gathered, gate_weight, preferred_element_type=jnp.float32)  11.3 us
    dot_general x1, matrix products, local(): up_part = jnp.dot(gathered, up_weight, preferred_element_type=jnp.float32)  11.2 us
    all_to_all x1, blocking collectives, local(): mine_out = lax.all_to_all(slots, AXIS, split_axis=0, concat_axis=0)  10.8 us
    ppermute x3, starting transfers between devices, gather_rows(): blocks.append(lax.ppermute(rows, AXIS, perm))  7.01 us
    ppermute x1, waiting for transfers between devices, gather_rows(): planes.append(lax.ppermute(column, AXIS, perm))  6.23 us
    all_to_all x1, starting transfers between devices, local(): landed = lax.all_to_all(pieces, AXIS, split_axis=0, concat_axis=0)  3.89 us
  transfers between devices with their start and end apart: 6, of which 6 were waited for; matrix products, arithmetic and copies ran while one was open for 0% of the time, Pallas kernels for 0%

profile of v1, /device:TPU:0, one launch (start us, length us, event | category | flops | bytes accessed | tf_op | source)
XLA Modules:
  0.0 91.7 jit_solution(3565850510332222745)
XLA Ops:
  0.0 0.8 iota_compare_fusion.3
  0.8 0.3 copy-done
  1.1 1.2 %fusion.3 = f32[8,2,16,128]{3,2,1,0:T(8,128)S(1)} fusion(bf16[8,2,16,128]{3,2,1,0:T(8,128)(2,1)} %bitcast.68, bf16[8,128,2,128]{3,2,1,0:T(2,128)(2,1)S(1)} %copy-done, pred[8,128]{1,0:T(8,128)(4,1)S(1)} %iota_compare_fusion.3), kind=kOutput, calls=%fused_computation.11 | convolution fusion | flops 8454144 | bytes 721920 | tf_op jit(solution)/shard_map/rgqd,rlgd->rgql/dot_general | solution.py:64
  2.3 0.2 fusion.32
  2.5 1.5 %fusion.8 = f32[8,2,16,128]{3,2,1,0:T(8,128)S(1)} fusion(bf16[8,128,2,128]{3,2,1,0:T(2,128)(2,1)} %param.11, f32[8,2,16]{2,1,0:T(2,128)S(1)} %fusion.32, f32[8,2,16,128]{3,2,1,0:T(8,128)S(1)} %fusion.3, pred[8,128]{1,0:T(8,128)(4,1)S(1)} %iota_compare_fusion.3), kind=kOutput, calls=%fused_computation.21 | convolution fusion | flops 8520063 | bytes 788480 | tf_op jit(solution)/shard_map/rgql,rlgd->rgqd/dot_general | solution.py:74
  4.0 0.9 %fusion.13 = bf16[8,4096]{1,0:T(8,128)(2,1)S(1)} fusion(f32[1,8,32,128]{3,2,1,0:T(8,128)S(1)} %bitcast.64, bf16[8,4096]{1,0:T(8,128)(2,1)} %param.13), kind=kLoop, calls=%fused_computation.27 | loop fusion | flops 98304 | bytes 262144 | tf_op jit(solution)/shard_map/convert_element_type | solution.py:78
  5.0 3.1 %collective-permute-start = (bf16[8,4096]{1,0:T(8,128)(2,1)S(1)}, bf16[8,4096]{1,0:T(8,128)(2,1)S(1)}, u32[]{:S(2)}, u32[]{:S(2)}) collective-permute-start(bf16[8,4096]{1,0:T(8,128)(2,1)S(1)} %fusion.13), channel_id=1, source_target_pairs={{0,4},{2,6},{4,8},{6,10},{8,12},{10,14},{12,0},{14,2},{1,5},{3,7},... | collective-permute-start | bytes 196616 | tf_op jit(solution)/shard_map/ppermute | solution.py:36
  8.0 2.6 %collective-permute-start.1 = (bf16[8,4096]{1,0:T(8,128)(2,1)S(1)}, bf16[8,4096]{1,0:T(8,128)(2,1)S(1)}, u32[]{:S(2)}, u32[]{:S(2)}) collective-permute-start(bf16[8,4096]{1,0:T(8,128)(2,1)S(1)} %fusion.13), channel_id=1, source_target_pairs={{0,8},{2,10},{4,12},{6,14},{8,0},{10,2},{12,4},{14,6},{1,9},{3,11}... | collective-permute-start | bytes 196616 | tf_op jit(solution)/shard_map/ppermute | solution.py:36
  10.6 1.3 %collective-permute-start.2 = (bf16[8,4096]{1,0:T(8,128)(2,1)S(1)}, bf16[8,4096]{1,0:T(8,128)(2,1)S(1)}, u32[]{:S(2)}, u32[]{:S(2)}) collective-permute-start(bf16[8,4096]{1,0:T(8,128)(2,1)S(1)} %fusion.13), channel_id=1, source_target_pairs={{0,12},{2,14},{4,0},{6,2},{8,4},{10,6},{12,8},{14,10},{1,13},{3,15... | collective-permute-start | bytes 196616 | tf_op jit(solution)/shard_map/ppermute | solution.py:36
  12.0 0.6 collective-permute-done
  12.6 2.5 %collective-permute-done.1 = bf16[8,4096]{1,0:T(8,128)(2,1)S(1)} collective-permute-done((bf16[8,4096]{1,0:T(8,128)(2,1)S(1)}, bf16[8,4096]{1,0:T(8,128)(2,1)S(1)}, u32[]{:S(2)}, u32[]{:S(2)}) %collective-permute-start.1) | collective-permute-done | bytes 65568 | tf_op jit(solution)/shard_map/ppermute | solution.py:36
  15.1 0.2 collective-permute-done.2
  15.4 1.6 %collective-permute-start.3 = (bf16[4,8,4096]{2,1,0:T(8,128)(2,1)S(1)}, bf16[4,8,4096]{2,1,0:T(8,128)(2,1)S(1)}, u32[]{:S(2)}, u32[]{:S(2)}) collective-permute-start(bf16[4,8,4096]{2,1,0:T(8,128)(2,1)S(1)} %get-tuple-element.6), channel_id=1, source_target_pairs={{0,2},{2,0},{4,6},{6,4},{8,10},{10,8},{12,14},{14,12},{1,3},{3,1},... | collective-permute-start | bytes 786440 | tf_op jit(solution)/shard_map/ppermute | solution.py:43
  17.0 6.2 %collective-permute-done.3 = bf16[4,8,4096]{2,1,0:T(8,128)(2,1)S(1)} collective-permute-done((bf16[4,8,4096]{2,1,0:T(8,128)(2,1)S(1)}, bf16[4,8,4096]{2,1,0:T(8,128)(2,1)S(1)}, u32[]{:S(2)}, u32[]{:S(2)}) %collective-permute-start.3) | collective-permute-done | bytes 262176 | tf_op jit(solution)/shard_map/ppermute | solution.py:43
  23.3 0.6 gather_fusion
  23.9 11.2 %convolution_bitcast_fusion = f32[1,64,3328]{2,1,0:T(8,128)S(1)} fusion(bf16[4096,3328]{1,0:T(8,128)(2,1)} %param.16, bf16[8,8,4096]{2,1,0:T(8,128)(2,1)S(1)} %gather_fusion), kind=kOutput, calls=%fused_computation.2 | convolution fusion | flops 1744830464 | bytes 28639232 | tf_op jit(solution)/shard_map/dot_general | solution.py:99
  35.1 11.3 %convolution_bitcast_fusion.1 = f32[1,64,3328]{2,1,0:T(8,128)S(1)} fusion(bf16[4096,3328]{1,0:T(8,128)(2,1)} %param.15, bf16[8,8,4096]{2,1,0:T(8,128)(2,1)S(1)} %gather_fusion), kind=kOutput, calls=%fused_computation.3 | convolution fusion | flops 1744830464 | bytes 28639232 | tf_op jit(solution)/shard_map/dot_general | solution.py:98
  46.6 2.4 %collective-permute-done.4 = bf16[2,64,3328]{2,1,0:T(8,128)(2,1)S(1)} collective-permute-done((bf16[2,64,3328]{2,1,0:T(8,128)(2,1)S(1)}, bf16[2,64,3328]{2,1,0:T(8,128)(2,1)S(1)}, u32[]{:S(2)}, u32[]{:S(2)}) %collective-permute-start.4) | collective-permute-done | bytes 852000 | tf_op jit(solution)/shard_map/ppermute | solution.py:101
  49.1 11.3 %convolution_convert_fusion = bf16[64,4096]{1,0:T(8,128)(2,1)S(1)} fusion(bf16[3328,4096]{1,0:T(8,128)(2,1)} %param.17, f32[2,64,3328]{2,1,0:T(8,128)S(1)} %convert_add_fusion), kind=kOutput, calls=%fused_computation.4 | convolution fusion | flops 1746370560 | bytes 29491200 | tf_op jit(solution)/shard_map/dot_general | solution.py:104
  60.4 0.8 copy.26
  61.3 3.9 %all-to-all-start = ((bf16[8,64,512]{2,1,0:T(8,128)(2,1)}), bf16[8,64,512]{2,1,0:T(8,128)(2,1)S(1)}, u32[]{:S(2)}, u32[]{:S(2)}) async-start(bf16[8,64,512]{2,1,0:T(8,128)(2,1)} %bitcast.56), calls=%async_computation | async-start | bytes 1048576 | tf_op jit(solution)/shard_map/all_to_all | solution.py:109
  65.5 14.4 %all-to-all-done = bf16[8,64,512]{2,1,0:T(8,128)(2,1)S(1)} async-done(((bf16[8,64,512]{2,1,0:T(8,128)(2,1)}), bf16[8,64,512]{2,1,0:T(8,128)(2,1)S(1)}, u32[]{:S(2)}, u32[]{:S(2)}) %all-to-all-start) | async-done | bytes 524320 | tf_op jit(solution)/shard_map/all_to_all | solution.py:109
  80.2 10.8 %all_to_all.10 = bf16[8,16,512]{2,1,0:T(8,128)(2,1)S(1)} all-to-all(bf16[8,16,512]{2,1,0:T(8,128)(2,1)S(1)} %bitcast.60), channel_id=1, replica_groups=mesh['parts'=2,'attn'=8,'ffn'=2] {'attn'}, dimensions={0} | all-to-all | bytes 262144 | tf_op jit(solution)/shard_map/all_to_all | solution.py:120
  91.0 0.7 copy.18
  (18 shorter events, 1.1 us)
Async XLA Ops:
  0.0 1.1 %copy-start = (bf16[8,128,2,128]{3,2,1,0:T(2,128)(2,1)S(1)}, bf16[8,128,2,128]{3,2,1,0:T(2,128)(2,1)}, u32[]{:S(2)}) copy-start(bf16[8,128,2,128]{3,2,1,0:T(2,128)(2,1)} %param.10) | copy-start | bytes 1572868
  5.0 7.6 %collective-permute-start = (bf16[8,4096]{1,0:T(8,128)(2,1)S(1)}, bf16[8,4096]{1,0:T(8,128)(2,1)S(1)}, u32[]{:S(2)}, u32[]{:S(2)}) collective-permute-start(bf16[8,4096]{1,0:T(8,128)(2,1)S(1)} %fusion.13), channel_id=1, source_target_pairs={{0,4},{2,6},{4,8},{6,10},{8,12},{10,14},{12,0},{14,2},{1,5},{3,7},... | collective-permute-start | bytes 196616 | tf_op jit(solution)/shard_map/ppermute | solution.py:36
  8.0 7.1 %collective-permute-start.1 = (bf16[8,4096]{1,0:T(8,128)(2,1)S(1)}, bf16[8,4096]{1,0:T(8,128)(2,1)S(1)}, u32[]{:S(2)}, u32[]{:S(2)}) collective-permute-start(bf16[8,4096]{1,0:T(8,128)(2,1)S(1)} %fusion.13), channel_id=1, source_target_pairs={{0,8},{2,10},{4,12},{6,14},{8,0},{10,2},{12,4},{14,6},{1,9},{3,11}... | collective-permute-start | bytes 196616 | tf_op jit(solution)/shard_map/ppermute | solution.py:36
  10.6 4.7 %collective-permute-start.2 = (bf16[8,4096]{1,0:T(8,128)(2,1)S(1)}, bf16[8,4096]{1,0:T(8,128)(2,1)S(1)}, u32[]{:S(2)}, u32[]{:S(2)}) collective-permute-start(bf16[8,4096]{1,0:T(8,128)(2,1)S(1)} %fusion.13), channel_id=1, source_target_pairs={{0,12},{2,14},{4,0},{6,2},{8,4},{10,6},{12,8},{14,10},{1,13},{3,15... | collective-permute-start | bytes 196616 | tf_op jit(solution)/shard_map/ppermute | solution.py:36
  15.4 7.9 %collective-permute-start.3 = (bf16[4,8,4096]{2,1,0:T(8,128)(2,1)S(1)}, bf16[4,8,4096]{2,1,0:T(8,128)(2,1)S(1)}, u32[]{:S(2)}, u32[]{:S(2)}) collective-permute-start(bf16[4,8,4096]{2,1,0:T(8,128)(2,1)S(1)} %get-tuple-element.6), channel_id=1, source_target_pairs={{0,2},{2,0},{4,6},{6,4},{8,10},{10,8},{12,14},{14,12},{1,3},{3,1},... | collective-permute-start | bytes 786440 | tf_op jit(solution)/shard_map/ppermute | solution.py:43
  35.1 56.6 %copy-start.1 = (bf16[8,128,2,128]{3,2,1,0:T(2,128)(2,1)S(1)}, bf16[8,128,2,128]{3,2,1,0:T(2,128)(2,1)}, u32[]{:S(2)}) copy-start(bf16[8,128,2,128]{3,2,1,0:T(2,128)(2,1)} %param.10) | copy-start | bytes 1572868
  46.4 18.8 %copy-start.2 = (s32[64,1]{0,1:T(1,128)S(1)}, s32[64,1]{0,1:T(1,128)}, u32[]{:S(2)}) copy-start(s32[64,1]{0,1:T(1,128)} %param.14) | copy-start | bytes 772
  46.5 2.4 %collective-permute-start.4 = (bf16[2,64,3328]{2,1,0:T(8,128)(2,1)S(1)}, bf16[2,64,3328]{2,1,0:T(8,128)(2,1)S(1)}, u32[]{:S(2)}, u32[]{:S(2)}) collective-permute-start(bf16[2,64,3328]{2,1,0:T(8,128)(2,1)S(1)} %fusion.1), channel_id=1, source_target_pairs={{0,1},{1,0},{2,3},{3,2},{4,5},{5,4},{6,7},{7,6},{8,9},{9,8},{10,11... | collective-permute-start | bytes 2555912 | tf_op jit(solution)/shard_map/ppermute | solution.py:101
  61.3 18.7 %all-to-all-start = ((bf16[8,64,512]{2,1,0:T(8,128)(2,1)}), bf16[8,64,512]{2,1,0:T(8,128)(2,1)S(1)}, u32[]{:S(2)}, u32[]{:S(2)}) async-start(bf16[8,64,512]{2,1,0:T(8,128)(2,1)} %bitcast.56), calls=%async_computation | async-start | bytes 1048576 | tf_op jit(solution)/shard_map/all_to_all | solution.py:109

commit v2 on v0

v2 whole, which is shorter than its diff:
```python
import functools
import math

import jax
import jax.numpy as jnp
from jax import lax
from jax.experimental import pallas as pl
from jax.experimental.pallas import tpu as pltpu
from jax.sharding import PartitionSpec as P

AXIS = "attn"
TILE = 256
MIB = 1 << 20
VMEM = pl.BlockSpec(memory_space=pltpu.VMEM)
SMEM = pl.BlockSpec(memory_space=pltpu.SMEM)
ANY = pl.BlockSpec(memory_space=pl.ANY)
F32 = jnp.float32
BF16 = jnp.bfloat16


def params(mib):
    return pltpu.CompilerParams(vmem_limit_bytes=mib * MIB)


def cost(flops, moved):
    return pl.CostEstimate(flops=flops, bytes_accessed=moved, transcendentals=0)


def grid_of(devices):
    nx = 1
    while 4 * nx * nx < devices:
        nx *= 2
    if devices % nx:
        nx = 1
    return devices // nx, nx


def shift_z(devices, shift):
    nz, nx = grid_of(devices)
    return [(z * nx + x, ((z + shift) % nz) * nx + x) for z in range(nz) for x in range(nx)]


def shift_x(devices, shift):
    nz, nx = grid_of(devices)
    return [(z * nx + x, z * nx + (x + shift) % nx) for z in range(nz) for x in range(nx)]


def attend_kernel(kv, lengths, q_ref, k_ref, v_ref, res_ref, out_ref, att_ref):
    rows, heads, dim = q_ref.shape
    span = k_ref.shape[1]
    per_group = heads // kv
    column = lax.broadcasted_iota(jnp.int32, (heads, span), 1)
    head = lax.broadcasted_iota(jnp.int32, (heads, span), 0)
    right_group = (column % kv) == (head // per_group)
    position = column // kv
    for r in range(rows):
        scores = lax.dot_general(
            q_ref[r], k_ref[r], (((1,), (1,)), ((), ())), preferred_element_type=F32
        ) * (1.0 / math.sqrt(dim))
        live = right_group & (position < lengths[r])
        masked = jnp.where(live, scores, -1e30)
        peak = jnp.max(masked, axis=-1, keepdims=True)
        raw = jnp.where(live, jnp.exp(masked - peak), 0.0)
        probs = (raw / jnp.sum(raw, axis=-1, keepdims=True)).astype(BF16)
        att_ref[r * heads : (r + 1) * heads, :] = jnp.dot(
            probs, v_ref[r], preferred_element_type=F32
        )
    for h in range(heads):
        at = slice(h * dim, (h + 1) * dim)
        mine = att_ref[pl.ds(h, rows, stride=heads), :]
        out_ref[:, at] = (res_ref[:, at].astype(F32) + mine).astype(BF16)


def attend(queries, cache_keys, stored_value_cache, lengths, residual):
    rows, heads, dim = queries.shape
    kv = cache_keys.shape[2]
    span = cache_keys.shape[1] * kv
    return pl.pallas_call(
        functools.partial(attend_kernel, kv),
        out_shape=jax.ShapeDtypeStruct((rows, heads * dim), BF16),
        in_specs=[SMEM, VMEM, VMEM, VMEM, VMEM],
        out_specs=VMEM,
        scratch_shapes=[pltpu.VMEM((rows * heads, dim), F32)],
        compiler_params=params(8),
        cost_estimate=cost(rows * heads * span * dim * 4, rows * span * dim * 4),
        name="attention",
    )(
        lengths,
        queries,
        cache_keys.reshape(rows, span, dim),
        stored_value_cache.reshape(rows, span, dim),
        residual,
    )


def tile_at(index):
    return pl.ds(pl.multiple_of(index * TILE, TILE), TILE)


def gate_up_kernel(devices, depth, own_ref, far_ref, g_hbm, u_hbm, part_ref, rows_ref, buf, sems):
    nz, nx = grid_of(devices)
    columns = g_hbm.shape[1]
    tiles = columns // TILE

    def copies(i, slot):
        return (
            pltpu.make_async_copy(g_hbm.at[:, tile_at(i)], buf.at[slot, 0], sems.at[slot, 0]),
            pltpu.make_async_copy(u_hbm.at[:, tile_at(i)], buf.at[slot, 1], sems.at[slot, 1]),
        )

    for i in range(min(depth, tiles)):
        for c in copies(i, i):
            c.start()
    me = lax.axis_index(AXIS)
    my_z, my_x = me // nx, me % nx
    per = own_ref.shape[1]
    for dz in range(nz):
        z = lax.rem(my_z - dz + nz, nz)
        a, b = own_ref[dz].astype(F32), far_ref[dz].astype(F32)
        first = jnp.where(my_x == 0, a, b)
        second = jnp.where(my_x == 0, b, a)
        at = pl.ds(pl.multiple_of(z * (2 * per), 2 * per), 2 * per)
        rows_ref[at, :] = jnp.concatenate([first, second], axis=0).astype(BF16)

    def step(i, _):
        slot = lax.rem(i, depth)
        for kind, c in enumerate(copies(i, slot)):
            c.wait()
            part = jnp.dot(rows_ref[...], buf[slot, kind], preferred_element_type=F32)
            part_ref[kind, :, tile_at(i)] = part.astype(BF16)

        @pl.when(i + depth < tiles)
        def _():
            for c in copies(i + depth, slot):
                c.start()

        return 0

    lax.fori_loop(0, tiles, step, 0)


def gate_up(own, far, gate_weight, up_weight, devices):
    depth = 4
    total = devices * own.shape[1]
    features, columns = gate_weight.shape
    return pl.pallas_call(
        functools.partial(gate_up_kernel, devices, depth),
        out_shape=(
            jax.ShapeDtypeStruct((2, total, columns), BF16),
            jax.ShapeDtypeStruct((total, features), BF16),
        ),
        in_specs=[VMEM, VMEM, ANY, ANY],
        out_specs=(VMEM, VMEM),
        scratch_shapes=[
            pltpu.VMEM((depth, 2, features, TILE), BF16),
            pltpu.SemaphoreType.DMA((depth, 2)),
        ],
        compiler_params=params(24),
        cost_estimate=cost(4 * total * features * columns, 4 * features * columns),
        name="gate_up",
    )(own, far, gate_weight, up_weight)


def down_kernel(devices, mine, depth, hidden_of, w_hbm, out_ref, hidden_ref, buf, sems):
    nx = grid_of(devices)[1]
    half = out_ref.shape[1]
    tiles = half // TILE
    my_x = lax.axis_index(AXIS) % nx
    base = (my_x if mine else 1 - my_x) * tiles

    def copy(i, slot):
        return pltpu.make_async_copy(w_hbm.at[:, tile_at(base + i)], buf.at[slot], sems.at[slot])

    for i in range(min(depth, tiles)):
        copy(i, i).start()
    if len(hidden_of) == 2:
        own, other = hidden_of
        gate = own[0].astype(F32) + other[0].astype(F32)
        up = own[1].astype(F32) + other[1].astype(F32)
        hidden_ref[...] = (gate / (1.0 + jnp.exp(-gate)) * up).astype(BF16)
    else:
        hidden_ref = hidden_of[0]

    def step(i, _):
        slot = lax.rem(i, depth)
        copy(i, slot).wait()
        part = jnp.dot(hidden_ref[...], buf[slot], preferred_element_type=F32)
        out_ref[:, tile_at(i)] = part.astype(out_ref.dtype)

        @pl.when(i + depth < tiles)
        def _():
            copy(i + depth, slot).start()

        return 0

    lax.fori_loop(0, tiles, step, 0)


def down_far(own, other, down_weight, devices):
    depth = 6
    total = own.shape[1]
    columns, features = down_weight.shape

    def kernel(own_ref, other_ref, w_hbm, out_ref, hidden_ref, buf, sems):
        down_kernel(devices, False, depth, (own_ref, other_ref), w_hbm, out_ref, hidden_ref, buf, sems)

    return pl.pallas_call(
        kernel,
        out_shape=(
            jax.ShapeDtypeStruct((total, features // 2), BF16),
            jax.ShapeDtypeStruct((total, columns), BF16),
        ),
        in_specs=[VMEM, VMEM, ANY],
        out_specs=(VMEM, VMEM),
        scratch_shapes=[
            pltpu.VMEM((depth, columns, TILE), BF16),
            pltpu.SemaphoreType.DMA((depth,)),
        ],
        compiler_params=params(24),
        cost_estimate=cost(total * features * columns, features * columns),
        name="down_far_half",
    )(own, other, down_weight)


def down_near(hidden, down_weight, devices):
    depth = 6
    total = hidden.shape[0]
    columns, features = down_weight.shape

    def kernel(hidden_ref, w_hbm, out_ref, buf, sems):
        down_kernel(devices, True, depth, (hidden_ref,), w_hbm, out_ref, None, buf, sems)

    return pl.pallas_call(
        kernel,
        out_shape=jax.ShapeDtypeStruct((total, features // 2), F32),
        in_specs=[VMEM, ANY],
        out_specs=VMEM,
        scratch_shapes=[
            pltpu.VMEM((depth, columns, TILE), BF16),
            pltpu.SemaphoreType.DMA((depth,)),
        ],
        compiler_params=params(24),
        cost_estimate=cost(total * features * columns, features * columns),
        name="down_near_half",
    )(hidden, down_weight)


def pick(column_ref, row_ref, capacity, first_slot, slots):
    total = row_ref.shape[1]
    same = column_ref[...] == row_ref[...]
    earlier = lax.broadcasted_iota(jnp.int32, (total, total), 0) < lax.broadcasted_iota(
        jnp.int32, (total, total), 1
    )
    rank = jnp.sum((same & earlier).astype(F32), axis=0, keepdims=True).astype(jnp.int32)
    position = row_ref[...] * capacity + rank
    slot = first_slot + lax.broadcasted_iota(jnp.int32, (slots, total), 0)
    return (slot == position).astype(F32).astype(BF16)


def to_slots_kernel(devices, capacity, column_ref, row_ref, near_ref, far_ref, own_ref, *sends):
    nz, nx = grid_of(devices)
    my_z = lax.axis_index(AXIS) // nx
    slots = own_ref.shape[0]
    total = near_ref[...] + far_ref[...].astype(F32)
    rounded = total.astype(BF16)
    for dz, send_ref in enumerate((own_ref,) + sends):
        z = lax.rem(my_z + dz, nz)
        chosen = pick(column_ref, row_ref, capacity, z * slots, slots)
        if dz:
            send_ref[...] = jnp.dot(chosen, rounded, preferred_element_type=F32).astype(BF16)
        else:
            high = rounded.astype(F32)
            low = (total - high).astype(BF16)
            own_ref[...] = jnp.dot(chosen, rounded, preferred_element_type=F32) + jnp.dot(
                chosen, low, preferred_element_type=F32
            )


def to_slots(column, row, near, far, devices, capacity):
    nz, nx = grid_of(devices)
    slots = nx * 2 * capacity
    width = near.shape[1]
    return pl.pallas_call(
        functools.partial(to_slots_kernel, devices, capacity),
        out_shape=(jax.ShapeDtypeStruct((slots, width), F32),)
        + (jax.ShapeDtypeStruct((slots, width), BF16),) * (nz - 1),
        in_specs=[VMEM] * 4,
        out_specs=(VMEM,) * nz,
        compiler_params=params(8),
        name="to_slots",
    )(column, row, near, far)


def finish_kernel(devices, capacity, column_ref, row_ref, rows_ref, own_ref, *refs):
    *landed, keep_ref, send_ref = refs
    nz, nx = grid_of(devices)
    me = lax.axis_index(AXIS)
    my_z, my_x = me // nx, me % nx
    slots, width = own_ref.shape
    chosen = pick(column_ref, row_ref, capacity, my_z * slots, slots)
    mixed = rows_ref[:, pl.ds(pl.multiple_of(my_x * width, width), width)]
    total = own_ref[...]
    for ref in landed:
        total = total + ref[...].astype(F32)
    done = jnp.dot(chosen, mixed, preferred_element_type=F32) + total
    half = slots // 2
    first, second = done[:half], done[half:]
    keep_ref[...] = jnp.where(my_x == 0, first, second).astype(BF16)
    send_ref[...] = jnp.where(my_x == 0, second, first).astype(BF16)


def finish(column, row, rows, own, landed, devices, capacity):
    slots, width = own.shape
    shape = jax.ShapeDtypeStruct((slots // 2, width), BF16)
    return pl.pallas_call(
        functools.partial(finish_kernel, devices, capacity),
        out_shape=(shape, shape),
        in_specs=[VMEM] * (4 + len(landed)),
        out_specs=(VMEM, VMEM),
        compiler_params=params(8),
        name="finish",
    )(column, row, rows, own, *landed)


def join_kernel(nx, keep_ref, other_ref, out_ref):
    my_x = lax.axis_index(AXIS) % nx
    width = keep_ref.shape[1]
    out_ref[:, :width] = jnp.where(my_x == 0, keep_ref[...], other_ref[...])
    out_ref[:, width:] = jnp.where(my_x == 0, other_ref[...], keep_ref[...])


def join(keep, other, devices):
    slots, width = keep.shape
    return pl.pallas_call(
        functools.partial(join_kernel, grid_of(devices)[1]),
        out_shape=jax.ShapeDtypeStruct((slots, 2 * width), BF16),
        in_specs=[VMEM, VMEM],
        out_specs=VMEM,
        compiler_params=params(8),
        name="join_halves",
    )(keep, other)


def slot_positions(column, destinations, capacity):
    onehot = (column[:, None] == jnp.arange(destinations, dtype=jnp.int32)[None, :]).astype(
        jnp.int32
    )
    before = jnp.cumsum(onehot, axis=0) - onehot
    slot_rank = jnp.sum(before * onehot, axis=1)
    return column * capacity + slot_rank


def plain(mixed_rows, target, gate_weight, up_weight, down_weight, devices):
    rows_dev, features = mixed_rows.shape
    me = lax.axis_index(AXIS)
    gathered = lax.all_gather(mixed_rows, AXIS, axis=0, tiled=True)
    mine = jnp.stack(
        [
            jnp.dot(gathered, gate_weight, preferred_element_type=F32),
            jnp.dot(gathered, up_weight, preferred_element_type=F32),
        ]
    )
    other = lax.ppermute(mine.astype(BF16), "ffn", [(0, 1), (1, 0)])
    gate_sum, up_sum = mine + other.astype(F32)
    hidden = (jax.nn.silu(gate_sum) * up_sum).astype(BF16)
    down = jnp.dot(hidden, down_weight, preferred_element_type=F32)
    share = features // devices
    landed = lax.all_to_all(
        jnp.moveaxis(down.astype(BF16).reshape(-1, devices, share), 1, 0), AXIS, 0, 0
    )
    summed = jnp.sum(landed.astype(F32), axis=0)
    mixed_share = lax.dynamic_slice_in_dim(gathered, me * share, share, axis=1)
    finished = (mixed_share.astype(F32) + summed).astype(BF16)
    slot_count = 2 * devices * rows_dev
    position = slot_positions(target[:, 0], 2 * devices, rows_dev)
    chosen = (jnp.arange(slot_count, dtype=jnp.int32)[:, None] == position[None, :]).astype(BF16)
    slots = jnp.dot(chosen, finished, preferred_element_type=F32).astype(BF16)
    slots = slots.reshape(devices, 2 * rows_dev, share)
    mine_out = lax.all_to_all(slots, AXIS, split_axis=0, concat_axis=0)
    return jnp.moveaxis(mine_out, 0, 1).reshape(2 * rows_dev, features)


def local(
    queries,
    cache_keys,
    stored_value_cache,
    lengths,
    residual,
    target,
    gate_weight,
    up_weight,
    down_weight,
):
    devices = lax.axis_size(AXIS)
    nz, nx = grid_of(devices)
    capacity = cache_keys.shape[0]
    mixed_rows = attend(queries, cache_keys, stored_value_cache, lengths, residual)
    columns, features = down_weight.shape
    if nx != 2 or columns % TILE or features % (2 * TILE):
        return plain(mixed_rows, target, gate_weight, up_weight, down_weight, devices)

    own = jnp.stack(
        [mixed_rows]
        + [lax.ppermute(mixed_rows, AXIS, shift_z(devices, shift)) for shift in range(1, nz)]
    )
    far = lax.ppermute(own, AXIS, shift_x(devices, 1))
    part, rows = gate_up(own, far, gate_weight, up_weight, devices)
    other = lax.ppermute(part, "ffn", [(0, 1), (1, 0)])
    far_half, hidden = down_far(part, other, down_weight, devices)
    arrived = lax.ppermute(far_half, AXIS, shift_x(devices, 1))
    near_half = down_near(hidden, down_weight, devices)
    row = target.reshape(1, -1)
    own_slots, *sends = to_slots(target, row, near_half, arrived, devices, capacity)
    landed = [
        lax.ppermute(send, AXIS, shift_z(devices, dz + 1)) for dz, send in enumerate(sends)
    ]
    keep, send = finish(target, row, rows, own_slots, landed, devices, capacity)
    return join(keep, lax.ppermute(send, AXIS, shift_x(devices, 1)), devices)


def solution(mesh):
    return jax.shard_map(
        local,
        mesh=mesh,
        in_specs=(
            P(("parts", "attn"), "ffn", None),
            P(("parts", "attn"), None, "ffn", None),
            P(("parts", "attn"), None, "ffn", None),
            P(("parts", "attn")),
            P(("parts", "attn"), "ffn"),
            P("parts", None),
            P("ffn", "attn"),
            P("ffn", "attn"),
            P("attn", "ffn"),
        ),
        out_specs=P(("parts", "attn"), "ffn"),
        check_vma=False,
    )
```

time: 186 us -> 107 us (0.58)
  waiting for transfers between devices: 89.3 us -> 22.9 us
  matrix products: 40.9 us -> 0 us
  Pallas kernels: 0 us -> 37 us
  blocking collectives: 33 us -> 0 us
  local copies, waits for them, and re-layouts: 2.78 us -> 30.8 us
  starting transfers between devices: 0.04 us -> 15.7 us
  between operations: 13.5 us -> 0.09 us
  other arithmetic: 5.74 us -> 0.04 us
    reduce_scatter x1 -> x0, waiting for transfers between devices: 68.6 us -> none  [local(): lax.psum_scatter(jnp.dot(take_rows(hidden, slot_owner), down_weight, pref...]
    dot_general x5 -> x0, matrix products: 40.9 us -> none  [the longest x1 13.9 us: local(): jnp.dot(take_rows(hidden, slot_owner), down_weight, preferred_element_typ...]
    pallas_call x0 -> x7, Pallas kernels: none -> 37 us  [the longest x1 21.1 us: gate_up(): pl.pallas_call(functools.partial(gate_up_kernel, devices, depth), out_sha...]
    all_gather x1 -> x0, blocking collectives: 33 us -> none  [local(): gathered = lax.all_gather(mixed_rows, 'attn', axis=0, tiled=True)]
    unnamed x6 -> x19, local copies, waits for them, and re-layouts: 0.28 us -> 30.8 us
    ppermute x0 -> x10, waiting for transfers between devices: none -> 22.9 us  [the longest x3 7.92 us: local(): lax.ppermute(send, AXIS, shift_z(devices, dz + 1))]
    psum x1 -> x0, waiting for transfers between devices: 20.7 us -> none  [local(): gate_sum, up_sum = lax.psum((gate_part, up_part), 'ffn')]
    ppermute x0 -> x10, starting transfers between devices: none -> 15.7 us  [the longest x3 7.01 us: local(): lax.ppermute(mixed_rows, AXIS, shift_z(devices, shift))]
  transfers between devices with their start and end apart: 2 -> 10, of which waited for: 2 -> 8; matrix products, arithmetic and copies ran while one was open for 1% -> 0% of each run, Pallas kernels for 0% -> 5%
where the time goes in v2:
time: 107 us
  Pallas kernels  37 us (35%)
  local copies, waits for them, and re-layouts  30.8 us (29%)
  waiting for transfers between devices  22.9 us (21%)
  starting transfers between devices  15.7 us (15%)
    unnamed x19, local copies, waits for them, and re-layouts  30.8 us
    pallas_call x1, Pallas kernels, gate_up(): pl.pallas_call(functools.partial(gate_up_kernel, devices, depth), out_sha...  21.1 us
    ppermute x3, waiting for transfers between devices, local(): lax.ppermute(send, AXIS, shift_z(devices, dz + 1))  7.92 us
    ppermute x3, starting transfers between devices, local(): lax.ppermute(mixed_rows, AXIS, shift_z(devices, shift))  7.01 us
    ppermute x1, waiting for transfers between devices, local(): far = lax.ppermute(own, AXIS, shift_x(devices, 1))  6.26 us
    pallas_call x1, Pallas kernels, down_far(): pl.pallas_call(kernel, out_shape=(jax.ShapeDtypeStruct((total, features /...  5.84 us
    pallas_call x1, Pallas kernels, down_near(): pl.pallas_call(kernel, out_shape=jax.ShapeDtypeStruct((total, features //...  5.45 us
    ppermute x3, starting transfers between devices, local(): lax.ppermute(send, AXIS, shift_z(devices, dz + 1))  4.9 us
  transfers between devices with their start and end apart: 10, of which 8 were waited for; matrix products, arithmetic and copies ran while one was open for 0% of the time, Pallas kernels for 5%

profile of v2, /device:TPU:0, one launch (start us, length us, event | category | flops | bytes accessed | tf_op | source)
XLA Modules:
  0.0 106.5 jit_solution(10862476306712939433)
XLA Ops:
  0.0 1.0 copy-done.3
  1.0 1.0 copy-done.4
  2.1 0.8 copy-done.5
  4.4 3.2 %attention.1 = bf16[8,4096]{1,0:T(8,128)(2,1)S(1)} custom-call(s32[8]{0:T(128)S(1)} %copy-done.8, bf16[8,32,128]{2,1,0:T(8,128)(2,1)S(1)} %copy-done.5, bf16[8,256,128]{2,1,0:T(8,128)(2,1)S(1)} %bitcast.7, bf16[8,256,128]{2,1,0:T(8,128)(2,1)S(1)} %bitcast.8, bf16[8,4096]{1,0:T(8,128)(2,1)S(1)} %copy-done.6), custom_call_target="tpu_custom_call" | custom-call | flops 33554432 | bytes 1048576 | tf_op jit(solution)/shard_map/attention/pallas_call | solution.py:78
  7.7 3.1 %collective-permute-start = (bf16[8,4096]{1,0:T(8,128)(2,1)S(1)}, bf16[8,4096]{1,0:T(8,128)(2,1)S(1)}, u32[]{:S(2)}, u32[]{:S(2)}) collective-permute-start(bf16[8,4096]{1,0:T(8,128)(2,1)S(1)} %attention.1), channel_id=1, source_target_pairs={{0,4},{2,6},{4,8},{6,10},{8,12},{10,14},{12,0},{14,2},{1,5},{3,7},... | collective-permute-start | bytes 196616 | tf_op jit(solution)/shard_map/ppermute | solution.py:404
  10.7 2.6 %collective-permute-start.1 = (bf16[8,4096]{1,0:T(8,128)(2,1)S(1)}, bf16[8,4096]{1,0:T(8,128)(2,1)S(1)}, u32[]{:S(2)}, u32[]{:S(2)}) collective-permute-start(bf16[8,4096]{1,0:T(8,128)(2,1)S(1)} %attention.1), channel_id=1, source_target_pairs={{0,8},{2,10},{4,12},{6,14},{8,0},{10,2},{12,4},{14,6},{1,9},{3,11}... | collective-permute-start | bytes 196616 | tf_op jit(solution)/shard_map/ppermute | solution.py:404
  13.3 1.3 %collective-permute-start.2 = (bf16[8,4096]{1,0:T(8,128)(2,1)S(1)}, bf16[8,4096]{1,0:T(8,128)(2,1)S(1)}, u32[]{:S(2)}, u32[]{:S(2)}) collective-permute-start(bf16[8,4096]{1,0:T(8,128)(2,1)S(1)} %attention.1), channel_id=1, source_target_pairs={{0,12},{2,14},{4,0},{6,2},{8,4},{10,6},{12,8},{14,10},{1,13},{3,15... | collective-permute-start | bytes 196616 | tf_op jit(solution)/shard_map/ppermute | solution.py:404
  15.3 2.5 %collective-permute-done.1 = bf16[8,4096]{1,0:T(8,128)(2,1)S(1)} collective-permute-done((bf16[8,4096]{1,0:T(8,128)(2,1)S(1)}, bf16[8,4096]{1,0:T(8,128)(2,1)S(1)}, u32[]{:S(2)}, u32[]{:S(2)}) %collective-permute-start.1) | collective-permute-done | bytes 65568 | tf_op jit(solution)/shard_map/ppermute | solution.py:404
  18.1 1.6 %collective-permute-start.3 = (bf16[4,8,4096]{2,1,0:T(8,128)(2,1)S(1)}, bf16[4,8,4096]{2,1,0:T(8,128)(2,1)S(1)}, u32[]{:S(2)}, u32[]{:S(2)}) collective-permute-start(bf16[4,8,4096]{2,1,0:T(8,128)(2,1)S(1)} %pad_maximum_fusion.own_ref), channel_id=1, source_target_pairs={{0,2},{2,0},{4,6},{6,4},{8,10},{10,8},{12,14},{14,12},{1,3},{3,1},... | collective-permute-start | bytes 786440 | tf_op jit(solution)/shard_map/ppermute | solution.py:406
  19.7 6.3 %collective-permute-done.3.far_ref = bf16[4,8,4096]{2,1,0:T(8,128)(2,1)S(1)} collective-permute-done((bf16[4,8,4096]{2,1,0:T(8,128)(2,1)S(1)}, bf16[4,8,4096]{2,1,0:T(8,128)(2,1)S(1)}, u32[]{:S(2)}, u32[]{:S(2)}) %collective-permute-start.3) | collective-permute-done | bytes 262176 | tf_op jit(solution)/shard_map/ppermute | solution.py:406
  26.0 8.8 %copy-done.2 = bf16[4096,3328]{1,0:T(8,128)(2,1)S(1)} copy-done((bf16[4096,3328]{1,0:T(8,128)(2,1)S(1)}, bf16[4096,3328]{1,0:T(8,128)(2,1)}, u32[]{:S(2)}) %copy-start.2) | copy-done | bytes 27263000
  34.7 21.1 %gate_up.1 = (bf16[2,64,3328]{2,1,0:T(8,128)(2,1)S(1)}, bf16[64,4096]{1,0:T(8,128)(2,1)S(1)}) custom-call(bf16[4,8,4096]{2,1,0:T(8,128)(2,1)S(1)} %pad_maximum_fusion.own_ref, bf16[4,8,4096]{2,1,0:T(8,128)(2,1)S(1)} %collective-permute-done.3.far_ref, bf16[4096,3328]{1,0:T(8,128)(2,1)S(1)} %copy-done.2, bf16[4096,3328]{1,0:T(8,128)(2,1)} %u_hbm.1), custom_call_target="tpu_custom_call" | custom-call | flops 3489660928 | bytes 54525952 | tf_op jit(solution)/shard_map/gate_up/pallas_call | solution.py:146
  55.9 2.4 %collective-permute-done.4.other_ref = bf16[2,64,3328]{2,1,0:T(8,128)(2,1)S(1)} collective-permute-done((bf16[2,64,3328]{2,1,0:T(8,128)(2,1)S(1)}, bf16[2,64,3328]{2,1,0:T(8,128)(2,1)S(1)}, u32[]{:S(2)}, u32[]{:S(2)}) %collective-permute-start.4) | collective-permute-done | bytes 852000 | tf_op jit(solution)/shard_map/ppermute | solution.py:408
  58.3 8.8 %copy-done = bf16[3328,4096]{1,0:T(8,128)(2,1)S(1)} copy-done((bf16[3328,4096]{1,0:T(8,128)(2,1)S(1)}, bf16[3328,4096]{1,0:T(8,128)(2,1)}, u32[]{:S(2)}) %copy-start) | copy-done | bytes 27263000
  67.0 5.8 %down_far_half.1 = (bf16[64,2048]{1,0:T(8,128)(2,1)S(1)}, bf16[64,3328]{1,0:T(8,128)(2,1)S(1)}) custom-call(bf16[2,64,3328]{2,1,0:T(8,128)(2,1)S(1)} %get-tuple-element.16.own_ref, bf16[2,64,3328]{2,1,0:T(8,128)(2,1)S(1)} %collective-permute-done.4.other_ref, bf16[3328,4096]{1,0:T(8,128)(2,1)S(1)} %copy-done), custom_call_target="tpu_custom_call" | custom-call | flops 872415232 | bytes 13631488 | tf_op jit(solution)/shard_map/down_far_half/pallas_call | solution.py:207
  72.9 0.8 collective-permute-start.5
  73.8 8.8 %copy-done.1 = bf16[3328,4096]{1,0:T(8,128)(2,1)S(1)} copy-done((bf16[3328,4096]{1,0:T(8,128)(2,1)S(1)}, bf16[3328,4096]{1,0:T(8,128)(2,1)}, u32[]{:S(2)}) %copy-start.1) | copy-done | bytes 27263000
  82.6 5.5 %down_near_half.1.near_ref = f32[64,2048]{1,0:T(8,128)S(1)} custom-call(bf16[64,3328]{1,0:T(8,128)(2,1)S(1)} %get-tuple-element.17.hidden_ref, bf16[3328,4096]{1,0:T(8,128)(2,1)S(1)} %copy-done.1), custom_call_target="tpu_custom_call" | custom-call | flops 872415232 | bytes 13631488 | tf_op jit(solution)/shard_map/down_near_half/pallas_call | solution.py:233
  88.5 2.5 %collective-permute-start.6 = (bf16[32,2048]{1,0:T(8,128)(2,1)S(1)}, bf16[32,2048]{1,0:T(8,128)(2,1)S(1)}, u32[]{:S(2)}, u32[]{:S(2)}) collective-permute-start(bf16[32,2048]{1,0:T(8,128)(2,1)S(1)} %get-tuple-element.20), channel_id=1, source_target_pairs={{0,4},{2,6},{4,8},{6,10},{8,12},{10,14},{12,0},{14,2},{1,5},{3,7},... | collective-permute-start | bytes 393224 | tf_op jit(solution)/shard_map/ppermute | solution.py:415
  91.5 1.9 %collective-permute-start.8 = (bf16[32,2048]{1,0:T(8,128)(2,1)S(1)}, bf16[32,2048]{1,0:T(8,128)(2,1)S(1)}, u32[]{:S(2)}, u32[]{:S(2)}) collective-permute-start(bf16[32,2048]{1,0:T(8,128)(2,1)S(1)} %get-tuple-element.22), channel_id=1, source_target_pairs={{0,12},{2,14},{4,0},{6,2},{8,4},{10,6},{12,8},{14,10},{1,13},{3,15... | collective-permute-start | bytes 393224 | tf_op jit(solution)/shard_map/ppermute | solution.py:415
  93.4 3.4 %collective-permute-done.6.refs_0_ = bf16[32,2048]{1,0:T(8,128)(2,1)S(1)} collective-permute-done((bf16[32,2048]{1,0:T(8,128)(2,1)S(1)}, bf16[32,2048]{1,0:T(8,128)(2,1)S(1)}, u32[]{:S(2)}, u32[]{:S(2)}) %collective-permute-start.6) | collective-permute-done | bytes 131104 | tf_op jit(solution)/shard_map/ppermute | solution.py:415
  96.8 4.5 %collective-permute-done.7.refs_1_ = bf16[32,2048]{1,0:T(8,128)(2,1)S(1)} collective-permute-done((bf16[32,2048]{1,0:T(8,128)(2,1)S(1)}, bf16[32,2048]{1,0:T(8,128)(2,1)S(1)}, u32[]{:S(2)}, u32[]{:S(2)}) %collective-permute-start.7) | collective-permute-done | bytes 131104 | tf_op jit(solution)/shard_map/ppermute | solution.py:415
  101.5 1.3 %collective-permute-start.9 = (bf16[16,2048]{1,0:T(8,128)(2,1)S(1)}, bf16[16,2048]{1,0:T(8,128)(2,1)S(1)}, u32[]{:S(2)}, u32[]{:S(2)}) collective-permute-start(bf16[16,2048]{1,0:T(8,128)(2,1)S(1)} %get-tuple-element.24), channel_id=1, source_target_pairs={{0,2},{2,0},{4,6},{6,4},{8,10},{10,8},{12,14},{14,12},{1,3},{3,1},... | collective-permute-start | bytes 196616 | tf_op jit(solution)/shard_map/ppermute | solution.py:418
  102.9 3.0 %collective-permute-done.9.other_ref = bf16[16,2048]{1,0:T(8,128)(2,1)S(1)} collective-permute-done((bf16[16,2048]{1,0:T(8,128)(2,1)S(1)}, bf16[16,2048]{1,0:T(8,128)(2,1)S(1)}, u32[]{:S(2)}, u32[]{:S(2)}) %collective-permute-start.9) | collective-permute-done | bytes 65568 | tf_op jit(solution)/shard_map/ppermute | solution.py:418
  (23 shorter events, 4.5 us)
Async XLA Ops:
  0.0 1.0 copy-start.3
  1.0 1.0 copy-start.4
  2.1 0.8 copy-start.5
  2.9 0.8 copy-start.6
  3.8 0.7 copy-start.8
  7.7 7.6 %collective-permute-start = (bf16[8,4096]{1,0:T(8,128)(2,1)S(1)}, bf16[8,4096]{1,0:T(8,128)(2,1)S(1)}, u32[]{:S(2)}, u32[]{:S(2)}) collective-permute-start(bf16[8,4096]{1,0:T(8,128)(2,1)S(1)} %attention.1), channel_id=1, source_target_pairs={{0,4},{2,6},{4,8},{6,10},{8,12},{10,14},{12,0},{14,2},{1,5},{3,7},... | collective-permute-start | bytes 196616 | tf_op jit(solution)/shard_map/ppermute | solution.py:404
  10.7 7.1 %collective-permute-start.1 = (bf16[8,4096]{1,0:T(8,128)(2,1)S(1)}, bf16[8,4096]{1,0:T(8,128)(2,1)S(1)}, u32[]{:S(2)}, u32[]{:S(2)}) collective-permute-start(bf16[8,4096]{1,0:T(8,128)(2,1)S(1)} %attention.1), channel_id=1, source_target_pairs={{0,8},{2,10},{4,12},{6,14},{8,0},{10,2},{12,4},{14,6},{1,9},{3,11}... | collective-permute-start | bytes 196616 | tf_op jit(solution)/shard_map/ppermute | solution.py:404
  13.3 4.7 %collective-permute-start.2 = (bf16[8,4096]{1,0:T(8,128)(2,1)S(1)}, bf16[8,4096]{1,0:T(8,128)(2,1)S(1)}, u32[]{:S(2)}, u32[]{:S(2)}) collective-permute-start(bf16[8,4096]{1,0:T(8,128)(2,1)S(1)} %attention.1), channel_id=1, source_target_pairs={{0,12},{2,14},{4,0},{6,2},{8,4},{10,6},{12,8},{14,10},{1,13},{3,15... | collective-permute-start | bytes 196616 | tf_op jit(solution)/shard_map/ppermute | solution.py:404
  18.1 7.9 %collective-permute-start.3 = (bf16[4,8,4096]{2,1,0:T(8,128)(2,1)S(1)}, bf16[4,8,4096]{2,1,0:T(8,128)(2,1)S(1)}, u32[]{:S(2)}, u32[]{:S(2)}) collective-permute-start(bf16[4,8,4096]{2,1,0:T(8,128)(2,1)S(1)} %pad_maximum_fusion.own_ref), channel_id=1, source_target_pairs={{0,2},{2,0},{4,6},{6,4},{8,10},{10,8},{12,14},{14,12},{1,3},{3,1},... | collective-permute-start | bytes 786440 | tf_op jit(solution)/shard_map/ppermute | solution.py:406
  26.0 8.8 %copy-start.2 = (bf16[4096,3328]{1,0:T(8,128)(2,1)S(1)}, bf16[4096,3328]{1,0:T(8,128)(2,1)}, u32[]{:S(2)}) copy-start(bf16[4096,3328]{1,0:T(8,128)(2,1)} %g_hbm.1) | copy-start | bytes 81788928
  55.8 17.9 %copy-start.7 = (s32[64,1]{0,1:T(1,128)S(1)}, s32[64,1]{0,1:T(1,128)}, u32[]{:S(2)}) copy-start(s32[64,1]{0,1:T(1,128)} %param.14) | copy-start | bytes 772
  55.8 2.4 %collective-permute-start.4 = (bf16[2,64,3328]{2,1,0:T(8,128)(2,1)S(1)}, bf16[2,64,3328]{2,1,0:T(8,128)(2,1)S(1)}, u32[]{:S(2)}, u32[]{:S(2)}) collective-permute-start(bf16[2,64,3328]{2,1,0:T(8,128)(2,1)S(1)} %get-tuple-element.16.own_ref), channel_id=1, source_target_pairs={{0,1},{1,0},{2,3},{3,2},{4,5},{5,4},{6,7},{7,6},{8,9},{9,8},{10,11... | collective-permute-start | bytes 2555912 | tf_op jit(solution)/shard_map/ppermute | solution.py:408
  58.3 8.8 %copy-start = (bf16[3328,4096]{1,0:T(8,128)(2,1)S(1)}, bf16[3328,4096]{1,0:T(8,128)(2,1)}, u32[]{:S(2)}) copy-start(bf16[3328,4096]{1,0:T(8,128)(2,1)} %w_hbm.3) | copy-start | bytes 81788928
  72.9 15.2 %collective-permute-start.5 = (bf16[64,2048]{1,0:T(8,128)(2,1)S(1)}, bf16[64,2048]{1,0:T(8,128)(2,1)S(1)}, u32[]{:S(2)}, u32[]{:S(2)}) collective-permute-start(bf16[64,2048]{1,0:T(8,128)(2,1)S(1)} %get-tuple-element.18), channel_id=1, source_target_pairs={{0,2},{2,0},{4,6},{6,4},{8,10},{10,8},{12,14},{14,12},{1,3},{3,1},... | collective-permute-start | bytes 786440 | tf_op jit(solution)/shard_map/ppermute | solution.py:410
  73.8 8.8 %copy-start.1 = (bf16[3328,4096]{1,0:T(8,128)(2,1)S(1)}, bf16[3328,4096]{1,0:T(8,128)(2,1)}, u32[]{:S(2)}) copy-start(bf16[3328,4096]{1,0:T(8,128)(2,1)} %w_hbm.3) | copy-start | bytes 81788928
  88.5 8.3 %collective-permute-start.6 = (bf16[32,2048]{1,0:T(8,128)(2,1)S(1)}, bf16[32,2048]{1,0:T(8,128)(2,1)S(1)}, u32[]{:S(2)}, u32[]{:S(2)}) collective-permute-start(bf16[32,2048]{1,0:T(8,128)(2,1)S(1)} %get-tuple-element.20), channel_id=1, source_target_pairs={{0,4},{2,6},{4,8},{6,10},{8,12},{10,14},{12,0},{14,2},{1,5},{3,7},... | collective-permute-start | bytes 393224 | tf_op jit(solution)/shard_map/ppermute | solution.py:415
  90.9 10.4 %collective-permute-start.7 = (bf16[32,2048]{1,0:T(8,128)(2,1)S(1)}, bf16[32,2048]{1,0:T(8,128)(2,1)S(1)}, u32[]{:S(2)}, u32[]{:S(2)}) collective-permute-start(bf16[32,2048]{1,0:T(8,128)(2,1)S(1)} %get-tuple-element.21), channel_id=1, source_target_pairs={{0,8},{2,10},{4,12},{6,14},{8,0},{10,2},{12,4},{14,6},{1,9},{3,11}... | collective-permute-start | bytes 393224 | tf_op jit(solution)/shard_map/ppermute | solution.py:415
  91.5 9.8 %collective-permute-start.8 = (bf16[32,2048]{1,0:T(8,128)(2,1)S(1)}, bf16[32,2048]{1,0:T(8,128)(2,1)S(1)}, u32[]{:S(2)}, u32[]{:S(2)}) collective-permute-start(bf16[32,2048]{1,0:T(8,128)(2,1)S(1)} %get-tuple-element.22), channel_id=1, source_target_pairs={{0,12},{2,14},{4,0},{6,2},{8,4},{10,6},{12,8},{14,10},{1,13},{3,15... | collective-permute-start | bytes 393224 | tf_op jit(solution)/shard_map/ppermute | solution.py:415
  101.5 4.3 %collective-permute-start.9 = (bf16[16,2048]{1,0:T(8,128)(2,1)S(1)}, bf16[16,2048]{1,0:T(8,128)(2,1)S(1)}, u32[]{:S(2)}, u32[]{:S(2)}) collective-permute-start(bf16[16,2048]{1,0:T(8,128)(2,1)S(1)} %get-tuple-element.24), channel_id=1, source_target_pairs={{0,2},{2,0},{4,6},{6,4},{8,10},{10,8},{12,14},{14,12},{1,3},{3,1},... | collective-permute-start | bytes 196616 | tf_op jit(solution)/shard_map/ppermute | solution.py:418

commit v3 on v2

--- a/solution.py
+++ b/solution.py
@@ -35,24 +35,36 @@
     return devices // nx, nx
 
 
-def shift_z(devices, shift):
-    nz, nx = grid_of(devices)
-    return [(z * nx + x, ((z + shift) % nz) * nx + x) for z in range(nz) for x in range(nx)]
-
-
-def shift_x(devices, shift):
-    nz, nx = grid_of(devices)
-    return [(z * nx + x, z * nx + (x + shift) % nx) for z in range(nz) for x in range(nx)]
-
-
-def attend_kernel(kv, lengths, q_ref, k_ref, v_ref, res_ref, out_ref, att_ref):
+def swap_z(devices, bits):
+    nz, nx = grid_of(devices)
+    return [(z * nx + x, (z ^ bits) * nx + x) for z in range(nz) for x in range(nx)]
+
+
+def swap_x(devices):
+    nz, nx = grid_of(devices)
+    return [(z * nx + x, z * nx + (x ^ 1)) for z in range(nz) for x in range(nx)]
+
+
+def attend_kernel(
+    kv, lengths, q_hbm, k_hbm, v_hbm, res_ref, out_ref, att_ref, q_ref, k_ref, v_ref, sems
+):
     rows, heads, dim = q_ref.shape
     span = k_ref.shape[1]
+    loads = [
+        pltpu.make_async_copy(source, held, sems.at[i])
+        for i, (source, held) in enumerate(
+            ((q_hbm, q_ref), (k_hbm, k_ref), (v_hbm, v_ref))
+        )
+    ]
+    for load in loads:
+        load.start()
     per_group = heads // kv
     column = lax.broadcasted_iota(jnp.int32, (heads, span), 1)
     head = lax.broadcasted_iota(jnp.int32, (heads, span), 0)
     right_group = (column % kv) == (head // per_group)
     position = column // kv
+    for load in loads:
+        load.wait()
     for r in range(rows):
         scores = lax.dot_general(
             q_ref[r], k_ref[r], (((1,), (1,)), ((), ())), preferred_element_type=F32
@@ -78,10 +90,16 @@
     return pl.pallas_call(
         functools.partial(attend_kernel, kv),
         out_shape=jax.ShapeDtypeStruct((rows, heads * dim), BF16),
-        in_specs=[SMEM, VMEM, VMEM, VMEM, VMEM],
+        in_specs=[SMEM, ANY, ANY, ANY, VMEM],
         out_specs=VMEM,
-        scratch_shapes=[pltpu.VMEM((rows * heads, dim), F32)],
-        compiler_params=params(8),
+        scratch_shapes=[
+            pltpu.VMEM((rows * heads, dim), F32),
+            pltpu.VMEM(queries.shape, BF16),
+            pltpu.VMEM((rows, span, dim), BF16),
+            pltpu.VMEM((rows, span, dim), BF16),
+            pltpu.SemaphoreType.DMA((3,)),
+        ],
+        compiler_params=params(56),
         cost_estimate=cost(rows * heads * span * dim * 4, rows * span * dim * 4),
         name="attention",
     )(
@@ -97,54 +115,61 @@
     return pl.ds(pl.multiple_of(index * TILE, TILE), TILE)
 
 
-def gate_up_kernel(devices, depth, own_ref, far_ref, g_hbm, u_hbm, part_ref, rows_ref, buf, sems):
-    nz, nx = grid_of(devices)
-    columns = g_hbm.shape[1]
-    tiles = columns // TILE
+def gate_up_kernel(
+    devices, depth, deep, own_ref, far_ref, g_hbm, u_hbm, part_ref, rows_ref, total_ref, buf, sems
+):
+    nz, nx = grid_of(devices)
+    steps = g_hbm.shape[0] // deep
+
+    def band(i):
+        return pl.ds(pl.multiple_of(i * deep, deep), deep)
 
     def copies(i, slot):
         return (
-            pltpu.make_async_copy(g_hbm.at[:, tile_at(i)], buf.at[slot, 0], sems.at[slot, 0]),
-            pltpu.make_async_copy(u_hbm.at[:, tile_at(i)], buf.at[slot, 1], sems.at[slot, 1]),
-        )
-
-    for i in range(min(depth, tiles)):
+            pltpu.make_async_copy(g_hbm.at[band(i)], buf.at[slot, 0], sems.at[slot, 0]),
+            pltpu.make_async_copy(u_hbm.at[band(i)], buf.at[slot, 1], sems.at[slot, 1]),
+        )
+
+    for i in range(min(depth, steps)):
         for c in copies(i, i):
             c.start()
     me = lax.axis_index(AXIS)
     my_z, my_x = me // nx, me % nx
     per = own_ref.shape[1]
     for dz in range(nz):
-        z = lax.rem(my_z - dz + nz, nz)
+        z = my_z ^ dz
         a, b = own_ref[dz].astype(F32), far_ref[dz].astype(F32)
         first = jnp.where(my_x == 0, a, b)
         second = jnp.where(my_x == 0, b, a)
         at = pl.ds(pl.multiple_of(z * (2 * per), 2 * per), 2 * per)
         rows_ref[at, :] = jnp.concatenate([first, second], axis=0).astype(BF16)
+    total_ref[...] = jnp.zeros_like(total_ref)
 
     def step(i, _):
         slot = lax.rem(i, depth)
         for kind, c in enumerate(copies(i, slot)):
             c.wait()
-            part = jnp.dot(rows_ref[...], buf[slot, kind], preferred_element_type=F32)
-            part_ref[kind, :, tile_at(i)] = part.astype(BF16)
-
-        @pl.when(i + depth < tiles)
+            total_ref[kind] += jnp.dot(
+                rows_ref[:, band(i)], buf[slot, kind], preferred_element_type=F32
+            )
+
+        @pl.when(i + depth < steps)
         def _():
             for c in copies(i + depth, slot):
                 c.start()
 
         return 0
 
-    lax.fori_loop(0, tiles, step, 0)
+    lax.fori_loop(0, steps, step, 0)
+    part_ref[...] = total_ref[...].astype(BF16)
 
 
 def gate_up(own, far, gate_weight, up_weight, devices):
-    depth = 4
+    depth, deep = 3, 2 * TILE
     total = devices * own.shape[1]
     features, columns = gate_weight.shape
     return pl.pallas_call(
-        functools.partial(gate_up_kernel, devices, depth),
+        functools.partial(gate_up_kernel, devices, depth, deep),
         out_shape=(
             jax.ShapeDtypeStruct((2, total, columns), BF16),
             jax.ShapeDtypeStruct((total, features), BF16),
@@ -152,60 +177,59 @@
         in_specs=[VMEM, VMEM, ANY, ANY],
         out_specs=(VMEM, VMEM),
         scratch_shapes=[
-            pltpu.VMEM((depth, 2, features, TILE), BF16),
+            pltpu.VMEM((2, total, columns), F32),
+            pltpu.VMEM((depth, 2, deep, columns), BF16),
             pltpu.SemaphoreType.DMA((depth, 2)),
         ],
-        compiler_params=params(24),
+        compiler_params=params(44),
         cost_estimate=cost(4 * total * features * columns, 4 * features * columns),
         name="gate_up",
     )(own, far, gate_weight, up_weight)
 
 
-def down_kernel(devices, mine, depth, hidden_of, w_hbm, out_ref, hidden_ref, buf, sems):
+def down_far_kernel(
+    devices, depth, own_ref, other_ref, w_hbm, out_ref, hidden_ref, total_ref, buf, sems
+):
     nx = grid_of(devices)[1]
     half = out_ref.shape[1]
-    tiles = half // TILE
-    my_x = lax.axis_index(AXIS) % nx
-    base = (my_x if mine else 1 - my_x) * tiles
+    steps = w_hbm.shape[0] // TILE
+    base = pl.multiple_of((1 - lax.axis_index(AXIS) % nx) * half, half)
 
     def copy(i, slot):
-        return pltpu.make_async_copy(w_hbm.at[:, tile_at(base + i)], buf.at[slot], sems.at[slot])
-
-    for i in range(min(depth, tiles)):
+        return pltpu.make_async_copy(
+            w_hbm.at[tile_at(i), pl.ds(base, half)], buf.at[slot], sems.at[slot]
+        )
+
+    for i in range(min(depth, steps)):
         copy(i, i).start()
-    if len(hidden_of) == 2:
-        own, other = hidden_of
-        gate = own[0].astype(F32) + other[0].astype(F32)
-        up = own[1].astype(F32) + other[1].astype(F32)
-        hidden_ref[...] = (gate / (1.0 + jnp.exp(-gate)) * up).astype(BF16)
-    else:
-        hidden_ref = hidden_of[0]
+    gate = own_ref[0].astype(F32) + other_ref[0].astype(F32)
+    up = own_ref[1].astype(F32) + other_ref[1].astype(F32)
+    hidden_ref[...] = (gate / (1.0 + jnp.exp(-gate)) * up).astype(BF16)
+    total_ref[...] = jnp.zeros_like(total_ref)
 
     def step(i, _):
         slot = lax.rem(i, depth)
         copy(i, slot).wait()
-        part = jnp.dot(hidden_ref[...], buf[slot], preferred_element_type=F32)
-        out_ref[:, tile_at(i)] = part.astype(out_ref.dtype)
-
-        @pl.when(i + depth < tiles)
+        total_ref[...] += jnp.dot(
+            hidden_ref[:, tile_at(i)], buf[slot], preferred_element_type=F32
+        )
+
+        @pl.when(i + depth < steps)
         def _():
             copy(i + depth, slot).start()
 
         return 0
 
-    lax.fori_loop(0, tiles, step, 0)
+    lax.fori_loop(0, steps, step, 0)
+    out_ref[...] = total_ref[...].astype(BF16)
 
 
 def down_far(own, other, down_weight, devices):
-    depth = 6
+    depth = 10
     total = own.shape[1]
     columns, features = down_weight.shape
-
-    def kernel(own_ref, other_ref, w_hbm, out_ref, hidden_ref, buf, sems):
-        down_kernel(devices, False, depth, (own_ref, other_ref), w_hbm, out_ref, hidden_ref, buf, sems)
-
-    return pl.pallas_call(
-        kernel,
+    return pl.pallas_call(
+        functools.partial(down_far_kernel, devices, depth),
         out_shape=(
             jax.ShapeDtypeStruct((total, features // 2), BF16),
             jax.ShapeDtypeStruct((total, columns), BF16),
@@ -213,33 +237,53 @@
         in_specs=[VMEM, VMEM, ANY],
         out_specs=(VMEM, VMEM),
         scratch_shapes=[
-            pltpu.VMEM((depth, columns, TILE), BF16),
+            pltpu.VMEM((total, features // 2), F32),
+            pltpu.VMEM((depth, TILE, features // 2), BF16),
             pltpu.SemaphoreType.DMA((depth,)),
         ],
-        compiler_params=params(24),
+        compiler_params=params(44),
         cost_estimate=cost(total * features * columns, features * columns),
         name="down_far_half",
     )(own, other, down_weight)
 
 
+def down_near_kernel(devices, hidden_ref, w_hbm, out_ref, buf, sems):
+    nx = grid_of(devices)[1]
+    half = out_ref.shape[1]
+    wide = buf.shape[2]
+    base = (lax.axis_index(AXIS) % nx) * half
+    copies = [
+        pltpu.make_async_copy(
+            w_hbm.at[:, pl.ds(pl.multiple_of(base + i * wide, wide), wide)],
+            buf.at[i],
+            sems.at[i],
+        )
+        for i in range(half // wide)
+    ]
+    for c in copies:
+        c.start()
+    for i, c in enumerate(copies):
+        c.wait()
+        out_ref[:, i * wide : (i + 1) * wide] = jnp.dot(
+            hidden_ref[...], buf[i], preferred_element_type=F32
+        )
+
+
 def down_near(hidden, down_weight, devices):
-    depth = 6
     total = hidden.shape[0]
     columns, features = down_weight.shape
-
-    def kernel(hidden_ref, w_hbm, out_ref, buf, sems):
-        down_kernel(devices, True, depth, (hidden_ref,), w_hbm, out_ref, None, buf, sems)
-
-    return pl.pallas_call(
-        kernel,
+    wide = 2 * TILE
+    tiles = features // 2 // wide
+    return pl.pallas_call(
+        functools.partial(down_near_kernel, devices),
         out_shape=jax.ShapeDtypeStruct((total, features // 2), F32),
         in_specs=[VMEM, ANY],
         out_specs=VMEM,
         scratch_shapes=[
-            pltpu.VMEM((depth, columns, TILE), BF16),
-            pltpu.SemaphoreType.DMA((depth,)),
+            pltpu.VMEM((tiles, columns, wide), BF16),
+            pltpu.SemaphoreType.DMA((tiles,)),
         ],
-        compiler_params=params(24),
+        compiler_params=params(44),
         cost_estimate=cost(total * features * columns, features * columns),
         name="down_near_half",
     )(hidden, down_weight)
@@ -264,7 +308,7 @@
     total = near_ref[...] + far_ref[...].astype(F32)
     rounded = total.astype(BF16)
     for dz, send_ref in enumerate((own_ref,) + sends):
-        z = lax.rem(my_z + dz, nz)
+        z = my_z ^ dz
         chosen = pick(column_ref, row_ref, capacity, z * slots, slots)
         if dz:
             send_ref[...] = jnp.dot(chosen, rounded, preferred_element_type=F32).astype(BF16)
@@ -396,26 +440,26 @@
     capacity = cache_keys.shape[0]
     mixed_rows = attend(queries, cache_keys, stored_value_cache, lengths, residual)
     columns, features = down_weight.shape
-    if nx != 2 or columns % TILE or features % (2 * TILE):
+    if nx != 2 or nz & (nz - 1) or columns % TILE or features % (4 * TILE):
         return plain(mixed_rows, target, gate_weight, up_weight, down_weight, devices)
 
     own = jnp.stack(
         [mixed_rows]
-        + [lax.ppermute(mixed_rows, AXIS, shift_z(devices, shift)) for shift in range(1, nz)]
-    )
-    far = lax.ppermute(own, AXIS, shift_x(devices, 1))
+        + [lax.ppermute(mixed_rows, AXIS, swap_z(devices, bits)) for bits in range(1, nz)]
+    )
+    far = lax.ppermute(own, AXIS, swap_x(devices))
     part, rows = gate_up(own, far, gate_weight, up_weight, devices)
     other = lax.ppermute(part, "ffn", [(0, 1), (1, 0)])
     far_half, hidden = down_far(part, other, down_weight, devices)
-    arrived = lax.ppermute(far_half, AXIS, shift_x(devices, 1))
+    arrived = lax.ppermute(far_half, AXIS, swap_x(devices))
     near_half = down_near(hidden, down_weight, devices)
     row = target.reshape(1, -1)
     own_slots, *sends = to_slots(target, row, near_half, arrived, devices, capacity)
     landed = [
-        lax.ppermute(send, AXIS, shift_z(devices, dz + 1)) for dz, send in enumerate(sends)
+        lax.ppermute(send, AXIS, swap_z(devices, bits + 1)) for bits, send in enumerate(sends)
     ]
     keep, send = finish(target, row, rows, own_slots, landed, devices, capacity)
-    return join(keep, lax.ppermute(send, AXIS, shift_x(devices, 1)), devices)
+    return join(keep, lax.ppermute(send, AXIS, swap_x(devices)), devices)
 
 
 def solution(mesh):

time: 107 us -> 78.1 us (0.73)
  local copies, waits for them, and re-layouts: 30.8 us -> 0.1 us
  waiting for transfers between devices: 22.9 us -> 26.2 us
  Pallas kernels: 37 us -> 35.7 us
    unnamed x19 -> x3, local copies, waits for them, and re-layouts: 30.8 us -> 0.1 us
    pallas_call x3, Pallas kernels: 32.4 us -> 28.9 us  [the longest x1 17.7 us: gate_up(): pl.pallas_call(functools.partial(gate_up_kernel, devices, depth, deep), o...]
    ppermute x9, waiting for transfers between devices: 20.6 us -> 23.8 us  [the longest x3 8.8 us: local(): lax.ppermute(send, AXIS, swap_z(devices, bits + 1))]
    pallas_call x1, Pallas kernels: 3.24 us -> 5.44 us  [attend(): pl.pallas_call(functools.partial(attend_kernel, kv), out_shape=jax.ShapeD...]
  transfers between devices with their start and end apart: 10 -> 10, of which waited for: 8 -> 8; matrix products, arithmetic and copies ran while one was open for 0% -> 0% of each run, Pallas kernels for 5% -> 7%
where the time goes in v3:
time: 78.1 us; the launch traced here: 77.8 us
  Pallas kernels  35.7 us (46%)
  waiting for transfers between devices  26.2 us (34%)
  starting transfers between devices  14.9 us (19%)
  other arithmetic  0.87 us (1%)
    pallas_call x1, Pallas kernels, gate_up(): pl.pallas_call(functools.partial(gate_up_kernel, devices, depth, deep), o...  17.7 us
    ppermute x3, waiting for transfers between devices, local(): lax.ppermute(send, AXIS, swap_z(devices, bits + 1))  8.8 us
    ppermute x3, waiting for transfers between devices, local(): lax.ppermute(mixed_rows, AXIS, swap_z(devices, bits))  6.3 us
    pallas_call x1, Pallas kernels, down_near(): pl.pallas_call(functools.partial(down_near_kernel, devices), out_shape=ja...  5.73 us
    ppermute x3, starting transfers between devices, local(): lax.ppermute(mixed_rows, AXIS, swap_z(devices, bits))  5.68 us
    pallas_call x1, Pallas kernels, down_far(): pl.pallas_call(functools.partial(down_far_kernel, devices, depth), out_sh...  5.55 us
    pallas_call x1, Pallas kernels, attend(): pl.pallas_call(functools.partial(attend_kernel, kv), out_shape=jax.ShapeD...  5.44 us
    ppermute x1, waiting for transfers between devices, local(): far = lax.ppermute(own, AXIS, swap_x(devices))  4.92 us
  transfers between devices with their start and end apart: 10, of which 8 were waited for; matrix products, arithmetic and copies ran while one was open for 0% of the time, Pallas kernels for 7%

profile of v3, /device:TPU:0, one launch (start us, length us, event | category | flops | bytes accessed | tf_op | source)
XLA Modules:
  0.0 77.8 jit_solution(5413098565539380083)
XLA Ops:
  0.0 5.4 %attention.1 = bf16[8,4096]{1,0:T(8,128)(2,1)} custom-call(s32[8]{0:T(128)} %lengths.1, bf16[8,32,128]{2,1,0:T(8,128)(2,1)} %q_hbm.1, bf16[8,256,128]{2,1,0:T(8,128)(2,1)} %bitcast.9, bf16[8,256,128]{2,1,0:T(8,128)(2,1)} %bitcast.10, bf16[8,4096]{1,0:T(8,128)(2,1)} %res_ref.1), custom_call_target="tpu_custom_call" | custom-call | flops 33554432 | bytes 1048576 | tf_op jit(solution)/shard_map/attention/pallas_call | solution.py:90
  5.4 3.1 %collective-permute-start = (bf16[8,4096]{1,0:T(8,128)(2,1)}, bf16[8,4096]{1,0:T(8,128)(2,1)S(1)}, u32[]{:S(2)}, u32[]{:S(2)}) collective-permute-start(bf16[8,4096]{1,0:T(8,128)(2,1)} %attention.1), channel_id=1, source_target_pairs={{0,4},{2,6},{4,0},{6,2},{8,12},{10,14},{12,8},{14,10},{1,5},{3,7},... | collective-permute-start | bytes 196616 | tf_op jit(solution)/shard_map/ppermute | solution.py:448
  8.5 2.6 %collective-permute-start.1 = (bf16[8,4096]{1,0:T(8,128)(2,1)}, bf16[8,4096]{1,0:T(8,128)(2,1)S(1)}, u32[]{:S(2)}, u32[]{:S(2)}) collective-permute-start(bf16[8,4096]{1,0:T(8,128)(2,1)} %attention.1), channel_id=1, source_target_pairs={{0,8},{2,10},{4,12},{6,14},{8,0},{10,2},{12,4},{14,6},{1,9},{3,11}... | collective-permute-start | bytes 196616 | tf_op jit(solution)/shard_map/ppermute | solution.py:448
  11.1 4.9 %collective-permute-done.1 = bf16[8,4096]{1,0:T(8,128)(2,1)S(1)} collective-permute-done((bf16[8,4096]{1,0:T(8,128)(2,1)}, bf16[8,4096]{1,0:T(8,128)(2,1)S(1)}, u32[]{:S(2)}, u32[]{:S(2)}) %collective-permute-start.1) | collective-permute-done | bytes 65568 | tf_op jit(solution)/shard_map/ppermute | solution.py:448
  16.0 1.4 %collective-permute-done.2 = bf16[8,4096]{1,0:T(8,128)(2,1)S(1)} collective-permute-done((bf16[8,4096]{1,0:T(8,128)(2,1)}, bf16[8,4096]{1,0:T(8,128)(2,1)S(1)}, u32[]{:S(2)}, u32[]{:S(2)}) %collective-permute-start.2) | collective-permute-done | bytes 65568 | tf_op jit(solution)/shard_map/ppermute | solution.py:448
  17.4 0.9 %pad_maximum_fusion.own_ref = bf16[4,8,4096]{2,1,0:T(8,128)(2,1)S(1)} fusion(bf16[1,8,4096]{2,1,0:T(8,128)(2,1)S(1)} %bitcast.14, bf16[1,8,4096]{2,1,0:T(8,128)(2,1)S(1)} %bitcast.13, bf16[1,8,4096]{2,1,0:T(8,128)(2,1)S(1)} %bitcast.12, bf16[1,8,4096]{2,1,0:T(8,128)(2,1)} %bitcast.11), kind=kLoop, calls=%fused_computation | loop fusion | flops 393216 | bytes 524288 | tf_op jit(solution)/shard_map/stack | solution.py:446
  18.3 1.6 %collective-permute-start.3 = (bf16[4,8,4096]{2,1,0:T(8,128)(2,1)S(1)}, bf16[4,8,4096]{2,1,0:T(8,128)(2,1)S(1)}, u32[]{:S(2)}, u32[]{:S(2)}) collective-permute-start(bf16[4,8,4096]{2,1,0:T(8,128)(2,1)S(1)} %pad_maximum_fusion.own_ref), channel_id=1, source_target_pairs={{0,2},{2,0},{4,6},{6,4},{8,10},{10,8},{12,14},{14,12},{1,3},{3,1},... | collective-permute-start | bytes 786440 | tf_op jit(solution)/shard_map/ppermute | solution.py:450
  19.9 4.9 %collective-permute-done.3.far_ref = bf16[4,8,4096]{2,1,0:T(8,128)(2,1)S(1)} collective-permute-done((bf16[4,8,4096]{2,1,0:T(8,128)(2,1)S(1)}, bf16[4,8,4096]{2,1,0:T(8,128)(2,1)S(1)}, u32[]{:S(2)}, u32[]{:S(2)}) %collective-permute-start.3) | collective-permute-done | bytes 262176 | tf_op jit(solution)/shard_map/ppermute | solution.py:450
  24.8 17.7 %gate_up.1 = (bf16[2,64,3328]{2,1,0:T(8,128)(2,1)S(1)}, bf16[64,4096]{1,0:T(8,128)(2,1)S(1)}) custom-call(bf16[4,8,4096]{2,1,0:T(8,128)(2,1)S(1)} %pad_maximum_fusion.own_ref, bf16[4,8,4096]{2,1,0:T(8,128)(2,1)S(1)} %collective-permute-done.3.far_ref, bf16[4096,3328]{1,0:T(8,128)(2,1)} %g_hbm.1, bf16[4096,3328]{1,0:T(8,128)(2,1)} %u_hbm.1), custom_call_target="tpu_custom_call" | custom-call | flops 3489660928 | bytes 54525952 | tf_op jit(solution)/shard_map/gate_up/pallas_call | solution.py:171
  42.5 2.4 %collective-permute-done.4.other_ref = bf16[2,64,3328]{2,1,0:T(8,128)(2,1)S(1)} collective-permute-done((bf16[2,64,3328]{2,1,0:T(8,128)(2,1)S(1)}, bf16[2,64,3328]{2,1,0:T(8,128)(2,1)S(1)}, u32[]{:S(2)}, u32[]{:S(2)}) %collective-permute-start.4) | collective-permute-done | bytes 852000 | tf_op jit(solution)/shard_map/ppermute | solution.py:452
  44.9 5.6 %down_far_half.1 = (bf16[64,2048]{1,0:T(8,128)(2,1)S(1)}, bf16[64,3328]{1,0:T(8,128)(2,1)S(1)}) custom-call(bf16[2,64,3328]{2,1,0:T(8,128)(2,1)S(1)} %get-tuple-element.16.own_ref, bf16[2,64,3328]{2,1,0:T(8,128)(2,1)S(1)} %collective-permute-done.4.other_ref, bf16[3328,4096]{1,0:T(8,128)(2,1)} %w_hbm.3), custom_call_target="tpu_custom_call" | custom-call | flops 872415232 | bytes 13631488 | tf_op jit(solution)/shard_map/down_far_half/pallas_call | solution.py:231
  50.5 1.6 %collective-permute-start.5 = (bf16[64,2048]{1,0:T(8,128)(2,1)S(1)}, bf16[64,2048]{1,0:T(8,128)(2,1)S(1)}, u32[]{:S(2)}, u32[]{:S(2)}) collective-permute-start(bf16[64,2048]{1,0:T(8,128)(2,1)S(1)} %get-tuple-element.18), channel_id=1, source_target_pairs={{0,2},{2,0},{4,6},{6,4},{8,10},{10,8},{12,14},{14,12},{1,3},{3,1},... | collective-permute-start | bytes 786440 | tf_op jit(solution)/shard_map/ppermute | solution.py:454
  52.1 5.7 %down_near_half.1.near_ref = f32[64,2048]{1,0:T(8,128)S(1)} custom-call(bf16[64,3328]{1,0:T(8,128)(2,1)S(1)} %get-tuple-element.17.hidden_ref, bf16[3328,4096]{1,0:T(8,128)(2,1)} %w_hbm.3), custom_call_target="tpu_custom_call" | custom-call | flops 872415232 | bytes 13631488 | tf_op jit(solution)/shard_map/down_near_half/pallas_call | solution.py:277
  57.9 1.0 %collective-permute-done.5.far_ref = bf16[64,2048]{1,0:T(8,128)(2,1)S(1)} collective-permute-done((bf16[64,2048]{1,0:T(8,128)(2,1)S(1)}, bf16[64,2048]{1,0:T(8,128)(2,1)S(1)}, u32[]{:S(2)}, u32[]{:S(2)}) %collective-permute-start.5) | collective-permute-done | bytes 262176 | tf_op jit(solution)/shard_map/ppermute | solution.py:454
  58.9 0.4 to_slots.1
  59.3 0.8 collective-permute-start.6
  60.1 1.6 %collective-permute-start.7 = (bf16[32,2048]{1,0:T(8,128)(2,1)S(1)}, bf16[32,2048]{1,0:T(8,128)(2,1)S(1)}, u32[]{:S(2)}, u32[]{:S(2)}) collective-permute-start(bf16[32,2048]{1,0:T(8,128)(2,1)S(1)} %get-tuple-element.21), channel_id=1, source_target_pairs={{0,8},{2,10},{4,12},{6,14},{8,0},{10,2},{12,4},{14,6},{1,9},{3,11}... | collective-permute-start | bytes 393224 | tf_op jit(solution)/shard_map/ppermute | solution.py:459
  61.7 2.1 %collective-permute-start.8 = (bf16[32,2048]{1,0:T(8,128)(2,1)S(1)}, bf16[32,2048]{1,0:T(8,128)(2,1)S(1)}, u32[]{:S(2)}, u32[]{:S(2)}) collective-permute-start(bf16[32,2048]{1,0:T(8,128)(2,1)S(1)} %get-tuple-element.22), channel_id=1, source_target_pairs={{0,12},{2,14},{4,8},{6,10},{8,4},{10,6},{12,0},{14,2},{1,13},{3,15... | collective-permute-start | bytes 393224 | tf_op jit(solution)/shard_map/ppermute | solution.py:459
  63.8 2.0 %collective-permute-done.6.refs_0_ = bf16[32,2048]{1,0:T(8,128)(2,1)S(1)} collective-permute-done((bf16[32,2048]{1,0:T(8,128)(2,1)S(1)}, bf16[32,2048]{1,0:T(8,128)(2,1)S(1)}, u32[]{:S(2)}, u32[]{:S(2)}) %collective-permute-start.6) | collective-permute-done | bytes 131104 | tf_op jit(solution)/shard_map/ppermute | solution.py:459
  65.8 6.8 %collective-permute-done.7.refs_1_ = bf16[32,2048]{1,0:T(8,128)(2,1)S(1)} collective-permute-done((bf16[32,2048]{1,0:T(8,128)(2,1)S(1)}, bf16[32,2048]{1,0:T(8,128)(2,1)S(1)}, u32[]{:S(2)}, u32[]{:S(2)}) %collective-permute-start.7) | collective-permute-done | bytes 131104 | tf_op jit(solution)/shard_map/ppermute | solution.py:459
  72.6 0.3 finish.1
  72.8 1.6 %collective-permute-start.9 = (bf16[16,2048]{1,0:T(8,128)(2,1)S(1)}, bf16[16,2048]{1,0:T(8,128)(2,1)S(1)}, u32[]{:S(2)}, u32[]{:S(2)}) collective-permute-start(bf16[16,2048]{1,0:T(8,128)(2,1)S(1)} %get-tuple-element.24), channel_id=1, source_target_pairs={{0,2},{2,0},{4,6},{6,4},{8,10},{10,8},{12,14},{14,12},{1,3},{3,1},... | collective-permute-start | bytes 196616 | tf_op jit(solution)/shard_map/ppermute | solution.py:462
  74.4 2.8 %collective-permute-done.9.other_ref = bf16[16,2048]{1,0:T(8,128)(2,1)S(1)} collective-permute-done((bf16[16,2048]{1,0:T(8,128)(2,1)S(1)}, bf16[16,2048]{1,0:T(8,128)(2,1)S(1)}, u32[]{:S(2)}, u32[]{:S(2)}) %collective-permute-start.9) | collective-permute-done | bytes 65568 | tf_op jit(solution)/shard_map/ppermute | solution.py:462
  77.2 0.7 join_halves.1
  (7 shorter events, 0.2 us)
Async XLA Ops:
  5.4 5.7 %collective-permute-start = (bf16[8,4096]{1,0:T(8,128)(2,1)}, bf16[8,4096]{1,0:T(8,128)(2,1)S(1)}, u32[]{:S(2)}, u32[]{:S(2)}) collective-permute-start(bf16[8,4096]{1,0:T(8,128)(2,1)} %attention.1), channel_id=1, source_target_pairs={{0,4},{2,6},{4,0},{6,2},{8,12},{10,14},{12,8},{14,10},{1,5},{3,7},... | collective-permute-start | bytes 196616 | tf_op jit(solution)/shard_map/ppermute | solution.py:448
  8.5 7.5 %collective-permute-start.1 = (bf16[8,4096]{1,0:T(8,128)(2,1)}, bf16[8,4096]{1,0:T(8,128)(2,1)S(1)}, u32[]{:S(2)}, u32[]{:S(2)}) collective-permute-start(bf16[8,4096]{1,0:T(8,128)(2,1)} %attention.1), channel_id=1, source_target_pairs={{0,8},{2,10},{4,12},{6,14},{8,0},{10,2},{12,4},{14,6},{1,9},{3,11}... | collective-permute-start | bytes 196616 | tf_op jit(solution)/shard_map/ppermute | solution.py:448
  11.1 6.3 %collective-permute-start.2 = (bf16[8,4096]{1,0:T(8,128)(2,1)}, bf16[8,4096]{1,0:T(8,128)(2,1)S(1)}, u32[]{:S(2)}, u32[]{:S(2)}) collective-permute-start(bf16[8,4096]{1,0:T(8,128)(2,1)} %attention.1), channel_id=1, source_target_pairs={{0,12},{2,14},{4,8},{6,10},{8,4},{10,6},{12,0},{14,2},{1,13},{3,15... | collective-permute-start | bytes 196616 | tf_op jit(solution)/shard_map/ppermute | solution.py:448
  18.3 6.5 %collective-permute-start.3 = (bf16[4,8,4096]{2,1,0:T(8,128)(2,1)S(1)}, bf16[4,8,4096]{2,1,0:T(8,128)(2,1)S(1)}, u32[]{:S(2)}, u32[]{:S(2)}) collective-permute-start(bf16[4,8,4096]{2,1,0:T(8,128)(2,1)S(1)} %pad_maximum_fusion.own_ref), channel_id=1, source_target_pairs={{0,2},{2,0},{4,6},{6,4},{8,10},{10,8},{12,14},{14,12},{1,3},{3,1},... | collective-permute-start | bytes 786440 | tf_op jit(solution)/shard_map/ppermute | solution.py:450
  42.5 9.6 %copy-start = (s32[64,1]{0,1:T(1,128)S(1)}, s32[64,1]{0,1:T(1,128)}, u32[]{:S(2)}) copy-start(s32[64,1]{0,1:T(1,128)} %param.14) | copy-start | bytes 772
  42.5 2.4 %collective-permute-start.4 = (bf16[2,64,3328]{2,1,0:T(8,128)(2,1)S(1)}, bf16[2,64,3328]{2,1,0:T(8,128)(2,1)S(1)}, u32[]{:S(2)}, u32[]{:S(2)}) collective-permute-start(bf16[2,64,3328]{2,1,0:T(8,128)(2,1)S(1)} %get-tuple-element.16.own_ref), channel_id=1, source_target_pairs={{0,1},{1,0},{2,3},{3,2},{4,5},{5,4},{6,7},{7,6},{8,9},{9,8},{10,11... | collective-permute-start | bytes 2555912 | tf_op jit(solution)/shard_map/ppermute | solution.py:452
  50.5 8.4 %collective-permute-start.5 = (bf16[64,2048]{1,0:T(8,128)(2,1)S(1)}, bf16[64,2048]{1,0:T(8,128)(2,1)S(1)}, u32[]{:S(2)}, u32[]{:S(2)}) collective-permute-start(bf16[64,2048]{1,0:T(8,128)(2,1)S(1)} %get-tuple-element.18), channel_id=1, source_target_pairs={{0,2},{2,0},{4,6},{6,4},{8,10},{10,8},{12,14},{14,12},{1,3},{3,1},... | collective-permute-start | bytes 786440 | tf_op jit(solution)/shard_map/ppermute | solution.py:454
  59.3 6.5 %collective-permute-start.6 = (bf16[32,2048]{1,0:T(8,128)(2,1)S(1)}, bf16[32,2048]{1,0:T(8,128)(2,1)S(1)}, u32[]{:S(2)}, u32[]{:S(2)}) collective-permute-start(bf16[32,2048]{1,0:T(8,128)(2,1)S(1)} %get-tuple-element.20), channel_id=1, source_target_pairs={{0,4},{2,6},{4,0},{6,2},{8,12},{10,14},{12,8},{14,10},{1,5},{3,7},... | collective-permute-start | bytes 393224 | tf_op jit(solution)/shard_map/ppermute | solution.py:459
  60.1 12.5 %collective-permute-start.7 = (bf16[32,2048]{1,0:T(8,128)(2,1)S(1)}, bf16[32,2048]{1,0:T(8,128)(2,1)S(1)}, u32[]{:S(2)}, u32[]{:S(2)}) collective-permute-start(bf16[32,2048]{1,0:T(8,128)(2,1)S(1)} %get-tuple-element.21), channel_id=1, source_target_pairs={{0,8},{2,10},{4,12},{6,14},{8,0},{10,2},{12,4},{14,6},{1,9},{3,11}... | collective-permute-start | bytes 393224 | tf_op jit(solution)/shard_map/ppermute | solution.py:459
  61.7 10.9 %collective-permute-start.8 = (bf16[32,2048]{1,0:T(8,128)(2,1)S(1)}, bf16[32,2048]{1,0:T(8,128)(2,1)S(1)}, u32[]{:S(2)}, u32[]{:S(2)}) collective-permute-start(bf16[32,2048]{1,0:T(8,128)(2,1)S(1)} %get-tuple-element.22), channel_id=1, source_target_pairs={{0,12},{2,14},{4,8},{6,10},{8,4},{10,6},{12,0},{14,2},{1,13},{3,15... | collective-permute-start | bytes 393224 | tf_op jit(solution)/shard_map/ppermute | solution.py:459
  72.8 4.3 %collective-permute-start.9 = (bf16[16,2048]{1,0:T(8,128)(2,1)S(1)}, bf16[16,2048]{1,0:T(8,128)(2,1)S(1)}, u32[]{:S(2)}, u32[]{:S(2)}) collective-permute-start(bf16[16,2048]{1,0:T(8,128)(2,1)S(1)} %get-tuple-element.24), channel_id=1, source_target_pairs={{0,2},{2,0},{4,6},{6,4},{8,10},{10,8},{12,14},{14,12},{1,3},{3,1},... | collective-permute-start | bytes 196616 | tf_op jit(solution)/shard_map/ppermute | solution.py:462

commit v4 on v3

v4 whole, which is shorter than its diff:
```python
import functools
import math

import jax
import jax.numpy as jnp
from jax import lax
from jax.experimental import pallas as pl
from jax.experimental.pallas import tpu as pltpu
from jax.sharding import PartitionSpec as P

AXIS = "attn"
TILE = 256
BAND = 256
MIB = 1 << 20
VMEM = pl.BlockSpec(memory_space=pltpu.VMEM)
SMEM = pl.BlockSpec(memory_space=pltpu.SMEM)
ANY = pl.BlockSpec(memory_space=pl.ANY)
HBM = pl.BlockSpec(memory_space=pltpu.HBM)
F32 = jnp.float32
BF16 = jnp.bfloat16


def params(mib):
    return pltpu.CompilerParams(vmem_limit_bytes=mib * MIB)


def in_vmem(array):
    return pltpu.with_memory_space_constraint(array, pltpu.VMEM)


def in_hbm(array):
    return pltpu.with_memory_space_constraint(array, pltpu.HBM)


def cost(flops, moved):
    return pl.CostEstimate(flops=flops, bytes_accessed=moved, transcendentals=0)


def grid_of(devices):
    nx = 1
    while 4 * nx * nx < devices:
        nx *= 2
    if devices % nx:
        nx = 1
    return devices // nx, nx


def swap_z(devices, bits):
    nz, nx = grid_of(devices)
    return [(z * nx + x, (z ^ bits) * nx + x) for z in range(nz) for x in range(nx)]


def swap_x(devices):
    nz, nx = grid_of(devices)
    return [(z * nx + x, z * nx + (x ^ 1)) for z in range(nz) for x in range(nx)]


def attend_kernel(kv, bands, lengths, q_hbm, k_hbm, v_hbm, res_ref, *refs):
    weights = ()
    if bands:
        g_hbm, u_hbm, out_ref, held_ref, *refs, band_sems = refs
        weights = band_copies(g_hbm, u_hbm, held_ref, band_sems, 0)
    else:
        out_ref, *refs = refs
    att_ref, scores_ref, probs_ref, q_ref, k_ref, v_ref, sems = refs
    rows, heads, dim = q_ref.shape
    span = k_ref.shape[1]
    per_group = heads // kv
    loads = [
        pltpu.make_async_copy(source, held, sems.at[i])
        for i, (source, held) in enumerate(((q_hbm, q_ref), (k_hbm, k_ref), (v_hbm, v_ref)))
    ]
    for load in loads:
        load.start()
    for c in weights:
        c.start()
    column = lax.broadcasted_iota(jnp.int32, (heads, span), 1)
    head = lax.broadcasted_iota(jnp.int32, (heads, span), 0)
    right_group = (column % kv) == (head // per_group)
    position = column // kv

    def at(r):
        return slice(r * heads, (r + 1) * heads)

    loads[0].wait()
    loads[1].wait()
    for r in range(rows):
        scores = lax.dot_general(
            q_ref[r], k_ref[r], (((1,), (1,)), ((), ())), preferred_element_type=F32
        ) * (1.0 / math.sqrt(dim))
        scores_ref[at(r), :] = jnp.where(right_group & (position < lengths[r]), scores, -1e30)
    for r in range(rows):
        scores = scores_ref[at(r), :]
        raw = jnp.exp(scores - jnp.max(scores, axis=-1, keepdims=True))
        probs_ref[at(r), :] = (raw / jnp.sum(raw, axis=-1, keepdims=True)).astype(BF16)
    loads[2].wait()
    for r in range(rows):
        att_ref[at(r), :] = jnp.dot(probs_ref[at(r), :], v_ref[r], preferred_element_type=F32)
    for h in range(heads):
        lanes = slice(h * dim, (h + 1) * dim)
        mine = att_ref[pl.ds(h, rows, stride=heads), :]
        out_ref[:, lanes] = (res_ref[:, lanes].astype(F32) + mine).astype(BF16)
    for c in weights:
        c.wait()


def attend(queries, cache_keys, stored_value_cache, lengths, residual, weights, bands):
    rows, heads, dim = queries.shape
    kv = cache_keys.shape[2]
    span = cache_keys.shape[1] * kv
    held = [pltpu.VMEM((bands, 2, BAND, w.shape[1]), BF16) for w in weights[:1]]
    band_sems = [pltpu.SemaphoreType.DMA((bands, 2)) for _ in held]
    return pl.pallas_call(
        functools.partial(attend_kernel, kv, bands),
        out_shape=(jax.ShapeDtypeStruct((rows, heads * dim), BF16), *held),
        in_specs=[SMEM, HBM, HBM, HBM, VMEM] + [HBM for _ in weights],
        out_specs=(VMEM,) + tuple(VMEM for _ in held),
        scratch_shapes=[
            pltpu.VMEM((rows * heads, dim), F32),
            pltpu.VMEM((rows * heads, span), F32),
            pltpu.VMEM((rows * heads, span), BF16),
            pltpu.VMEM(queries.shape, BF16),
            pltpu.VMEM((rows, span, dim), BF16),
            pltpu.VMEM((rows, span, dim), BF16),
            pltpu.SemaphoreType.DMA((3,)),
        ]
        + band_sems,
        compiler_params=params(8),
        cost_estimate=cost(rows * heads * span * dim * 4, rows * span * dim * 4),
        name="attention",
    )(
        in_hbm(lengths),
        in_hbm(queries),
        in_hbm(cache_keys.reshape(rows, span, dim)),
        in_hbm(stored_value_cache.reshape(rows, span, dim)),
        in_hbm(residual),
        *(in_hbm(w) for w in weights),
    )


def band_copies(g_hbm, u_hbm, held_ref, sems, first):
    return [
        pltpu.make_async_copy(
            w.at[pl.ds((first + i) * BAND, BAND)], held_ref.at[i, kind], sems.at[i, kind]
        )
        for i in range(held_ref.shape[0])
        for kind, w in enumerate((g_hbm, u_hbm))
    ]


def load_kernel(first, after_ref, g_hbm, u_hbm, held_ref, sems):
    copies = band_copies(g_hbm, u_hbm, held_ref, sems, first)
    for c in copies:
        c.start()
    for c in copies:
        c.wait()


def load_bands(after, gate_weight, up_weight, first, bands):
    columns = gate_weight.shape[1]
    return pl.pallas_call(
        functools.partial(load_kernel, first),
        out_shape=pltpu.VMEM((bands, 2, BAND, columns), BF16),
        in_specs=[ANY, HBM, HBM],
        out_specs=VMEM,
        scratch_shapes=[pltpu.SemaphoreType.DMA((bands, 2))],
        compiler_params=params(2),
        cost_estimate=cost(0, bands * 2 * BAND * columns * 2),
        name="load_bands",
    )(after, in_hbm(gate_weight), in_hbm(up_weight))


def hold(array, after):
    return pl.pallas_call(
        lambda array_ref, after_ref, out_ref: None,
        out_shape=jax.ShapeDtypeStruct(array.shape, array.dtype),
        in_specs=[ANY, ANY],
        out_specs=ANY,
        input_output_aliases={0: 0},
        compiler_params=params(2),
        name="hold",
    )(array, after)


def pack_kernel(a_ref, b_ref, after_ref, out_ref):
    out_ref[0] = a_ref[...]
    out_ref[1] = b_ref[...]


def pack(a, b, after):
    return pl.pallas_call(
        pack_kernel,
        out_shape=jax.ShapeDtypeStruct((2,) + a.shape, a.dtype),
        in_specs=[VMEM, VMEM, ANY],
        out_specs=VMEM,
        compiler_params=params(4),
        name="pack",
    )(a, b, after)


def tile_at(index):
    return pl.ds(pl.multiple_of(index * TILE, TILE), TILE)


def gate_up_kernel(devices, holders, first, *refs):
    a_ref, b_ref, c_ref, d_ref, g_hbm, u_hbm = refs[:6]
    held_refs = refs[6 : 6 + holders]
    part_ref, rows_ref, total_ref, buf, sems = refs[6 + holders :]
    nx = grid_of(devices)[1]
    slots = buf.shape[0]
    streamed = band_copies(g_hbm, u_hbm, buf, sems, first)
    late = band_copies(g_hbm, u_hbm, buf.at[0:1], sems, first + slots)
    for c in streamed:
        c.start()
    me = lax.axis_index(AXIS)
    my_z, my_x = me // nx, me % nx
    per = a_ref.shape[1]
    for near, far, flip in ((a_ref, b_ref, 0), (c_ref, d_ref, 1)):
        for i in range(2):
            z = my_z ^ (flip + 2 * i)
            here, there = near[i].astype(F32), far[i].astype(F32)
            pair = [jnp.where(my_x == 0, here, there), jnp.where(my_x == 0, there, here)]
            at = pl.ds(pl.multiple_of(z * (2 * per), 2 * per), 2 * per)
            rows_ref[at, :] = jnp.concatenate(pair, axis=0).astype(BF16)

    def band(i):
        if isinstance(i, int):
            return slice(i * BAND, (i + 1) * BAND)
        return pl.ds(pl.multiple_of(i * BAND, BAND), BAND)

    def add(i, weight, kind):
        total_ref[kind] += jnp.dot(rows_ref[:, band(i)], weight, preferred_element_type=F32)

    def add_streamed(index, slot, copies):
        for kind, c in enumerate(copies):
            c.wait()
            add(index, buf[slot, kind], kind)

    total_ref[...] = jnp.zeros_like(total_ref)
    start = 0
    for number, held in enumerate(held_refs):

        def step(i, _, held=held, start=start):
            for kind in range(2):
                add(start + i, held[i, kind], kind)
            return 0

        lax.fori_loop(0, held.shape[0], step, 0)
        start += held.shape[0]
        if number == 1:
            add_streamed(first, 0, streamed[:2])
            for c in late:
                c.start()
    for slot in range(1, slots):
        add_streamed(first + slot, slot, streamed[2 * slot : 2 * slot + 2])
    add_streamed(first + slots, 0, late)
    part_ref[...] = total_ref[...].astype(BF16)


def gate_up(blocks, gate_weight, up_weight, held, devices):
    total = devices * blocks[0].shape[1]
    features, columns = gate_weight.shape
    first = sum(h.shape[0] for h in held)
    slots = features // BAND - first - 1
    return pl.pallas_call(
        functools.partial(gate_up_kernel, devices, len(held), first),
        out_shape=(
            jax.ShapeDtypeStruct((2, total, columns), BF16),
            jax.ShapeDtypeStruct((total, features), BF16),
        ),
        in_specs=[VMEM] * 4 + [HBM, HBM] + [VMEM] * len(held),
        out_specs=(VMEM, VMEM),
        scratch_shapes=[
            pltpu.VMEM((2, total, columns), F32),
            pltpu.VMEM((slots, 2, BAND, columns), BF16),
            pltpu.SemaphoreType.DMA((slots, 2)),
        ],
        compiler_params=params(13),
        cost_estimate=cost(4 * total * features * columns, 4 * features * columns),
        name="gate_up",
    )(*blocks, in_hbm(gate_weight), in_hbm(up_weight), *(in_vmem(h) for h in held))


def half_copies(w_hbm, base, held_ref, sems, first):
    half = held_ref.shape[2]
    return [
        pltpu.make_async_copy(
            w_hbm.at[pl.ds((first + i) * TILE, TILE), pl.ds(base, half)],
            held_ref.at[i],
            sems.at[i],
        )
        for i in range(held_ref.shape[0])
    ]


def half_base(devices, mine, half):
    my_x = lax.axis_index(AXIS) % grid_of(devices)[1]
    return pl.multiple_of((my_x if mine else 1 - my_x) * half, half)


def down_load_kernel(devices, after_ref, w_hbm, held_ref, sems):
    base = half_base(devices, False, held_ref.shape[2])
    copies = half_copies(w_hbm, base, held_ref, sems, 0)
    for c in copies:
        c.start()
    for c in copies:
        c.wait()


def load_down(after, down_weight, devices, tiles):
    half = down_weight.shape[1] // 2
    return pl.pallas_call(
        functools.partial(down_load_kernel, devices),
        out_shape=pltpu.VMEM((tiles, TILE, half), BF16),
        in_specs=[ANY, HBM],
        out_specs=VMEM,
        scratch_shapes=[pltpu.SemaphoreType.DMA((tiles,))],
        compiler_params=params(2),
        cost_estimate=cost(0, tiles * TILE * half * 2),
        name="load_down",
    )(after, in_hbm(down_weight))


def add_half(hidden_ref, held_ref, buf, copies, total_ref):
    held = held_ref.shape[0]
    total_ref[...] = jnp.zeros_like(total_ref)

    def step(i, _):
        total_ref[...] += jnp.dot(
            hidden_ref[:, tile_at(i)], held_ref[i], preferred_element_type=F32
        )
        return 0

    lax.fori_loop(0, held, step, 0)
    for i, c in enumerate(copies):
        c.wait()
        at = slice((held + i) * TILE, (held + i + 1) * TILE)
        total_ref[...] += jnp.dot(hidden_ref[:, at], buf[i], preferred_element_type=F32)


def down_far_kernel(
    devices,
    own_ref,
    other_ref,
    held_ref,
    w_hbm,
    out_ref,
    hidden_ref,
    next_ref,
    total_ref,
    buf,
    sems,
    next_sems,
):
    half = out_ref.shape[1]
    copies = half_copies(w_hbm, half_base(devices, False, half), buf, sems, held_ref.shape[0])
    ahead = half_copies(w_hbm, half_base(devices, True, half), next_ref, next_sems, 0)
    for c in copies + ahead:
        c.start()
    gate = own_ref[0].astype(F32) + other_ref[0].astype(F32)
    up = own_ref[1].astype(F32) + other_ref[1].astype(F32)
    hidden_ref[...] = (gate / (1.0 + jnp.exp(-gate)) * up).astype(BF16)
    add_half(hidden_ref, held_ref, buf, copies, total_ref)
    out_ref[...] = total_ref[...].astype(BF16)
    for c in ahead:
        c.wait()


def down_far(own, other, held, down_weight, devices, ahead):
    total = own.shape[1]
    columns, features = down_weight.shape
    half = features // 2
    left = columns // TILE - held.shape[0]
    return pl.pallas_call(
        functools.partial(down_far_kernel, devices),
        out_shape=(
            jax.ShapeDtypeStruct((total, half), BF16),
            jax.ShapeDtypeStruct((total, columns), BF16),
            pltpu.VMEM((ahead, TILE, half), BF16),
        ),
        in_specs=[VMEM, VMEM, VMEM, HBM],
        out_specs=(VMEM, VMEM, VMEM),
        scratch_shapes=[
            pltpu.VMEM((total, half), F32),
            pltpu.VMEM((left, TILE, half), BF16),
            pltpu.SemaphoreType.DMA((left,)),
            pltpu.SemaphoreType.DMA((ahead,)),
        ],
        compiler_params=params(20),
        cost_estimate=cost(total * features * columns, features * columns),
        name="down_far_half",
    )(own, other, in_vmem(held), in_hbm(down_weight))


def down_near_kernel(devices, hidden_ref, held_ref, w_hbm, out_ref, buf, sems):
    half = out_ref.shape[1]
    copies = half_copies(w_hbm, half_base(devices, True, half), buf, sems, held_ref.shape[0])
    for c in copies:
        c.start()
    add_half(hidden_ref, held_ref, buf, copies, out_ref)


def down_near(hidden, held, down_weight, devices):
    total = hidden.shape[0]
    columns, features = down_weight.shape
    half = features // 2
    left = columns // TILE - held.shape[0]
    return pl.pallas_call(
        functools.partial(down_near_kernel, devices),
        out_shape=jax.ShapeDtypeStruct((total, half), F32),
        in_specs=[VMEM, VMEM, HBM],
        out_specs=VMEM,
        scratch_shapes=[
            pltpu.VMEM((left, TILE, half), BF16),
            pltpu.SemaphoreType.DMA((left,)),
        ],
        compiler_params=params(20),
        cost_estimate=cost(total * features * columns, features * columns),
        name="down_near_half",
    )(hidden, in_vmem(held), in_hbm(down_weight))


def pick(row_ref, capacity, first_slot, slots):
    row = row_ref[...]
    total = row.shape[1]
    down = lax.broadcasted_iota(jnp.int32, (total, total), 0)
    across = lax.broadcasted_iota(jnp.int32, (total, total), 1)
    diagonal = jnp.where(down == across, row, 0).astype(F32).astype(BF16)
    column = jnp.dot(diagonal, jnp.ones((total, total), BF16), preferred_element_type=F32)
    earlier = (column == row.astype(F32)) & (down < across)
    rank = jnp.sum(earlier.astype(F32), axis=0, keepdims=True).astype(jnp.int32)
    slot = first_slot + lax.broadcasted_iota(jnp.int32, (slots, total), 0)
    return (slot == row * capacity + rank).astype(F32).astype(BF16)


def to_slots_kernel(devices, capacity, row_ref, near_ref, far_ref, own_ref, *sends):
    nz, nx = grid_of(devices)
    my_z = lax.axis_index(AXIS) // nx
    slots = own_ref.shape[0]
    total = near_ref[...] + far_ref[...].astype(F32)
    rounded = total.astype(BF16)
    for dz, send_ref in enumerate((own_ref,) + sends):
        z = my_z ^ dz
        chosen = pick(row_ref, capacity, z * slots, slots)
        if dz:
            send_ref[...] = jnp.dot(chosen, rounded, preferred_element_type=F32).astype(BF16)
        else:
            high = rounded.astype(F32)
            low = (total - high).astype(BF16)
            own_ref[...] = jnp.dot(chosen, rounded, preferred_element_type=F32) + jnp.dot(
                chosen, low, preferred_element_type=F32
            )


def to_slots(row, near, far, devices, capacity):
    nz, nx = grid_of(devices)
    slots = nx * 2 * capacity
    width = near.shape[1]
    return pl.pallas_call(
        functools.partial(to_slots_kernel, devices, capacity),
        out_shape=(jax.ShapeDtypeStruct((slots, width), F32),)
        + (jax.ShapeDtypeStruct((slots, width), BF16),) * (nz - 1),
        in_specs=[VMEM] * 3,
        out_specs=(VMEM,) * nz,
        compiler_params=params(8),
        name="to_slots",
    )(row, near, far)


def finish_kernel(devices, capacity, row_ref, rows_ref, own_ref, *refs):
    *landed, keep_ref, send_ref = refs
    nz, nx = grid_of(devices)
    me = lax.axis_index(AXIS)
    my_z, my_x = me // nx, me % nx
    slots, width = own_ref.shape
    chosen = pick(row_ref, capacity, my_z * slots, slots)
    mixed = rows_ref[:, pl.ds(pl.multiple_of(my_x * width, width), width)]
    total = own_ref[...]
    for ref in landed:
        total = total + ref[...].astype(F32)
    done = jnp.dot(chosen, mixed, preferred_element_type=F32) + total
    half = slots // 2
    first, second = done[:half], done[half:]
    keep_ref[...] = jnp.where(my_x == 0, first, second).astype(BF16)
    send_ref[...] = jnp.where(my_x == 0, second, first).astype(BF16)


def finish(row, rows, own, landed, devices, capacity):
    slots, width = own.shape
    shape = jax.ShapeDtypeStruct((slots // 2, width), BF16)
    return pl.pallas_call(
        functools.partial(finish_kernel, devices, capacity),
        out_shape=(shape, shape),
        in_specs=[VMEM] * (3 + len(landed)),
        out_specs=(VMEM, VMEM),
        compiler_params=params(8),
        name="finish",
    )(row, rows, own, *landed)


def join_kernel(nx, keep_ref, other_ref, out_ref):
    my_x = lax.axis_index(AXIS) % nx
    width = keep_ref.shape[1]
    out_ref[:, :width] = jnp.where(my_x == 0, keep_ref[...], other_ref[...])
    out_ref[:, width:] = jnp.where(my_x == 0, other_ref[...], keep_ref[...])


def join(keep, other, devices):
    slots, width = keep.shape
    return pl.pallas_call(
        functools.partial(join_kernel, grid_of(devices)[1]),
        out_shape=jax.ShapeDtypeStruct((slots, 2 * width), BF16),
        in_specs=[VMEM, VMEM],
        out_specs=VMEM,
        compiler_params=params(8),
        name="join_halves",
    )(keep, other)


def slot_positions(column, destinations, capacity):
    onehot = (column[:, None] == jnp.arange(destinations, dtype=jnp.int32)[None, :]).astype(
        jnp.int32
    )
    before = jnp.cumsum(onehot, axis=0) - onehot
    slot_rank = jnp.sum(before * onehot, axis=1)
    return column * capacity + slot_rank


def plain(mixed_rows, target, gate_weight, up_weight, down_weight, devices):
    rows_dev, features = mixed_rows.shape
    me = lax.axis_index(AXIS)
    gathered = lax.all_gather(mixed_rows, AXIS, axis=0, tiled=True)
    mine = jnp.stack(
        [
            jnp.dot(gathered, gate_weight, preferred_element_type=F32),
            jnp.dot(gathered, up_weight, preferred_element_type=F32),
        ]
    )
    other = lax.ppermute(mine.astype(BF16), "ffn", [(0, 1), (1, 0)])
    gate_sum, up_sum = mine + other.astype(F32)
    hidden = (jax.nn.silu(gate_sum) * up_sum).astype(BF16)
    down = jnp.dot(hidden, down_weight, preferred_element_type=F32)
    share = features // devices
    landed = lax.all_to_all(
        jnp.moveaxis(down.astype(BF16).reshape(-1, devices, share), 1, 0), AXIS, 0, 0
    )
    summed = jnp.sum(landed.astype(F32), axis=0)
    mixed_share = lax.dynamic_slice_in_dim(gathered, me * share, share, axis=1)
    finished = (mixed_share.astype(F32) + summed).astype(BF16)
    slot_count = 2 * devices * rows_dev
    position = slot_positions(target[:, 0], 2 * devices, rows_dev)
    chosen = (jnp.arange(slot_count, dtype=jnp.int32)[:, None] == position[None, :]).astype(BF16)
    slots = jnp.dot(chosen, finished, preferred_element_type=F32).astype(BF16)
    slots = slots.reshape(devices, 2 * rows_dev, share)
    mine_out = lax.all_to_all(slots, AXIS, split_axis=0, concat_axis=0)
    return jnp.moveaxis(mine_out, 0, 1).reshape(2 * rows_dev, features)


def local(
    queries,
    cache_keys,
    stored_value_cache,
    lengths,
    residual,
    target,
    gate_weight,
    up_weight,
    down_weight,
):
    devices = lax.axis_size(AXIS)
    nz, nx = grid_of(devices)
    capacity = cache_keys.shape[0]
    columns, features = down_weight.shape
    fits = nz == 4 and nx == 2 and columns % TILE == 0 and features % (16 * TILE) == 0
    share = 3 * (gate_weight.shape[0] // BAND) // 16 if fits else 0
    mixed_rows, *held = attend(
        queries,
        cache_keys,
        stored_value_cache,
        lengths,
        residual,
        (gate_weight, up_weight) if fits else (),
        share,
    )
    if not fits:
        return plain(mixed_rows, target, gate_weight, up_weight, down_weight, devices)

    two = lax.ppermute(mixed_rows, AXIS, swap_z(devices, 2))
    held.append(load_bands(mixed_rows, gate_weight, up_weight, share, share))
    a = pack(mixed_rows, two, held[-1])
    b = lax.ppermute(a, AXIS, swap_x(devices))
    c = lax.ppermute(a, AXIS, swap_z(devices, 1))
    held.append(load_bands(a, gate_weight, up_weight, 2 * share, share))
    c = hold(c, held[-1])
    d = lax.ppermute(c, AXIS, swap_x(devices))
    held.append(load_bands(c, gate_weight, up_weight, 3 * share, share))
    part, rows = gate_up((a, b, c, d), gate_weight, up_weight, held, devices)
    other = lax.ppermute(part, "ffn", [(0, 1), (1, 0)])
    tiles = columns // TILE
    held_down = load_down(part, down_weight, devices, 6 * tiles // 13)
    far_half, hidden, held_near = down_far(
        part, other, held_down, down_weight, devices, 4 * tiles // 13
    )
    arrived = lax.ppermute(far_half, AXIS, swap_x(devices))
    near_half = down_near(hidden, held_near, down_weight, devices)
    row = target.reshape(1, -1)
    own_slots, *sends = to_slots(row, near_half, arrived, devices, capacity)
    landed = [
        lax.ppermute(send, AXIS, swap_z(devices, bits + 1)) for bits, send in enumerate(sends)
    ]
    keep, send = finish(row, rows, own_slots, landed, devices, capacity)
    return join(keep, lax.ppermute(send, AXIS, swap_x(devices)), devices)


def solution(mesh):
    return jax.shard_map(
        local,
        mesh=mesh,
        in_specs=(
            P(("parts", "attn"), "ffn", None),
            P(("parts", "attn"), None, "ffn", None),
            P(("parts", "attn"), None, "ffn", None),
            P(("parts", "attn")),
            P(("parts", "attn"), "ffn"),
            P("parts", None),
            P("ffn", "attn"),
            P("ffn", "attn"),
            P("attn", "ffn"),
        ),
        out_specs=P(("parts", "attn"), "ffn"),
        check_vma=False,
    )
```

time: 78.1 us -> 73.3 us (0.939)
  waiting for transfers between devices: 26.2 us -> 15.7 us
  Pallas kernels: 35.7 us -> 42.6 us
  other arithmetic: 0.87 us -> 0 us
    ppermute x4, waiting for transfers between devices: 11.2 us -> 0.41 us  [the longest x1 0.4 us: local(): d = lax.ppermute(c, AXIS, swap_x(devices))]
    pallas_call x3 -> x9, Pallas kernels: 28.7 us -> 36.6 us  [the longest x3 12 us: load_bands(): pl.pallas_call(functools.partial(load_kernel, first), out_shape=pltpu.VME...]
    ppermute x1, waiting for transfers between devices: 1.02 us -> 3.46 us  [local(): arrived = lax.ppermute(far_half, AXIS, swap_x(devices))]
    ppermute x1, waiting for transfers between devices: 2.37 us -> 0.01 us  [local(): other = lax.ppermute(part, 'ffn', [(0, 1), (1, 0)])]
    pallas_call x1, Pallas kernels: 5.73 us -> 4.11 us  [down_near(): pl.pallas_call(functools.partial(down_near_kernel, devices), out_shape=ja...]
    another operation x1 -> x0, other arithmetic: 0.87 us -> none  [local(): jnp.stack([mixed_rows] + [lax.ppermute(mixed_rows, AXIS, swap_z(devices,...]
  transfers between devices with their start and end apart: 10 -> 10, of which waited for: 8 -> 5; matrix products, arithmetic and copies ran while one was open for 0% -> 0% of each run, Pallas kernels for 7% -> 26%
where the time goes in v4:
time: 73.3 us; the launch traced here: 73.1 us
  Pallas kernels  42.6 us (58%)
  waiting for transfers between devices  15.7 us (21%)
  starting transfers between devices  14.7 us (20%)
    pallas_call x3, Pallas kernels, load_bands(): pl.pallas_call(functools.partial(load_kernel, first), out_shape=pltpu.VME...  12 us
    pallas_call x1, Pallas kernels, gate_up(): pl.pallas_call(functools.partial(gate_up_kernel, devices, len(held), firs...  12 us
    ppermute x3, waiting for transfers between devices, local(): lax.ppermute(send, AXIS, swap_z(devices, bits + 1))  8.69 us
    pallas_call x1, Pallas kernels, attend(): pl.pallas_call(functools.partial(attend_kernel, kv, bands), out_shape=(ja...  5.21 us
    ppermute x3, starting transfers between devices, local(): lax.ppermute(send, AXIS, swap_z(devices, bits + 1))  4.45 us
    pallas_call x1, Pallas kernels, down_far(): pl.pallas_call(functools.partial(down_far_kernel, devices), out_shape=(ja...  4.42 us
    pallas_call x1, Pallas kernels, down_near(): pl.pallas_call(functools.partial(down_near_kernel, devices), out_shape=ja...  4.11 us
    ppermute x1, starting transfers between devices, local(): two = lax.ppermute(mixed_rows, AXIS, swap_z(devices, 2))  4.1 us
  transfers between devices with their start and end apart: 10, of which 5 were waited for; matrix products, arithmetic and copies ran while one was open for 0% of the time, Pallas kernels for 26%

profile of v4, /device:TPU:0, one launch (start us, length us, event | category | flops | bytes accessed | tf_op | source)
XLA Modules:
  0.0 73.1 jit_solution(4096011211031313438)
XLA Ops:
  0.0 5.2 %attention.1 = (bf16[8,4096]{1,0:T(8,128)(2,1)S(1)}, bf16[3,2,256,3328]{3,2,1,0:T(8,128)(2,1)S(1)}) custom-call(s32[8]{0:T(128)} %lengths.1, bf16[8,32,128]{2,1,0:T(8,128)(2,1)} %q_hbm.1, bf16[8,256,128]{2,1,0:T(8,128)(2,1)} %bitcast.5, bf16[8,256,128]{2,1,0:T(8,128)(2,1)} %bitcast.6, bf16[8,4096]{1,0:T(8,128)(2,1)} %res_ref.1, bf16[4096,3328]{1,0:T(8,128)(2,1)} %refs_4_.1, ...), custom_call_target="tpu_custom_call" | custom-call | flops 33554432 | bytes 1048576 | tf_op jit(solution)/shard_map/attention/pallas_call | solution.py:113
  5.2 4.1 %collective-permute-start = (bf16[8,4096]{1,0:T(8,128)(2,1)S(1)}, bf16[8,4096]{1,0:T(8,128)(2,1)S(1)}, u32[]{:S(2)}, u32[]{:S(2)}) collective-permute-start(bf16[8,4096]{1,0:T(8,128)(2,1)S(1)} %get-tuple-element.18.after_ref.a_ref), channel_id=1, source_target_pairs={{0,8},{2,10},{4,12},{6,14},{8,0},{10,2},{12,4},{14,6},{1,9},{3,11}... | collective-permute-start | bytes 196616 | tf_op jit(solution)/shard_map/ppermute | solution.py:588
  9.3 4.0 %load_bands.3.after_ref.refs_7_ = bf16[3,2,256,3328]{3,2,1,0:T(8,128)(2,1)S(1)} custom-call(bf16[8,4096]{1,0:T(8,128)(2,1)S(1)} %get-tuple-element.18.after_ref.a_ref, bf16[4096,3328]{1,0:T(8,128)(2,1)} %refs_4_.1, bf16[4096,3328]{1,0:T(8,128)(2,1)} %refs_5_.1), custom_call_target="tpu_custom_call" | custom-call | bytes 10223616 | tf_op jit(solution)/shard_map/load_bands/pallas_call | solution.py:161
  13.4 1.6 %collective-permute-start.2 = (bf16[2,8,4096]{2,1,0:T(8,128)(2,1)S(1)}, bf16[2,8,4096]{2,1,0:T(8,128)(2,1)S(1)}, u32[]{:S(2)}, u32[]{:S(2)}) collective-permute-start(bf16[2,8,4096]{2,1,0:T(8,128)(2,1)S(1)} %pack.1.after_ref.refs_0_), channel_id=1, source_target_pairs={{0,4},{2,6},{4,0},{6,2},{8,12},{10,14},{12,8},{14,10},{1,5},{3,7},... | collective-permute-start | bytes 393224 | tf_op jit(solution)/shard_map/ppermute | solution.py:592
  15.0 1.5 %collective-permute-start.1 = (bf16[2,8,4096]{2,1,0:T(8,128)(2,1)S(1)}, bf16[2,8,4096]{2,1,0:T(8,128)(2,1)S(1)}, u32[]{:S(2)}, u32[]{:S(2)}) collective-permute-start(bf16[2,8,4096]{2,1,0:T(8,128)(2,1)S(1)} %pack.1.after_ref.refs_0_), channel_id=1, source_target_pairs={{0,2},{2,0},{4,6},{6,4},{8,10},{10,8},{12,14},{14,12},{1,3},{3,1},... | collective-permute-start | bytes 393224 | tf_op jit(solution)/shard_map/ppermute | solution.py:591
  16.5 4.0 %load_bands.4.after_ref.refs_8_ = bf16[3,2,256,3328]{3,2,1,0:T(8,128)(2,1)S(1)} custom-call(bf16[2,8,4096]{2,1,0:T(8,128)(2,1)S(1)} %pack.1.after_ref.refs_0_, bf16[4096,3328]{1,0:T(8,128)(2,1)} %refs_4_.1, bf16[4096,3328]{1,0:T(8,128)(2,1)} %refs_5_.1), custom_call_target="tpu_custom_call" | custom-call | bytes 10223616 | tf_op jit(solution)/shard_map/load_bands/pallas_call | solution.py:161
  20.5 0.6 collective-permute-start.3
  21.1 4.0 %load_bands.5.refs_9_ = bf16[3,2,256,3328]{3,2,1,0:T(8,128)(2,1)S(1)} custom-call(bf16[2,8,4096]{2,1,0:T(8,128)(2,1)S(1)} %hold.1.after_ref.refs_2_, bf16[4096,3328]{1,0:T(8,128)(2,1)} %refs_4_.1, bf16[4096,3328]{1,0:T(8,128)(2,1)} %refs_5_.1), custom_call_target="tpu_custom_call" | custom-call | bytes 10223616 | tf_op jit(solution)/shard_map/load_bands/pallas_call | solution.py:161
  25.2 0.4 collective-permute-done.3.refs_3_
  25.6 12.0 %gate_up.1 = (bf16[2,64,3328]{2,1,0:T(8,128)(2,1)S(1)}, bf16[64,4096]{1,0:T(8,128)(2,1)S(1)}) custom-call(bf16[2,8,4096]{2,1,0:T(8,128)(2,1)S(1)} %pack.1.after_ref.refs_0_, bf16[2,8,4096]{2,1,0:T(8,128)(2,1)S(1)} %collective-permute-done.1.refs_1_, bf16[2,8,4096]{2,1,0:T(8,128)(2,1)S(1)} %hold.1.after_ref.refs_2_, ...), custom_call_target="tpu_custom_call" | custom-call | flops 3489660928 | bytes 54525952 | tf_op jit(solution)/shard_map/gate_up/pallas_call | solution.py:265
  37.7 2.9 %load_down.1.held_ref = bf16[6,256,2048]{2,1,0:T(8,128)(2,1)S(1)} custom-call(bf16[2,64,3328]{2,1,0:T(8,128)(2,1)S(1)} %get-tuple-element.21.after_ref.own_ref, bf16[3328,4096]{1,0:T(8,128)(2,1)} %w_hbm.5), custom_call_target="tpu_custom_call" | custom-call | bytes 6291456 | tf_op jit(solution)/shard_map/load_down/pallas_call | solution.py:312
  40.6 4.4 %down_far_half.1 = (bf16[64,2048]{1,0:T(8,128)(2,1)S(1)}, bf16[64,3328]{1,0:T(8,128)(2,1)S(1)}, bf16[4,256,2048]{2,1,0:T(8,128)(2,1)S(1)}) custom-call(bf16[2,64,3328]{2,1,0:T(8,128)(2,1)S(1)} %get-tuple-element.21.after_ref.own_ref, bf16[2,64,3328]{2,1,0:T(8,128)(2,1)S(1)} %collective-permute-done.4.other_ref, bf16[6,256,2048]{2,1,0:T(8,128)(2,1)S(1)} %load_down.1.held_ref, ...), custom_call_target="tpu_custom_call" | custom-call | flops 872415232 | bytes 13631488 | tf_op jit(solution)/shard_map/down_far_half/pallas_call | solution.py:374
  45.0 1.2 %collective-permute-start.5 = (bf16[64,2048]{1,0:T(8,128)(2,1)S(1)}, bf16[64,2048]{1,0:T(8,128)(2,1)S(1)}, u32[]{:S(2)}, u32[]{:S(2)}) collective-permute-start(bf16[64,2048]{1,0:T(8,128)(2,1)S(1)} %get-tuple-element.24), channel_id=1, source_target_pairs={{0,2},{2,0},{4,6},{6,4},{8,10},{10,8},{12,14},{14,12},{1,3},{3,1},... | collective-permute-start | bytes 786440 | tf_op jit(solution)/shard_map/ppermute | solution.py:604
  46.2 4.1 %down_near_half.1.near_ref = f32[64,2048]{1,0:T(8,128)S(1)} custom-call(bf16[64,3328]{1,0:T(8,128)(2,1)S(1)} %get-tuple-element.22.hidden_ref, bf16[4,256,2048]{2,1,0:T(8,128)(2,1)S(1)} %get-tuple-element.23.held_ref, bf16[3328,4096]{1,0:T(8,128)(2,1)} %w_hbm.5), custom_call_target="tpu_custom_call" | custom-call | flops 872415232 | bytes 13631488 | tf_op jit(solution)/shard_map/down_near_half/pallas_call | solution.py:408
  50.3 3.5 %collective-permute-done.5.far_ref = bf16[64,2048]{1,0:T(8,128)(2,1)S(1)} collective-permute-done((bf16[64,2048]{1,0:T(8,128)(2,1)S(1)}, bf16[64,2048]{1,0:T(8,128)(2,1)S(1)}, u32[]{:S(2)}, u32[]{:S(2)}) %collective-permute-start.5) | collective-permute-done | bytes 262176 | tf_op jit(solution)/shard_map/ppermute | solution.py:604
  53.7 0.9 %to_slots.1 = (f32[32,2048]{1,0:T(8,128)S(1)}, bf16[32,2048]{1,0:T(8,128)(2,1)S(1)}, bf16[32,2048]{1,0:T(8,128)(2,1)S(1)}, bf16[32,2048]{1,0:T(8,128)(2,1)S(1)}) custom-call(s32[1,64]{1,0:T(1,128)S(1)} %bitcast.3, f32[64,2048]{1,0:T(8,128)S(1)} %down_near_half.1.near_ref, bf16[64,2048]{1,0:T(8,128)(2,1)S(1)} %collective-permute-done.5.far_ref), custom_call_target="tpu_custom_call" | custom-call | tf_op jit(solution)/shard_map/to_slots/pallas_call | solution.py:459
  54.7 0.5 collective-permute-start.6
  55.2 1.6 %collective-permute-start.7 = (bf16[32,2048]{1,0:T(8,128)(2,1)S(1)}, bf16[32,2048]{1,0:T(8,128)(2,1)S(1)}, u32[]{:S(2)}, u32[]{:S(2)}) collective-permute-start(bf16[32,2048]{1,0:T(8,128)(2,1)S(1)} %get-tuple-element.27), channel_id=1, source_target_pairs={{0,8},{2,10},{4,12},{6,14},{8,0},{10,2},{12,4},{14,6},{1,9},{3,11}... | collective-permute-start | bytes 393224 | tf_op jit(solution)/shard_map/ppermute | solution.py:609
  56.8 2.3 %collective-permute-start.8 = (bf16[32,2048]{1,0:T(8,128)(2,1)S(1)}, bf16[32,2048]{1,0:T(8,128)(2,1)S(1)}, u32[]{:S(2)}, u32[]{:S(2)}) collective-permute-start(bf16[32,2048]{1,0:T(8,128)(2,1)S(1)} %get-tuple-element.28), channel_id=1, source_target_pairs={{0,12},{2,14},{4,8},{6,10},{8,4},{10,6},{12,0},{14,2},{1,13},{3,15... | collective-permute-start | bytes 393224 | tf_op jit(solution)/shard_map/ppermute | solution.py:609
  59.1 2.9 %collective-permute-done.6.refs_0_ = bf16[32,2048]{1,0:T(8,128)(2,1)S(1)} collective-permute-done((bf16[32,2048]{1,0:T(8,128)(2,1)S(1)}, bf16[32,2048]{1,0:T(8,128)(2,1)S(1)}, u32[]{:S(2)}, u32[]{:S(2)}) %collective-permute-start.6) | collective-permute-done | bytes 131104 | tf_op jit(solution)/shard_map/ppermute | solution.py:609
  62.0 5.8 %collective-permute-done.7.refs_1_ = bf16[32,2048]{1,0:T(8,128)(2,1)S(1)} collective-permute-done((bf16[32,2048]{1,0:T(8,128)(2,1)S(1)}, bf16[32,2048]{1,0:T(8,128)(2,1)S(1)}, u32[]{:S(2)}, u32[]{:S(2)}) %collective-permute-start.7) | collective-permute-done | bytes 131104 | tf_op jit(solution)/shard_map/ppermute | solution.py:609
  68.1 1.2 %collective-permute-start.9 = (bf16[16,2048]{1,0:T(8,128)(2,1)S(1)}, bf16[16,2048]{1,0:T(8,128)(2,1)S(1)}, u32[]{:S(2)}, u32[]{:S(2)}) collective-permute-start(bf16[16,2048]{1,0:T(8,128)(2,1)S(1)} %get-tuple-element.30), channel_id=1, source_target_pairs={{0,2},{2,0},{4,6},{6,4},{8,10},{10,8},{12,14},{14,12},{1,3},{3,1},... | collective-permute-start | bytes 196616 | tf_op jit(solution)/shard_map/ppermute | solution.py:612
  69.3 3.2 %collective-permute-done.9.other_ref = bf16[16,2048]{1,0:T(8,128)(2,1)S(1)} collective-permute-done((bf16[16,2048]{1,0:T(8,128)(2,1)S(1)}, bf16[16,2048]{1,0:T(8,128)(2,1)S(1)}, u32[]{:S(2)}, u32[]{:S(2)}) %collective-permute-start.9) | collective-permute-done | bytes 65568 | tf_op jit(solution)/shard_map/ppermute | solution.py:612
  72.5 0.7 join_halves.1
  (11 shorter events, 0.4 us)
Async XLA Ops:
  5.2 8.1 %collective-permute-start = (bf16[8,4096]{1,0:T(8,128)(2,1)S(1)}, bf16[8,4096]{1,0:T(8,128)(2,1)S(1)}, u32[]{:S(2)}, u32[]{:S(2)}) collective-permute-start(bf16[8,4096]{1,0:T(8,128)(2,1)S(1)} %get-tuple-element.18.after_ref.a_ref), channel_id=1, source_target_pairs={{0,8},{2,10},{4,12},{6,14},{8,0},{10,2},{12,4},{14,6},{1,9},{3,11}... | collective-permute-start | bytes 196616 | tf_op jit(solution)/shard_map/ppermute | solution.py:588
  13.4 7.2 %collective-permute-start.2 = (bf16[2,8,4096]{2,1,0:T(8,128)(2,1)S(1)}, bf16[2,8,4096]{2,1,0:T(8,128)(2,1)S(1)}, u32[]{:S(2)}, u32[]{:S(2)}) collective-permute-start(bf16[2,8,4096]{2,1,0:T(8,128)(2,1)S(1)} %pack.1.after_ref.refs_0_), channel_id=1, source_target_pairs={{0,4},{2,6},{4,0},{6,2},{8,12},{10,14},{12,8},{14,10},{1,5},{3,7},... | collective-permute-start | bytes 393224 | tf_op jit(solution)/shard_map/ppermute | solution.py:592
  15.0 10.2 %collective-permute-start.1 = (bf16[2,8,4096]{2,1,0:T(8,128)(2,1)S(1)}, bf16[2,8,4096]{2,1,0:T(8,128)(2,1)S(1)}, u32[]{:S(2)}, u32[]{:S(2)}) collective-permute-start(bf16[2,8,4096]{2,1,0:T(8,128)(2,1)S(1)} %pack.1.after_ref.refs_0_), channel_id=1, source_target_pairs={{0,2},{2,0},{4,6},{6,4},{8,10},{10,8},{12,14},{14,12},{1,3},{3,1},... | collective-permute-start | bytes 393224 | tf_op jit(solution)/shard_map/ppermute | solution.py:591
  20.5 5.0 %collective-permute-start.3 = (bf16[2,8,4096]{2,1,0:T(8,128)(2,1)S(1)}, bf16[2,8,4096]{2,1,0:T(8,128)(2,1)S(1)}, u32[]{:S(2)}, u32[]{:S(2)}) collective-permute-start(bf16[2,8,4096]{2,1,0:T(8,128)(2,1)S(1)} %hold.1.after_ref.refs_2_), channel_id=1, source_target_pairs={{0,2},{2,0},{4,6},{6,4},{8,10},{10,8},{12,14},{14,12},{1,3},{3,1},... | collective-permute-start | bytes 393224 | tf_op jit(solution)/shard_map/ppermute | solution.py:595
  37.6 3.0 %collective-permute-start.4 = (bf16[2,64,3328]{2,1,0:T(8,128)(2,1)S(1)}, bf16[2,64,3328]{2,1,0:T(8,128)(2,1)S(1)}, u32[]{:S(2)}, u32[]{:S(2)}) collective-permute-start(bf16[2,64,3328]{2,1,0:T(8,128)(2,1)S(1)} %get-tuple-element.21.after_ref.own_ref), channel_id=1, source_target_pairs={{0,1},{1,0},{2,3},{3,2},{4,5},{5,4},{6,7},{7,6},{8,9},{9,8},{10,11... | collective-permute-start | bytes 2555912 | tf_op jit(solution)/shard_map/ppermute | solution.py:598
  45.0 8.8 %collective-permute-start.5 = (bf16[64,2048]{1,0:T(8,128)(2,1)S(1)}, bf16[64,2048]{1,0:T(8,128)(2,1)S(1)}, u32[]{:S(2)}, u32[]{:S(2)}) collective-permute-start(bf16[64,2048]{1,0:T(8,128)(2,1)S(1)} %get-tuple-element.24), channel_id=1, source_target_pairs={{0,2},{2,0},{4,6},{6,4},{8,10},{10,8},{12,14},{14,12},{1,3},{3,1},... | collective-permute-start | bytes 786440 | tf_op jit(solution)/shard_map/ppermute | solution.py:604
  46.2 7.6 %copy-start = (s32[64,1]{0,1:T(1,128)S(1)}, s32[64,1]{0,1:T(1,128)}, u32[]{:S(2)}) copy-start(s32[64,1]{0,1:T(1,128)} %param.14) | copy-start | bytes 772
  54.7 7.4 %collective-permute-start.6 = (bf16[32,2048]{1,0:T(8,128)(2,1)S(1)}, bf16[32,2048]{1,0:T(8,128)(2,1)S(1)}, u32[]{:S(2)}, u32[]{:S(2)}) collective-permute-start(bf16[32,2048]{1,0:T(8,128)(2,1)S(1)} %get-tuple-element.26), channel_id=1, source_target_pairs={{0,4},{2,6},{4,0},{6,2},{8,12},{10,14},{12,8},{14,10},{1,5},{3,7},... | collective-permute-start | bytes 393224 | tf_op jit(solution)/shard_map/ppermute | solution.py:609
  55.2 12.6 %collective-permute-start.7 = (bf16[32,2048]{1,0:T(8,128)(2,1)S(1)}, bf16[32,2048]{1,0:T(8,128)(2,1)S(1)}, u32[]{:S(2)}, u32[]{:S(2)}) collective-permute-start(bf16[32,2048]{1,0:T(8,128)(2,1)S(1)} %get-tuple-element.27), channel_id=1, source_target_pairs={{0,8},{2,10},{4,12},{6,14},{8,0},{10,2},{12,4},{14,6},{1,9},{3,11}... | collective-permute-start | bytes 393224 | tf_op jit(solution)/shard_map/ppermute | solution.py:609
  56.8 11.0 %collective-permute-start.8 = (bf16[32,2048]{1,0:T(8,128)(2,1)S(1)}, bf16[32,2048]{1,0:T(8,128)(2,1)S(1)}, u32[]{:S(2)}, u32[]{:S(2)}) collective-permute-start(bf16[32,2048]{1,0:T(8,128)(2,1)S(1)} %get-tuple-element.28), channel_id=1, source_target_pairs={{0,12},{2,14},{4,8},{6,10},{8,4},{10,6},{12,0},{14,2},{1,13},{3,15... | collective-permute-start | bytes 393224 | tf_op jit(solution)/shard_map/ppermute | solution.py:609
  68.1 4.3 %collective-permute-start.9 = (bf16[16,2048]{1,0:T(8,128)(2,1)S(1)}, bf16[16,2048]{1,0:T(8,128)(2,1)S(1)}, u32[]{:S(2)}, u32[]{:S(2)}) collective-permute-start(bf16[16,2048]{1,0:T(8,128)(2,1)S(1)} %get-tuple-element.30), channel_id=1, source_target_pairs={{0,2},{2,0},{4,6},{6,4},{8,10},{10,8},{12,14},{14,12},{1,3},{3,1},... | collective-permute-start | bytes 196616 | tf_op jit(solution)/shard_map/ppermute | solution.py:612

commit v5 on v4

--- a/solution.py
+++ b/solution.py
@@ -11,6 +11,7 @@
 AXIS = "attn"
 TILE = 256
 BAND = 256
+ORDER = (0, 2, 1, 3)
 MIB = 1 << 20
 VMEM = pl.BlockSpec(memory_space=pltpu.VMEM)
 SMEM = pl.BlockSpec(memory_space=pltpu.SMEM)
@@ -53,6 +54,9 @@
 def swap_x(devices):
     nz, nx = grid_of(devices)
     return [(z * nx + x, z * nx + (x ^ 1)) for z in range(nz) for x in range(nx)]
+
+
+COST = cost(0, 1024)
 
 
 def attend_kernel(kv, bands, lengths, q_hbm, k_hbm, v_hbm, res_ref, *refs):
@@ -92,7 +96,7 @@
     for r in range(rows):
         scores = scores_ref[at(r), :]
         raw = jnp.exp(scores - jnp.max(scores, axis=-1, keepdims=True))
-        probs_ref[at(r), :] = (raw / jnp.sum(raw, axis=-1, keepdims=True)).astype(BF16)
+        probs_ref[at(r), :] = (raw * (1.0 / jnp.sum(raw, axis=-1, keepdims=True))).astype(BF16)
     loads[2].wait()
     for r in range(rows):
         att_ref[at(r), :] = jnp.dot(probs_ref[at(r), :], v_ref[r], preferred_element_type=F32)
@@ -203,14 +207,27 @@
 
 
 def gate_up_kernel(devices, holders, first, *refs):
-    a_ref, b_ref, c_ref, d_ref, g_hbm, u_hbm = refs[:6]
-    held_refs = refs[6 : 6 + holders]
-    part_ref, rows_ref, total_ref, buf, sems = refs[6 + holders :]
+    a_ref, b_ref, c_ref, d_ref, g_hbm, u_hbm, w_hbm = refs[:7]
+    held_refs = refs[7 : 7 + holders]
+    part_ref, rows_ref, far_ref, total_ref, buf, sems, far_sems = refs[7 + holders :]
     nx = grid_of(devices)[1]
     slots = buf.shape[0]
-    streamed = band_copies(g_hbm, u_hbm, buf, sems, first)
-    late = band_copies(g_hbm, u_hbm, buf.at[0:1], sems, first + slots)
-    for c in streamed:
+    left = g_hbm.shape[0] // BAND - first
+
+    def streamed(j):
+        slot = lax.rem(j, slots)
+        at = pl.ds(pl.multiple_of((first + j) * BAND, BAND), BAND)
+        return [
+            pltpu.make_async_copy(w.at[at], buf.at[slot, kind], sems.at[slot, kind])
+            for kind, w in enumerate((g_hbm, u_hbm))
+        ]
+
+    for j in range(min(slots, left)):
+        for c in streamed(j):
+            c.start()
+    half = far_ref.shape[2]
+    ahead = down_copies(w_hbm, half_base(devices, False, half), far_ref, far_sems, 0)
+    for c in ahead:
         c.start()
     me = lax.axis_index(AXIS)
     my_z, my_x = me // nx, me % nx
@@ -223,69 +240,84 @@
             at = pl.ds(pl.multiple_of(z * (2 * per), 2 * per), 2 * per)
             rows_ref[at, :] = jnp.concatenate(pair, axis=0).astype(BF16)
 
-    def band(i):
-        if isinstance(i, int):
-            return slice(i * BAND, (i + 1) * BAND)
-        return pl.ds(pl.multiple_of(i * BAND, BAND), BAND)
-
     def add(i, weight, kind):
-        total_ref[kind] += jnp.dot(rows_ref[:, band(i)], weight, preferred_element_type=F32)
-
-    def add_streamed(index, slot, copies):
-        for kind, c in enumerate(copies):
+        at = pl.ds(pl.multiple_of(i * BAND, BAND), BAND)
+        total_ref[kind] += jnp.dot(rows_ref[:, at], weight, preferred_element_type=F32)
+
+    def add_streamed(j):
+        slot = lax.rem(j, slots)
+        for kind, c in enumerate(streamed(j)):
             c.wait()
-            add(index, buf[slot, kind], kind)
+            add(first + j, buf[slot, kind], kind)
+
+        @pl.when(j + slots < left)
+        def _():
+            for c in streamed(j + slots):
+                c.start()
 
     total_ref[...] = jnp.zeros_like(total_ref)
-    start = 0
-    for number, held in enumerate(held_refs):
-
-        def step(i, _, held=held, start=start):
+    start, came = 0, 0
+    for held in held_refs:
+
+        def step(i, _, held=held, start=start, came=came):
             for kind in range(2):
                 add(start + i, held[i, kind], kind)
+            if start:
+                add_streamed(came + i)
             return 0
 
         lax.fori_loop(0, held.shape[0], step, 0)
+        came += held.shape[0] if start else 0
         start += held.shape[0]
-        if number == 1:
-            add_streamed(first, 0, streamed[:2])
-            for c in late:
-                c.start()
-    for slot in range(1, slots):
-        add_streamed(first + slot, slot, streamed[2 * slot : 2 * slot + 2])
-    add_streamed(first + slots, 0, late)
+
+    def rest(j, _):
+        add_streamed(j)
+        return 0
+
+    lax.fori_loop(came, left, rest, 0)
     part_ref[...] = total_ref[...].astype(BF16)
-
-
-def gate_up(blocks, gate_weight, up_weight, held, devices):
+    for c in ahead:
+        c.wait()
+
+
+def gate_up(blocks, gate_weight, up_weight, down_weight, held, devices, tiles):
     total = devices * blocks[0].shape[1]
     features, columns = gate_weight.shape
     first = sum(h.shape[0] for h in held)
-    slots = features // BAND - first - 1
+    slots = 2
+    far = (tiles, TILE, features // 2)
     return pl.pallas_call(
         functools.partial(gate_up_kernel, devices, len(held), first),
         out_shape=(
             jax.ShapeDtypeStruct((2, total, columns), BF16),
             jax.ShapeDtypeStruct((total, features), BF16),
+            pltpu.VMEM(far, BF16),
         ),
-        in_specs=[VMEM] * 4 + [HBM, HBM] + [VMEM] * len(held),
-        out_specs=(VMEM, VMEM),
+        in_specs=[VMEM] * 4 + [HBM] * 3 + [VMEM] * len(held),
+        out_specs=(VMEM, VMEM, VMEM),
         scratch_shapes=[
             pltpu.VMEM((2, total, columns), F32),
             pltpu.VMEM((slots, 2, BAND, columns), BF16),
             pltpu.SemaphoreType.DMA((slots, 2)),
+            pltpu.SemaphoreType.DMA((far[0],)),
         ],
-        compiler_params=params(13),
+        compiler_params=params(10),
         cost_estimate=cost(4 * total * features * columns, 4 * features * columns),
         name="gate_up",
-    )(*blocks, in_hbm(gate_weight), in_hbm(up_weight), *(in_vmem(h) for h in held))
-
-
-def half_copies(w_hbm, base, held_ref, sems, first):
-    half = held_ref.shape[2]
+    )(
+        *blocks,
+        in_hbm(gate_weight),
+        in_hbm(up_weight),
+        in_hbm(down_weight),
+        *(in_vmem(h) for h in held),
+    )
+
+
+def down_copies(w_hbm, base, held_ref, sems, first):
+    wide = held_ref.shape[2]
     return [
         pltpu.make_async_copy(
-            w_hbm.at[pl.ds((first + i) * TILE, TILE), pl.ds(base, half)],
+            w_hbm.at[pl.ds((first + i) * TILE, TILE), pl.ds(base, wide)],
             held_ref.at[i],
             sems.at[i],
         )
@@ -298,126 +330,9 @@
     return pl.multiple_of((my_x if mine else 1 - my_x) * half, half)
 
 
-def down_load_kernel(devices, after_ref, w_hbm, held_ref, sems):
-    base = half_base(devices, False, held_ref.shape[2])
-    copies = half_copies(w_hbm, base, held_ref, sems, 0)
-    for c in copies:
-        c.start()
-    for c in copies:
-        c.wait()
-
-
-def load_down(after, down_weight, devices, tiles):
-    half = down_weight.shape[1] // 2
-    return pl.pallas_call(
-        functools.partial(down_load_kernel, devices),
-        out_shape=pltpu.VMEM((tiles, TILE, half), BF16),
-        in_specs=[ANY, HBM],
-        out_specs=VMEM,
-        scratch_shapes=[pltpu.SemaphoreType.DMA((tiles,))],
-        compiler_params=params(2),
-        cost_estimate=cost(0, tiles * TILE * half * 2),
-        name="load_down",
-    )(after, in_hbm(down_weight))
-
-
-def add_half(hidden_ref, held_ref, buf, copies, total_ref):
-    held = held_ref.shape[0]
-    total_ref[...] = jnp.zeros_like(total_ref)
-
-    def step(i, _):
-        total_ref[...] += jnp.dot(
-            hidden_ref[:, tile_at(i)], held_ref[i], preferred_element_type=F32
-        )
-        return 0
-
-    lax.fori_loop(0, held, step, 0)
-    for i, c in enumerate(copies):
-        c.wait()
-        at = slice((held + i) * TILE, (held + i + 1) * TILE)
-        total_ref[...] += jnp.dot(hidden_ref[:, at], buf[i], preferred_element_type=F32)
-
-
-def down_far_kernel(
-    devices,
-    own_ref,
-    other_ref,
-    held_ref,
-    w_hbm,
-    out_ref,
-    hidden_ref,
-    next_ref,
-    total_ref,
-    buf,
-    sems,
-    next_sems,
-):
-    half = out_ref.shape[1]
-    copies = half_copies(w_hbm, half_base(devices, False, half), buf, sems, held_ref.shape[0])
-    ahead = half_copies(w_hbm, half_base(devices, True, half), next_ref, next_sems, 0)
-    for c in copies + ahead:
-        c.start()
-    gate = own_ref[0].astype(F32) + other_ref[0].astype(F32)
-    up = own_ref[1].astype(F32) + other_ref[1].astype(F32)
-    hidden_ref[...] = (gate / (1.0 + jnp.exp(-gate)) * up).astype(BF16)
-    add_half(hidden_ref, held_ref, buf, copies, total_ref)
-    out_ref[...] = total_ref[...].astype(BF16)
-    for c in ahead:
-        c.wait()
-
-
-def down_far(own, other, held, down_weight, devices, ahead):
-    total = own.shape[1]
-    columns, features = down_weight.shape
-    half = features // 2
-    left = columns // TILE - held.shape[0]
-    return pl.pallas_call(
-        functools.partial(down_far_kernel, devices),
-        out_shape=(
-            jax.ShapeDtypeStruct((total, half), BF16),
-            jax.ShapeDtypeStruct((total, columns), BF16),
-            pltpu.VMEM((ahead, TILE, half), BF16),
-        ),
-        in_specs=[VMEM, VMEM, VMEM, HBM],
-        out_specs=(VMEM, VMEM, VMEM),
-        scratch_shapes=[
-            pltpu.VMEM((total, half), F32),
-            pltpu.VMEM((left, TILE, half), BF16),
-            pltpu.SemaphoreType.DMA((left,)),
-            pltpu.SemaphoreType.DMA((ahead,)),
-        ],
-        compiler_params=params(20),
-        cost_estimate=cost(total * features * columns, features * columns),
-        name="down_far_half",
-    )(own, other, in_vmem(held), in_hbm(down_weight))
-
-
-def down_near_kernel(devices, hidden_ref, held_ref, w_hbm, out_ref, buf, sems):
-    half = out_ref.shape[1]
-    copies = half_copies(w_hbm, half_base(devices, True, half), buf, sems, held_ref.shape[0])
-    for c in copies:
-        c.start()
-    add_half(hidden_ref, held_ref, buf, copies, out_ref)
-
-
-def down_near(hidden, held, down_weight, devices):
-    total = hidden.shape[0]
-    columns, features = down_weight.shape
-    half = features // 2
-    left = columns // TILE - held.shape[0]
-    return pl.pallas_call(
-        functools.partial(down_near_kernel, devices),
-        out_shape=jax.ShapeDtypeStruct((total, half), F32),
-        in_specs=[VMEM, VMEM, HBM],
-        out_specs=VMEM,
-        scratch_shapes=[
-            pltpu.VMEM((left, TILE, half), BF16),
-            pltpu.SemaphoreType.DMA((left,)),
-        ],
-        compiler_params=params(20),
-        cost_estimate=cost(total * features * columns, features * columns),
-        name="down_near_half",
-    )(hidden, in_vmem(held), in_hbm(down_weight))
+def quarter_base(devices, quarter, wide):
+    my_x = lax.axis_index(AXIS) % grid_of(devices)[1]
+    return pl.multiple_of((2 * my_x + quarter) * wide, wide)
 
 
 def pick(row_ref, capacity, first_slot, slots):
@@ -433,69 +348,187 @@
     return (slot == row * capacity + rank).astype(F32).astype(BF16)
 
 
-def to_slots_kernel(devices, capacity, row_ref, near_ref, far_ref, own_ref, *sends):
+def prepare_kernel(devices, capacity, first, after_ref, row_ref, w_hbm, held_ref, chosen_ref, sems):
+    base = half_base(devices, False, held_ref.shape[2])
+    copies = down_copies(w_hbm, base, held_ref, sems, first)
+    for c in copies:
+        c.start()
     nz, nx = grid_of(devices)
     my_z = lax.axis_index(AXIS) // nx
+    slots = chosen_ref.shape[0] // nz
+    for i, bits in enumerate(ORDER):
+        chosen_ref[i * slots : (i + 1) * slots, :] = pick(
+            row_ref, capacity, (my_z ^ bits) * slots, slots
+        )
+    for c in copies:
+        c.wait()
+
+
+def prepare(after, row, down_weight, devices, capacity, first, tiles):
+    wide = down_weight.shape[1] // 2
+    total = row.shape[1]
+    return pl.pallas_call(
+        functools.partial(prepare_kernel, devices, capacity, first),
+        out_shape=(
+            pltpu.VMEM((tiles, TILE, wide), BF16),
+            jax.ShapeDtypeStruct((devices * 2 * capacity, total), BF16),
+        ),
+        in_specs=[ANY, VMEM, HBM],
+        out_specs=(VMEM, VMEM),
+        scratch_shapes=[pltpu.SemaphoreType.DMA((tiles,))],
+        compiler_params=params(2),
+        cost_estimate=cost(0, tiles * TILE * wide * 2),
+        name="prepare",
+    )(after, row, in_hbm(down_weight))
+
+
+def add_held(hidden_ref, held_refs, at, total_ref):
+    start = 0
+    for held_ref in held_refs:
+
+        def step(i, _, held_ref=held_ref, start=start):
+            total_ref[...] += jnp.dot(
+                hidden_ref[:, tile_at(start + i)],
+                held_ref[i, :, at],
+                preferred_element_type=F32,
+            )
+            return 0
+
+        lax.fori_loop(0, held_ref.shape[0], step, 0)
+        start += held_ref.shape[0]
+
+
+def down_far_kernel(devices, quarter, *refs):
+    if quarter == 0:
+        own_ref, other_ref, *refs = refs
+        *held_refs, w_hbm, out_ref, next_ref, hidden_ref, total_ref, sems = refs
+    else:
+        hidden_ref, *held_refs, w_hbm, out_ref, next_ref, total_ref, sems = refs
+    wide = out_ref.shape[1]
+    ahead = down_copies(w_hbm, quarter_base(devices, quarter, wide), next_ref, sems, 0)
+    for c in ahead:
+        c.start()
+    if quarter == 0:
+        gate = own_ref[0].astype(F32) + other_ref[0].astype(F32)
+        up = own_ref[1].astype(F32) + other_ref[1].astype(F32)
+        hidden_ref[...] = (gate / (1.0 + jnp.exp(-gate)) * up).astype(BF16)
+    total_ref[...] = jnp.zeros_like(total_ref)
+    add_held(hidden_ref, held_refs, slice(quarter * wide, (quarter + 1) * wide), total_ref)
+    out_ref[...] = total_ref[...].astype(BF16)
+    for c in ahead:
+        c.wait()
+
+
+def down_far(inputs, held, down_weight, devices, quarter, ahead):
+    total = inputs[0].shape[-2]
+    columns, features = down_weight.shape
+    wide = features // 4
+    hidden = [jax.ShapeDtypeStruct((total, columns), BF16)] if quarter == 0 else []
+    return pl.pallas_call(
+        functools.partial(down_far_kernel, devices, quarter),
+        out_shape=(
+            jax.ShapeDtypeStruct((total, wide), BF16),
+            pltpu.VMEM((ahead, TILE, wide), BF16),
+            *hidden,
+        ),
+        in_specs=[VMEM] * (len(inputs) + len(held)) + [HBM],
+        out_specs=(VMEM, VMEM) + tuple(VMEM for _ in hidden),
+        scratch_shapes=[
+            pltpu.VMEM((total, wide), F32),
+            pltpu.SemaphoreType.DMA((ahead,)),
+        ],
+        compiler_params=params(6),
+        cost_estimate=COST,
+        name="down_far",
+    )(*inputs, *(in_vmem(h) for h in held), in_hbm(down_weight))
+
+
+def down_near_kernel(devices, quarter, *refs):
+    hidden_ref, arrived_ref, chosen_ref, held_ref, w_hbm, keep_ref, send_ref, total_ref, buf, sems = refs
+    held = held_ref.shape[0]
+    copies = down_copies(w_hbm, quarter_base(devices, quarter, buf.shape[2]), buf, sems, held)
+    for c in copies:
+        c.start()
+    total_ref[...] = arrived_ref[...].astype(F32)
+    add_held(hidden_ref, (held_ref,), slice(None), total_ref)
+    for i, c in enumerate(copies):
+        c.wait()
+        at = slice((held + i) * TILE, (held + i + 1) * TILE)
+        total_ref[...] += jnp.dot(hidden_ref[:, at], buf[i], preferred_element_type=F32)
+    slots = keep_ref.shape[0]
+    rounded = total_ref[...].astype(BF16)
+    keep_ref[...] = jnp.dot(chosen_ref[:slots], rounded, preferred_element_type=F32).astype(BF16)
+    send_ref[...] = jnp.dot(chosen_ref[slots:], rounded, preferred_element_type=F32).astype(BF16)
+
+
+def down_near(hidden, arrived, chosen, down_weight, held, devices, quarter):
+    total, wide = arrived.shape
+    left = down_weight.shape[0] // TILE - held.shape[0]
+    shape = jax.ShapeDtypeStruct((chosen.shape[0] // 2, wide), BF16)
+    return pl.pallas_call(
+        functools.partial(down_near_kernel, devices, quarter),
+        out_shape=(shape, shape),
+        in_specs=[VMEM] * 4 + [HBM],
+        out_specs=(VMEM, VMEM),
+        scratch_shapes=[
+            pltpu.VMEM((total, wide), F32),
+            pltpu.VMEM((left, TILE, wide), BF16),
+            pltpu.SemaphoreType.DMA((left,)),
+        ],
+        compiler_params=params(8),
+        cost_estimate=COST,
+        name="down_near",
+    )(hidden, arrived, chosen, in_vmem(held), in_hbm(down_weight))
+
+
+def add_kernel(keep_ref, came_ref, own_ref, send_ref):
     slots = own_ref.shape[0]
-    total = near_ref[...] + far_ref[...].astype(F32)
-    rounded = total.astype(BF16)
-    for dz, send_ref in enumerate((own_ref,) + sends):
-        z = my_z ^ dz
-        chosen = pick(row_ref, capacity, z * slots, slots)
-        if dz:
-            send_ref[...] = jnp.dot(chosen, rounded, preferred_element_type=F32).astype(BF16)
-        else:
-            high = rounded.astype(F32)
-            low = (total - high).astype(BF16)
-            own_ref[...] = jnp.dot(chosen, rounded, preferred_element_type=F32) + jnp.dot(
-                chosen, low, preferred_element_type=F32
-            )
-
-
-def to_slots(row, near, far, devices, capacity):
-    nz, nx = grid_of(devices)
-    slots = nx * 2 * capacity
-    width = near.shape[1]
-    return pl.pallas_call(
-        functools.partial(to_slots_kernel, devices, capacity),
-        out_shape=(jax.ShapeDtypeStruct((slots, width), F32),)
-        + (jax.ShapeDtypeStruct((slots, width), BF16),) * (nz - 1),
-        in_specs=[VMEM] * 3,
-        out_specs=(VMEM,) * nz,
-        compiler_params=params(8),
-        name="to_slots",
-    )(row, near, far)
-
-
-def finish_kernel(devices, capacity, row_ref, rows_ref, own_ref, *refs):
-    *landed, keep_ref, send_ref = refs
-    nz, nx = grid_of(devices)
-    me = lax.axis_index(AXIS)
-    my_z, my_x = me // nx, me % nx
-    slots, width = own_ref.shape
-    chosen = pick(row_ref, capacity, my_z * slots, slots)
-    mixed = rows_ref[:, pl.ds(pl.multiple_of(my_x * width, width), width)]
-    total = own_ref[...]
-    for ref in landed:
-        total = total + ref[...].astype(F32)
-    done = jnp.dot(chosen, mixed, preferred_element_type=F32) + total
+    total = keep_ref[...].astype(F32) + came_ref[...].astype(F32)
+    own_ref[...] = total[:slots]
+    send_ref[...] = total[slots:].astype(BF16)
+
+
+def add(keep, came):
+    slots, wide = keep.shape
+    return pl.pallas_call(
+        add_kernel,
+        out_shape=(
+            jax.ShapeDtypeStruct((slots // 2, wide), F32),
+            jax.ShapeDtypeStruct((slots // 2, wide), BF16),
+        ),
+        in_specs=[VMEM, VMEM],
+        out_specs=(VMEM, VMEM),
+        compiler_params=params(4),
+        name="add",
+    )(keep, came)
+
+
+def finish_kernel(devices, chosen_ref, rows_ref, *refs):
+    own_refs, came_refs, (keep_ref, send_ref) = refs[:2], refs[2:4], refs[4:]
+    my_x = lax.axis_index(AXIS) % grid_of(devices)[1]
+    slots, wide = own_refs[0].shape
     half = slots // 2
-    first, second = done[:half], done[half:]
-    keep_ref[...] = jnp.where(my_x == 0, first, second).astype(BF16)
-    send_ref[...] = jnp.where(my_x == 0, second, first).astype(BF16)
-
-
-def finish(row, rows, own, landed, devices, capacity):
-    slots, width = own.shape
-    shape = jax.ShapeDtypeStruct((slots // 2, width), BF16)
-    return pl.pallas_call(
-        functools.partial(finish_kernel, devices, capacity),
+    for quarter, (own_ref, came_ref) in enumerate(zip(own_refs, came_refs)):
+        mixed = rows_ref[:, pl.ds(quarter_base(devices, quarter, wide), wide)]
+        done = jnp.dot(chosen_ref[:slots], mixed, preferred_element_type=F32)
+        done = done + (own_ref[...] + came_ref[...].astype(F32))
+        first, second = done[:half], done[half:]
+        at = slice(quarter * wide, (quarter + 1) * wide)
+        keep_ref[:, at] = jnp.where(my_x == 0, first, second).astype(BF16)
+        send_ref[:, at] = jnp.where(my_x == 0, second, first).astype(BF16)
+
+
+def finish(chosen, rows, own, came, devices):
+    slots, wide = own[0].shape
+    shape = jax.ShapeDtypeStruct((slots // 2, 2 * wide), BF16)
+    return pl.pallas_call(
+        functools.partial(finish_kernel, devices),
         out_shape=(shape, shape),
-        in_specs=[VMEM] * (3 + len(landed)),
+        in_specs=[VMEM] * 6,
         out_specs=(VMEM, VMEM),
-        compiler_params=params(8),
+        compiler_params=params(6),
         name="finish",
-    )(row, rows, own, *landed)
+    )(chosen, rows, *own, *came)
 
 
 def join_kernel(nx, keep_ref, other_ref, out_ref):
@@ -572,7 +605,7 @@
     capacity = cache_keys.shape[0]
     columns, features = down_weight.shape
     fits = nz == 4 and nx == 2 and columns % TILE == 0 and features % (16 * TILE) == 0
-    share = 3 * (gate_weight.shape[0] // BAND) // 16 if fits else 0
+    share = gate_weight.shape[0] // BAND // 8 if fits else 0
     mixed_rows, *held = attend(
         queries,
         cache_keys,
@@ -594,21 +627,30 @@
     c = hold(c, held[-1])
     d = lax.ppermute(c, AXIS, swap_x(devices))
     held.append(load_bands(c, gate_weight, up_weight, 3 * share, share))
-    part, rows = gate_up((a, b, c, d), gate_weight, up_weight, held, devices)
+    tiles = columns // TILE
+    most = 8 * tiles // 13
+    part, rows, *held_far = gate_up(
+        (a, b, c, d), gate_weight, up_weight, down_weight, held, devices, most
+    )
     other = lax.ppermute(part, "ffn", [(0, 1), (1, 0)])
-    tiles = columns // TILE
-    held_down = load_down(part, down_weight, devices, 6 * tiles // 13)
-    far_half, hidden, held_near = down_far(
-        part, other, held_down, down_weight, devices, 4 * tiles // 13
-    )
-    arrived = lax.ppermute(far_half, AXIS, swap_x(devices))
-    near_half = down_near(hidden, held_near, down_weight, devices)
-    row = target.reshape(1, -1)
-    own_slots, *sends = to_slots(row, near_half, arrived, devices, capacity)
-    landed = [
-        lax.ppermute(send, AXIS, swap_z(devices, bits + 1)) for bits, send in enumerate(sends)
-    ]
-    keep, send = finish(row, rows, own_slots, landed, devices, capacity)
+    rest, chosen = prepare(
+        part, target.reshape(1, -1), down_weight, devices, capacity, most, tiles - most
+    )
+    held_far.append(rest)
+
+    far, near_first, hidden = down_far((part, other), held_far, down_weight, devices, 0, 9 * tiles // 13)
+    arrived = [lax.ppermute(far, AXIS, swap_x(devices))]
+    far, near_second = down_far((hidden,), held_far, down_weight, devices, 1, 8 * tiles // 13)
+    arrived.append(lax.ppermute(far, AXIS, swap_x(devices)))
+    own, came = [], []
+    for quarter, held_near in enumerate((near_first, near_second)):
+        keep, send = down_near(
+            hidden, arrived[quarter], chosen, down_weight, held_near, devices, quarter
+        )
+        mine, send = add(keep, lax.ppermute(send, AXIS, swap_z(devices, 1)))
+        own.append(mine)
+        came.append(lax.ppermute(send, AXIS, swap_z(devices, 2)))
+    keep, send = finish(chosen, rows, own, came, devices)
     return join(keep, lax.ppermute(send, AXIS, swap_x(devices)), devices)
 
 

time: 73.3 us -> 72.2 us (0.985)
  waiting for transfers between devices: 15.7 us -> 11.3 us
  starting transfers between devices: 14.7 us -> 18.4 us
    ppermute x4 -> x6, waiting for transfers between devices: 12.2 us -> 6.58 us  [the longest x2 3.83 us: local(): came.append(lax.ppermute(send, AXIS, swap_z(devices, 2)))]
    ppermute x4 -> x6, starting transfers between devices: 5.63 us -> 9.45 us  [the longest x2 5.14 us: local(): came.append(lax.ppermute(send, AXIS, swap_z(devices, 2)))]
    pallas_call x3, Pallas kernels: 12 us -> 9.08 us  [load_bands(): pl.pallas_call(functools.partial(load_kernel, first), out_shape=pltpu.VME...]
    pallas_call x1, Pallas kernels: 12 us -> 14.1 us  [gate_up(): pl.pallas_call(functools.partial(gate_up_kernel, devices, len(held), firs...]
    pallas_call x5 -> x8, Pallas kernels: 12.6 us -> 14.1 us  [the longest x2 6.1 us: down_far(): pl.pallas_call(functools.partial(down_far_kernel, devices, quarter), out_...]
    pallas_call x1, Pallas kernels: 5.21 us -> 4.22 us  [attend(): pl.pallas_call(functools.partial(attend_kernel, kv, bands), out_shape=(ja...]
  transfers between devices with their start and end apart: 10 -> 12, of which waited for: 5 -> 7; matrix products, arithmetic and copies ran while one was open for 0% -> 0% of each run, Pallas kernels for 26% -> 28%
where the time goes in v5:
time: 72.2 us; the launch traced here: 72 us
  Pallas kernels  42.2 us (58%)
  starting transfers between devices  18.4 us (25%)
  waiting for transfers between devices  11.3 us (16%)
    pallas_call x1, Pallas kernels, gate_up(): pl.pallas_call(functools.partial(gate_up_kernel, devices, len(held), firs...  14.1 us
    pallas_call x3, Pallas kernels, load_bands(): pl.pallas_call(functools.partial(load_kernel, first), out_shape=pltpu.VME...  9.08 us
    pallas_call x2, Pallas kernels, down_far(): pl.pallas_call(functools.partial(down_far_kernel, devices, quarter), out_...  6.1 us
    pallas_call x2, Pallas kernels, down_near(): pl.pallas_call(functools.partial(down_near_kernel, devices, quarter), out...  5.26 us
    ppermute x2, starting transfers between devices, local(): came.append(lax.ppermute(send, AXIS, swap_z(devices, 2)))  5.14 us
    pallas_call x1, Pallas kernels, attend(): pl.pallas_call(functools.partial(attend_kernel, kv, bands), out_shape=(ja...  4.22 us
    ppermute x1, starting transfers between devices, local(): two = lax.ppermute(mixed_rows, AXIS, swap_z(devices, 2))  4.1 us
    ppermute x2, waiting for transfers between devices, local(): came.append(lax.ppermute(send, AXIS, swap_z(devices, 2)))  3.83 us
  transfers between devices with their start and end apart: 12, of which 7 were waited for; matrix products, arithmetic and copies ran while one was open for 0% of the time, Pallas kernels for 28%

profile of v5, /device:TPU:0, one launch (start us, length us, event | category | flops | bytes accessed | tf_op | source)
XLA Modules:
  0.0 72.0 jit_solution(689257739702245078)
XLA Ops:
  0.0 4.2 %attention.1 = (bf16[8,4096]{1,0:T(8,128)(2,1)S(1)}, bf16[2,2,256,3328]{3,2,1,0:T(8,128)(2,1)S(1)}) custom-call(s32[8]{0:T(128)} %lengths.1, bf16[8,32,128]{2,1,0:T(8,128)(2,1)} %q_hbm.1, bf16[8,256,128]{2,1,0:T(8,128)(2,1)} %bitcast.4, bf16[8,256,128]{2,1,0:T(8,128)(2,1)} %bitcast.5, bf16[8,4096]{1,0:T(8,128)(2,1)} %res_ref.1, bf16[4096,3328]{1,0:T(8,128)(2,1)} %refs_4_.4, ...), custom_call_target="tpu_custom_call" | custom-call | flops 33554432 | bytes 1048576 | tf_op jit(solution)/shard_map/attention/pallas_call | solution.py:117
  4.2 4.1 %collective-permute-start = (bf16[8,4096]{1,0:T(8,128)(2,1)S(1)}, bf16[8,4096]{1,0:T(8,128)(2,1)S(1)}, u32[]{:S(2)}, u32[]{:S(2)}) collective-permute-start(bf16[8,4096]{1,0:T(8,128)(2,1)S(1)} %get-tuple-element.27.after_ref.a_ref), channel_id=1, source_target_pairs={{0,8},{2,10},{4,12},{6,14},{8,0},{10,2},{12,4},{14,6},{1,9},{3,11}... | collective-permute-start | bytes 196616 | tf_op jit(solution)/shard_map/ppermute | solution.py:621
  8.3 3.0 %load_bands.3.after_ref.refs_8_ = bf16[2,2,256,3328]{3,2,1,0:T(8,128)(2,1)S(1)} custom-call(bf16[8,4096]{1,0:T(8,128)(2,1)S(1)} %get-tuple-element.27.after_ref.a_ref, bf16[4096,3328]{1,0:T(8,128)(2,1)} %refs_4_.4, bf16[4096,3328]{1,0:T(8,128)(2,1)} %refs_5_.1), custom_call_target="tpu_custom_call" | custom-call | bytes 6815744 | tf_op jit(solution)/shard_map/load_bands/pallas_call | solution.py:165
  12.0 1.0 %collective-permute-start.2 = (bf16[2,8,4096]{2,1,0:T(8,128)(2,1)S(1)}, bf16[2,8,4096]{2,1,0:T(8,128)(2,1)S(1)}, u32[]{:S(2)}, u32[]{:S(2)}) collective-permute-start(bf16[2,8,4096]{2,1,0:T(8,128)(2,1)S(1)} %pack.1.after_ref.refs_0_), channel_id=1, source_target_pairs={{0,4},{2,6},{4,0},{6,2},{8,12},{10,14},{12,8},{14,10},{1,5},{3,7},... | collective-permute-start | bytes 393224 | tf_op jit(solution)/shard_map/ppermute | solution.py:625
  13.0 1.5 %collective-permute-start.1 = (bf16[2,8,4096]{2,1,0:T(8,128)(2,1)S(1)}, bf16[2,8,4096]{2,1,0:T(8,128)(2,1)S(1)}, u32[]{:S(2)}, u32[]{:S(2)}) collective-permute-start(bf16[2,8,4096]{2,1,0:T(8,128)(2,1)S(1)} %pack.1.after_ref.refs_0_), channel_id=1, source_target_pairs={{0,2},{2,0},{4,6},{6,4},{8,10},{10,8},{12,14},{14,12},{1,3},{3,1},... | collective-permute-start | bytes 393224 | tf_op jit(solution)/shard_map/ppermute | solution.py:624
  14.5 3.0 %load_bands.4.after_ref.refs_9_ = bf16[2,2,256,3328]{3,2,1,0:T(8,128)(2,1)S(1)} custom-call(bf16[2,8,4096]{2,1,0:T(8,128)(2,1)S(1)} %pack.1.after_ref.refs_0_, bf16[4096,3328]{1,0:T(8,128)(2,1)} %refs_4_.4, bf16[4096,3328]{1,0:T(8,128)(2,1)} %refs_5_.1), custom_call_target="tpu_custom_call" | custom-call | bytes 6815744 | tf_op jit(solution)/shard_map/load_bands/pallas_call | solution.py:165
  17.6 1.1 %collective-permute-start.3 = (bf16[2,8,4096]{2,1,0:T(8,128)(2,1)S(1)}, bf16[2,8,4096]{2,1,0:T(8,128)(2,1)S(1)}, u32[]{:S(2)}, u32[]{:S(2)}) collective-permute-start(bf16[2,8,4096]{2,1,0:T(8,128)(2,1)S(1)} %hold.1.after_ref.refs_2_), channel_id=1, source_target_pairs={{0,2},{2,0},{4,6},{6,4},{8,10},{10,8},{12,14},{14,12},{1,3},{3,1},... | collective-permute-start | bytes 393224 | tf_op jit(solution)/shard_map/ppermute | solution.py:628
  18.7 3.0 %load_bands.5.refs_10_ = bf16[2,2,256,3328]{3,2,1,0:T(8,128)(2,1)S(1)} custom-call(bf16[2,8,4096]{2,1,0:T(8,128)(2,1)S(1)} %hold.1.after_ref.refs_2_, bf16[4096,3328]{1,0:T(8,128)(2,1)} %refs_4_.4, bf16[4096,3328]{1,0:T(8,128)(2,1)} %refs_5_.1), custom_call_target="tpu_custom_call" | custom-call | bytes 6815744 | tf_op jit(solution)/shard_map/load_bands/pallas_call | solution.py:165
  22.6 14.1 %gate_up.1 = (bf16[2,64,3328]{2,1,0:T(8,128)(2,1)S(1)}, bf16[64,4096]{1,0:T(8,128)(2,1)S(1)}, bf16[8,256,2048]{2,1,0:T(8,128)(2,1)S(1)}) custom-call(bf16[2,8,4096]{2,1,0:T(8,128)(2,1)S(1)} %pack.1.after_ref.refs_0_, bf16[2,8,4096]{2,1,0:T(8,128)(2,1)S(1)} %collective-permute-done.1.refs_1_, bf16[2,8,4096]{2,1,0:T(8,128)(2,1)S(1)} %hold.1.after_ref.refs_2_, ...), custom_call_target="tpu_custom_call" | custom-call | flops 3489660928 | bytes 54525952 | tf_op jit(solution)/shard_map/gate_up/pallas_call | solution.py:289
  36.8 2.6 %prepare.1 = (bf16[5,256,2048]{2,1,0:T(8,128)(2,1)S(1)}, bf16[128,64]{1,0:T(8,128)(2,1)S(1)}) custom-call(bf16[2,64,3328]{2,1,0:T(8,128)(2,1)S(1)} %get-tuple-element.29.after_ref.refs_0_, s32[1,64]{1,0:T(1,128)S(1)} %bitcast.3, bf16[3328,4096]{1,0:T(8,128)(2,1)} %refs_4_.7), custom_call_target="tpu_custom_call" | custom-call | bytes 5242880 | tf_op jit(solution)/shard_map/prepare/pallas_call | solution.py:370
  39.3 3.2 %down_far.2 = (bf16[64,1024]{1,0:T(8,128)(2,1)S(1)}, bf16[9,256,1024]{2,1,0:T(8,128)(2,1)S(1)}, bf16[64,3328]{1,0:T(8,128)(2,1)S(1)}) custom-call(bf16[2,64,3328]{2,1,0:T(8,128)(2,1)S(1)} %get-tuple-element.29.after_ref.refs_0_, bf16[2,64,3328]{2,1,0:T(8,128)(2,1)S(1)} %collective-permute-done.4.refs_1_, ...), custom_call_target="tpu_custom_call" | custom-call | bytes 1024 | tf_op jit(solution)/shard_map/down_far/pallas_call | solution.py:427
  42.6 1.1 %collective-permute-start.5 = (bf16[64,1024]{1,0:T(8,128)(2,1)S(1)}, bf16[64,1024]{1,0:T(8,128)(2,1)S(1)}, u32[]{:S(2)}, u32[]{:S(2)}) collective-permute-start(bf16[64,1024]{1,0:T(8,128)(2,1)S(1)} %get-tuple-element.35), channel_id=1, source_target_pairs={{0,2},{2,0},{4,6},{6,4},{8,10},{10,8},{12,14},{14,12},{1,3},{3,1},... | collective-permute-start | bytes 393224 | tf_op jit(solution)/shard_map/ppermute | solution.py:642
  43.7 2.9 %down_far.3 = (bf16[64,1024]{1,0:T(8,128)(2,1)S(1)}, bf16[8,256,1024]{2,1,0:T(8,128)(2,1)S(1)}) custom-call(bf16[64,3328]{1,0:T(8,128)(2,1)S(1)} %get-tuple-element.34.refs_0_, bf16[8,256,2048]{2,1,0:T(8,128)(2,1)S(1)} %get-tuple-element.32.refs_2_.refs_1_, bf16[5,256,2048]{2,1,0:T(8,128)(2,1)S(1)} %get-tuple-element.33.refs_3_.refs_2_, ...), custom_call_target="tpu_custom_call" | custom-call | bytes 1024 | tf_op jit(solution)/shard_map/down_far/pallas_call | solution.py:427
  46.6 1.0 %collective-permute-start.7 = (bf16[64,1024]{1,0:T(8,128)(2,1)S(1)}, bf16[64,1024]{1,0:T(8,128)(2,1)S(1)}, u32[]{:S(2)}, u32[]{:S(2)}) collective-permute-start(bf16[64,1024]{1,0:T(8,128)(2,1)S(1)} %get-tuple-element.40), channel_id=1, source_target_pairs={{0,2},{2,0},{4,6},{6,4},{8,10},{10,8},{12,14},{14,12},{1,3},{3,1},... | collective-permute-start | bytes 393224 | tf_op jit(solution)/shard_map/ppermute | solution.py:644
  47.6 0.9 %collective-permute-done.5.refs_1_ = bf16[64,1024]{1,0:T(8,128)(2,1)S(1)} collective-permute-done((bf16[64,1024]{1,0:T(8,128)(2,1)S(1)}, bf16[64,1024]{1,0:T(8,128)(2,1)S(1)}, u32[]{:S(2)}, u32[]{:S(2)}) %collective-permute-start.5) | collective-permute-done | bytes 131104 | tf_op jit(solution)/shard_map/ppermute | solution.py:642
  48.5 2.7 %down_near.2 = (bf16[64,1024]{1,0:T(8,128)(2,1)S(1)}, bf16[64,1024]{1,0:T(8,128)(2,1)S(1)}) custom-call(bf16[64,3328]{1,0:T(8,128)(2,1)S(1)} %get-tuple-element.34.refs_0_, bf16[64,1024]{1,0:T(8,128)(2,1)S(1)} %collective-permute-done.5.refs_1_, bf16[128,64]{1,0:T(8,128)(2,1)S(1)} %get-tuple-element.30.refs_2_.chosen_ref, ...), custom_call_target="tpu_custom_call" | custom-call | bytes 1024 | tf_op jit(solution)/shard_map/down_near/pallas_call | solution.py:468
  51.2 1.3 %collective-permute-start.6 = (bf16[64,1024]{1,0:T(8,128)(2,1)S(1)}, bf16[64,1024]{1,0:T(8,128)(2,1)S(1)}, u32[]{:S(2)}, u32[]{:S(2)}) collective-permute-start(bf16[64,1024]{1,0:T(8,128)(2,1)S(1)} %get-tuple-element.38), channel_id=1, source_target_pairs={{0,4},{2,6},{4,0},{6,2},{8,12},{10,14},{12,8},{14,10},{1,5},{3,7},... | collective-permute-start | bytes 393224 | tf_op jit(solution)/shard_map/ppermute | solution.py:650
  52.5 2.6 %down_near.3 = (bf16[64,1024]{1,0:T(8,128)(2,1)S(1)}, bf16[64,1024]{1,0:T(8,128)(2,1)S(1)}) custom-call(bf16[64,3328]{1,0:T(8,128)(2,1)S(1)} %get-tuple-element.34.refs_0_, bf16[64,1024]{1,0:T(8,128)(2,1)S(1)} %collective-permute-done.7.refs_1_, bf16[128,64]{1,0:T(8,128)(2,1)S(1)} %get-tuple-element.30.refs_2_.chosen_ref, ...), custom_call_target="tpu_custom_call" | custom-call | bytes 1024 | tf_op jit(solution)/shard_map/down_near/pallas_call | solution.py:468
  56.4 3.0 %collective-permute-start.9 = (bf16[32,1024]{1,0:T(8,128)(2,1)S(1)}, bf16[32,1024]{1,0:T(8,128)(2,1)S(1)}, u32[]{:S(2)}, u32[]{:S(2)}) collective-permute-start(bf16[32,1024]{1,0:T(8,128)(2,1)S(1)} %get-tuple-element.45), channel_id=1, source_target_pairs={{0,8},{2,10},{4,12},{6,14},{8,0},{10,2},{12,4},{14,6},{1,9},{3,11}... | collective-permute-start | bytes 196616 | tf_op jit(solution)/shard_map/ppermute | solution.py:652
  59.5 1.4 %collective-permute-done.8.came_ref = bf16[64,1024]{1,0:T(8,128)(2,1)S(1)} collective-permute-done((bf16[64,1024]{1,0:T(8,128)(2,1)S(1)}, bf16[64,1024]{1,0:T(8,128)(2,1)S(1)}, u32[]{:S(2)}, u32[]{:S(2)}) %collective-permute-start.8) | collective-permute-done | bytes 131104 | tf_op jit(solution)/shard_map/ppermute | solution.py:650
  60.9 2.1 %collective-permute-start.10 = (bf16[32,1024]{1,0:T(8,128)(2,1)S(1)}, bf16[32,1024]{1,0:T(8,128)(2,1)S(1)}, u32[]{:S(2)}, u32[]{:S(2)}) collective-permute-start(bf16[32,1024]{1,0:T(8,128)(2,1)S(1)} %get-tuple-element.46), channel_id=1, source_target_pairs={{0,8},{2,10},{4,12},{6,14},{8,0},{10,2},{12,4},{14,6},{1,9},{3,11}... | collective-permute-start | bytes 196616 | tf_op jit(solution)/shard_map/ppermute | solution.py:652
  63.0 3.8 %collective-permute-done.10.refs_3_ = bf16[32,1024]{1,0:T(8,128)(2,1)S(1)} collective-permute-done((bf16[32,1024]{1,0:T(8,128)(2,1)S(1)}, bf16[32,1024]{1,0:T(8,128)(2,1)S(1)}, u32[]{:S(2)}, u32[]{:S(2)}) %collective-permute-start.10) | collective-permute-done | bytes 65568 | tf_op jit(solution)/shard_map/ppermute | solution.py:652
  67.0 1.1 %collective-permute-start.11 = (bf16[16,2048]{1,0:T(8,128)(2,1)S(1)}, bf16[16,2048]{1,0:T(8,128)(2,1)S(1)}, u32[]{:S(2)}, u32[]{:S(2)}) collective-permute-start(bf16[16,2048]{1,0:T(8,128)(2,1)S(1)} %get-tuple-element.48), channel_id=1, source_target_pairs={{0,2},{2,0},{4,6},{6,4},{8,10},{10,8},{12,14},{14,12},{1,3},{3,1},... | collective-permute-start | bytes 196616 | tf_op jit(solution)/shard_map/ppermute | solution.py:654
  68.1 3.2 %collective-permute-done.11.other_ref = bf16[16,2048]{1,0:T(8,128)(2,1)S(1)} collective-permute-done((bf16[16,2048]{1,0:T(8,128)(2,1)S(1)}, bf16[16,2048]{1,0:T(8,128)(2,1)S(1)}, u32[]{:S(2)}, u32[]{:S(2)}) %collective-permute-start.11) | collective-permute-done | bytes 65568 | tf_op jit(solution)/shard_map/ppermute | solution.py:654
  (18 shorter events, 3.7 us)
Async XLA Ops:
  4.2 7.8 %collective-permute-start = (bf16[8,4096]{1,0:T(8,128)(2,1)S(1)}, bf16[8,4096]{1,0:T(8,128)(2,1)S(1)}, u32[]{:S(2)}, u32[]{:S(2)}) collective-permute-start(bf16[8,4096]{1,0:T(8,128)(2,1)S(1)} %get-tuple-element.27.after_ref.a_ref), channel_id=1, source_target_pairs={{0,8},{2,10},{4,12},{6,14},{8,0},{10,2},{12,4},{14,6},{1,9},{3,11}... | collective-permute-start | bytes 196616 | tf_op jit(solution)/shard_map/ppermute | solution.py:621
  12.0 5.6 %collective-permute-start.2 = (bf16[2,8,4096]{2,1,0:T(8,128)(2,1)S(1)}, bf16[2,8,4096]{2,1,0:T(8,128)(2,1)S(1)}, u32[]{:S(2)}, u32[]{:S(2)}) collective-permute-start(bf16[2,8,4096]{2,1,0:T(8,128)(2,1)S(1)} %pack.1.after_ref.refs_0_), channel_id=1, source_target_pairs={{0,4},{2,6},{4,0},{6,2},{8,12},{10,14},{12,8},{14,10},{1,5},{3,7},... | collective-permute-start | bytes 393224 | tf_op jit(solution)/shard_map/ppermute | solution.py:625
  13.0 8.7 %collective-permute-start.1 = (bf16[2,8,4096]{2,1,0:T(8,128)(2,1)S(1)}, bf16[2,8,4096]{2,1,0:T(8,128)(2,1)S(1)}, u32[]{:S(2)}, u32[]{:S(2)}) collective-permute-start(bf16[2,8,4096]{2,1,0:T(8,128)(2,1)S(1)} %pack.1.after_ref.refs_0_), channel_id=1, source_target_pairs={{0,2},{2,0},{4,6},{6,4},{8,10},{10,8},{12,14},{14,12},{1,3},{3,1},... | collective-permute-start | bytes 393224 | tf_op jit(solution)/shard_map/ppermute | solution.py:624
  17.6 5.0 %collective-permute-start.3 = (bf16[2,8,4096]{2,1,0:T(8,128)(2,1)S(1)}, bf16[2,8,4096]{2,1,0:T(8,128)(2,1)S(1)}, u32[]{:S(2)}, u32[]{:S(2)}) collective-permute-start(bf16[2,8,4096]{2,1,0:T(8,128)(2,1)S(1)} %hold.1.after_ref.refs_2_), channel_id=1, source_target_pairs={{0,2},{2,0},{4,6},{6,4},{8,10},{10,8},{12,14},{14,12},{1,3},{3,1},... | collective-permute-start | bytes 393224 | tf_op jit(solution)/shard_map/ppermute | solution.py:628
  22.6 14.1 %copy-start = (s32[64,1]{0,1:T(1,128)S(1)}, s32[64,1]{0,1:T(1,128)}, u32[]{:S(2)}) copy-start(s32[64,1]{0,1:T(1,128)} %param.14) | copy-start | bytes 772
  36.7 2.7 %collective-permute-start.4 = (bf16[2,64,3328]{2,1,0:T(8,128)(2,1)S(1)}, bf16[2,64,3328]{2,1,0:T(8,128)(2,1)S(1)}, u32[]{:S(2)}, u32[]{:S(2)}) collective-permute-start(bf16[2,64,3328]{2,1,0:T(8,128)(2,1)S(1)} %get-tuple-element.29.after_ref.refs_0_), channel_id=1, source_target_pairs={{0,1},{1,0},{2,3},{3,2},{4,5},{5,4},{6,7},{7,6},{8,9},{9,8},{10,11... | collective-permute-start | bytes 2555912 | tf_op jit(solution)/shard_map/ppermute | solution.py:635
  42.6 6.0 %collective-permute-start.5 = (bf16[64,1024]{1,0:T(8,128)(2,1)S(1)}, bf16[64,1024]{1,0:T(8,128)(2,1)S(1)}, u32[]{:S(2)}, u32[]{:S(2)}) collective-permute-start(bf16[64,1024]{1,0:T(8,128)(2,1)S(1)} %get-tuple-element.35), channel_id=1, source_target_pairs={{0,2},{2,0},{4,6},{6,4},{8,10},{10,8},{12,14},{14,12},{1,3},{3,1},... | collective-permute-start | bytes 393224 | tf_op jit(solution)/shard_map/ppermute | solution.py:642
  46.6 6.0 %collective-permute-start.7 = (bf16[64,1024]{1,0:T(8,128)(2,1)S(1)}, bf16[64,1024]{1,0:T(8,128)(2,1)S(1)}, u32[]{:S(2)}, u32[]{:S(2)}) collective-permute-start(bf16[64,1024]{1,0:T(8,128)(2,1)S(1)} %get-tuple-element.40), channel_id=1, source_target_pairs={{0,2},{2,0},{4,6},{6,4},{8,10},{10,8},{12,14},{14,12},{1,3},{3,1},... | collective-permute-start | bytes 393224 | tf_op jit(solution)/shard_map/ppermute | solution.py:644
  51.2 5.2 %collective-permute-start.6 = (bf16[64,1024]{1,0:T(8,128)(2,1)S(1)}, bf16[64,1024]{1,0:T(8,128)(2,1)S(1)}, u32[]{:S(2)}, u32[]{:S(2)}) collective-permute-start(bf16[64,1024]{1,0:T(8,128)(2,1)S(1)} %get-tuple-element.38), channel_id=1, source_target_pairs={{0,4},{2,6},{4,0},{6,2},{8,12},{10,14},{12,8},{14,10},{1,5},{3,7},... | collective-permute-start | bytes 393224 | tf_op jit(solution)/shard_map/ppermute | solution.py:650
  55.1 5.7 %collective-permute-start.8 = (bf16[64,1024]{1,0:T(8,128)(2,1)S(1)}, bf16[64,1024]{1,0:T(8,128)(2,1)S(1)}, u32[]{:S(2)}, u32[]{:S(2)}) collective-permute-start(bf16[64,1024]{1,0:T(8,128)(2,1)S(1)} %get-tuple-element.43), channel_id=1, source_target_pairs={{0,4},{2,6},{4,0},{6,2},{8,12},{10,14},{12,8},{14,10},{1,5},{3,7},... | collective-permute-start | bytes 393224 | tf_op jit(solution)/shard_map/ppermute | solution.py:650
  56.4 6.6 %collective-permute-start.9 = (bf16[32,1024]{1,0:T(8,128)(2,1)S(1)}, bf16[32,1024]{1,0:T(8,128)(2,1)S(1)}, u32[]{:S(2)}, u32[]{:S(2)}) collective-permute-start(bf16[32,1024]{1,0:T(8,128)(2,1)S(1)} %get-tuple-element.45), channel_id=1, source_target_pairs={{0,8},{2,10},{4,12},{6,14},{8,0},{10,2},{12,4},{14,6},{1,9},{3,11}... | collective-permute-start | bytes 196616 | tf_op jit(solution)/shard_map/ppermute | solution.py:652
  60.9 5.9 %collective-permute-start.10 = (bf16[32,1024]{1,0:T(8,128)(2,1)S(1)}, bf16[32,1024]{1,0:T(8,128)(2,1)S(1)}, u32[]{:S(2)}, u32[]{:S(2)}) collective-permute-start(bf16[32,1024]{1,0:T(8,128)(2,1)S(1)} %get-tuple-element.46), channel_id=1, source_target_pairs={{0,8},{2,10},{4,12},{6,14},{8,0},{10,2},{12,4},{14,6},{1,9},{3,11}... | collective-permute-start | bytes 196616 | tf_op jit(solution)/shard_map/ppermute | solution.py:652
  67.0 4.3 %collective-permute-start.11 = (bf16[16,2048]{1,0:T(8,128)(2,1)S(1)}, bf16[16,2048]{1,0:T(8,128)(2,1)S(1)}, u32[]{:S(2)}, u32[]{:S(2)}) collective-permute-start(bf16[16,2048]{1,0:T(8,128)(2,1)S(1)} %get-tuple-element.48), channel_id=1, source_target_pairs={{0,2},{2,0},{4,6},{6,4},{8,10},{10,8},{12,14},{14,12},{1,3},{3,1},... | collective-permute-start | bytes 196616 | tf_op jit(solution)/shard_map/ppermute | solution.py:654

commit v6 on v5

--- a/solution.py
+++ b/solution.py
@@ -10,7 +10,8 @@
 
 AXIS = "attn"
 TILE = 256
-BAND = 256
+BAND = 512
+PIECES = 2
 ORDER = (0, 2, 1, 3)
 MIB = 1 << 20
 VMEM = pl.BlockSpec(memory_space=pltpu.VMEM)
@@ -63,7 +64,7 @@
     weights = ()
     if bands:
         g_hbm, u_hbm, out_ref, held_ref, *refs, band_sems = refs
-        weights = band_copies(g_hbm, u_hbm, held_ref, band_sems, 0)
+        weights = band_copies(g_hbm, u_hbm, held_ref, band_sems, 0, 0)
     else:
         out_ref, *refs = refs
     att_ref, scores_ref, probs_ref, q_ref, k_ref, v_ref, sems = refs
@@ -113,7 +114,7 @@
     kv = cache_keys.shape[2]
     span = cache_keys.shape[1] * kv
     held = [pltpu.VMEM((bands, 2, BAND, w.shape[1]), BF16) for w in weights[:1]]
-    band_sems = [pltpu.SemaphoreType.DMA((bands, 2)) for _ in held]
+    band_sems = [pltpu.SemaphoreType.DMA((2, PIECES)) for _ in held]
     return pl.pallas_call(
         functools.partial(attend_kernel, kv, bands),
         out_shape=(jax.ShapeDtypeStruct((rows, heads * dim), BF16), *held),
@@ -142,35 +143,38 @@
     )
 
 
-def band_copies(g_hbm, u_hbm, held_ref, sems, first):
+def band_copies(g_hbm, u_hbm, held_ref, sems, place, band):
+    rows = BAND // PIECES
     return [
         pltpu.make_async_copy(
-            w.at[pl.ds((first + i) * BAND, BAND)], held_ref.at[i, kind], sems.at[i, kind]
+            w.at[pl.ds(pl.multiple_of(band * BAND + i * rows, rows), rows)],
+            held_ref.at[place, kind, pl.ds(i * rows, rows)],
+            sems.at[kind, i],
         )
-        for i in range(held_ref.shape[0])
         for kind, w in enumerate((g_hbm, u_hbm))
+        for i in range(PIECES)
     ]
 
 
-def load_kernel(first, after_ref, g_hbm, u_hbm, held_ref, sems):
-    copies = band_copies(g_hbm, u_hbm, held_ref, sems, first)
+def load_kernel(band, after_ref, g_hbm, u_hbm, held_ref, sems):
+    copies = band_copies(g_hbm, u_hbm, held_ref, sems, 0, band)
     for c in copies:
         c.start()
     for c in copies:
         c.wait()
 
 
-def load_bands(after, gate_weight, up_weight, first, bands):
+def load_band(after, gate_weight, up_weight, band):
     columns = gate_weight.shape[1]
     return pl.pallas_call(
-        functools.partial(load_kernel, first),
-        out_shape=pltpu.VMEM((bands, 2, BAND, columns), BF16),
+        functools.partial(load_kernel, band),
+        out_shape=pltpu.VMEM((1, 2, BAND, columns), BF16),
         in_specs=[ANY, HBM, HBM],
         out_specs=VMEM,
-        scratch_shapes=[pltpu.SemaphoreType.DMA((bands, 2))],
+        scratch_shapes=[pltpu.SemaphoreType.DMA((2, PIECES))],
         compiler_params=params(2),
-        cost_estimate=cost(0, bands * 2 * BAND * columns * 2),
-        name="load_bands",
+        cost_estimate=cost(0, 4 * BAND * columns),
+        name="load_band",
     )(after, in_hbm(gate_weight), in_hbm(up_weight))
 
 
@@ -206,27 +210,28 @@
     return pl.ds(pl.multiple_of(index * TILE, TILE), TILE)
 
 
-def gate_up_kernel(devices, holders, first, *refs):
+def gate_up_kernel(
+    devices,
+    held,
+    *refs,
+):
     a_ref, b_ref, c_ref, d_ref, g_hbm, u_hbm, w_hbm = refs[:7]
-    held_refs = refs[7 : 7 + holders]
-    part_ref, rows_ref, far_ref, total_ref, buf, sems, far_sems = refs[7 + holders :]
+    held_refs = refs[7 : 7 + held]
+    part_ref, rows_ref, far_ref, total_ref, buf, sems, far_sems = refs[7 + held :]
     nx = grid_of(devices)[1]
     slots = buf.shape[0]
-    left = g_hbm.shape[0] // BAND - first
+    left = g_hbm.shape[0] // BAND - held
 
     def streamed(j):
         slot = lax.rem(j, slots)
-        at = pl.ds(pl.multiple_of((first + j) * BAND, BAND), BAND)
-        return [
-            pltpu.make_async_copy(w.at[at], buf.at[slot, kind], sems.at[slot, kind])
-            for kind, w in enumerate((g_hbm, u_hbm))
-        ]
+        return band_copies(g_hbm, u_hbm, buf, sems.at[slot], slot, held + j)
 
     for j in range(min(slots, left)):
         for c in streamed(j):
             c.start()
-    half = far_ref.shape[2]
-    ahead = down_copies(w_hbm, half_base(devices, False, half), far_ref, far_sems, 0)
+    ahead = down_copies(
+        w_hbm, half_base(devices, False, far_ref.shape[1]), far_ref, far_sems, 0
+    )
     for c in ahead:
         c.start()
     me = lax.axis_index(AXIS)
@@ -244,64 +249,56 @@
         at = pl.ds(pl.multiple_of(i * BAND, BAND), BAND)
         total_ref[kind] += jnp.dot(rows_ref[:, at], weight, preferred_element_type=F32)
 
-    def add_streamed(j):
-        slot = lax.rem(j, slots)
-        for kind, c in enumerate(streamed(j)):
-            c.wait()
-            add(first + j, buf[slot, kind], kind)
-
-        @pl.when(j + slots < left)
+    total_ref[...] = jnp.zeros_like(total_ref)
+
+    def step(i, _):
+        for number, held_ref in enumerate(held_refs):
+
+            @pl.when(i == number)
+            def _():
+                for kind in range(2):
+                    add(number, held_ref[0, kind], kind)
+
+        slot = lax.rem(i, slots)
+        copies = streamed(i)
+        for kind in range(2):
+            for c in copies[kind * PIECES : (kind + 1) * PIECES]:
+                c.wait()
+            add(held + i, buf[slot, kind], kind)
+
+        @pl.when(i + slots < left)
         def _():
-            for c in streamed(j + slots):
+            for c in streamed(i + slots):
                 c.start()
 
-    total_ref[...] = jnp.zeros_like(total_ref)
-    start, came = 0, 0
-    for held in held_refs:
-
-        def step(i, _, held=held, start=start, came=came):
-            for kind in range(2):
-                add(start + i, held[i, kind], kind)
-            if start:
-                add_streamed(came + i)
-            return 0
-
-        lax.fori_loop(0, held.shape[0], step, 0)
-        came += held.shape[0] if start else 0
-        start += held.shape[0]
-
-    def rest(j, _):
-        add_streamed(j)
         return 0
 
-    lax.fori_loop(came, left, rest, 0)
+    lax.fori_loop(0, held, step, 0)
     part_ref[...] = total_ref[...].astype(BF16)
     for c in ahead:
         c.wait()
 
 
-def gate_up(blocks, gate_weight, up_weight, down_weight, held, devices, tiles):
+def gate_up(blocks, gate_weight, up_weight, down_weight, held, devices, ahead):
     total = devices * blocks[0].shape[1]
     features, columns = gate_weight.shape
-    first = sum(h.shape[0] for h in held)
     slots = 2
-    far = (tiles, TILE, features // 2)
-    return pl.pallas_call(
-        functools.partial(gate_up_kernel, devices, len(held), first),
+    return pl.pallas_call(
+        functools.partial(gate_up_kernel, devices, len(held)),
         out_shape=(
             jax.ShapeDtypeStruct((2, total, columns), BF16),
             jax.ShapeDtypeStruct((total, features), BF16),
-            pltpu.VMEM(far, BF16),
+            pltpu.VMEM((ahead, features // 2), BF16),
         ),
         in_specs=[VMEM] * 4 + [HBM] * 3 + [VMEM] * len(held),
         out_specs=(VMEM, VMEM, VMEM),
         scratch_shapes=[
             pltpu.VMEM((2, total, columns), F32),
             pltpu.VMEM((slots, 2, BAND, columns), BF16),
-            pltpu.SemaphoreType.DMA((slots, 2)),
-            pltpu.SemaphoreType.DMA((far[0],)),
+            pltpu.SemaphoreType.DMA((slots, 2, PIECES)),
+            pltpu.SemaphoreType.DMA((ahead // TILE,)),
         ],
-        compiler_params=params(10),
+        compiler_params=params(18),
         cost_estimate=cost(4 * total * features * columns, 4 * features * columns),
         name="gate_up",
     )(
@@ -314,14 +311,14 @@
 
 
 def down_copies(w_hbm, base, held_ref, sems, first):
-    wide = held_ref.shape[2]
+    rows, wide = held_ref.shape
     return [
         pltpu.make_async_copy(
-            w_hbm.at[pl.ds((first + i) * TILE, TILE), pl.ds(base, wide)],
-            held_ref.at[i],
+            w_hbm.at[pl.ds(first + i * TILE, TILE), pl.ds(base, wide)],
+            held_ref.at[pl.ds(i * TILE, TILE)],
             sems.at[i],
         )
-        for i in range(held_ref.shape[0])
+        for i in range(rows // TILE)
     ]
 
 
@@ -330,9 +327,10 @@
     return pl.multiple_of((my_x if mine else 1 - my_x) * half, half)
 
 
-def quarter_base(devices, quarter, wide):
+def quarter_base(devices, far, quarter, wide):
     my_x = lax.axis_index(AXIS) % grid_of(devices)[1]
-    return pl.multiple_of((2 * my_x + quarter) * wide, wide)
+    half = 1 - my_x if far else my_x
+    return pl.multiple_of((2 * half + quarter) * wide, wide)
 
 
 def pick(row_ref, capacity, first_slot, slots):
@@ -349,7 +347,7 @@
 
 
 def prepare_kernel(devices, capacity, first, after_ref, row_ref, w_hbm, held_ref, chosen_ref, sems):
-    base = half_base(devices, False, held_ref.shape[2])
+    base = half_base(devices, False, held_ref.shape[1])
     copies = down_copies(w_hbm, base, held_ref, sems, first)
     for c in copies:
         c.start()
@@ -364,121 +362,132 @@
         c.wait()
 
 
-def prepare(after, row, down_weight, devices, capacity, first, tiles):
+def prepare(after, row, down_weight, devices, capacity, first, rows):
     wide = down_weight.shape[1] // 2
     total = row.shape[1]
     return pl.pallas_call(
         functools.partial(prepare_kernel, devices, capacity, first),
         out_shape=(
-            pltpu.VMEM((tiles, TILE, wide), BF16),
+            pltpu.VMEM((rows, wide), BF16),
             jax.ShapeDtypeStruct((devices * 2 * capacity, total), BF16),
         ),
         in_specs=[ANY, VMEM, HBM],
         out_specs=(VMEM, VMEM),
-        scratch_shapes=[pltpu.SemaphoreType.DMA((tiles,))],
+        scratch_shapes=[pltpu.SemaphoreType.DMA((rows // TILE,))],
         compiler_params=params(2),
-        cost_estimate=cost(0, tiles * TILE * wide * 2),
+        cost_estimate=cost(0, rows * wide * 2),
         name="prepare",
     )(after, row, in_hbm(down_weight))
 
 
-def add_held(hidden_ref, held_refs, at, total_ref):
+def multiply(hidden_ref, held_refs, quarter, total_ref, buf, copies):
+    wide = total_ref.shape[1]
     start = 0
     for held_ref in held_refs:
-
-        def step(i, _, held_ref=held_ref, start=start):
+        rows = held_ref.shape[0]
+        at = slice(quarter * wide, (quarter + 1) * wide)
+        weight = held_ref[...] if held_ref.shape[1] == wide else held_ref[:, at]
+        total_ref[...] += jnp.dot(
+            hidden_ref[:, start : start + rows], weight, preferred_element_type=F32
+        )
+        start += rows
+    if copies:
+        cut = (len(copies) + 1) // 2
+        for some in (slice(0, cut), slice(cut, len(copies))):
+            if not copies[some]:
+                continue
+            for c in copies[some]:
+                c.wait()
+            at = slice(some.start * TILE, some.stop * TILE)
             total_ref[...] += jnp.dot(
-                hidden_ref[:, tile_at(start + i)],
-                held_ref[i, :, at],
+                hidden_ref[:, start + at.start : start + at.stop],
+                buf[at],
                 preferred_element_type=F32,
             )
-            return 0
-
-        lax.fori_loop(0, held_ref.shape[0], step, 0)
-        start += held_ref.shape[0]
-
-
-def down_far_kernel(devices, quarter, *refs):
-    if quarter == 0:
-        own_ref, other_ref, *refs = refs
-        *held_refs, w_hbm, out_ref, next_ref, hidden_ref, total_ref, sems = refs
-    else:
-        hidden_ref, *held_refs, w_hbm, out_ref, next_ref, total_ref, sems = refs
-    wide = out_ref.shape[1]
-    ahead = down_copies(w_hbm, quarter_base(devices, quarter, wide), next_ref, sems, 0)
-    for c in ahead:
+
+
+def down_kernel(devices, far, quarter, held_count, next_base, next_first, streams, aheads, *refs):
+    refs = list(refs)
+    take = lambda count: [refs.pop(0) for _ in range(count)]
+    first_call = far and quarter == 0
+    sources = take(2 if first_call else 1)
+    arrived_ref, chosen_ref = take(2) if not far else (None, None)
+    held_refs = take(held_count)
+    (w_hbm,) = take(1)
+    out_refs = take(1 if far else 2)
+    next_refs = take(1 if aheads else 0)
+    (hidden_ref,) = take(1) if first_call else sources
+    (total_ref,) = take(1)
+    wide = total_ref.shape[1]
+    copies, ahead, buf = [], [], None
+    base = quarter_base(devices, far, quarter, wide)
+    if streams:
+        buf, sems = take(2)
+        copies = down_copies(w_hbm, base, buf, sems, sum(h.shape[0] for h in held_refs))
+    if aheads:
+        (next_sems,) = take(1)
+        ahead = down_copies(
+            w_hbm, quarter_base(devices, *next_base, wide), next_refs[0], next_sems, next_first
+        )
+    for c in copies + ahead:
         c.start()
-    if quarter == 0:
+    if first_call:
+        own_ref, other_ref = sources
         gate = own_ref[0].astype(F32) + other_ref[0].astype(F32)
         up = own_ref[1].astype(F32) + other_ref[1].astype(F32)
         hidden_ref[...] = (gate / (1.0 + jnp.exp(-gate)) * up).astype(BF16)
-    total_ref[...] = jnp.zeros_like(total_ref)
-    add_held(hidden_ref, held_refs, slice(quarter * wide, (quarter + 1) * wide), total_ref)
-    out_ref[...] = total_ref[...].astype(BF16)
+    if far:
+        total_ref[...] = jnp.zeros_like(total_ref)
+    else:
+        total_ref[...] = arrived_ref[...].astype(F32)
+    multiply(hidden_ref, held_refs, quarter, total_ref, buf, copies)
+    rounded = total_ref[...].astype(BF16)
+    if far:
+        out_refs[0][...] = rounded
+    else:
+        slots = out_refs[0].shape[0]
+        for i, ref in enumerate(out_refs):
+            chosen = chosen_ref[i * slots : (i + 1) * slots]
+            ref[...] = jnp.dot(chosen, rounded, preferred_element_type=F32).astype(BF16)
     for c in ahead:
         c.wait()
 
 
-def down_far(inputs, held, down_weight, devices, quarter, ahead):
-    total = inputs[0].shape[-2]
+def down(sources, held, down_weight, devices, far, quarter, ahead=None):
+    total = sources[0].shape[-2]
     columns, features = down_weight.shape
     wide = features // 4
-    hidden = [jax.ShapeDtypeStruct((total, columns), BF16)] if quarter == 0 else []
-    return pl.pallas_call(
-        functools.partial(down_far_kernel, devices, quarter),
-        out_shape=(
-            jax.ShapeDtypeStruct((total, wide), BF16),
-            pltpu.VMEM((ahead, TILE, wide), BF16),
-            *hidden,
+    streams = columns - sum(h.shape[0] for h in held)
+    next_base, next_first, aheads = ahead or (None, 0, 0)
+    first_call = far and quarter == 0
+    if far:
+        out_shape = [jax.ShapeDtypeStruct((total, wide), BF16)]
+    else:
+        out_shape = [jax.ShapeDtypeStruct((sources[2].shape[0] // 2, wide), BF16)] * 2
+    if aheads:
+        out_shape.append(pltpu.VMEM((aheads, wide), BF16))
+    if first_call:
+        out_shape.append(jax.ShapeDtypeStruct((total, columns), BF16))
+    scratch = [pltpu.VMEM((total, wide), F32)]
+    if streams:
+        scratch += [
+            pltpu.VMEM((streams, wide), BF16),
+            pltpu.SemaphoreType.DMA((streams // TILE,)),
+        ]
+    if aheads:
+        scratch.append(pltpu.SemaphoreType.DMA((aheads // TILE,)))
+    return pl.pallas_call(
+        functools.partial(
+            down_kernel, devices, far, quarter, len(held), next_base, next_first, streams, aheads
         ),
-        in_specs=[VMEM] * (len(inputs) + len(held)) + [HBM],
-        out_specs=(VMEM, VMEM) + tuple(VMEM for _ in hidden),
-        scratch_shapes=[
-            pltpu.VMEM((total, wide), F32),
-            pltpu.SemaphoreType.DMA((ahead,)),
-        ],
-        compiler_params=params(6),
+        out_shape=tuple(out_shape),
+        in_specs=[VMEM] * (len(sources) + len(held)) + [HBM],
+        out_specs=tuple(VMEM for _ in out_shape),
+        scratch_shapes=scratch,
+        compiler_params=params(10),
         cost_estimate=COST,
-        name="down_far",
-    )(*inputs, *(in_vmem(h) for h in held), in_hbm(down_weight))
-
-
-def down_near_kernel(devices, quarter, *refs):
-    hidden_ref, arrived_ref, chosen_ref, held_ref, w_hbm, keep_ref, send_ref, total_ref, buf, sems = refs
-    held = held_ref.shape[0]
-    copies = down_copies(w_hbm, quarter_base(devices, quarter, buf.shape[2]), buf, sems, held)
-    for c in copies:
-        c.start()
-    total_ref[...] = arrived_ref[...].astype(F32)
-    add_held(hidden_ref, (held_ref,), slice(None), total_ref)
-    for i, c in enumerate(copies):
-        c.wait()
-        at = slice((held + i) * TILE, (held + i + 1) * TILE)
-        total_ref[...] += jnp.dot(hidden_ref[:, at], buf[i], preferred_element_type=F32)
-    slots = keep_ref.shape[0]
-    rounded = total_ref[...].astype(BF16)
-    keep_ref[...] = jnp.dot(chosen_ref[:slots], rounded, preferred_element_type=F32).astype(BF16)
-    send_ref[...] = jnp.dot(chosen_ref[slots:], rounded, preferred_element_type=F32).astype(BF16)
-
-
-def down_near(hidden, arrived, chosen, down_weight, held, devices, quarter):
-    total, wide = arrived.shape
-    left = down_weight.shape[0] // TILE - held.shape[0]
-    shape = jax.ShapeDtypeStruct((chosen.shape[0] // 2, wide), BF16)
-    return pl.pallas_call(
-        functools.partial(down_near_kernel, devices, quarter),
-        out_shape=(shape, shape),
-        in_specs=[VMEM] * 4 + [HBM],
-        out_specs=(VMEM, VMEM),
-        scratch_shapes=[
-            pltpu.VMEM((total, wide), F32),
-            pltpu.VMEM((left, TILE, wide), BF16),
-            pltpu.SemaphoreType.DMA((left,)),
-        ],
-        compiler_params=params(8),
-        cost_estimate=COST,
-        name="down_near",
-    )(hidden, arrived, chosen, in_vmem(held), in_hbm(down_weight))
+        name="down_far" if far else "down_near",
+    )(*sources, *(in_vmem(h) for h in held), in_hbm(down_weight))
 
 
 def add_kernel(keep_ref, came_ref, own_ref, send_ref):
@@ -509,7 +518,7 @@
     slots, wide = own_refs[0].shape
     half = slots // 2
     for quarter, (own_ref, came_ref) in enumerate(zip(own_refs, came_refs)):
-        mixed = rows_ref[:, pl.ds(quarter_base(devices, quarter, wide), wide)]
+        mixed = rows_ref[:, pl.ds(quarter_base(devices, False, quarter, wide), wide)]
         done = jnp.dot(chosen_ref[:slots], mixed, preferred_element_type=F32)
         done = done + (own_ref[...] + came_ref[...].astype(F32))
         first, second = done[:half], done[half:]
@@ -604,8 +613,7 @@
     nz, nx = grid_of(devices)
     capacity = cache_keys.shape[0]
     columns, features = down_weight.shape
-    fits = nz == 4 and nx == 2 and columns % TILE == 0 and features % (16 * TILE) == 0
-    share = gate_weight.shape[0] // BAND // 8 if fits else 0
+    fits = nz == 4 and nx == 2 and columns % TILE == 0 and features % (8 * BAND) == 0
     mixed_rows, *held = attend(
         queries,
         cache_keys,
@@ -613,40 +621,61 @@
         lengths,
         residual,
         (gate_weight, up_weight) if fits else (),
-        share,
+        1 if fits else 0,
     )
     if not fits:
         return plain(mixed_rows, target, gate_weight, up_weight, down_weight, devices)
 
     two = lax.ppermute(mixed_rows, AXIS, swap_z(devices, 2))
-    held.append(load_bands(mixed_rows, gate_weight, up_weight, share, share))
+    held.append(load_band(mixed_rows, gate_weight, up_weight, 1))
     a = pack(mixed_rows, two, held[-1])
     b = lax.ppermute(a, AXIS, swap_x(devices))
     c = lax.ppermute(a, AXIS, swap_z(devices, 1))
-    held.append(load_bands(a, gate_weight, up_weight, 2 * share, share))
+    held.append(load_band(a, gate_weight, up_weight, 2))
     c = hold(c, held[-1])
     d = lax.ppermute(c, AXIS, swap_x(devices))
-    held.append(load_bands(c, gate_weight, up_weight, 3 * share, share))
+    held.append(load_band(c, gate_weight, up_weight, 3))
     tiles = columns // TILE
-    most = 8 * tiles // 13
-    part, rows, *held_far = gate_up(
-        (a, b, c, d), gate_weight, up_weight, down_weight, held, devices, most
+    early, middle = 3 * tiles // 13 * TILE, 5 * tiles // 13 * TILE
+    part, rows, far_a = gate_up(
+        (a, b, c, d), gate_weight, up_weight, down_weight, held, devices, early
     )
     other = lax.ppermute(part, "ffn", [(0, 1), (1, 0)])
-    rest, chosen = prepare(
-        part, target.reshape(1, -1), down_weight, devices, capacity, most, tiles - most
-    )
-    held_far.append(rest)
-
-    far, near_first, hidden = down_far((part, other), held_far, down_weight, devices, 0, 9 * tiles // 13)
+    far_b, chosen = prepare(
+        part, target.reshape(1, -1), down_weight, devices, capacity, early, middle
+    )
+
+    first = early + middle
+    far, far_c, hidden = down(
+        (part, other),
+        (far_a, far_b),
+        down_weight,
+        devices,
+        True,
+        0,
+        ((True, 1), first, columns - first),
+    )
     arrived = [lax.ppermute(far, AXIS, swap_x(devices))]
-    far, near_second = down_far((hidden,), held_far, down_weight, devices, 1, 8 * tiles // 13)
+    far, near_a = down(
+        (hidden,),
+        (far_a, far_b, far_c),
+        down_weight,
+        devices,
+        True,
+        1,
+        ((False, 0), 0, 9 * tiles // 13 * TILE),
+    )
     arrived.append(lax.ppermute(far, AXIS, swap_x(devices)))
     own, came = [], []
-    for quarter, held_near in enumerate((near_first, near_second)):
-        keep, send = down_near(
-            hidden, arrived[quarter], chosen, down_weight, held_near, devices, quarter
-        )
+    for quarter in range(2):
+        sources = (hidden, arrived[quarter], chosen)
+        if quarter == 0:
+            ahead = ((False, 1), 0, 5 * tiles // 13 * TILE)
+            keep, send, near_b = down(
+                sources, (near_a,), down_weight, devices, False, 0, ahead
+            )
+        else:
+            keep, send = down(sources, (near_b,), down_weight, devices, False, 1)
         mine, send = add(keep, lax.ppermute(send, AXIS, swap_z(devices, 1)))
         own.append(mine)
         came.append(lax.ppermute(send, AXIS, swap_z(devices, 2)))

time: 72.2 us -> 70.8 us (0.981)
  waiting for transfers between devices: 11.3 us -> 9.63 us
  starting transfers between devices: 18.4 us -> 19.2 us
    ppermute x2, waiting for transfers between devices: 3.83 us -> 3.1 us  [local(): came.append(lax.ppermute(send, AXIS, swap_z(devices, 2)))]
  transfers between devices with their start and end apart: 12 -> 12, of which waited for: 7 -> 7; matrix products, arithmetic and copies ran while one was open for 0% -> 0% of each run, Pallas kernels for 28% -> 30%
where the time goes in v6:
time: 70.8 us; the launch traced here: 70.6 us
  Pallas kernels  41.6 us (59%)
  starting transfers between devices  19.2 us (27%)
  waiting for transfers between devices  9.63 us (14%)
    pallas_call x4, Pallas kernels, down(): pl.pallas_call(functools.partial(down_kernel, devices, far, quarter, len(...  12.6 us
    pallas_call x1, Pallas kernels, gate_up(): pl.pallas_call(functools.partial(gate_up_kernel, devices, len(held)), out...  12.2 us
    pallas_call x3, Pallas kernels, load_band(): pl.pallas_call(functools.partial(load_kernel, band), out_shape=pltpu.VMEM...  9.08 us
    ppermute x2, starting transfers between devices, local(): came.append(lax.ppermute(send, AXIS, swap_z(devices, 2)))  5.27 us
    pallas_call x1, Pallas kernels, attend(): pl.pallas_call(functools.partial(attend_kernel, kv, bands), out_shape=(ja...  4.22 us
    ppermute x1, starting transfers between devices, local(): two = lax.ppermute(mixed_rows, AXIS, swap_z(devices, 2))  4.1 us
    ppermute x2, waiting for transfers between devices, local(): came.append(lax.ppermute(send, AXIS, swap_z(devices, 2)))  3.1 us
    ppermute x1, waiting for transfers between devices, local(): return join(keep, lax.ppermute(send, AXIS, swap_x(devices)), devices)  2.59 us
  transfers between devices with their start and end apart: 12, of which 7 were waited for; matrix products, arithmetic and copies ran while one was open for 0% of the time, Pallas kernels for 30%

profile of v6, /device:TPU:0, one launch (start us, length us, event | category | flops | bytes accessed | tf_op | source)
XLA Modules:
  0.0 70.6 jit_solution(5981930503725520672)
XLA Ops:
  0.0 4.2 %attention.1 = (bf16[8,4096]{1,0:T(8,128)(2,1)S(1)}, bf16[1,2,512,3328]{3,2,1,0:T(8,128)(2,1)S(1)}) custom-call(s32[8]{0:T(128)} %lengths.1, bf16[8,32,128]{2,1,0:T(8,128)(2,1)} %q_hbm.1, bf16[8,256,128]{2,1,0:T(8,128)(2,1)} %bitcast.4, bf16[8,256,128]{2,1,0:T(8,128)(2,1)} %bitcast.5, bf16[8,4096]{1,0:T(8,128)(2,1)} %res_ref.1, bf16[4096,3328]{1,0:T(8,128)(2,1)} %refs_4_.5, ...), custom_call_target="tpu_custom_call" | custom-call | flops 33554432 | bytes 1048576 | tf_op jit(solution)/shard_map/attention/pallas_call | solution.py:118
  4.2 4.1 %collective-permute-start = (bf16[8,4096]{1,0:T(8,128)(2,1)S(1)}, bf16[8,4096]{1,0:T(8,128)(2,1)S(1)}, u32[]{:S(2)}, u32[]{:S(2)}) collective-permute-start(bf16[8,4096]{1,0:T(8,128)(2,1)S(1)} %get-tuple-element.28.after_ref.a_ref), channel_id=1, source_target_pairs={{0,8},{2,10},{4,12},{6,14},{8,0},{10,2},{12,4},{14,6},{1,9},{3,11}... | collective-permute-start | bytes 196616 | tf_op jit(solution)/shard_map/ppermute | solution.py:629
  8.3 3.0 %load_band.3.after_ref.refs_8_ = bf16[1,2,512,3328]{3,2,1,0:T(8,128)(2,1)S(1)} custom-call(bf16[8,4096]{1,0:T(8,128)(2,1)S(1)} %get-tuple-element.28.after_ref.a_ref, bf16[4096,3328]{1,0:T(8,128)(2,1)} %refs_4_.5, bf16[4096,3328]{1,0:T(8,128)(2,1)} %refs_5_.1), custom_call_target="tpu_custom_call" | custom-call | bytes 6815744 | tf_op jit(solution)/shard_map/load_band/pallas_call | solution.py:169
  12.0 1.0 %collective-permute-start.2 = (bf16[2,8,4096]{2,1,0:T(8,128)(2,1)S(1)}, bf16[2,8,4096]{2,1,0:T(8,128)(2,1)S(1)}, u32[]{:S(2)}, u32[]{:S(2)}) collective-permute-start(bf16[2,8,4096]{2,1,0:T(8,128)(2,1)S(1)} %pack.1.after_ref.refs_0_), channel_id=1, source_target_pairs={{0,4},{2,6},{4,0},{6,2},{8,12},{10,14},{12,8},{14,10},{1,5},{3,7},... | collective-permute-start | bytes 393224 | tf_op jit(solution)/shard_map/ppermute | solution.py:633
  13.0 1.5 %collective-permute-start.1 = (bf16[2,8,4096]{2,1,0:T(8,128)(2,1)S(1)}, bf16[2,8,4096]{2,1,0:T(8,128)(2,1)S(1)}, u32[]{:S(2)}, u32[]{:S(2)}) collective-permute-start(bf16[2,8,4096]{2,1,0:T(8,128)(2,1)S(1)} %pack.1.after_ref.refs_0_), channel_id=1, source_target_pairs={{0,2},{2,0},{4,6},{6,4},{8,10},{10,8},{12,14},{14,12},{1,3},{3,1},... | collective-permute-start | bytes 393224 | tf_op jit(solution)/shard_map/ppermute | solution.py:632
  14.5 3.0 %load_band.4.after_ref.refs_9_ = bf16[1,2,512,3328]{3,2,1,0:T(8,128)(2,1)S(1)} custom-call(bf16[2,8,4096]{2,1,0:T(8,128)(2,1)S(1)} %pack.1.after_ref.refs_0_, bf16[4096,3328]{1,0:T(8,128)(2,1)} %refs_4_.5, bf16[4096,3328]{1,0:T(8,128)(2,1)} %refs_5_.1), custom_call_target="tpu_custom_call" | custom-call | bytes 6815744 | tf_op jit(solution)/shard_map/load_band/pallas_call | solution.py:169
  17.6 1.1 %collective-permute-start.3 = (bf16[2,8,4096]{2,1,0:T(8,128)(2,1)S(1)}, bf16[2,8,4096]{2,1,0:T(8,128)(2,1)S(1)}, u32[]{:S(2)}, u32[]{:S(2)}) collective-permute-start(bf16[2,8,4096]{2,1,0:T(8,128)(2,1)S(1)} %hold.1.after_ref.refs_2_), channel_id=1, source_target_pairs={{0,2},{2,0},{4,6},{6,4},{8,10},{10,8},{12,14},{14,12},{1,3},{3,1},... | collective-permute-start | bytes 393224 | tf_op jit(solution)/shard_map/ppermute | solution.py:636
  18.7 3.0 %load_band.5.refs_10_ = bf16[1,2,512,3328]{3,2,1,0:T(8,128)(2,1)S(1)} custom-call(bf16[2,8,4096]{2,1,0:T(8,128)(2,1)S(1)} %hold.1.after_ref.refs_2_, bf16[4096,3328]{1,0:T(8,128)(2,1)} %refs_4_.5, bf16[4096,3328]{1,0:T(8,128)(2,1)} %refs_5_.1), custom_call_target="tpu_custom_call" | custom-call | bytes 6815744 | tf_op jit(solution)/shard_map/load_band/pallas_call | solution.py:169
  21.8 0.8 %collective-permute-done.3.refs_3_ = bf16[2,8,4096]{2,1,0:T(8,128)(2,1)S(1)} collective-permute-done((bf16[2,8,4096]{2,1,0:T(8,128)(2,1)S(1)}, bf16[2,8,4096]{2,1,0:T(8,128)(2,1)S(1)}, u32[]{:S(2)}, u32[]{:S(2)}) %collective-permute-start.3) | collective-permute-done | bytes 131104 | tf_op jit(solution)/shard_map/ppermute | solution.py:636
  22.6 12.2 %gate_up.1 = (bf16[2,64,3328]{2,1,0:T(8,128)(2,1)S(1)}, bf16[64,4096]{1,0:T(8,128)(2,1)S(1)}, bf16[768,2048]{1,0:T(8,128)(2,1)S(1)}) custom-call(bf16[2,8,4096]{2,1,0:T(8,128)(2,1)S(1)} %pack.1.after_ref.refs_0_, bf16[2,8,4096]{2,1,0:T(8,128)(2,1)S(1)} %collective-permute-done.1.refs_1_, bf16[2,8,4096]{2,1,0:T(8,128)(2,1)S(1)} %hold.1.after_ref.refs_2_, ...), custom_call_target="tpu_custom_call" | custom-call | flops 3489660928 | bytes 54525952 | tf_op jit(solution)/shard_map/gate_up/pallas_call | solution.py:286
  34.9 2.6 %prepare.1 = (bf16[1280,2048]{1,0:T(8,128)(2,1)S(1)}, bf16[128,64]{1,0:T(8,128)(2,1)S(1)}) custom-call(bf16[2,64,3328]{2,1,0:T(8,128)(2,1)S(1)} %get-tuple-element.30.after_ref.refs_0_, s32[1,64]{1,0:T(1,128)S(1)} %bitcast.3, bf16[3328,4096]{1,0:T(8,128)(2,1)} %refs_4_.9), custom_call_target="tpu_custom_call" | custom-call | bytes 5242880 | tf_op jit(solution)/shard_map/prepare/pallas_call | solution.py:368
  37.5 3.4 %down_far.2 = (bf16[64,1024]{1,0:T(8,128)(2,1)S(1)}, bf16[1280,1024]{1,0:T(8,128)(2,1)S(1)}, bf16[64,3328]{1,0:T(8,128)(2,1)S(1)}) custom-call(bf16[2,64,3328]{2,1,0:T(8,128)(2,1)S(1)} %get-tuple-element.30.after_ref.refs_0_, bf16[2,64,3328]{2,1,0:T(8,128)(2,1)S(1)} %collective-permute-done.4.refs_1_, ...), custom_call_target="tpu_custom_call" | custom-call | bytes 1024 | tf_op jit(solution)/shard_map/down_far/pallas_call | solution.py:479
  40.9 1.1 %collective-permute-start.5 = (bf16[64,1024]{1,0:T(8,128)(2,1)S(1)}, bf16[64,1024]{1,0:T(8,128)(2,1)S(1)}, u32[]{:S(2)}, u32[]{:S(2)}) collective-permute-start(bf16[64,1024]{1,0:T(8,128)(2,1)S(1)} %get-tuple-element.36), channel_id=1, source_target_pairs={{0,2},{2,0},{4,6},{6,4},{8,10},{10,8},{12,14},{14,12},{1,3},{3,1},... | collective-permute-start | bytes 393224 | tf_op jit(solution)/shard_map/ppermute | solution.py:658
  42.1 3.5 %down_far.3 = (bf16[64,1024]{1,0:T(8,128)(2,1)S(1)}, bf16[2304,1024]{1,0:T(8,128)(2,1)S(1)}) custom-call(bf16[64,3328]{1,0:T(8,128)(2,1)S(1)} %get-tuple-element.35.refs_0_, bf16[768,2048]{1,0:T(8,128)(2,1)S(1)} %get-tuple-element.33.refs_2_.refs_1_, bf16[1280,2048]{1,0:T(8,128)(2,1)S(1)} %get-tuple-element.34.refs_3_.refs_2_, ...), custom_call_target="tpu_custom_call" | custom-call | bytes 1024 | tf_op jit(solution)/shard_map/down_far/pallas_call | solution.py:479
  45.6 1.0 %collective-permute-start.7 = (bf16[64,1024]{1,0:T(8,128)(2,1)S(1)}, bf16[64,1024]{1,0:T(8,128)(2,1)S(1)}, u32[]{:S(2)}, u32[]{:S(2)}) collective-permute-start(bf16[64,1024]{1,0:T(8,128)(2,1)S(1)} %get-tuple-element.42), channel_id=1, source_target_pairs={{0,2},{2,0},{4,6},{6,4},{8,10},{10,8},{12,14},{14,12},{1,3},{3,1},... | collective-permute-start | bytes 393224 | tf_op jit(solution)/shard_map/ppermute | solution.py:668
  46.9 2.8 %down_near.2 = (bf16[64,1024]{1,0:T(8,128)(2,1)S(1)}, bf16[64,1024]{1,0:T(8,128)(2,1)S(1)}, bf16[1280,1024]{1,0:T(8,128)(2,1)S(1)}) custom-call(bf16[64,3328]{1,0:T(8,128)(2,1)S(1)} %get-tuple-element.35.refs_0_, bf16[64,1024]{1,0:T(8,128)(2,1)S(1)} %collective-permute-done.5.refs_1_, bf16[128,64]{1,0:T(8,128)(2,1)S(1)} %get-tuple-element.31.refs_2_.chosen_ref, ...), custom_call_target="tpu_custom_call" | custom-call | bytes 1024 | tf_op jit(solution)/shard_map/down_near/pallas_call | solution.py:479
  49.6 1.3 %collective-permute-start.6 = (bf16[64,1024]{1,0:T(8,128)(2,1)S(1)}, bf16[64,1024]{1,0:T(8,128)(2,1)S(1)}, u32[]{:S(2)}, u32[]{:S(2)}) collective-permute-start(bf16[64,1024]{1,0:T(8,128)(2,1)S(1)} %get-tuple-element.40), channel_id=1, source_target_pairs={{0,4},{2,6},{4,0},{6,2},{8,12},{10,14},{12,8},{14,10},{1,5},{3,7},... | collective-permute-start | bytes 393224 | tf_op jit(solution)/shard_map/ppermute | solution.py:679
  51.3 2.9 %down_near.3 = (bf16[64,1024]{1,0:T(8,128)(2,1)S(1)}, bf16[64,1024]{1,0:T(8,128)(2,1)S(1)}) custom-call(bf16[64,3328]{1,0:T(8,128)(2,1)S(1)} %get-tuple-element.35.refs_0_, bf16[64,1024]{1,0:T(8,128)(2,1)S(1)} %collective-permute-done.7.refs_1_, bf16[128,64]{1,0:T(8,128)(2,1)S(1)} %get-tuple-element.31.refs_2_.chosen_ref, ...), custom_call_target="tpu_custom_call" | custom-call | bytes 1024 | tf_op jit(solution)/shard_map/down_near/pallas_call | solution.py:479
  55.1 3.1 %collective-permute-start.9 = (bf16[32,1024]{1,0:T(8,128)(2,1)S(1)}, bf16[32,1024]{1,0:T(8,128)(2,1)S(1)}, u32[]{:S(2)}, u32[]{:S(2)}) collective-permute-start(bf16[32,1024]{1,0:T(8,128)(2,1)S(1)} %get-tuple-element.47), channel_id=1, source_target_pairs={{0,8},{2,10},{4,12},{6,14},{8,0},{10,2},{12,4},{14,6},{1,9},{3,11}... | collective-permute-start | bytes 196616 | tf_op jit(solution)/shard_map/ppermute | solution.py:681
  58.2 1.9 %collective-permute-done.8.came_ref = bf16[64,1024]{1,0:T(8,128)(2,1)S(1)} collective-permute-done((bf16[64,1024]{1,0:T(8,128)(2,1)S(1)}, bf16[64,1024]{1,0:T(8,128)(2,1)S(1)}, u32[]{:S(2)}, u32[]{:S(2)}) %collective-permute-start.8) | collective-permute-done | bytes 131104 | tf_op jit(solution)/shard_map/ppermute | solution.py:679
  60.2 2.1 %collective-permute-start.10 = (bf16[32,1024]{1,0:T(8,128)(2,1)S(1)}, bf16[32,1024]{1,0:T(8,128)(2,1)S(1)}, u32[]{:S(2)}, u32[]{:S(2)}) collective-permute-start(bf16[32,1024]{1,0:T(8,128)(2,1)S(1)} %get-tuple-element.48), channel_id=1, source_target_pairs={{0,8},{2,10},{4,12},{6,14},{8,0},{10,2},{12,4},{14,6},{1,9},{3,11}... | collective-permute-start | bytes 196616 | tf_op jit(solution)/shard_map/ppermute | solution.py:681
  62.3 3.1 %collective-permute-done.10.refs_3_ = bf16[32,1024]{1,0:T(8,128)(2,1)S(1)} collective-permute-done((bf16[32,1024]{1,0:T(8,128)(2,1)S(1)}, bf16[32,1024]{1,0:T(8,128)(2,1)S(1)}, u32[]{:S(2)}, u32[]{:S(2)}) %collective-permute-start.10) | collective-permute-done | bytes 65568 | tf_op jit(solution)/shard_map/ppermute | solution.py:681
  65.6 1.7 %collective-permute-start.11 = (bf16[16,2048]{1,0:T(8,128)(2,1)S(1)}, bf16[16,2048]{1,0:T(8,128)(2,1)S(1)}, u32[]{:S(2)}, u32[]{:S(2)}) collective-permute-start(bf16[16,2048]{1,0:T(8,128)(2,1)S(1)} %get-tuple-element.50), channel_id=1, source_target_pairs={{0,2},{2,0},{4,6},{6,4},{8,10},{10,8},{12,14},{14,12},{1,3},{3,1},... | collective-permute-start | bytes 196616 | tf_op jit(solution)/shard_map/ppermute | solution.py:683
  67.3 2.6 %collective-permute-done.11.other_ref = bf16[16,2048]{1,0:T(8,128)(2,1)S(1)} collective-permute-done((bf16[16,2048]{1,0:T(8,128)(2,1)S(1)}, bf16[16,2048]{1,0:T(8,128)(2,1)S(1)}, u32[]{:S(2)}, u32[]{:S(2)}) %collective-permute-start.11) | collective-permute-done | bytes 65568 | tf_op jit(solution)/shard_map/ppermute | solution.py:683
  (18 shorter events, 3.0 us)
Async XLA Ops:
  4.2 7.8 %collective-permute-start = (bf16[8,4096]{1,0:T(8,128)(2,1)S(1)}, bf16[8,4096]{1,0:T(8,128)(2,1)S(1)}, u32[]{:S(2)}, u32[]{:S(2)}) collective-permute-start(bf16[8,4096]{1,0:T(8,128)(2,1)S(1)} %get-tuple-element.28.after_ref.a_ref), channel_id=1, source_target_pairs={{0,8},{2,10},{4,12},{6,14},{8,0},{10,2},{12,4},{14,6},{1,9},{3,11}... | collective-permute-start | bytes 196616 | tf_op jit(solution)/shard_map/ppermute | solution.py:629
  12.0 5.6 %collective-permute-start.2 = (bf16[2,8,4096]{2,1,0:T(8,128)(2,1)S(1)}, bf16[2,8,4096]{2,1,0:T(8,128)(2,1)S(1)}, u32[]{:S(2)}, u32[]{:S(2)}) collective-permute-start(bf16[2,8,4096]{2,1,0:T(8,128)(2,1)S(1)} %pack.1.after_ref.refs_0_), channel_id=1, source_target_pairs={{0,4},{2,6},{4,0},{6,2},{8,12},{10,14},{12,8},{14,10},{1,5},{3,7},... | collective-permute-start | bytes 393224 | tf_op jit(solution)/shard_map/ppermute | solution.py:633
  13.0 8.7 %collective-permute-start.1 = (bf16[2,8,4096]{2,1,0:T(8,128)(2,1)S(1)}, bf16[2,8,4096]{2,1,0:T(8,128)(2,1)S(1)}, u32[]{:S(2)}, u32[]{:S(2)}) collective-permute-start(bf16[2,8,4096]{2,1,0:T(8,128)(2,1)S(1)} %pack.1.after_ref.refs_0_), channel_id=1, source_target_pairs={{0,2},{2,0},{4,6},{6,4},{8,10},{10,8},{12,14},{14,12},{1,3},{3,1},... | collective-permute-start | bytes 393224 | tf_op jit(solution)/shard_map/ppermute | solution.py:632
  17.6 5.0 %collective-permute-start.3 = (bf16[2,8,4096]{2,1,0:T(8,128)(2,1)S(1)}, bf16[2,8,4096]{2,1,0:T(8,128)(2,1)S(1)}, u32[]{:S(2)}, u32[]{:S(2)}) collective-permute-start(bf16[2,8,4096]{2,1,0:T(8,128)(2,1)S(1)} %hold.1.after_ref.refs_2_), channel_id=1, source_target_pairs={{0,2},{2,0},{4,6},{6,4},{8,10},{10,8},{12,14},{14,12},{1,3},{3,1},... | collective-permute-start | bytes 393224 | tf_op jit(solution)/shard_map/ppermute | solution.py:636
  22.6 12.3 %copy-start = (s32[64,1]{0,1:T(1,128)S(1)}, s32[64,1]{0,1:T(1,128)}, u32[]{:S(2)}) copy-start(s32[64,1]{0,1:T(1,128)} %param.14) | copy-start | bytes 772
  34.9 2.7 %collective-permute-start.4 = (bf16[2,64,3328]{2,1,0:T(8,128)(2,1)S(1)}, bf16[2,64,3328]{2,1,0:T(8,128)(2,1)S(1)}, u32[]{:S(2)}, u32[]{:S(2)}) collective-permute-start(bf16[2,64,3328]{2,1,0:T(8,128)(2,1)S(1)} %get-tuple-element.30.after_ref.refs_0_), channel_id=1, source_target_pairs={{0,1},{1,0},{2,3},{3,2},{4,5},{5,4},{6,7},{7,6},{8,9},{9,8},{10,11... | collective-permute-start | bytes 2555912 | tf_op jit(solution)/shard_map/ppermute | solution.py:643
  40.9 6.0 %collective-permute-start.5 = (bf16[64,1024]{1,0:T(8,128)(2,1)S(1)}, bf16[64,1024]{1,0:T(8,128)(2,1)S(1)}, u32[]{:S(2)}, u32[]{:S(2)}) collective-permute-start(bf16[64,1024]{1,0:T(8,128)(2,1)S(1)} %get-tuple-element.36), channel_id=1, source_target_pairs={{0,2},{2,0},{4,6},{6,4},{8,10},{10,8},{12,14},{14,12},{1,3},{3,1},... | collective-permute-start | bytes 393224 | tf_op jit(solution)/shard_map/ppermute | solution.py:658
  45.6 5.7 %collective-permute-start.7 = (bf16[64,1024]{1,0:T(8,128)(2,1)S(1)}, bf16[64,1024]{1,0:T(8,128)(2,1)S(1)}, u32[]{:S(2)}, u32[]{:S(2)}) collective-permute-start(bf16[64,1024]{1,0:T(8,128)(2,1)S(1)} %get-tuple-element.42), channel_id=1, source_target_pairs={{0,2},{2,0},{4,6},{6,4},{8,10},{10,8},{12,14},{14,12},{1,3},{3,1},... | collective-permute-start | bytes 393224 | tf_op jit(solution)/shard_map/ppermute | solution.py:668
  49.6 5.4 %collective-permute-start.6 = (bf16[64,1024]{1,0:T(8,128)(2,1)S(1)}, bf16[64,1024]{1,0:T(8,128)(2,1)S(1)}, u32[]{:S(2)}, u32[]{:S(2)}) collective-permute-start(bf16[64,1024]{1,0:T(8,128)(2,1)S(1)} %get-tuple-element.40), channel_id=1, source_target_pairs={{0,4},{2,6},{4,0},{6,2},{8,12},{10,14},{12,8},{14,10},{1,5},{3,7},... | collective-permute-start | bytes 393224 | tf_op jit(solution)/shard_map/ppermute | solution.py:679
  54.2 5.9 %collective-permute-start.8 = (bf16[64,1024]{1,0:T(8,128)(2,1)S(1)}, bf16[64,1024]{1,0:T(8,128)(2,1)S(1)}, u32[]{:S(2)}, u32[]{:S(2)}) collective-permute-start(bf16[64,1024]{1,0:T(8,128)(2,1)S(1)} %get-tuple-element.45), channel_id=1, source_target_pairs={{0,4},{2,6},{4,0},{6,2},{8,12},{10,14},{12,8},{14,10},{1,5},{3,7},... | collective-permute-start | bytes 393224 | tf_op jit(solution)/shard_map/ppermute | solution.py:679
  55.1 7.2 %collective-permute-start.9 = (bf16[32,1024]{1,0:T(8,128)(2,1)S(1)}, bf16[32,1024]{1,0:T(8,128)(2,1)S(1)}, u32[]{:S(2)}, u32[]{:S(2)}) collective-permute-start(bf16[32,1024]{1,0:T(8,128)(2,1)S(1)} %get-tuple-element.47), channel_id=1, source_target_pairs={{0,8},{2,10},{4,12},{6,14},{8,0},{10,2},{12,4},{14,6},{1,9},{3,11}... | collective-permute-start | bytes 196616 | tf_op jit(solution)/shard_map/ppermute | solution.py:681
  60.2 5.2 %collective-permute-start.10 = (bf16[32,1024]{1,0:T(8,128)(2,1)S(1)}, bf16[32,1024]{1,0:T(8,128)(2,1)S(1)}, u32[]{:S(2)}, u32[]{:S(2)}) collective-permute-start(bf16[32,1024]{1,0:T(8,128)(2,1)S(1)} %get-tuple-element.48), channel_id=1, source_target_pairs={{0,8},{2,10},{4,12},{6,14},{8,0},{10,2},{12,4},{14,6},{1,9},{3,11}... | collective-permute-start | bytes 196616 | tf_op jit(solution)/shard_map/ppermute | solution.py:681
  65.6 4.3 %collective-permute-start.11 = (bf16[16,2048]{1,0:T(8,128)(2,1)S(1)}, bf16[16,2048]{1,0:T(8,128)(2,1)S(1)}, u32[]{:S(2)}, u32[]{:S(2)}) collective-permute-start(bf16[16,2048]{1,0:T(8,128)(2,1)S(1)} %get-tuple-element.50), channel_id=1, source_target_pairs={{0,2},{2,0},{4,6},{6,4},{8,10},{10,8},{12,14},{14,12},{1,3},{3,1},... | collective-permute-start | bytes 196616 | tf_op jit(solution)/shard_map/ppermute | solution.py:683

commit v7 on v6

--- a/solution.py
+++ b/solution.py
@@ -10,8 +10,8 @@
 
 AXIS = "attn"
 TILE = 256
-BAND = 512
-PIECES = 2
+BAND = 256
+GATE_MIB = 11
 ORDER = (0, 2, 1, 3)
 MIB = 1 << 20
 VMEM = pl.BlockSpec(memory_space=pltpu.VMEM)
@@ -60,11 +60,11 @@
 COST = cost(0, 1024)
 
 
-def attend_kernel(kv, bands, lengths, q_hbm, k_hbm, v_hbm, res_ref, *refs):
+def attend_kernel(kv, ahead, lengths, q_hbm, k_hbm, v_hbm, res_ref, *refs):
     weights = ()
-    if bands:
+    if ahead:
         g_hbm, u_hbm, out_ref, held_ref, *refs, band_sems = refs
-        weights = band_copies(g_hbm, u_hbm, held_ref, band_sems, 0, 0)
+        weights = band_copies(g_hbm, u_hbm, held_ref, band_sems, 0)
     else:
         out_ref, *refs = refs
     att_ref, scores_ref, probs_ref, q_ref, k_ref, v_ref, sems = refs
@@ -109,14 +109,14 @@
         c.wait()
 
 
-def attend(queries, cache_keys, stored_value_cache, lengths, residual, weights, bands):
+def attend(queries, cache_keys, stored_value_cache, lengths, residual, weights, ahead):
     rows, heads, dim = queries.shape
     kv = cache_keys.shape[2]
     span = cache_keys.shape[1] * kv
-    held = [pltpu.VMEM((bands, 2, BAND, w.shape[1]), BF16) for w in weights[:1]]
-    band_sems = [pltpu.SemaphoreType.DMA((2, PIECES)) for _ in held]
-    return pl.pallas_call(
-        functools.partial(attend_kernel, kv, bands),
+    held = [pltpu.VMEM((2, ahead, w.shape[1]), BF16) for w in weights[:1]]
+    band_sems = [pltpu.SemaphoreType.DMA((2, ahead // BAND)) for _ in held]
+    return pl.pallas_call(
+        functools.partial(attend_kernel, kv, ahead),
         out_shape=(jax.ShapeDtypeStruct((rows, heads * dim), BF16), *held),
         in_specs=[SMEM, HBM, HBM, HBM, VMEM] + [HBM for _ in weights],
         out_specs=(VMEM,) + tuple(VMEM for _ in held),
@@ -143,38 +143,37 @@
     )
 
 
-def band_copies(g_hbm, u_hbm, held_ref, sems, place, band):
-    rows = BAND // PIECES
+def band_copies(g_hbm, u_hbm, held_ref, sems, first):
     return [
         pltpu.make_async_copy(
-            w.at[pl.ds(pl.multiple_of(band * BAND + i * rows, rows), rows)],
-            held_ref.at[place, kind, pl.ds(i * rows, rows)],
+            w.at[pl.ds(pl.multiple_of(first + i * BAND, BAND), BAND)],
+            held_ref.at[kind, pl.ds(i * BAND, BAND)],
             sems.at[kind, i],
         )
         for kind, w in enumerate((g_hbm, u_hbm))
-        for i in range(PIECES)
+        for i in range(held_ref.shape[1] // BAND)
     ]
 
 
-def load_kernel(band, after_ref, g_hbm, u_hbm, held_ref, sems):
-    copies = band_copies(g_hbm, u_hbm, held_ref, sems, 0, band)
+def load_kernel(first, after_ref, g_hbm, u_hbm, held_ref, sems):
+    copies = band_copies(g_hbm, u_hbm, held_ref, sems, first)
     for c in copies:
         c.start()
     for c in copies:
         c.wait()
 
 
-def load_band(after, gate_weight, up_weight, band):
+def load_rows(after, gate_weight, up_weight, first, rows):
     columns = gate_weight.shape[1]
     return pl.pallas_call(
-        functools.partial(load_kernel, band),
-        out_shape=pltpu.VMEM((1, 2, BAND, columns), BF16),
+        functools.partial(load_kernel, first),
+        out_shape=pltpu.VMEM((2, rows, columns), BF16),
         in_specs=[ANY, HBM, HBM],
         out_specs=VMEM,
-        scratch_shapes=[pltpu.SemaphoreType.DMA((2, PIECES))],
+        scratch_shapes=[pltpu.SemaphoreType.DMA((2, rows // BAND))],
         compiler_params=params(2),
-        cost_estimate=cost(0, 4 * BAND * columns),
-        name="load_band",
+        cost_estimate=cost(0, 4 * rows * columns),
+        name="load_rows",
     )(after, in_hbm(gate_weight), in_hbm(up_weight))
 
 
@@ -220,11 +219,12 @@
     part_ref, rows_ref, far_ref, total_ref, buf, sems, far_sems = refs[7 + held :]
     nx = grid_of(devices)[1]
     slots = buf.shape[0]
-    left = g_hbm.shape[0] // BAND - held
+    first = sum(ref.shape[1] for ref in held_refs)
+    left = (g_hbm.shape[0] - first) // BAND
 
     def streamed(j):
         slot = lax.rem(j, slots)
-        return band_copies(g_hbm, u_hbm, buf, sems.at[slot], slot, held + j)
+        return band_copies(g_hbm, u_hbm, buf.at[slot], sems.at[slot], first + j * BAND)
 
     for j in range(min(slots, left)):
         for c in streamed(j):
@@ -245,35 +245,36 @@
             at = pl.ds(pl.multiple_of(z * (2 * per), 2 * per), 2 * per)
             rows_ref[at, :] = jnp.concatenate(pair, axis=0).astype(BF16)
 
-    def add(i, weight, kind):
-        at = pl.ds(pl.multiple_of(i * BAND, BAND), BAND)
+    def add(at, weight, kind):
         total_ref[kind] += jnp.dot(rows_ref[:, at], weight, preferred_element_type=F32)
 
     total_ref[...] = jnp.zeros_like(total_ref)
 
-    def step(i, _):
+    def step(j, _):
+        start = 0
         for number, held_ref in enumerate(held_refs):
-
-            @pl.when(i == number)
-            def _():
+            stop = start + held_ref.shape[1]
+
+            @pl.when(j == number * left // held)
+            def _(start=start, stop=stop, held_ref=held_ref):
                 for kind in range(2):
-                    add(number, held_ref[0, kind], kind)
-
-        slot = lax.rem(i, slots)
-        copies = streamed(i)
-        for kind in range(2):
-            for c in copies[kind * PIECES : (kind + 1) * PIECES]:
-                c.wait()
-            add(held + i, buf[slot, kind], kind)
-
-        @pl.when(i + slots < left)
+                    add(slice(start, stop), held_ref[kind], kind)
+
+            start = stop
+        slot = lax.rem(j, slots)
+        for kind, c in enumerate(streamed(j)):
+            c.wait()
+            at = pl.ds(pl.multiple_of(first + j * BAND, BAND), BAND)
+            add(at, buf[slot, kind], kind)
+
+        @pl.when(j + slots < left)
         def _():
-            for c in streamed(i + slots):
+            for c in streamed(j + slots):
                 c.start()
 
         return 0
 
-    lax.fori_loop(0, held, step, 0)
+    lax.fori_loop(0, left, step, 0)
     part_ref[...] = total_ref[...].astype(BF16)
     for c in ahead:
         c.wait()
@@ -295,10 +296,10 @@
         scratch_shapes=[
             pltpu.VMEM((2, total, columns), F32),
             pltpu.VMEM((slots, 2, BAND, columns), BF16),
-            pltpu.SemaphoreType.DMA((slots, 2, PIECES)),
+            pltpu.SemaphoreType.DMA((slots, 2, 1)),
             pltpu.SemaphoreType.DMA((ahead // TILE,)),
         ],
-        compiler_params=params(18),
+        compiler_params=params(GATE_MIB),
         cost_estimate=cost(4 * total * features * columns, 4 * features * columns),
         name="gate_up",
     )(
@@ -346,9 +347,13 @@
     return (slot == row * capacity + rank).astype(F32).astype(BF16)
 
 
-def prepare_kernel(devices, capacity, first, after_ref, row_ref, w_hbm, held_ref, chosen_ref, sems):
-    base = half_base(devices, False, held_ref.shape[1])
-    copies = down_copies(w_hbm, base, held_ref, sems, first)
+def prepare_kernel(
+    devices, capacity, first, after_ref, row_ref, w_hbm, far_ref, near_ref, chosen_ref, far_sems, sems
+):
+    base = half_base(devices, False, far_ref.shape[1])
+    copies = down_copies(w_hbm, base, far_ref, far_sems, first)
+    base = quarter_base(devices, False, 0, near_ref.shape[1])
+    copies += down_copies(w_hbm, base, near_ref, sems, 0)
     for c in copies:
         c.start()
     nz, nx = grid_of(devices)
@@ -362,74 +367,49 @@
         c.wait()
 
 
-def prepare(after, row, down_weight, devices, capacity, first, rows):
-    wide = down_weight.shape[1] // 2
+def prepare(after, row, down_weight, devices, capacity, first, near_rows):
+    columns, features = down_weight.shape
     total = row.shape[1]
+    far_rows = columns - first
     return pl.pallas_call(
         functools.partial(prepare_kernel, devices, capacity, first),
         out_shape=(
-            pltpu.VMEM((rows, wide), BF16),
+            pltpu.VMEM((far_rows, features // 2), BF16),
+            pltpu.VMEM((near_rows, features // 4), BF16),
             jax.ShapeDtypeStruct((devices * 2 * capacity, total), BF16),
         ),
         in_specs=[ANY, VMEM, HBM],
-        out_specs=(VMEM, VMEM),
-        scratch_shapes=[pltpu.SemaphoreType.DMA((rows // TILE,))],
+        out_specs=(VMEM, VMEM, VMEM),
+        scratch_shapes=[
+            pltpu.SemaphoreType.DMA((far_rows // TILE,)),
+            pltpu.SemaphoreType.DMA((near_rows // TILE,)),
+        ],
         compiler_params=params(2),
-        cost_estimate=cost(0, rows * wide * 2),
+        cost_estimate=cost(0, (2 * far_rows + near_rows) * features // 2),
         name="prepare",
     )(after, row, in_hbm(down_weight))
 
 
-def multiply(hidden_ref, held_refs, quarter, total_ref, buf, copies):
-    wide = total_ref.shape[1]
-    start = 0
-    for held_ref in held_refs:
-        rows = held_ref.shape[0]
-        at = slice(quarter * wide, (quarter + 1) * wide)
-        weight = held_ref[...] if held_ref.shape[1] == wide else held_ref[:, at]
-        total_ref[...] += jnp.dot(
-            hidden_ref[:, start : start + rows], weight, preferred_element_type=F32
-        )
-        start += rows
-    if copies:
-        cut = (len(copies) + 1) // 2
-        for some in (slice(0, cut), slice(cut, len(copies))):
-            if not copies[some]:
-                continue
-            for c in copies[some]:
-                c.wait()
-            at = slice(some.start * TILE, some.stop * TILE)
-            total_ref[...] += jnp.dot(
-                hidden_ref[:, start + at.start : start + at.stop],
-                buf[at],
-                preferred_element_type=F32,
-            )
-
-
-def down_kernel(devices, far, quarter, held_count, next_base, next_first, streams, aheads, *refs):
+def down_kernel(devices, far, quarter, held_count, aheads, *refs):
     refs = list(refs)
-    take = lambda count: [refs.pop(0) for _ in range(count)]
+
+    def take(count):
+        return [refs.pop(0) for _ in range(count)]
+
     first_call = far and quarter == 0
     sources = take(2 if first_call else 1)
-    arrived_ref, chosen_ref = take(2) if not far else (None, None)
+    arrived_ref, chosen_ref = (None, None) if far else take(2)
     held_refs = take(held_count)
     (w_hbm,) = take(1)
     out_refs = take(1 if far else 2)
-    next_refs = take(1 if aheads else 0)
+    next_refs = take(len(aheads))
     (hidden_ref,) = take(1) if first_call else sources
     (total_ref,) = take(1)
     wide = total_ref.shape[1]
-    copies, ahead, buf = [], [], None
-    base = quarter_base(devices, far, quarter, wide)
-    if streams:
-        buf, sems = take(2)
-        copies = down_copies(w_hbm, base, buf, sems, sum(h.shape[0] for h in held_refs))
-    if aheads:
-        (next_sems,) = take(1)
-        ahead = down_copies(
-            w_hbm, quarter_base(devices, *next_base, wide), next_refs[0], next_sems, next_first
-        )
-    for c in copies + ahead:
+    ahead = []
+    for (their, start, _), ref, sems in zip(aheads, next_refs, take(len(aheads))):
+        ahead += down_copies(w_hbm, quarter_base(devices, False, their, wide), ref, sems, start)
+    for c in ahead:
         c.start()
     if first_call:
         own_ref, other_ref = sources
@@ -440,7 +420,14 @@
         total_ref[...] = jnp.zeros_like(total_ref)
     else:
         total_ref[...] = arrived_ref[...].astype(F32)
-    multiply(hidden_ref, held_refs, quarter, total_ref, buf, copies)
+    start = 0
+    for held_ref in held_refs:
+        stop = start + held_ref.shape[0]
+        at = slice(quarter * wide, (quarter + 1) * wide) if far else slice(None)
+        total_ref[...] += jnp.dot(
+            hidden_ref[:, start:stop], held_ref[:, at], preferred_element_type=F32
+        )
+        start = stop
     rounded = total_ref[...].astype(BF16)
     if far:
         out_refs[0][...] = rounded
@@ -453,38 +440,25 @@
         c.wait()
 
 
-def down(sources, held, down_weight, devices, far, quarter, ahead=None):
+def down(sources, held, down_weight, devices, far, quarter, aheads=()):
     total = sources[0].shape[-2]
     columns, features = down_weight.shape
     wide = features // 4
-    streams = columns - sum(h.shape[0] for h in held)
-    next_base, next_first, aheads = ahead or (None, 0, 0)
-    first_call = far and quarter == 0
     if far:
         out_shape = [jax.ShapeDtypeStruct((total, wide), BF16)]
     else:
         out_shape = [jax.ShapeDtypeStruct((sources[2].shape[0] // 2, wide), BF16)] * 2
-    if aheads:
-        out_shape.append(pltpu.VMEM((aheads, wide), BF16))
-    if first_call:
+    out_shape += [pltpu.VMEM((rows, wide), BF16) for _, _, rows in aheads]
+    if far and quarter == 0:
         out_shape.append(jax.ShapeDtypeStruct((total, columns), BF16))
-    scratch = [pltpu.VMEM((total, wide), F32)]
-    if streams:
-        scratch += [
-            pltpu.VMEM((streams, wide), BF16),
-            pltpu.SemaphoreType.DMA((streams // TILE,)),
-        ]
-    if aheads:
-        scratch.append(pltpu.SemaphoreType.DMA((aheads // TILE,)))
-    return pl.pallas_call(
-        functools.partial(
-            down_kernel, devices, far, quarter, len(held), next_base, next_first, streams, aheads
-        ),
+    return pl.pallas_call(
+        functools.partial(down_kernel, devices, far, quarter, len(held), aheads),
         out_shape=tuple(out_shape),
         in_specs=[VMEM] * (len(sources) + len(held)) + [HBM],
         out_specs=tuple(VMEM for _ in out_shape),
-        scratch_shapes=scratch,
-        compiler_params=params(10),
+        scratch_shapes=[pltpu.VMEM((total, wide), F32)]
+        + [pltpu.SemaphoreType.DMA((rows // TILE,)) for _, _, rows in aheads],
+        compiler_params=params(6),
         cost_estimate=COST,
         name="down_far" if far else "down_near",
     )(*sources, *(in_vmem(h) for h in held), in_hbm(down_weight))
@@ -613,7 +587,7 @@
     nz, nx = grid_of(devices)
     capacity = cache_keys.shape[0]
     columns, features = down_weight.shape
-    fits = nz == 4 and nx == 2 and columns % TILE == 0 and features % (8 * BAND) == 0
+    fits = nz == 4 and nx == 2 and columns % TILE == 0 and features == 16 * BAND
     mixed_rows, *held = attend(
         queries,
         cache_keys,
@@ -621,62 +595,64 @@
         lengths,
         residual,
         (gate_weight, up_weight) if fits else (),
-        1 if fits else 0,
+        3 * BAND if fits else 0,
     )
     if not fits:
         return plain(mixed_rows, target, gate_weight, up_weight, down_weight, devices)
 
     two = lax.ppermute(mixed_rows, AXIS, swap_z(devices, 2))
-    held.append(load_band(mixed_rows, gate_weight, up_weight, 1))
+    held.append(load_rows(mixed_rows, gate_weight, up_weight, 3 * BAND, 2 * BAND))
     a = pack(mixed_rows, two, held[-1])
     b = lax.ppermute(a, AXIS, swap_x(devices))
     c = lax.ppermute(a, AXIS, swap_z(devices, 1))
-    held.append(load_band(a, gate_weight, up_weight, 2))
+    held.append(load_rows(a, gate_weight, up_weight, 5 * BAND, 2 * BAND))
     c = hold(c, held[-1])
     d = lax.ppermute(c, AXIS, swap_x(devices))
-    held.append(load_band(c, gate_weight, up_weight, 3))
+    held.append(load_rows(c, gate_weight, up_weight, 7 * BAND, 2 * BAND))
     tiles = columns // TILE
-    early, middle = 3 * tiles // 13 * TILE, 5 * tiles // 13 * TILE
+    far_cut = 11 * tiles // 13 * TILE
+    first = 6 * tiles // 13 * TILE
+    cut = 2 * tiles // 13 * TILE, 8 * tiles // 13 * TILE
     part, rows, far_a = gate_up(
-        (a, b, c, d), gate_weight, up_weight, down_weight, held, devices, early
+        (a, b, c, d), gate_weight, up_weight, down_weight, held, devices, far_cut
     )
     other = lax.ppermute(part, "ffn", [(0, 1), (1, 0)])
-    far_b, chosen = prepare(
-        part, target.reshape(1, -1), down_weight, devices, capacity, early, middle
-    )
-
-    first = early + middle
-    far, far_c, hidden = down(
+    far_b, near_a, chosen = prepare(
+        part, target.reshape(1, -1), down_weight, devices, capacity, far_cut, first
+    )
+    held_far = far_a, far_b
+
+    far, near_b, near_c, hidden = down(
         (part, other),
-        (far_a, far_b),
+        held_far,
         down_weight,
         devices,
         True,
         0,
-        ((True, 1), first, columns - first),
+        ((0, first, columns - first), (1, 0, cut[0])),
     )
     arrived = [lax.ppermute(far, AXIS, swap_x(devices))]
-    far, near_a = down(
-        (hidden,),
-        (far_a, far_b, far_c),
+    far, near_d = down(
+        (hidden,), held_far, down_weight, devices, True, 1, ((1, cut[0], cut[1] - cut[0]),)
+    )
+    arrived.append(lax.ppermute(far, AXIS, swap_x(devices)))
+    keep_a, send_a, near_e = down(
+        (hidden, arrived[0], chosen),
+        (near_a, near_b),
         down_weight,
         devices,
-        True,
-        1,
-        ((False, 0), 0, 9 * tiles // 13 * TILE),
-    )
-    arrived.append(lax.ppermute(far, AXIS, swap_x(devices)))
+        False,
+        0,
+        ((1, cut[1], columns - cut[1]),),
+    )
+    came_a = lax.ppermute(send_a, AXIS, swap_z(devices, 1))
+    keep_b, send_b = down(
+        (hidden, arrived[1], chosen), (near_c, near_d, near_e), down_weight, devices, False, 1
+    )
+    came_b = lax.ppermute(send_b, AXIS, swap_z(devices, 1))
     own, came = [], []
-    for quarter in range(2):
-        sources = (hidden, arrived[quarter], chosen)
-        if quarter == 0:
-            ahead = ((False, 1), 0, 5 * tiles // 13 * TILE)
-            keep, send, near_b = down(
-                sources, (near_a,), down_weight, devices, False, 0, ahead
-            )
-        else:
-            keep, send = down(sources, (near_b,), down_weight, devices, False, 1)
-        mine, send = add(keep, lax.ppermute(send, AXIS, swap_z(devices, 1)))
+    for keep, arrived in ((keep_a, came_a), (keep_b, came_b)):
+        mine, send = add(keep, arrived)
         own.append(mine)
         came.append(lax.ppermute(send, AXIS, swap_z(devices, 2)))
     keep, send = finish(chosen, rows, own, came, devices)

time: 70.8 us -> 73.6 us (1.040)
  waiting for transfers between devices: 9.63 us -> 11.6 us
  Pallas kernels: 41.6 us -> 43.2 us
    pallas_call x1, Pallas kernels: 12.2 us -> 14.3 us  [gate_up(): pl.pallas_call(functools.partial(gate_up_kernel, devices, len(held)), out...]
    ppermute x1, waiting for transfers between devices: 2.59 us -> 4.22 us  [local(): return join(keep, lax.ppermute(send, AXIS, swap_x(devices)), devices)]
    ppermute x1, starting transfers between devices: 1.74 us -> 0.11 us  [local(): return join(keep, lax.ppermute(send, AXIS, swap_x(devices)), devices)]
    pallas_call x4, Pallas kernels: 12.6 us -> 11.1 us  [down(): pl.pallas_call(functools.partial(down_kernel, devices, far, quarter, len(...]
    ppermute x2, starting transfers between devices: 5.27 us -> 6.26 us  [local(): came.append(lax.ppermute(send, AXIS, swap_z(devices, 2)))]
    pallas_call x4, Pallas kernels: 13.3 us -> 14.3 us  [the longest x3 9.08 us: load_rows(): pl.pallas_call(functools.partial(load_kernel, first), out_shape=pltpu.VME...]
  transfers between devices with their start and end apart: 12 -> 12, of which waited for: 7 -> 7; matrix products, arithmetic and copies ran while one was open for 0% -> 0% of each run, Pallas kernels for 30% -> 26%
where the time goes in v7:
time: 73.6 us; the launch traced here: 73.4 us
  Pallas kernels  43.2 us (59%)
  starting transfers between devices  18.5 us (25%)
  waiting for transfers between devices  11.6 us (16%)
    pallas_call x1, Pallas kernels, gate_up(): pl.pallas_call(functools.partial(gate_up_kernel, devices, len(held)), out...  14.3 us
    pallas_call x4, Pallas kernels, down(): pl.pallas_call(functools.partial(down_kernel, devices, far, quarter, len(...  11.1 us
    pallas_call x3, Pallas kernels, load_rows(): pl.pallas_call(functools.partial(load_kernel, first), out_shape=pltpu.VME...  9.08 us
    ppermute x2, starting transfers between devices, local(): came.append(lax.ppermute(send, AXIS, swap_z(devices, 2)))  6.26 us
    pallas_call x1, Pallas kernels, attend(): pl.pallas_call(functools.partial(attend_kernel, kv, ahead), out_shape=(ja...  5.21 us
    ppermute x1, waiting for transfers between devices, local(): return join(keep, lax.ppermute(send, AXIS, swap_x(devices)), devices)  4.22 us
    ppermute x1, starting transfers between devices, local(): two = lax.ppermute(mixed_rows, AXIS, swap_z(devices, 2))  4.1 us
    ppermute x2, waiting for transfers between devices, local(): came.append(lax.ppermute(send, AXIS, swap_z(devices, 2)))  3.33 us
  transfers between devices with their start and end apart: 12, of which 7 were waited for; matrix products, arithmetic and copies ran while one was open for 0% of the time, Pallas kernels for 26%

profile of v7, /device:TPU:0, one launch (start us, length us, event | category | flops | bytes accessed | tf_op | source)
XLA Modules:
  0.0 73.4 jit_solution(461886223876196713)
XLA Ops:
  0.0 5.2 %attention.1 = (bf16[8,4096]{1,0:T(8,128)(2,1)S(1)}, bf16[2,768,3328]{2,1,0:T(8,128)(2,1)S(1)}) custom-call(s32[8]{0:T(128)} %lengths.1, bf16[8,32,128]{2,1,0:T(8,128)(2,1)} %q_hbm.1, bf16[8,256,128]{2,1,0:T(8,128)(2,1)} %bitcast.4, bf16[8,256,128]{2,1,0:T(8,128)(2,1)} %bitcast.5, bf16[8,4096]{1,0:T(8,128)(2,1)} %res_ref.1, bf16[4096,3328]{1,0:T(8,128)(2,1)} %refs_4_.2, ...), custom_call_target="tpu_custom_call" | custom-call | flops 33554432 | bytes 1048576 | tf_op jit(solution)/shard_map/attention/pallas_call | solution.py:118
  5.2 4.1 %collective-permute-start = (bf16[8,4096]{1,0:T(8,128)(2,1)S(1)}, bf16[8,4096]{1,0:T(8,128)(2,1)S(1)}, u32[]{:S(2)}, u32[]{:S(2)}) collective-permute-start(bf16[8,4096]{1,0:T(8,128)(2,1)S(1)} %get-tuple-element.30.after_ref.a_ref), channel_id=1, source_target_pairs={{0,8},{2,10},{4,12},{6,14},{8,0},{10,2},{12,4},{14,6},{1,9},{3,11}... | collective-permute-start | bytes 196616 | tf_op jit(solution)/shard_map/ppermute | solution.py:603
  9.3 3.0 %load_rows.3.after_ref.refs_8_ = bf16[2,512,3328]{2,1,0:T(8,128)(2,1)S(1)} custom-call(bf16[8,4096]{1,0:T(8,128)(2,1)S(1)} %get-tuple-element.30.after_ref.a_ref, bf16[4096,3328]{1,0:T(8,128)(2,1)} %refs_4_.2, bf16[4096,3328]{1,0:T(8,128)(2,1)} %refs_5_.2), custom_call_target="tpu_custom_call" | custom-call | bytes 6815744 | tf_op jit(solution)/shard_map/load_rows/pallas_call | solution.py:168
  13.0 1.0 %collective-permute-start.2 = (bf16[2,8,4096]{2,1,0:T(8,128)(2,1)S(1)}, bf16[2,8,4096]{2,1,0:T(8,128)(2,1)S(1)}, u32[]{:S(2)}, u32[]{:S(2)}) collective-permute-start(bf16[2,8,4096]{2,1,0:T(8,128)(2,1)S(1)} %pack.1.after_ref.refs_0_), channel_id=1, source_target_pairs={{0,4},{2,6},{4,0},{6,2},{8,12},{10,14},{12,8},{14,10},{1,5},{3,7},... | collective-permute-start | bytes 393224 | tf_op jit(solution)/shard_map/ppermute | solution.py:607
  14.0 1.5 %collective-permute-start.1 = (bf16[2,8,4096]{2,1,0:T(8,128)(2,1)S(1)}, bf16[2,8,4096]{2,1,0:T(8,128)(2,1)S(1)}, u32[]{:S(2)}, u32[]{:S(2)}) collective-permute-start(bf16[2,8,4096]{2,1,0:T(8,128)(2,1)S(1)} %pack.1.after_ref.refs_0_), channel_id=1, source_target_pairs={{0,2},{2,0},{4,6},{6,4},{8,10},{10,8},{12,14},{14,12},{1,3},{3,1},... | collective-permute-start | bytes 393224 | tf_op jit(solution)/shard_map/ppermute | solution.py:606
  15.5 3.0 %load_rows.4.after_ref.refs_9_ = bf16[2,512,3328]{2,1,0:T(8,128)(2,1)S(1)} custom-call(bf16[2,8,4096]{2,1,0:T(8,128)(2,1)S(1)} %pack.1.after_ref.refs_0_, bf16[4096,3328]{1,0:T(8,128)(2,1)} %refs_4_.2, bf16[4096,3328]{1,0:T(8,128)(2,1)} %refs_5_.2), custom_call_target="tpu_custom_call" | custom-call | bytes 6815744 | tf_op jit(solution)/shard_map/load_rows/pallas_call | solution.py:168
  18.6 1.1 %collective-permute-start.3 = (bf16[2,8,4096]{2,1,0:T(8,128)(2,1)S(1)}, bf16[2,8,4096]{2,1,0:T(8,128)(2,1)S(1)}, u32[]{:S(2)}, u32[]{:S(2)}) collective-permute-start(bf16[2,8,4096]{2,1,0:T(8,128)(2,1)S(1)} %hold.1.after_ref.refs_2_), channel_id=1, source_target_pairs={{0,2},{2,0},{4,6},{6,4},{8,10},{10,8},{12,14},{14,12},{1,3},{3,1},... | collective-permute-start | bytes 393224 | tf_op jit(solution)/shard_map/ppermute | solution.py:610
  19.7 3.0 %load_rows.5.refs_10_ = bf16[2,512,3328]{2,1,0:T(8,128)(2,1)S(1)} custom-call(bf16[2,8,4096]{2,1,0:T(8,128)(2,1)S(1)} %hold.1.after_ref.refs_2_, bf16[4096,3328]{1,0:T(8,128)(2,1)} %refs_4_.2, bf16[4096,3328]{1,0:T(8,128)(2,1)} %refs_5_.2), custom_call_target="tpu_custom_call" | custom-call | bytes 6815744 | tf_op jit(solution)/shard_map/load_rows/pallas_call | solution.py:168
  22.8 0.8 %collective-permute-done.3.refs_3_ = bf16[2,8,4096]{2,1,0:T(8,128)(2,1)S(1)} collective-permute-done((bf16[2,8,4096]{2,1,0:T(8,128)(2,1)S(1)}, bf16[2,8,4096]{2,1,0:T(8,128)(2,1)S(1)}, u32[]{:S(2)}, u32[]{:S(2)}) %collective-permute-start.3) | collective-permute-done | bytes 131104 | tf_op jit(solution)/shard_map/ppermute | solution.py:610
  23.6 14.3 %gate_up.1 = (bf16[2,64,3328]{2,1,0:T(8,128)(2,1)S(1)}, bf16[64,4096]{1,0:T(8,128)(2,1)S(1)}, bf16[2816,2048]{1,0:T(8,128)(2,1)S(1)}) custom-call(bf16[2,8,4096]{2,1,0:T(8,128)(2,1)S(1)} %pack.1.after_ref.refs_0_, bf16[2,8,4096]{2,1,0:T(8,128)(2,1)S(1)} %collective-permute-done.1.refs_1_, bf16[2,8,4096]{2,1,0:T(8,128)(2,1)S(1)} %hold.1.after_ref.refs_2_, ...), custom_call_target="tpu_custom_call" | custom-call | flops 3489660928 | bytes 54525952 | tf_op jit(solution)/shard_map/gate_up/pallas_call | solution.py:287
  38.0 2.6 %prepare.1 = (bf16[512,2048]{1,0:T(8,128)(2,1)S(1)}, bf16[1536,1024]{1,0:T(8,128)(2,1)S(1)}, bf16[128,64]{1,0:T(8,128)(2,1)S(1)}) custom-call(bf16[2,64,3328]{2,1,0:T(8,128)(2,1)S(1)} %get-tuple-element.32.after_ref.refs_0_, s32[1,64]{1,0:T(1,128)S(1)} %bitcast.3, bf16[3328,4096]{1,0:T(8,128)(2,1)} %refs_6_.3), custom_call_target="tpu_custom_call" | custom-call | bytes 5242880 | tf_op jit(solution)/shard_map/prepare/pallas_call | solution.py:374
  40.6 3.6 %down_far.2 = (bf16[64,1024]{1,0:T(8,128)(2,1)S(1)}, bf16[1792,1024]{1,0:T(8,128)(2,1)S(1)}, bf16[512,1024]{1,0:T(8,128)(2,1)S(1)}, bf16[64,3328]{1,0:T(8,128)(2,1)S(1)}) custom-call(bf16[2,64,3328]{2,1,0:T(8,128)(2,1)S(1)} %get-tuple-element.32.after_ref.refs_0_, bf16[2,64,3328]{2,1,0:T(8,128)(2,1)S(1)} %collective-permute-done.4.refs_1_, ...), custom_call_target="tpu_custom_call" | custom-call | bytes 1024 | tf_op jit(solution)/shard_map/down_far/pallas_call | solution.py:454
  44.1 1.1 %collective-permute-start.5 = (bf16[64,1024]{1,0:T(8,128)(2,1)S(1)}, bf16[64,1024]{1,0:T(8,128)(2,1)S(1)}, u32[]{:S(2)}, u32[]{:S(2)}) collective-permute-start(bf16[64,1024]{1,0:T(8,128)(2,1)S(1)} %get-tuple-element.38), channel_id=1, source_target_pairs={{0,2},{2,0},{4,6},{6,4},{8,10},{10,8},{12,14},{14,12},{1,3},{3,1},... | collective-permute-start | bytes 393224 | tf_op jit(solution)/shard_map/ppermute | solution.py:634
  45.3 3.1 %down_far.3 = (bf16[64,1024]{1,0:T(8,128)(2,1)S(1)}, bf16[1536,1024]{1,0:T(8,128)(2,1)S(1)}) custom-call(bf16[64,3328]{1,0:T(8,128)(2,1)S(1)} %get-tuple-element.37.refs_0_, bf16[2816,2048]{1,0:T(8,128)(2,1)S(1)} %get-tuple-element.35.refs_2_.refs_1_, bf16[512,2048]{1,0:T(8,128)(2,1)S(1)} %get-tuple-element.36.refs_3_.refs_2_, bf16[3328,4096]{1,0:T(8,128)(2,1)} %refs_6_.3), custom_call_target="tpu_custom_call" | custom-call | bytes 1024 | tf_op jit(solution)/shard_map/down_far/pallas_call | solution.py:454
  48.3 1.0 %collective-permute-start.7 = (bf16[64,1024]{1,0:T(8,128)(2,1)S(1)}, bf16[64,1024]{1,0:T(8,128)(2,1)S(1)}, u32[]{:S(2)}, u32[]{:S(2)}) collective-permute-start(bf16[64,1024]{1,0:T(8,128)(2,1)S(1)} %get-tuple-element.44), channel_id=1, source_target_pairs={{0,2},{2,0},{4,6},{6,4},{8,10},{10,8},{12,14},{14,12},{1,3},{3,1},... | collective-permute-start | bytes 393224 | tf_op jit(solution)/shard_map/ppermute | solution.py:638
  50.1 3.1 %down_near.2 = (bf16[64,1024]{1,0:T(8,128)(2,1)S(1)}, bf16[64,1024]{1,0:T(8,128)(2,1)S(1)}, bf16[1280,1024]{1,0:T(8,128)(2,1)S(1)}) custom-call(bf16[64,3328]{1,0:T(8,128)(2,1)S(1)} %get-tuple-element.37.refs_0_, bf16[64,1024]{1,0:T(8,128)(2,1)S(1)} %collective-permute-done.5.refs_1_, bf16[128,64]{1,0:T(8,128)(2,1)S(1)} %get-tuple-element.33.refs_2_.chosen_ref, ...), custom_call_target="tpu_custom_call" | custom-call | bytes 1024 | tf_op jit(solution)/shard_map/down_near/pallas_call | solution.py:454
  53.2 1.3 %collective-permute-start.6 = (bf16[64,1024]{1,0:T(8,128)(2,1)S(1)}, bf16[64,1024]{1,0:T(8,128)(2,1)S(1)}, u32[]{:S(2)}, u32[]{:S(2)}) collective-permute-start(bf16[64,1024]{1,0:T(8,128)(2,1)S(1)} %get-tuple-element.42), channel_id=1, source_target_pairs={{0,4},{2,6},{4,0},{6,2},{8,12},{10,14},{12,8},{14,10},{1,5},{3,7},... | collective-permute-start | bytes 393224 | tf_op jit(solution)/shard_map/ppermute | solution.py:648
  54.5 1.5 %down_near.3 = (bf16[64,1024]{1,0:T(8,128)(2,1)S(1)}, bf16[64,1024]{1,0:T(8,128)(2,1)S(1)}) custom-call(bf16[64,3328]{1,0:T(8,128)(2,1)S(1)} %get-tuple-element.37.refs_0_, bf16[64,1024]{1,0:T(8,128)(2,1)S(1)} %collective-permute-done.7.refs_1_, bf16[128,64]{1,0:T(8,128)(2,1)S(1)} %get-tuple-element.33.refs_2_.chosen_ref, ...), custom_call_target="tpu_custom_call" | custom-call | bytes 1024 | tf_op jit(solution)/shard_map/down_near/pallas_call | solution.py:454
  56.0 0.8 %collective-permute-start.8 = (bf16[64,1024]{1,0:T(8,128)(2,1)S(1)}, bf16[64,1024]{1,0:T(8,128)(2,1)S(1)}, u32[]{:S(2)}, u32[]{:S(2)}) collective-permute-start(bf16[64,1024]{1,0:T(8,128)(2,1)S(1)} %get-tuple-element.49), channel_id=1, source_target_pairs={{0,4},{2,6},{4,0},{6,2},{8,12},{10,14},{12,8},{14,10},{1,5},{3,7},... | collective-permute-start | bytes 393224 | tf_op jit(solution)/shard_map/ppermute | solution.py:652
  56.8 1.8 %collective-permute-done.6.came_ref = bf16[64,1024]{1,0:T(8,128)(2,1)S(1)} collective-permute-done((bf16[64,1024]{1,0:T(8,128)(2,1)S(1)}, bf16[64,1024]{1,0:T(8,128)(2,1)S(1)}, u32[]{:S(2)}, u32[]{:S(2)}) %collective-permute-start.6) | collective-permute-done | bytes 131104 | tf_op jit(solution)/shard_map/ppermute | solution.py:648
  58.6 3.9 %collective-permute-start.9 = (bf16[32,1024]{1,0:T(8,128)(2,1)S(1)}, bf16[32,1024]{1,0:T(8,128)(2,1)S(1)}, u32[]{:S(2)}, u32[]{:S(2)}) collective-permute-start(bf16[32,1024]{1,0:T(8,128)(2,1)S(1)} %get-tuple-element.51), channel_id=1, source_target_pairs={{0,8},{2,10},{4,12},{6,14},{8,0},{10,2},{12,4},{14,6},{1,9},{3,11}... | collective-permute-start | bytes 196616 | tf_op jit(solution)/shard_map/ppermute | solution.py:657
  62.5 2.4 %collective-permute-start.10 = (bf16[32,1024]{1,0:T(8,128)(2,1)S(1)}, bf16[32,1024]{1,0:T(8,128)(2,1)S(1)}, u32[]{:S(2)}, u32[]{:S(2)}) collective-permute-start(bf16[32,1024]{1,0:T(8,128)(2,1)S(1)} %get-tuple-element.52), channel_id=1, source_target_pairs={{0,8},{2,10},{4,12},{6,14},{8,0},{10,2},{12,4},{14,6},{1,9},{3,11}... | collective-permute-start | bytes 196616 | tf_op jit(solution)/shard_map/ppermute | solution.py:657
  64.9 2.6 %collective-permute-done.9.refs_2_ = bf16[32,1024]{1,0:T(8,128)(2,1)S(1)} collective-permute-done((bf16[32,1024]{1,0:T(8,128)(2,1)S(1)}, bf16[32,1024]{1,0:T(8,128)(2,1)S(1)}, u32[]{:S(2)}, u32[]{:S(2)}) %collective-permute-start.9) | collective-permute-done | bytes 65568 | tf_op jit(solution)/shard_map/ppermute | solution.py:657
  68.5 4.2 %collective-permute-done.11.other_ref = bf16[16,2048]{1,0:T(8,128)(2,1)S(1)} collective-permute-done((bf16[16,2048]{1,0:T(8,128)(2,1)S(1)}, bf16[16,2048]{1,0:T(8,128)(2,1)S(1)}, u32[]{:S(2)}, u32[]{:S(2)}) %collective-permute-start.11) | collective-permute-done | bytes 65568 | tf_op jit(solution)/shard_map/ppermute | solution.py:659
  (18 shorter events, 3.2 us)
Async XLA Ops:
  5.2 7.8 %collective-permute-start = (bf16[8,4096]{1,0:T(8,128)(2,1)S(1)}, bf16[8,4096]{1,0:T(8,128)(2,1)S(1)}, u32[]{:S(2)}, u32[]{:S(2)}) collective-permute-start(bf16[8,4096]{1,0:T(8,128)(2,1)S(1)} %get-tuple-element.30.after_ref.a_ref), channel_id=1, source_target_pairs={{0,8},{2,10},{4,12},{6,14},{8,0},{10,2},{12,4},{14,6},{1,9},{3,11}... | collective-permute-start | bytes 196616 | tf_op jit(solution)/shard_map/ppermute | solution.py:603
  13.0 5.6 %collective-permute-start.2 = (bf16[2,8,4096]{2,1,0:T(8,128)(2,1)S(1)}, bf16[2,8,4096]{2,1,0:T(8,128)(2,1)S(1)}, u32[]{:S(2)}, u32[]{:S(2)}) collective-permute-start(bf16[2,8,4096]{2,1,0:T(8,128)(2,1)S(1)} %pack.1.after_ref.refs_0_), channel_id=1, source_target_pairs={{0,4},{2,6},{4,0},{6,2},{8,12},{10,14},{12,8},{14,10},{1,5},{3,7},... | collective-permute-start | bytes 393224 | tf_op jit(solution)/shard_map/ppermute | solution.py:607
  14.0 8.7 %collective-permute-start.1 = (bf16[2,8,4096]{2,1,0:T(8,128)(2,1)S(1)}, bf16[2,8,4096]{2,1,0:T(8,128)(2,1)S(1)}, u32[]{:S(2)}, u32[]{:S(2)}) collective-permute-start(bf16[2,8,4096]{2,1,0:T(8,128)(2,1)S(1)} %pack.1.after_ref.refs_0_), channel_id=1, source_target_pairs={{0,2},{2,0},{4,6},{6,4},{8,10},{10,8},{12,14},{14,12},{1,3},{3,1},... | collective-permute-start | bytes 393224 | tf_op jit(solution)/shard_map/ppermute | solution.py:606
  18.6 5.0 %collective-permute-start.3 = (bf16[2,8,4096]{2,1,0:T(8,128)(2,1)S(1)}, bf16[2,8,4096]{2,1,0:T(8,128)(2,1)S(1)}, u32[]{:S(2)}, u32[]{:S(2)}) collective-permute-start(bf16[2,8,4096]{2,1,0:T(8,128)(2,1)S(1)} %hold.1.after_ref.refs_2_), channel_id=1, source_target_pairs={{0,2},{2,0},{4,6},{6,4},{8,10},{10,8},{12,14},{14,12},{1,3},{3,1},... | collective-permute-start | bytes 393224 | tf_op jit(solution)/shard_map/ppermute | solution.py:610
  23.6 14.4 %copy-start = (s32[64,1]{0,1:T(1,128)S(1)}, s32[64,1]{0,1:T(1,128)}, u32[]{:S(2)}) copy-start(s32[64,1]{0,1:T(1,128)} %param.14) | copy-start | bytes 772
  37.9 2.7 %collective-permute-start.4 = (bf16[2,64,3328]{2,1,0:T(8,128)(2,1)S(1)}, bf16[2,64,3328]{2,1,0:T(8,128)(2,1)S(1)}, u32[]{:S(2)}, u32[]{:S(2)}) collective-permute-start(bf16[2,64,3328]{2,1,0:T(8,128)(2,1)S(1)} %get-tuple-element.32.after_ref.refs_0_), channel_id=1, source_target_pairs={{0,1},{1,0},{2,3},{3,2},{4,5},{5,4},{6,7},{7,6},{8,9},{9,8},{10,11... | collective-permute-start | bytes 2555912 | tf_op jit(solution)/shard_map/ppermute | solution.py:619
  44.1 6.0 %collective-permute-start.5 = (bf16[64,1024]{1,0:T(8,128)(2,1)S(1)}, bf16[64,1024]{1,0:T(8,128)(2,1)S(1)}, u32[]{:S(2)}, u32[]{:S(2)}) collective-permute-start(bf16[64,1024]{1,0:T(8,128)(2,1)S(1)} %get-tuple-element.38), channel_id=1, source_target_pairs={{0,2},{2,0},{4,6},{6,4},{8,10},{10,8},{12,14},{14,12},{1,3},{3,1},... | collective-permute-start | bytes 393224 | tf_op jit(solution)/shard_map/ppermute | solution.py:634
  48.3 6.1 %collective-permute-start.7 = (bf16[64,1024]{1,0:T(8,128)(2,1)S(1)}, bf16[64,1024]{1,0:T(8,128)(2,1)S(1)}, u32[]{:S(2)}, u32[]{:S(2)}) collective-permute-start(bf16[64,1024]{1,0:T(8,128)(2,1)S(1)} %get-tuple-element.44), channel_id=1, source_target_pairs={{0,2},{2,0},{4,6},{6,4},{8,10},{10,8},{12,14},{14,12},{1,3},{3,1},... | collective-permute-start | bytes 393224 | tf_op jit(solution)/shard_map/ppermute | solution.py:638
  53.2 5.4 %collective-permute-start.6 = (bf16[64,1024]{1,0:T(8,128)(2,1)S(1)}, bf16[64,1024]{1,0:T(8,128)(2,1)S(1)}, u32[]{:S(2)}, u32[]{:S(2)}) collective-permute-start(bf16[64,1024]{1,0:T(8,128)(2,1)S(1)} %get-tuple-element.42), channel_id=1, source_target_pairs={{0,4},{2,6},{4,0},{6,2},{8,12},{10,14},{12,8},{14,10},{1,5},{3,7},... | collective-permute-start | bytes 393224 | tf_op jit(solution)/shard_map/ppermute | solution.py:648
  56.0 6.5 %collective-permute-start.8 = (bf16[64,1024]{1,0:T(8,128)(2,1)S(1)}, bf16[64,1024]{1,0:T(8,128)(2,1)S(1)}, u32[]{:S(2)}, u32[]{:S(2)}) collective-permute-start(bf16[64,1024]{1,0:T(8,128)(2,1)S(1)} %get-tuple-element.49), channel_id=1, source_target_pairs={{0,4},{2,6},{4,0},{6,2},{8,12},{10,14},{12,8},{14,10},{1,5},{3,7},... | collective-permute-start | bytes 393224 | tf_op jit(solution)/shard_map/ppermute | solution.py:652
  58.6 8.9 %collective-permute-start.9 = (bf16[32,1024]{1,0:T(8,128)(2,1)S(1)}, bf16[32,1024]{1,0:T(8,128)(2,1)S(1)}, u32[]{:S(2)}, u32[]{:S(2)}) collective-permute-start(bf16[32,1024]{1,0:T(8,128)(2,1)S(1)} %get-tuple-element.51), channel_id=1, source_target_pairs={{0,8},{2,10},{4,12},{6,14},{8,0},{10,2},{12,4},{14,6},{1,9},{3,11}... | collective-permute-start | bytes 196616 | tf_op jit(solution)/shard_map/ppermute | solution.py:657
  62.5 5.7 %collective-permute-start.10 = (bf16[32,1024]{1,0:T(8,128)(2,1)S(1)}, bf16[32,1024]{1,0:T(8,128)(2,1)S(1)}, u32[]{:S(2)}, u32[]{:S(2)}) collective-permute-start(bf16[32,1024]{1,0:T(8,128)(2,1)S(1)} %get-tuple-element.52), channel_id=1, source_target_pairs={{0,8},{2,10},{4,12},{6,14},{8,0},{10,2},{12,4},{14,6},{1,9},{3,11}... | collective-permute-start | bytes 196616 | tf_op jit(solution)/shard_map/ppermute | solution.py:657
  68.4 4.3 %collective-permute-start.11 = (bf16[16,2048]{1,0:T(8,128)(2,1)S(1)}, bf16[16,2048]{1,0:T(8,128)(2,1)S(1)}, u32[]{:S(2)}, u32[]{:S(2)}) collective-permute-start(bf16[16,2048]{1,0:T(8,128)(2,1)S(1)} %get-tuple-element.54), channel_id=1, source_target_pairs={{0,2},{2,0},{4,6},{6,4},{8,10},{10,8},{12,14},{14,12},{1,3},{3,1},... | collective-permute-start | bytes 196616 | tf_op jit(solution)/shard_map/ppermute | solution.py:659

commit v8 on v7

--- a/solution.py
+++ b/solution.py
@@ -229,11 +229,16 @@
     for j in range(min(slots, left)):
         for c in streamed(j):
             c.start()
-    ahead = down_copies(
-        w_hbm, half_base(devices, False, far_ref.shape[1]), far_ref, far_sems, 0
-    )
-    for c in ahead:
-        c.start()
+    far_tiles = far_ref.shape[0] // TILE
+    per_step = -(-far_tiles // left)
+    far_base = half_base(devices, False, far_ref.shape[1])
+
+    def far_copy(i):
+        at = tile_at(i)
+        return pltpu.make_async_copy(
+            w_hbm.at[at, pl.ds(far_base, far_ref.shape[1])], far_ref.at[at], far_sems.at[i]
+        )
+
     me = lax.axis_index(AXIS)
     my_z, my_x = me // nx, me % nx
     per = a_ref.shape[1]
@@ -272,12 +277,18 @@
             for c in streamed(j + slots):
                 c.start()
 
+        for k in range(per_step):
+
+            @pl.when(j * per_step + k < far_tiles)
+            def _(k=k):
+                far_copy(j * per_step + k).start()
+
         return 0
 
     lax.fori_loop(0, left, step, 0)
     part_ref[...] = total_ref[...].astype(BF16)
-    for c in ahead:
-        c.wait()
+    for i in range(far_tiles):
+        far_copy(i).wait()
 
 
 def gate_up(blocks, gate_weight, up_weight, down_weight, held, devices, ahead):
@@ -413,21 +424,28 @@
         c.start()
     if first_call:
         own_ref, other_ref = sources
-        gate = own_ref[0].astype(F32) + other_ref[0].astype(F32)
-        up = own_ref[1].astype(F32) + other_ref[1].astype(F32)
-        hidden_ref[...] = (gate / (1.0 + jnp.exp(-gate)) * up).astype(BF16)
+
+        @pl.when(lax.axis_index(AXIS) >= 0)
+        def _():
+            gate = own_ref[0].astype(F32) + other_ref[0].astype(F32)
+            up = own_ref[1].astype(F32) + other_ref[1].astype(F32)
+            hidden_ref[...] = (gate / (1.0 + jnp.exp(-gate)) * up).astype(BF16)
+
     if far:
         total_ref[...] = jnp.zeros_like(total_ref)
     else:
         total_ref[...] = arrived_ref[...].astype(F32)
-    start = 0
-    for held_ref in held_refs:
-        stop = start + held_ref.shape[0]
-        at = slice(quarter * wide, (quarter + 1) * wide) if far else slice(None)
-        total_ref[...] += jnp.dot(
-            hidden_ref[:, start:stop], held_ref[:, at], preferred_element_type=F32
-        )
-        start = stop
+    @pl.when(lax.axis_index(AXIS) >= 0)
+    def _():
+        start = 0
+        for held_ref in held_refs:
+            stop = start + held_ref.shape[0]
+            at = slice(quarter * wide, (quarter + 1) * wide) if far else slice(None)
+            total_ref[...] += jnp.dot(
+                hidden_ref[:, start:stop], held_ref[:, at], preferred_element_type=F32
+            )
+            start = stop
+
     rounded = total_ref[...].astype(BF16)
     if far:
         out_refs[0][...] = rounded
@@ -595,20 +613,20 @@
         lengths,
         residual,
         (gate_weight, up_weight) if fits else (),
-        3 * BAND if fits else 0,
+        2 * BAND if fits else 0,
     )
     if not fits:
         return plain(mixed_rows, target, gate_weight, up_weight, down_weight, devices)
 
     two = lax.ppermute(mixed_rows, AXIS, swap_z(devices, 2))
-    held.append(load_rows(mixed_rows, gate_weight, up_weight, 3 * BAND, 2 * BAND))
+    held.append(load_rows(mixed_rows, gate_weight, up_weight, 2 * BAND, 2 * BAND))
     a = pack(mixed_rows, two, held[-1])
     b = lax.ppermute(a, AXIS, swap_x(devices))
     c = lax.ppermute(a, AXIS, swap_z(devices, 1))
-    held.append(load_rows(a, gate_weight, up_weight, 5 * BAND, 2 * BAND))
+    held.append(load_rows(a, gate_weight, up_weight, 4 * BAND, 2 * BAND))
     c = hold(c, held[-1])
     d = lax.ppermute(c, AXIS, swap_x(devices))
-    held.append(load_rows(c, gate_weight, up_weight, 7 * BAND, 2 * BAND))
+    held.append(load_rows(c, gate_weight, up_weight, 6 * BAND, 2 * BAND))
     tiles = columns // TILE
     far_cut = 11 * tiles // 13 * TILE
     first = 6 * tiles // 13 * TILE

time: 73.6 us -> 69.4 us (0.943)
  Pallas kernels: 43.2 us -> 37.8 us
    pallas_call x4, Pallas kernels: 11.1 us -> 7.57 us  [down(): pl.pallas_call(functools.partial(down_kernel, devices, far, quarter, len(...]
    ppermute x1, waiting for transfers between devices: 0.74 us -> 1.88 us  [local(): arrived = [lax.ppermute(far, AXIS, swap_x(devices))]]
    pallas_call x1, Pallas kernels: 5.21 us -> 4.22 us  [attend(): pl.pallas_call(functools.partial(attend_kernel, kv, ahead), out_shape=(ja...]
    pallas_call x1, Pallas kernels: 14.3 us -> 13.4 us  [gate_up(): pl.pallas_call(functools.partial(gate_up_kernel, devices, len(held)), out...]
  transfers between devices with their start and end apart: 12 -> 12, of which waited for: 7 -> 7; matrix products, arithmetic and copies ran while one was open for 0% -> 0% of each run, Pallas kernels for 26% -> 24%
where the time goes in v8:
time: 69.4 us; the launch traced here: 69.2 us
  Pallas kernels  37.8 us (54%)
  starting transfers between devices  19 us (27%)
  waiting for transfers between devices  12.2 us (18%)
    pallas_call x1, Pallas kernels, gate_up(): pl.pallas_call(functools.partial(gate_up_kernel, devices, len(held)), out...  13.4 us
    pallas_call x3, Pallas kernels, load_rows(): pl.pallas_call(functools.partial(load_kernel, first), out_shape=pltpu.VME...  9.08 us
    pallas_call x4, Pallas kernels, down(): pl.pallas_call(functools.partial(down_kernel, devices, far, quarter, len(...  7.57 us
    ppermute x2, starting transfers between devices, local(): came.append(lax.ppermute(send, AXIS, swap_z(devices, 2)))  6.56 us
    ppermute x1, waiting for transfers between devices, local(): return join(keep, lax.ppermute(send, AXIS, swap_x(devices)), devices)  4.25 us
    pallas_call x1, Pallas kernels, attend(): pl.pallas_call(functools.partial(attend_kernel, kv, ahead), out_shape=(ja...  4.22 us
    ppermute x1, starting transfers between devices, local(): two = lax.ppermute(mixed_rows, AXIS, swap_z(devices, 2))  4.1 us
    ppermute x2, waiting for transfers between devices, local(): came.append(lax.ppermute(send, AXIS, swap_z(devices, 2)))  3.1 us
  transfers between devices with their start and end apart: 12, of which 7 were waited for; matrix products, arithmetic and copies ran while one was open for 0% of the time, Pallas kernels for 24%

profile of v8, /device:TPU:0, one launch (start us, length us, event | category | flops | bytes accessed | tf_op | source)
XLA Modules:
  0.0 69.2 jit_solution(7822647459024993184)
XLA Ops:
  0.0 4.2 %attention.1 = (bf16[8,4096]{1,0:T(8,128)(2,1)S(1)}, bf16[2,512,3328]{2,1,0:T(8,128)(2,1)S(1)}) custom-call(s32[8]{0:T(128)} %lengths.1, bf16[8,32,128]{2,1,0:T(8,128)(2,1)} %q_hbm.1, bf16[8,256,128]{2,1,0:T(8,128)(2,1)} %bitcast.4, bf16[8,256,128]{2,1,0:T(8,128)(2,1)} %bitcast.5, bf16[8,4096]{1,0:T(8,128)(2,1)} %res_ref.1, bf16[4096,3328]{1,0:T(8,128)(2,1)} %refs_4_.2, ...), custom_call_target="tpu_custom_call" | custom-call | flops 33554432 | bytes 1048576 | tf_op jit(solution)/shard_map/attention/pallas_call | solution.py:118
  4.2 4.1 %collective-permute-start = (bf16[8,4096]{1,0:T(8,128)(2,1)S(1)}, bf16[8,4096]{1,0:T(8,128)(2,1)S(1)}, u32[]{:S(2)}, u32[]{:S(2)}) collective-permute-start(bf16[8,4096]{1,0:T(8,128)(2,1)S(1)} %get-tuple-element.30.after_ref.a_ref), channel_id=1, source_target_pairs={{0,8},{2,10},{4,12},{6,14},{8,0},{10,2},{12,4},{14,6},{1,9},{3,11}... | collective-permute-start | bytes 196616 | tf_op jit(solution)/shard_map/ppermute | solution.py:621
  8.3 3.0 %load_rows.3.after_ref.refs_8_ = bf16[2,512,3328]{2,1,0:T(8,128)(2,1)S(1)} custom-call(bf16[8,4096]{1,0:T(8,128)(2,1)S(1)} %get-tuple-element.30.after_ref.a_ref, bf16[4096,3328]{1,0:T(8,128)(2,1)} %refs_4_.2, bf16[4096,3328]{1,0:T(8,128)(2,1)} %refs_5_.2), custom_call_target="tpu_custom_call" | custom-call | bytes 6815744 | tf_op jit(solution)/shard_map/load_rows/pallas_call | solution.py:168
  12.0 1.0 %collective-permute-start.2 = (bf16[2,8,4096]{2,1,0:T(8,128)(2,1)S(1)}, bf16[2,8,4096]{2,1,0:T(8,128)(2,1)S(1)}, u32[]{:S(2)}, u32[]{:S(2)}) collective-permute-start(bf16[2,8,4096]{2,1,0:T(8,128)(2,1)S(1)} %pack.1.after_ref.refs_0_), channel_id=1, source_target_pairs={{0,4},{2,6},{4,0},{6,2},{8,12},{10,14},{12,8},{14,10},{1,5},{3,7},... | collective-permute-start | bytes 393224 | tf_op jit(solution)/shard_map/ppermute | solution.py:625
  13.0 1.5 %collective-permute-start.1 = (bf16[2,8,4096]{2,1,0:T(8,128)(2,1)S(1)}, bf16[2,8,4096]{2,1,0:T(8,128)(2,1)S(1)}, u32[]{:S(2)}, u32[]{:S(2)}) collective-permute-start(bf16[2,8,4096]{2,1,0:T(8,128)(2,1)S(1)} %pack.1.after_ref.refs_0_), channel_id=1, source_target_pairs={{0,2},{2,0},{4,6},{6,4},{8,10},{10,8},{12,14},{14,12},{1,3},{3,1},... | collective-permute-start | bytes 393224 | tf_op jit(solution)/shard_map/ppermute | solution.py:624
  14.5 3.0 %load_rows.4.after_ref.refs_9_ = bf16[2,512,3328]{2,1,0:T(8,128)(2,1)S(1)} custom-call(bf16[2,8,4096]{2,1,0:T(8,128)(2,1)S(1)} %pack.1.after_ref.refs_0_, bf16[4096,3328]{1,0:T(8,128)(2,1)} %refs_4_.2, bf16[4096,3328]{1,0:T(8,128)(2,1)} %refs_5_.2), custom_call_target="tpu_custom_call" | custom-call | bytes 6815744 | tf_op jit(solution)/shard_map/load_rows/pallas_call | solution.py:168
  17.6 1.1 %collective-permute-start.3 = (bf16[2,8,4096]{2,1,0:T(8,128)(2,1)S(1)}, bf16[2,8,4096]{2,1,0:T(8,128)(2,1)S(1)}, u32[]{:S(2)}, u32[]{:S(2)}) collective-permute-start(bf16[2,8,4096]{2,1,0:T(8,128)(2,1)S(1)} %hold.1.after_ref.refs_2_), channel_id=1, source_target_pairs={{0,2},{2,0},{4,6},{6,4},{8,10},{10,8},{12,14},{14,12},{1,3},{3,1},... | collective-permute-start | bytes 393224 | tf_op jit(solution)/shard_map/ppermute | solution.py:628
  18.7 3.0 %load_rows.5.refs_10_ = bf16[2,512,3328]{2,1,0:T(8,128)(2,1)S(1)} custom-call(bf16[2,8,4096]{2,1,0:T(8,128)(2,1)S(1)} %hold.1.after_ref.refs_2_, bf16[4096,3328]{1,0:T(8,128)(2,1)} %refs_4_.2, bf16[4096,3328]{1,0:T(8,128)(2,1)} %refs_5_.2), custom_call_target="tpu_custom_call" | custom-call | bytes 6815744 | tf_op jit(solution)/shard_map/load_rows/pallas_call | solution.py:168
  22.6 13.4 %gate_up.1 = (bf16[2,64,3328]{2,1,0:T(8,128)(2,1)S(1)}, bf16[64,4096]{1,0:T(8,128)(2,1)S(1)}, bf16[2816,2048]{1,0:T(8,128)(2,1)S(1)}) custom-call(bf16[2,8,4096]{2,1,0:T(8,128)(2,1)S(1)} %pack.1.after_ref.refs_0_, bf16[2,8,4096]{2,1,0:T(8,128)(2,1)S(1)} %collective-permute-done.1.refs_1_, bf16[2,8,4096]{2,1,0:T(8,128)(2,1)S(1)} %hold.1.after_ref.refs_2_, ...), custom_call_target="tpu_custom_call" | custom-call | flops 3489660928 | bytes 54525952 | tf_op jit(solution)/shard_map/gate_up/pallas_call | solution.py:298
  36.2 2.6 %prepare.1 = (bf16[512,2048]{1,0:T(8,128)(2,1)S(1)}, bf16[1536,1024]{1,0:T(8,128)(2,1)S(1)}, bf16[128,64]{1,0:T(8,128)(2,1)S(1)}) custom-call(bf16[2,64,3328]{2,1,0:T(8,128)(2,1)S(1)} %get-tuple-element.32.after_ref.refs_0_, s32[1,64]{1,0:T(1,128)S(1)} %bitcast.3, bf16[3328,4096]{1,0:T(8,128)(2,1)} %refs_6_.3), custom_call_target="tpu_custom_call" | custom-call | bytes 5242880 | tf_op jit(solution)/shard_map/prepare/pallas_call | solution.py:385
  38.7 2.4 %down_far.2 = (bf16[64,1024]{1,0:T(8,128)(2,1)S(1)}, bf16[1792,1024]{1,0:T(8,128)(2,1)S(1)}, bf16[512,1024]{1,0:T(8,128)(2,1)S(1)}, bf16[64,3328]{1,0:T(8,128)(2,1)S(1)}) custom-call(bf16[2,64,3328]{2,1,0:T(8,128)(2,1)S(1)} %get-tuple-element.32.after_ref.refs_0_, bf16[2,64,3328]{2,1,0:T(8,128)(2,1)S(1)} %collective-permute-done.4.refs_1_, ...), custom_call_target="tpu_custom_call" | custom-call | bytes 1024 | tf_op jit(solution)/shard_map/down_far/pallas_call | solution.py:472
  41.2 1.1 %collective-permute-start.5 = (bf16[64,1024]{1,0:T(8,128)(2,1)S(1)}, bf16[64,1024]{1,0:T(8,128)(2,1)S(1)}, u32[]{:S(2)}, u32[]{:S(2)}) collective-permute-start(bf16[64,1024]{1,0:T(8,128)(2,1)S(1)} %get-tuple-element.38), channel_id=1, source_target_pairs={{0,2},{2,0},{4,6},{6,4},{8,10},{10,8},{12,14},{14,12},{1,3},{3,1},... | collective-permute-start | bytes 393224 | tf_op jit(solution)/shard_map/ppermute | solution.py:652
  42.3 1.9 %down_far.3 = (bf16[64,1024]{1,0:T(8,128)(2,1)S(1)}, bf16[1536,1024]{1,0:T(8,128)(2,1)S(1)}) custom-call(bf16[64,3328]{1,0:T(8,128)(2,1)S(1)} %get-tuple-element.37.refs_0_, bf16[2816,2048]{1,0:T(8,128)(2,1)S(1)} %get-tuple-element.35.refs_2_.refs_1_, bf16[512,2048]{1,0:T(8,128)(2,1)S(1)} %get-tuple-element.36.refs_3_.refs_2_, bf16[3328,4096]{1,0:T(8,128)(2,1)} %refs_6_.3), custom_call_target="tpu_custom_call" | custom-call | bytes 1024 | tf_op jit(solution)/shard_map/down_far/pallas_call | solution.py:472
  44.2 1.0 %collective-permute-start.7 = (bf16[64,1024]{1,0:T(8,128)(2,1)S(1)}, bf16[64,1024]{1,0:T(8,128)(2,1)S(1)}, u32[]{:S(2)}, u32[]{:S(2)}) collective-permute-start(bf16[64,1024]{1,0:T(8,128)(2,1)S(1)} %get-tuple-element.44), channel_id=1, source_target_pairs={{0,2},{2,0},{4,6},{6,4},{8,10},{10,8},{12,14},{14,12},{1,3},{3,1},... | collective-permute-start | bytes 393224 | tf_op jit(solution)/shard_map/ppermute | solution.py:656
  45.2 1.9 %collective-permute-done.5.refs_1_ = bf16[64,1024]{1,0:T(8,128)(2,1)S(1)} collective-permute-done((bf16[64,1024]{1,0:T(8,128)(2,1)S(1)}, bf16[64,1024]{1,0:T(8,128)(2,1)S(1)}, u32[]{:S(2)}, u32[]{:S(2)}) %collective-permute-start.5) | collective-permute-done | bytes 131104 | tf_op jit(solution)/shard_map/ppermute | solution.py:652
  47.1 1.7 %down_near.2 = (bf16[64,1024]{1,0:T(8,128)(2,1)S(1)}, bf16[64,1024]{1,0:T(8,128)(2,1)S(1)}, bf16[1280,1024]{1,0:T(8,128)(2,1)S(1)}) custom-call(bf16[64,3328]{1,0:T(8,128)(2,1)S(1)} %get-tuple-element.37.refs_0_, bf16[64,1024]{1,0:T(8,128)(2,1)S(1)} %collective-permute-done.5.refs_1_, bf16[128,64]{1,0:T(8,128)(2,1)S(1)} %get-tuple-element.33.refs_2_.chosen_ref, ...), custom_call_target="tpu_custom_call" | custom-call | bytes 1024 | tf_op jit(solution)/shard_map/down_near/pallas_call | solution.py:472
  48.9 1.7 %collective-permute-start.6 = (bf16[64,1024]{1,0:T(8,128)(2,1)S(1)}, bf16[64,1024]{1,0:T(8,128)(2,1)S(1)}, u32[]{:S(2)}, u32[]{:S(2)}) collective-permute-start(bf16[64,1024]{1,0:T(8,128)(2,1)S(1)} %get-tuple-element.42), channel_id=1, source_target_pairs={{0,4},{2,6},{4,0},{6,2},{8,12},{10,14},{12,8},{14,10},{1,5},{3,7},... | collective-permute-start | bytes 393224 | tf_op jit(solution)/shard_map/ppermute | solution.py:666
  50.6 1.5 %down_near.3 = (bf16[64,1024]{1,0:T(8,128)(2,1)S(1)}, bf16[64,1024]{1,0:T(8,128)(2,1)S(1)}) custom-call(bf16[64,3328]{1,0:T(8,128)(2,1)S(1)} %get-tuple-element.37.refs_0_, bf16[64,1024]{1,0:T(8,128)(2,1)S(1)} %collective-permute-done.7.refs_1_, bf16[128,64]{1,0:T(8,128)(2,1)S(1)} %get-tuple-element.33.refs_2_.chosen_ref, ...), custom_call_target="tpu_custom_call" | custom-call | bytes 1024 | tf_op jit(solution)/shard_map/down_near/pallas_call | solution.py:472
  52.8 1.5 %collective-permute-done.6.came_ref = bf16[64,1024]{1,0:T(8,128)(2,1)S(1)} collective-permute-done((bf16[64,1024]{1,0:T(8,128)(2,1)S(1)}, bf16[64,1024]{1,0:T(8,128)(2,1)S(1)}, u32[]{:S(2)}, u32[]{:S(2)}) %collective-permute-start.6) | collective-permute-done | bytes 131104 | tf_op jit(solution)/shard_map/ppermute | solution.py:666
  54.3 3.6 %collective-permute-start.9 = (bf16[32,1024]{1,0:T(8,128)(2,1)S(1)}, bf16[32,1024]{1,0:T(8,128)(2,1)S(1)}, u32[]{:S(2)}, u32[]{:S(2)}) collective-permute-start(bf16[32,1024]{1,0:T(8,128)(2,1)S(1)} %get-tuple-element.51), channel_id=1, source_target_pairs={{0,8},{2,10},{4,12},{6,14},{8,0},{10,2},{12,4},{14,6},{1,9},{3,11}... | collective-permute-start | bytes 196616 | tf_op jit(solution)/shard_map/ppermute | solution.py:675
  57.9 3.0 %collective-permute-start.10 = (bf16[32,1024]{1,0:T(8,128)(2,1)S(1)}, bf16[32,1024]{1,0:T(8,128)(2,1)S(1)}, u32[]{:S(2)}, u32[]{:S(2)}) collective-permute-start(bf16[32,1024]{1,0:T(8,128)(2,1)S(1)} %get-tuple-element.52), channel_id=1, source_target_pairs={{0,8},{2,10},{4,12},{6,14},{8,0},{10,2},{12,4},{14,6},{1,9},{3,11}... | collective-permute-start | bytes 196616 | tf_op jit(solution)/shard_map/ppermute | solution.py:675
  60.9 1.2 %collective-permute-done.9.refs_2_ = bf16[32,1024]{1,0:T(8,128)(2,1)S(1)} collective-permute-done((bf16[32,1024]{1,0:T(8,128)(2,1)S(1)}, bf16[32,1024]{1,0:T(8,128)(2,1)S(1)}, u32[]{:S(2)}, u32[]{:S(2)}) %collective-permute-start.9) | collective-permute-done | bytes 65568 | tf_op jit(solution)/shard_map/ppermute | solution.py:675
  62.0 1.9 %collective-permute-done.10.refs_3_ = bf16[32,1024]{1,0:T(8,128)(2,1)S(1)} collective-permute-done((bf16[32,1024]{1,0:T(8,128)(2,1)S(1)}, bf16[32,1024]{1,0:T(8,128)(2,1)S(1)}, u32[]{:S(2)}, u32[]{:S(2)}) %collective-permute-start.10) | collective-permute-done | bytes 65568 | tf_op jit(solution)/shard_map/ppermute | solution.py:675
  64.2 4.3 %collective-permute-done.11.other_ref = bf16[16,2048]{1,0:T(8,128)(2,1)S(1)} collective-permute-done((bf16[16,2048]{1,0:T(8,128)(2,1)S(1)}, bf16[16,2048]{1,0:T(8,128)(2,1)S(1)}, u32[]{:S(2)}, u32[]{:S(2)}) %collective-permute-start.11) | collective-permute-done | bytes 65568 | tf_op jit(solution)/shard_map/ppermute | solution.py:677
  (18 shorter events, 3.2 us)
Async XLA Ops:
  4.2 7.8 %collective-permute-start = (bf16[8,4096]{1,0:T(8,128)(2,1)S(1)}, bf16[8,4096]{1,0:T(8,128)(2,1)S(1)}, u32[]{:S(2)}, u32[]{:S(2)}) collective-permute-start(bf16[8,4096]{1,0:T(8,128)(2,1)S(1)} %get-tuple-element.30.after_ref.a_ref), channel_id=1, source_target_pairs={{0,8},{2,10},{4,12},{6,14},{8,0},{10,2},{12,4},{14,6},{1,9},{3,11}... | collective-permute-start | bytes 196616 | tf_op jit(solution)/shard_map/ppermute | solution.py:621
  12.0 5.6 %collective-permute-start.2 = (bf16[2,8,4096]{2,1,0:T(8,128)(2,1)S(1)}, bf16[2,8,4096]{2,1,0:T(8,128)(2,1)S(1)}, u32[]{:S(2)}, u32[]{:S(2)}) collective-permute-start(bf16[2,8,4096]{2,1,0:T(8,128)(2,1)S(1)} %pack.1.after_ref.refs_0_), channel_id=1, source_target_pairs={{0,4},{2,6},{4,0},{6,2},{8,12},{10,14},{12,8},{14,10},{1,5},{3,7},... | collective-permute-start | bytes 393224 | tf_op jit(solution)/shard_map/ppermute | solution.py:625
  13.0 8.7 %collective-permute-start.1 = (bf16[2,8,4096]{2,1,0:T(8,128)(2,1)S(1)}, bf16[2,8,4096]{2,1,0:T(8,128)(2,1)S(1)}, u32[]{:S(2)}, u32[]{:S(2)}) collective-permute-start(bf16[2,8,4096]{2,1,0:T(8,128)(2,1)S(1)} %pack.1.after_ref.refs_0_), channel_id=1, source_target_pairs={{0,2},{2,0},{4,6},{6,4},{8,10},{10,8},{12,14},{14,12},{1,3},{3,1},... | collective-permute-start | bytes 393224 | tf_op jit(solution)/shard_map/ppermute | solution.py:624
  17.6 5.0 %collective-permute-start.3 = (bf16[2,8,4096]{2,1,0:T(8,128)(2,1)S(1)}, bf16[2,8,4096]{2,1,0:T(8,128)(2,1)S(1)}, u32[]{:S(2)}, u32[]{:S(2)}) collective-permute-start(bf16[2,8,4096]{2,1,0:T(8,128)(2,1)S(1)} %hold.1.after_ref.refs_2_), channel_id=1, source_target_pairs={{0,2},{2,0},{4,6},{6,4},{8,10},{10,8},{12,14},{14,12},{1,3},{3,1},... | collective-permute-start | bytes 393224 | tf_op jit(solution)/shard_map/ppermute | solution.py:628
  22.6 13.5 %copy-start = (s32[64,1]{0,1:T(1,128)S(1)}, s32[64,1]{0,1:T(1,128)}, u32[]{:S(2)}) copy-start(s32[64,1]{0,1:T(1,128)} %param.14) | copy-start | bytes 772
  36.1 2.7 %collective-permute-start.4 = (bf16[2,64,3328]{2,1,0:T(8,128)(2,1)S(1)}, bf16[2,64,3328]{2,1,0:T(8,128)(2,1)S(1)}, u32[]{:S(2)}, u32[]{:S(2)}) collective-permute-start(bf16[2,64,3328]{2,1,0:T(8,128)(2,1)S(1)} %get-tuple-element.32.after_ref.refs_0_), channel_id=1, source_target_pairs={{0,1},{1,0},{2,3},{3,2},{4,5},{5,4},{6,7},{7,6},{8,9},{9,8},{10,11... | collective-permute-start | bytes 2555912 | tf_op jit(solution)/shard_map/ppermute | solution.py:637
  41.2 6.0 %collective-permute-start.5 = (bf16[64,1024]{1,0:T(8,128)(2,1)S(1)}, bf16[64,1024]{1,0:T(8,128)(2,1)S(1)}, u32[]{:S(2)}, u32[]{:S(2)}) collective-permute-start(bf16[64,1024]{1,0:T(8,128)(2,1)S(1)} %get-tuple-element.38), channel_id=1, source_target_pairs={{0,2},{2,0},{4,6},{6,4},{8,10},{10,8},{12,14},{14,12},{1,3},{3,1},... | collective-permute-start | bytes 393224 | tf_op jit(solution)/shard_map/ppermute | solution.py:652
  44.2 6.4 %collective-permute-start.7 = (bf16[64,1024]{1,0:T(8,128)(2,1)S(1)}, bf16[64,1024]{1,0:T(8,128)(2,1)S(1)}, u32[]{:S(2)}, u32[]{:S(2)}) collective-permute-start(bf16[64,1024]{1,0:T(8,128)(2,1)S(1)} %get-tuple-element.44), channel_id=1, source_target_pairs={{0,2},{2,0},{4,6},{6,4},{8,10},{10,8},{12,14},{14,12},{1,3},{3,1},... | collective-permute-start | bytes 393224 | tf_op jit(solution)/shard_map/ppermute | solution.py:656
  48.9 5.4 %collective-permute-start.6 = (bf16[64,1024]{1,0:T(8,128)(2,1)S(1)}, bf16[64,1024]{1,0:T(8,128)(2,1)S(1)}, u32[]{:S(2)}, u32[]{:S(2)}) collective-permute-start(bf16[64,1024]{1,0:T(8,128)(2,1)S(1)} %get-tuple-element.42), channel_id=1, source_target_pairs={{0,4},{2,6},{4,0},{6,2},{8,12},{10,14},{12,8},{14,10},{1,5},{3,7},... | collective-permute-start | bytes 393224 | tf_op jit(solution)/shard_map/ppermute | solution.py:666
  52.1 5.8 %collective-permute-start.8 = (bf16[64,1024]{1,0:T(8,128)(2,1)S(1)}, bf16[64,1024]{1,0:T(8,128)(2,1)S(1)}, u32[]{:S(2)}, u32[]{:S(2)}) collective-permute-start(bf16[64,1024]{1,0:T(8,128)(2,1)S(1)} %get-tuple-element.49), channel_id=1, source_target_pairs={{0,4},{2,6},{4,0},{6,2},{8,12},{10,14},{12,8},{14,10},{1,5},{3,7},... | collective-permute-start | bytes 393224 | tf_op jit(solution)/shard_map/ppermute | solution.py:670
  54.3 7.8 %collective-permute-start.9 = (bf16[32,1024]{1,0:T(8,128)(2,1)S(1)}, bf16[32,1024]{1,0:T(8,128)(2,1)S(1)}, u32[]{:S(2)}, u32[]{:S(2)}) collective-permute-start(bf16[32,1024]{1,0:T(8,128)(2,1)S(1)} %get-tuple-element.51), channel_id=1, source_target_pairs={{0,8},{2,10},{4,12},{6,14},{8,0},{10,2},{12,4},{14,6},{1,9},{3,11}... | collective-permute-start | bytes 196616 | tf_op jit(solution)/shard_map/ppermute | solution.py:675
  57.9 6.1 %collective-permute-start.10 = (bf16[32,1024]{1,0:T(8,128)(2,1)S(1)}, bf16[32,1024]{1,0:T(8,128)(2,1)S(1)}, u32[]{:S(2)}, u32[]{:S(2)}) collective-permute-start(bf16[32,1024]{1,0:T(8,128)(2,1)S(1)} %get-tuple-element.52), channel_id=1, source_target_pairs={{0,8},{2,10},{4,12},{6,14},{8,0},{10,2},{12,4},{14,6},{1,9},{3,11}... | collective-permute-start | bytes 196616 | tf_op jit(solution)/shard_map/ppermute | solution.py:675
  64.2 4.3 %collective-permute-start.11 = (bf16[16,2048]{1,0:T(8,128)(2,1)S(1)}, bf16[16,2048]{1,0:T(8,128)(2,1)S(1)}, u32[]{:S(2)}, u32[]{:S(2)}) collective-permute-start(bf16[16,2048]{1,0:T(8,128)(2,1)S(1)} %get-tuple-element.54), channel_id=1, source_target_pairs={{0,2},{2,0},{4,6},{6,4},{8,10},{10,8},{12,14},{14,12},{1,3},{3,1},... | collective-permute-start | bytes 196616 | tf_op jit(solution)/shard_map/ppermute | solution.py:677

commit v9 on v8

--- a/solution.py
+++ b/solution.py
@@ -52,22 +52,17 @@
     return [(z * nx + x, (z ^ bits) * nx + x) for z in range(nz) for x in range(nx)]
 
 
-def swap_x(devices):
+def swap_x(devices, bits=0):
     nz, nx = grid_of(devices)
-    return [(z * nx + x, z * nx + (x ^ 1)) for z in range(nz) for x in range(nx)]
+    return [(z * nx + x, (z ^ bits) * nx + (x ^ 1)) for z in range(nz) for x in range(nx)]
 
 
 COST = cost(0, 1024)
 
 
-def attend_kernel(kv, ahead, lengths, q_hbm, k_hbm, v_hbm, res_ref, *refs):
-    weights = ()
-    if ahead:
-        g_hbm, u_hbm, out_ref, held_ref, *refs, band_sems = refs
-        weights = band_copies(g_hbm, u_hbm, held_ref, band_sems, 0)
-    else:
-        out_ref, *refs = refs
-    att_ref, scores_ref, probs_ref, q_ref, k_ref, v_ref, sems = refs
+def attend_kernel(
+    kv, lengths, q_hbm, k_hbm, v_hbm, res_ref, up_hbm, out_ref, att_ref, scores_ref, probs_ref, q_ref, k_ref, v_ref, sems
+):
     rows, heads, dim = q_ref.shape
     span = k_ref.shape[1]
     per_group = heads // kv
@@ -77,8 +72,6 @@
     ]
     for load in loads:
         load.start()
-    for c in weights:
-        c.start()
     column = lax.broadcasted_iota(jnp.int32, (heads, span), 1)
     head = lax.broadcasted_iota(jnp.int32, (heads, span), 0)
     right_group = (column % kv) == (head // per_group)
@@ -105,21 +98,17 @@
         lanes = slice(h * dim, (h + 1) * dim)
         mine = att_ref[pl.ds(h, rows, stride=heads), :]
         out_ref[:, lanes] = (res_ref[:, lanes].astype(F32) + mine).astype(BF16)
-    for c in weights:
-        c.wait()
-
-
-def attend(queries, cache_keys, stored_value_cache, lengths, residual, weights, ahead):
+
+
+def attend(queries, cache_keys, stored_value_cache, lengths, residual, up):
     rows, heads, dim = queries.shape
     kv = cache_keys.shape[2]
     span = cache_keys.shape[1] * kv
-    held = [pltpu.VMEM((2, ahead, w.shape[1]), BF16) for w in weights[:1]]
-    band_sems = [pltpu.SemaphoreType.DMA((2, ahead // BAND)) for _ in held]
-    return pl.pallas_call(
-        functools.partial(attend_kernel, kv, ahead),
-        out_shape=(jax.ShapeDtypeStruct((rows, heads * dim), BF16), *held),
-        in_specs=[SMEM, HBM, HBM, HBM, VMEM] + [HBM for _ in weights],
-        out_specs=(VMEM,) + tuple(VMEM for _ in held),
+    return pl.pallas_call(
+        functools.partial(attend_kernel, kv),
+        out_shape=jax.ShapeDtypeStruct((rows, heads * dim), BF16),
+        in_specs=[SMEM, HBM, HBM, HBM, VMEM, HBM],
+        out_specs=VMEM,
         scratch_shapes=[
             pltpu.VMEM((rows * heads, dim), F32),
             pltpu.VMEM((rows * heads, span), F32),
@@ -128,8 +117,7 @@
             pltpu.VMEM((rows, span, dim), BF16),
             pltpu.VMEM((rows, span, dim), BF16),
             pltpu.SemaphoreType.DMA((3,)),
-        ]
-        + band_sems,
+        ],
         compiler_params=params(8),
         cost_estimate=cost(rows * heads * span * dim * 4, rows * span * dim * 4),
         name="attention",
@@ -139,70 +127,30 @@
         in_hbm(cache_keys.reshape(rows, span, dim)),
         in_hbm(stored_value_cache.reshape(rows, span, dim)),
         in_hbm(residual),
-        *(in_hbm(w) for w in weights),
-    )
-
-
-def band_copies(g_hbm, u_hbm, held_ref, sems, first):
-    return [
-        pltpu.make_async_copy(
-            w.at[pl.ds(pl.multiple_of(first + i * BAND, BAND), BAND)],
-            held_ref.at[kind, pl.ds(i * BAND, BAND)],
-            sems.at[kind, i],
-        )
-        for kind, w in enumerate((g_hbm, u_hbm))
-        for i in range(held_ref.shape[1] // BAND)
-    ]
-
-
-def load_kernel(first, after_ref, g_hbm, u_hbm, held_ref, sems):
-    copies = band_copies(g_hbm, u_hbm, held_ref, sems, first)
-    for c in copies:
-        c.start()
-    for c in copies:
-        c.wait()
-
-
-def load_rows(after, gate_weight, up_weight, first, rows):
-    columns = gate_weight.shape[1]
-    return pl.pallas_call(
-        functools.partial(load_kernel, first),
-        out_shape=pltpu.VMEM((2, rows, columns), BF16),
-        in_specs=[ANY, HBM, HBM],
-        out_specs=VMEM,
-        scratch_shapes=[pltpu.SemaphoreType.DMA((2, rows // BAND))],
-        compiler_params=params(2),
-        cost_estimate=cost(0, 4 * rows * columns),
-        name="load_rows",
-    )(after, in_hbm(gate_weight), in_hbm(up_weight))
-
-
-def hold(array, after):
-    return pl.pallas_call(
-        lambda array_ref, after_ref, out_ref: None,
-        out_shape=jax.ShapeDtypeStruct(array.shape, array.dtype),
-        in_specs=[ANY, ANY],
-        out_specs=ANY,
-        input_output_aliases={0: 0},
-        compiler_params=params(2),
-        name="hold",
-    )(array, after)
-
-
-def pack_kernel(a_ref, b_ref, after_ref, out_ref):
-    out_ref[0] = a_ref[...]
-    out_ref[1] = b_ref[...]
-
-
-def pack(a, b, after):
+        in_hbm(up),
+    )
+
+
+def row_copy(w_hbm, held_ref, sem, first):
+    rows = pl.ds(pl.multiple_of(first, BAND), BAND)
+    return pltpu.make_async_copy(w_hbm.at[rows], held_ref, sem)
+
+
+def pack_kernel(*refs):
+    *block_refs, out_ref = refs
+    for i, ref in enumerate(block_refs):
+        out_ref[i] = ref[...]
+
+
+def pack(*blocks):
     return pl.pallas_call(
         pack_kernel,
-        out_shape=jax.ShapeDtypeStruct((2,) + a.shape, a.dtype),
-        in_specs=[VMEM, VMEM, ANY],
+        out_shape=jax.ShapeDtypeStruct((len(blocks),) + blocks[0].shape, BF16),
+        in_specs=[VMEM] * len(blocks),
         out_specs=VMEM,
         compiler_params=params(4),
         name="pack",
-    )(a, b, after)
+    )(*blocks)
 
 
 def tile_at(index):
@@ -211,24 +159,31 @@
 
 def gate_up_kernel(
     devices,
-    held,
-    *refs,
+    a_ref,
+    c_ref,
+    d_ref,
+    e_ref,
+    u_hbm,
+    w_hbm,
+    gate_ref,
+    part_ref,
+    rows_ref,
+    far_ref,
+    total_ref,
+    buf,
+    sems,
+    far_sems,
 ):
-    a_ref, b_ref, c_ref, d_ref, g_hbm, u_hbm, w_hbm = refs[:7]
-    held_refs = refs[7 : 7 + held]
-    part_ref, rows_ref, far_ref, total_ref, buf, sems, far_sems = refs[7 + held :]
     nx = grid_of(devices)[1]
     slots = buf.shape[0]
-    first = sum(ref.shape[1] for ref in held_refs)
-    left = (g_hbm.shape[0] - first) // BAND
+    left = u_hbm.shape[0] // BAND
 
     def streamed(j):
         slot = lax.rem(j, slots)
-        return band_copies(g_hbm, u_hbm, buf.at[slot], sems.at[slot], first + j * BAND)
+        return row_copy(u_hbm, buf.at[slot], sems.at[slot], j * BAND)
 
     for j in range(min(slots, left)):
-        for c in streamed(j):
-            c.start()
+        streamed(j).start()
     far_tiles = far_ref.shape[0] // TILE
     per_step = -(-far_tiles // left)
     far_base = half_base(devices, False, far_ref.shape[1])
@@ -242,13 +197,16 @@
     me = lax.axis_index(AXIS)
     my_z, my_x = me // nx, me % nx
     per = a_ref.shape[1]
-    for near, far, flip in ((a_ref, b_ref, 0), (c_ref, d_ref, 1)):
-        for i in range(2):
-            z = my_z ^ (flip + 2 * i)
-            here, there = near[i].astype(F32), far[i].astype(F32)
-            pair = [jnp.where(my_x == 0, here, there), jnp.where(my_x == 0, there, here)]
-            at = pl.ds(pl.multiple_of(z * (2 * per), 2 * per), 2 * per)
-            rows_ref[at, :] = jnp.concatenate(pair, axis=0).astype(BF16)
+    for bits, near, far in (
+        (0, a_ref[0], a_ref[2]),
+        (1, c_ref[0], c_ref[2]),
+        (2, a_ref[1], d_ref[...]),
+        (3, c_ref[1], e_ref[...]),
+    ):
+        here, there = near.astype(F32), far.astype(F32)
+        pair = [jnp.where(my_x == 0, here, there), jnp.where(my_x == 0, there, here)]
+        at = pl.ds(pl.multiple_of((my_z ^ bits) * (2 * per), 2 * per), 2 * per)
+        rows_ref[at, :] = jnp.concatenate(pair, axis=0).astype(BF16)
 
     def add(at, weight, kind):
         total_ref[kind] += jnp.dot(rows_ref[:, at], weight, preferred_element_type=F32)
@@ -256,26 +214,14 @@
     total_ref[...] = jnp.zeros_like(total_ref)
 
     def step(j, _):
-        start = 0
-        for number, held_ref in enumerate(held_refs):
-            stop = start + held_ref.shape[1]
-
-            @pl.when(j == number * left // held)
-            def _(start=start, stop=stop, held_ref=held_ref):
-                for kind in range(2):
-                    add(slice(start, stop), held_ref[kind], kind)
-
-            start = stop
-        slot = lax.rem(j, slots)
-        for kind, c in enumerate(streamed(j)):
-            c.wait()
-            at = pl.ds(pl.multiple_of(first + j * BAND, BAND), BAND)
-            add(at, buf[slot, kind], kind)
+        at = pl.ds(pl.multiple_of(j * BAND, BAND), BAND)
+        add(at, gate_ref[at, :], 0)
+        streamed(j).wait()
+        add(at, buf[lax.rem(j, slots)], 1)
 
         @pl.when(j + slots < left)
         def _():
-            for c in streamed(j + slots):
-                c.start()
+            streamed(j + slots).start()
 
         for k in range(per_step):
 
@@ -291,23 +237,23 @@
         far_copy(i).wait()
 
 
-def gate_up(blocks, gate_weight, up_weight, down_weight, held, devices, ahead):
+def gate_up(blocks, gate_weight, up_weight, down_weight, devices, ahead):
     total = devices * blocks[0].shape[1]
     features, columns = gate_weight.shape
-    slots = 2
-    return pl.pallas_call(
-        functools.partial(gate_up_kernel, devices, len(held)),
+    slots = 4
+    return pl.pallas_call(
+        functools.partial(gate_up_kernel, devices),
         out_shape=(
             jax.ShapeDtypeStruct((2, total, columns), BF16),
             jax.ShapeDtypeStruct((total, features), BF16),
             pltpu.VMEM((ahead, features // 2), BF16),
         ),
-        in_specs=[VMEM] * 4 + [HBM] * 3 + [VMEM] * len(held),
+        in_specs=[VMEM] * 4 + [HBM] * 2 + [VMEM],
         out_specs=(VMEM, VMEM, VMEM),
         scratch_shapes=[
             pltpu.VMEM((2, total, columns), F32),
-            pltpu.VMEM((slots, 2, BAND, columns), BF16),
-            pltpu.SemaphoreType.DMA((slots, 2, 1)),
+            pltpu.VMEM((slots, BAND, columns), BF16),
+            pltpu.SemaphoreType.DMA((slots,)),
             pltpu.SemaphoreType.DMA((ahead // TILE,)),
         ],
         compiler_params=params(GATE_MIB),
@@ -315,10 +261,9 @@
         name="gate_up",
     )(
         *blocks,
-        in_hbm(gate_weight),
         in_hbm(up_weight),
         in_hbm(down_weight),
-        *(in_vmem(h) for h in held),
+        in_vmem(gate_weight),
     )
 
 
@@ -606,33 +551,22 @@
     capacity = cache_keys.shape[0]
     columns, features = down_weight.shape
     fits = nz == 4 and nx == 2 and columns % TILE == 0 and features == 16 * BAND
-    mixed_rows, *held = attend(
-        queries,
-        cache_keys,
-        stored_value_cache,
-        lengths,
-        residual,
-        (gate_weight, up_weight) if fits else (),
-        2 * BAND if fits else 0,
-    )
+    mixed_rows = attend(queries, cache_keys, stored_value_cache, lengths, residual, up_weight)
     if not fits:
         return plain(mixed_rows, target, gate_weight, up_weight, down_weight, devices)
 
     two = lax.ppermute(mixed_rows, AXIS, swap_z(devices, 2))
-    held.append(load_rows(mixed_rows, gate_weight, up_weight, 2 * BAND, 2 * BAND))
-    a = pack(mixed_rows, two, held[-1])
-    b = lax.ppermute(a, AXIS, swap_x(devices))
+    side = lax.ppermute(mixed_rows, AXIS, swap_x(devices))
+    e = lax.ppermute(mixed_rows, AXIS, swap_x(devices, 3))
+    a = pack(mixed_rows, two, side)
     c = lax.ppermute(a, AXIS, swap_z(devices, 1))
-    held.append(load_rows(a, gate_weight, up_weight, 4 * BAND, 2 * BAND))
-    c = hold(c, held[-1])
-    d = lax.ppermute(c, AXIS, swap_x(devices))
-    held.append(load_rows(c, gate_weight, up_weight, 6 * BAND, 2 * BAND))
+    d = lax.ppermute(two, AXIS, swap_x(devices))
     tiles = columns // TILE
     far_cut = 11 * tiles // 13 * TILE
     first = 6 * tiles // 13 * TILE
     cut = 2 * tiles // 13 * TILE, 8 * tiles // 13 * TILE
     part, rows, far_a = gate_up(
-        (a, b, c, d), gate_weight, up_weight, down_weight, held, devices, far_cut
+        (a, c, d, e), gate_weight, up_weight, down_weight, devices, far_cut
     )
     other = lax.ppermute(part, "ffn", [(0, 1), (1, 0)])
     far_b, near_a, chosen = prepare(

time: 69.4 us -> 69.2 us (level)
  waiting for transfers between devices: 12.2 us -> 24.6 us
  Pallas kernels: 37.8 us -> 29.2 us
  starting transfers between devices: 19 us -> 15.1 us
    pallas_call x7 -> x3, Pallas kernels: 26.8 us -> 18.2 us  [the longest x1 15.2 us: gate_up(): pl.pallas_call(functools.partial(gate_up_kernel, devices), out_shape=(jax...]
    ppermute x2, starting transfers between devices: 6.56 us -> 0.99 us  [local(): came.append(lax.ppermute(send, AXIS, swap_z(devices, 2)))]
    ppermute x2 -> x3, waiting for transfers between devices: 0.85 us -> 6.13 us  [the longest x1 5.51 us: local(): e = lax.ppermute(mixed_rows, AXIS, swap_x(devices, 3))]
    ppermute x1, waiting for transfers between devices: 0.01 us -> 2.89 us  [local(): came_b = lax.ppermute(send_b, AXIS, swap_z(devices, 1))]
    ppermute x1, starting transfers between devices: 1.72 us -> 0.07 us  [local(): came_a = lax.ppermute(send_a, AXIS, swap_z(devices, 1))]
    ppermute x2, waiting for transfers between devices: 3.1 us -> 4.71 us  [local(): came.append(lax.ppermute(send, AXIS, swap_z(devices, 2)))]
    ppermute x2 -> x3, starting transfers between devices: 2.64 us -> 4.23 us  [the longest x1 2.2 us: local(): e = lax.ppermute(mixed_rows, AXIS, swap_x(devices, 3))]
    ppermute x1, waiting for transfers between devices: 0.62 us -> 2.16 us  [local(): two = lax.ppermute(mixed_rows, AXIS, swap_z(devices, 2))]
  transfers between devices with their start and end apart: 12 -> 13, of which waited for: 7 -> 10; matrix products, arithmetic and copies ran while one was open for 0% -> 0% of each run, Pallas kernels for 24% -> 11%
where the time goes in v9:
time: 69.2 us; the launch traced here: 69.1 us
  Pallas kernels  29.2 us (42%)
  waiting for transfers between devices  24.6 us (36%)
  starting transfers between devices  15.1 us (22%)
    pallas_call x1, Pallas kernels, gate_up(): pl.pallas_call(functools.partial(gate_up_kernel, devices), out_shape=(jax...  15.2 us
    pallas_call x4, Pallas kernels, down(): pl.pallas_call(functools.partial(down_kernel, devices, far, quarter, len(...  7.57 us
    ppermute x1, waiting for transfers between devices, local(): e = lax.ppermute(mixed_rows, AXIS, swap_x(devices, 3))  5.51 us
    ppermute x2, waiting for transfers between devices, local(): came.append(lax.ppermute(send, AXIS, swap_z(devices, 2)))  4.71 us
    ppermute x1, starting transfers between devices, local(): two = lax.ppermute(mixed_rows, AXIS, swap_z(devices, 2))  4.1 us
    ppermute x1, waiting for transfers between devices, local(): return join(keep, lax.ppermute(send, AXIS, swap_x(devices)), devices)  4 us
    pallas_call x1, Pallas kernels, attend(): pl.pallas_call(functools.partial(attend_kernel, kv), out_shape=jax.ShapeD...  3 us
    ppermute x1, waiting for transfers between devices, local(): came_b = lax.ppermute(send_b, AXIS, swap_z(devices, 1))  2.89 us
  transfers between devices with their start and end apart: 13, of which 10 were waited for; matrix products, arithmetic and copies ran while one was open for 0% of the time, Pallas kernels for 11%

profile of v9, /device:TPU:0, one launch (start us, length us, event | category | flops | bytes accessed | tf_op | source)
XLA Modules:
  0.0 69.1 jit_solution(1961128967040622432)
XLA Ops:
  0.0 3.0 %attention.1.refs_0_ = bf16[8,4096]{1,0:T(8,128)(2,1)S(1)} custom-call(s32[8]{0:T(128)} %lengths.1, bf16[8,32,128]{2,1,0:T(8,128)(2,1)} %q_hbm.1, bf16[8,256,128]{2,1,0:T(8,128)(2,1)} %bitcast.4, bf16[8,256,128]{2,1,0:T(8,128)(2,1)} %bitcast.5, bf16[8,4096]{1,0:T(8,128)(2,1)} %res_ref.1, bf16[4096,3328]{1,0:T(8,128)(2,1)} %u_hbm.1), custom_call_target="tpu_custom_call" | custom-call | flops 33554432 | bytes 1048576 | tf_op jit(solution)/shard_map/attention/pallas_call | solution.py:107
  3.0 4.1 %collective-permute-start = (bf16[8,4096]{1,0:T(8,128)(2,1)S(1)}, bf16[8,4096]{1,0:T(8,128)(2,1)S(1)}, u32[]{:S(2)}, u32[]{:S(2)}) collective-permute-start(bf16[8,4096]{1,0:T(8,128)(2,1)S(1)} %attention.1.refs_0_), channel_id=1, source_target_pairs={{0,8},{2,10},{4,12},{6,14},{8,0},{10,2},{12,4},{14,6},{1,9},{3,11}... | collective-permute-start | bytes 196616 | tf_op jit(solution)/shard_map/ppermute | solution.py:558
  7.1 1.5 %collective-permute-start.1 = (bf16[8,4096]{1,0:T(8,128)(2,1)S(1)}, bf16[8,4096]{1,0:T(8,128)(2,1)S(1)}, u32[]{:S(2)}, u32[]{:S(2)}) collective-permute-start(bf16[8,4096]{1,0:T(8,128)(2,1)S(1)} %attention.1.refs_0_), channel_id=1, source_target_pairs={{0,2},{2,0},{4,6},{6,4},{8,10},{10,8},{12,14},{14,12},{1,3},{3,1},... | collective-permute-start | bytes 196616 | tf_op jit(solution)/shard_map/ppermute | solution.py:559
  8.6 2.2 %collective-permute-done.refs_1_ = bf16[8,4096]{1,0:T(8,128)(2,1)S(1)} collective-permute-done((bf16[8,4096]{1,0:T(8,128)(2,1)S(1)}, bf16[8,4096]{1,0:T(8,128)(2,1)S(1)}, u32[]{:S(2)}, u32[]{:S(2)}) %collective-permute-start) | collective-permute-done | bytes 65568 | tf_op jit(solution)/shard_map/ppermute | solution.py:558
  10.8 0.6 collective-permute-done.1.refs_2_
  11.4 1.6 %collective-permute-start.2 = (bf16[3,8,4096]{2,1,0:T(8,128)(2,1)S(1)}, bf16[3,8,4096]{2,1,0:T(8,128)(2,1)S(1)}, u32[]{:S(2)}, u32[]{:S(2)}) collective-permute-start(bf16[3,8,4096]{2,1,0:T(8,128)(2,1)S(1)} %pack.1.a_ref), channel_id=1, source_target_pairs={{0,4},{2,6},{4,0},{6,2},{8,12},{10,14},{12,8},{14,10},{1,5},{3,7},... | collective-permute-start | bytes 589832 | tf_op jit(solution)/shard_map/ppermute | solution.py:562
  13.0 2.2 %collective-permute-start.4 = (bf16[8,4096]{1,0:T(8,128)(2,1)S(1)}, bf16[8,4096]{1,0:T(8,128)(2,1)S(1)}, u32[]{:S(2)}, u32[]{:S(2)}) collective-permute-start(bf16[8,4096]{1,0:T(8,128)(2,1)S(1)} %attention.1.refs_0_), channel_id=1, source_target_pairs={{0,14},{2,12},{4,10},{6,8},{8,6},{10,4},{12,2},{14,0},{1,15},{3,13... | collective-permute-start | bytes 196616 | tf_op jit(solution)/shard_map/ppermute | solution.py:560
  15.8 5.5 %collective-permute-done.4.e_ref = bf16[8,4096]{1,0:T(8,128)(2,1)S(1)} collective-permute-done((bf16[8,4096]{1,0:T(8,128)(2,1)S(1)}, bf16[8,4096]{1,0:T(8,128)(2,1)S(1)}, u32[]{:S(2)}, u32[]{:S(2)}) %collective-permute-start.4) | collective-permute-done | bytes 65568 | tf_op jit(solution)/shard_map/ppermute | solution.py:560
  21.3 15.2 %gate_up.1 = (bf16[2,64,3328]{2,1,0:T(8,128)(2,1)S(1)}, bf16[64,4096]{1,0:T(8,128)(2,1)S(1)}, bf16[2816,2048]{1,0:T(8,128)(2,1)S(1)}) custom-call(bf16[3,8,4096]{2,1,0:T(8,128)(2,1)S(1)} %pack.1.a_ref, bf16[3,8,4096]{2,1,0:T(8,128)(2,1)S(1)} %collective-permute-done.2.c_ref, bf16[8,4096]{1,0:T(8,128)(2,1)S(1)} %collective-permute-done.3.d_ref, ...), custom_call_target="tpu_custom_call" | custom-call | flops 3489660928 | bytes 54525952 | tf_op jit(solution)/shard_map/gate_up/pallas_call | solution.py:244
  36.6 2.6 %prepare.1 = (bf16[512,2048]{1,0:T(8,128)(2,1)S(1)}, bf16[1536,1024]{1,0:T(8,128)(2,1)S(1)}, bf16[128,64]{1,0:T(8,128)(2,1)S(1)}) custom-call(bf16[2,64,3328]{2,1,0:T(8,128)(2,1)S(1)} %get-tuple-element.28.after_ref.refs_0_, s32[1,64]{1,0:T(1,128)S(1)} %bitcast.3, bf16[3328,4096]{1,0:T(8,128)(2,1)} %refs_6_.1), custom_call_target="tpu_custom_call" | custom-call | bytes 5242880 | tf_op jit(solution)/shard_map/prepare/pallas_call | solution.py:330
  39.2 2.4 %down_far.2 = (bf16[64,1024]{1,0:T(8,128)(2,1)S(1)}, bf16[1792,1024]{1,0:T(8,128)(2,1)S(1)}, bf16[512,1024]{1,0:T(8,128)(2,1)S(1)}, bf16[64,3328]{1,0:T(8,128)(2,1)S(1)}) custom-call(bf16[2,64,3328]{2,1,0:T(8,128)(2,1)S(1)} %get-tuple-element.28.after_ref.refs_0_, bf16[2,64,3328]{2,1,0:T(8,128)(2,1)S(1)} %collective-permute-done.5.refs_1_, ...), custom_call_target="tpu_custom_call" | custom-call | bytes 1024 | tf_op jit(solution)/shard_map/down_far/pallas_call | solution.py:417
  42.2 1.9 %down_far.3 = (bf16[64,1024]{1,0:T(8,128)(2,1)S(1)}, bf16[1536,1024]{1,0:T(8,128)(2,1)S(1)}) custom-call(bf16[64,3328]{1,0:T(8,128)(2,1)S(1)} %get-tuple-element.33.refs_0_, bf16[2816,2048]{1,0:T(8,128)(2,1)S(1)} %get-tuple-element.31.refs_2_.refs_1_, bf16[512,2048]{1,0:T(8,128)(2,1)S(1)} %get-tuple-element.32.refs_3_.refs_2_, bf16[3328,4096]{1,0:T(8,128)(2,1)} %refs_6_.1), custom_call_target="tpu_custom_call" | custom-call | bytes 1024 | tf_op jit(solution)/shard_map/down_far/pallas_call | solution.py:417
  44.1 1.6 %collective-permute-start.8 = (bf16[64,1024]{1,0:T(8,128)(2,1)S(1)}, bf16[64,1024]{1,0:T(8,128)(2,1)S(1)}, u32[]{:S(2)}, u32[]{:S(2)}) collective-permute-start(bf16[64,1024]{1,0:T(8,128)(2,1)S(1)} %get-tuple-element.40), channel_id=1, source_target_pairs={{0,2},{2,0},{4,6},{6,4},{8,10},{10,8},{12,14},{14,12},{1,3},{3,1},... | collective-permute-start | bytes 393224 | tf_op jit(solution)/shard_map/ppermute | solution.py:590
  45.7 2.3 %collective-permute-done.6.refs_1_ = bf16[64,1024]{1,0:T(8,128)(2,1)S(1)} collective-permute-done((bf16[64,1024]{1,0:T(8,128)(2,1)S(1)}, bf16[64,1024]{1,0:T(8,128)(2,1)S(1)}, u32[]{:S(2)}, u32[]{:S(2)}) %collective-permute-start.6) | collective-permute-done | bytes 131104 | tf_op jit(solution)/shard_map/ppermute | solution.py:586
  47.9 1.7 %down_near.2 = (bf16[64,1024]{1,0:T(8,128)(2,1)S(1)}, bf16[64,1024]{1,0:T(8,128)(2,1)S(1)}, bf16[1280,1024]{1,0:T(8,128)(2,1)S(1)}) custom-call(bf16[64,3328]{1,0:T(8,128)(2,1)S(1)} %get-tuple-element.33.refs_0_, bf16[64,1024]{1,0:T(8,128)(2,1)S(1)} %collective-permute-done.6.refs_1_, bf16[128,64]{1,0:T(8,128)(2,1)S(1)} %get-tuple-element.29.refs_2_.chosen_ref, ...), custom_call_target="tpu_custom_call" | custom-call | bytes 1024 | tf_op jit(solution)/shard_map/down_near/pallas_call | solution.py:417
  50.3 1.5 %down_near.3 = (bf16[64,1024]{1,0:T(8,128)(2,1)S(1)}, bf16[64,1024]{1,0:T(8,128)(2,1)S(1)}) custom-call(bf16[64,3328]{1,0:T(8,128)(2,1)S(1)} %get-tuple-element.33.refs_0_, bf16[64,1024]{1,0:T(8,128)(2,1)S(1)} %collective-permute-done.8.refs_1_, bf16[128,64]{1,0:T(8,128)(2,1)S(1)} %get-tuple-element.29.refs_2_.chosen_ref, ...), custom_call_target="tpu_custom_call" | custom-call | bytes 1024 | tf_op jit(solution)/shard_map/down_near/pallas_call | solution.py:417
  51.9 1.5 %collective-permute-start.9 = (bf16[64,1024]{1,0:T(8,128)(2,1)S(1)}, bf16[64,1024]{1,0:T(8,128)(2,1)S(1)}, u32[]{:S(2)}, u32[]{:S(2)}) collective-permute-start(bf16[64,1024]{1,0:T(8,128)(2,1)S(1)} %get-tuple-element.45), channel_id=1, source_target_pairs={{0,4},{2,6},{4,0},{6,2},{8,12},{10,14},{12,8},{14,10},{1,5},{3,7},... | collective-permute-start | bytes 393224 | tf_op jit(solution)/shard_map/ppermute | solution.py:604
  53.4 1.9 %collective-permute-done.7.came_ref = bf16[64,1024]{1,0:T(8,128)(2,1)S(1)} collective-permute-done((bf16[64,1024]{1,0:T(8,128)(2,1)S(1)}, bf16[64,1024]{1,0:T(8,128)(2,1)S(1)}, u32[]{:S(2)}, u32[]{:S(2)}) %collective-permute-start.7) | collective-permute-done | bytes 131104 | tf_op jit(solution)/shard_map/ppermute | solution.py:600
  55.3 2.9 %collective-permute-done.9.came_ref = bf16[64,1024]{1,0:T(8,128)(2,1)S(1)} collective-permute-done((bf16[64,1024]{1,0:T(8,128)(2,1)S(1)}, bf16[64,1024]{1,0:T(8,128)(2,1)S(1)}, u32[]{:S(2)}, u32[]{:S(2)}) %collective-permute-start.9) | collective-permute-done | bytes 131104 | tf_op jit(solution)/shard_map/ppermute | solution.py:604
  58.3 0.9 %collective-permute-start.11 = (bf16[32,1024]{1,0:T(8,128)(2,1)S(1)}, bf16[32,1024]{1,0:T(8,128)(2,1)S(1)}, u32[]{:S(2)}, u32[]{:S(2)}) collective-permute-start(bf16[32,1024]{1,0:T(8,128)(2,1)S(1)} %get-tuple-element.48), channel_id=1, source_target_pairs={{0,8},{2,10},{4,12},{6,14},{8,0},{10,2},{12,4},{14,6},{1,9},{3,11}... | collective-permute-start | bytes 196616 | tf_op jit(solution)/shard_map/ppermute | solution.py:609
  59.2 2.2 %collective-permute-done.10.refs_2_ = bf16[32,1024]{1,0:T(8,128)(2,1)S(1)} collective-permute-done((bf16[32,1024]{1,0:T(8,128)(2,1)S(1)}, bf16[32,1024]{1,0:T(8,128)(2,1)S(1)}, u32[]{:S(2)}, u32[]{:S(2)}) %collective-permute-start.10) | collective-permute-done | bytes 65568 | tf_op jit(solution)/shard_map/ppermute | solution.py:609
  61.4 2.5 %collective-permute-done.11.refs_3_ = bf16[32,1024]{1,0:T(8,128)(2,1)S(1)} collective-permute-done((bf16[32,1024]{1,0:T(8,128)(2,1)S(1)}, bf16[32,1024]{1,0:T(8,128)(2,1)S(1)}, u32[]{:S(2)}, u32[]{:S(2)}) %collective-permute-start.11) | collective-permute-done | bytes 65568 | tf_op jit(solution)/shard_map/ppermute | solution.py:609
  64.4 4.0 %collective-permute-done.12.other_ref = bf16[16,2048]{1,0:T(8,128)(2,1)S(1)} collective-permute-done((bf16[16,2048]{1,0:T(8,128)(2,1)S(1)}, bf16[16,2048]{1,0:T(8,128)(2,1)S(1)}, u32[]{:S(2)}, u32[]{:S(2)}) %collective-permute-start.12) | collective-permute-done | bytes 65568 | tf_op jit(solution)/shard_map/ppermute | solution.py:611
  68.4 0.7 join_halves.1
  (18 shorter events, 2.5 us)
Async XLA Ops:
  0.0 21.3 %copy-start = (bf16[4096,3328]{1,0:T(8,128)(2,1)S(1)}, bf16[4096,3328]{1,0:T(8,128)(2,1)}, u32[]{:S(2)}) copy-start(bf16[4096,3328]{1,0:T(8,128)(2,1)} %gate_ref.1) | copy-start | bytes 81788928
  3.0 7.7 %collective-permute-start = (bf16[8,4096]{1,0:T(8,128)(2,1)S(1)}, bf16[8,4096]{1,0:T(8,128)(2,1)S(1)}, u32[]{:S(2)}, u32[]{:S(2)}) collective-permute-start(bf16[8,4096]{1,0:T(8,128)(2,1)S(1)} %attention.1.refs_0_), channel_id=1, source_target_pairs={{0,8},{2,10},{4,12},{6,14},{8,0},{10,2},{12,4},{14,6},{1,9},{3,11}... | collective-permute-start | bytes 196616 | tf_op jit(solution)/shard_map/ppermute | solution.py:558
  7.1 4.3 %collective-permute-start.1 = (bf16[8,4096]{1,0:T(8,128)(2,1)S(1)}, bf16[8,4096]{1,0:T(8,128)(2,1)S(1)}, u32[]{:S(2)}, u32[]{:S(2)}) collective-permute-start(bf16[8,4096]{1,0:T(8,128)(2,1)S(1)} %attention.1.refs_0_), channel_id=1, source_target_pairs={{0,2},{2,0},{4,6},{6,4},{8,10},{10,8},{12,14},{14,12},{1,3},{3,1},... | collective-permute-start | bytes 196616 | tf_op jit(solution)/shard_map/ppermute | solution.py:559
  11.4 25.2 %copy-start.1 = (s32[64,1]{0,1:T(1,128)S(1)}, s32[64,1]{0,1:T(1,128)}, u32[]{:S(2)}) copy-start(s32[64,1]{0,1:T(1,128)} %param.14) | copy-start | bytes 772
  11.4 9.9 %collective-permute-start.2 = (bf16[3,8,4096]{2,1,0:T(8,128)(2,1)S(1)}, bf16[3,8,4096]{2,1,0:T(8,128)(2,1)S(1)}, u32[]{:S(2)}, u32[]{:S(2)}) collective-permute-start(bf16[3,8,4096]{2,1,0:T(8,128)(2,1)S(1)} %pack.1.a_ref), channel_id=1, source_target_pairs={{0,4},{2,6},{4,0},{6,2},{8,12},{10,14},{12,8},{14,10},{1,5},{3,7},... | collective-permute-start | bytes 589832 | tf_op jit(solution)/shard_map/ppermute | solution.py:562
  13.0 8.3 %collective-permute-start.4 = (bf16[8,4096]{1,0:T(8,128)(2,1)S(1)}, bf16[8,4096]{1,0:T(8,128)(2,1)S(1)}, u32[]{:S(2)}, u32[]{:S(2)}) collective-permute-start(bf16[8,4096]{1,0:T(8,128)(2,1)S(1)} %attention.1.refs_0_), channel_id=1, source_target_pairs={{0,14},{2,12},{4,10},{6,8},{8,6},{10,4},{12,2},{14,0},{1,15},{3,13... | collective-permute-start | bytes 196616 | tf_op jit(solution)/shard_map/ppermute | solution.py:560
  15.2 6.1 %collective-permute-start.3 = (bf16[8,4096]{1,0:T(8,128)(2,1)S(1)}, bf16[8,4096]{1,0:T(8,128)(2,1)S(1)}, u32[]{:S(2)}, u32[]{:S(2)}) collective-permute-start(bf16[8,4096]{1,0:T(8,128)(2,1)S(1)} %collective-permute-done.refs_1_), channel_id=1, source_target_pairs={{0,2},{2,0},{4,6},{6,4},{8,10},{10,8},{12,14},{14,12},{1,3},{3,1},... | collective-permute-start | bytes 196616 | tf_op jit(solution)/shard_map/ppermute | solution.py:563
  36.5 2.7 %collective-permute-start.5 = (bf16[2,64,3328]{2,1,0:T(8,128)(2,1)S(1)}, bf16[2,64,3328]{2,1,0:T(8,128)(2,1)S(1)}, u32[]{:S(2)}, u32[]{:S(2)}) collective-permute-start(bf16[2,64,3328]{2,1,0:T(8,128)(2,1)S(1)} %get-tuple-element.28.after_ref.refs_0_), channel_id=1, source_target_pairs={{0,1},{1,0},{2,3},{3,2},{4,5},{5,4},{6,7},{7,6},{8,9},{9,8},{10,11... | collective-permute-start | bytes 2555912 | tf_op jit(solution)/shard_map/ppermute | solution.py:571
  41.6 6.4 %collective-permute-start.6 = (bf16[64,1024]{1,0:T(8,128)(2,1)S(1)}, bf16[64,1024]{1,0:T(8,128)(2,1)S(1)}, u32[]{:S(2)}, u32[]{:S(2)}) collective-permute-start(bf16[64,1024]{1,0:T(8,128)(2,1)S(1)} %get-tuple-element.34), channel_id=1, source_target_pairs={{0,2},{2,0},{4,6},{6,4},{8,10},{10,8},{12,14},{14,12},{1,3},{3,1},... | collective-permute-start | bytes 393224 | tf_op jit(solution)/shard_map/ppermute | solution.py:586
  44.1 6.2 %collective-permute-start.8 = (bf16[64,1024]{1,0:T(8,128)(2,1)S(1)}, bf16[64,1024]{1,0:T(8,128)(2,1)S(1)}, u32[]{:S(2)}, u32[]{:S(2)}) collective-permute-start(bf16[64,1024]{1,0:T(8,128)(2,1)S(1)} %get-tuple-element.40), channel_id=1, source_target_pairs={{0,2},{2,0},{4,6},{6,4},{8,10},{10,8},{12,14},{14,12},{1,3},{3,1},... | collective-permute-start | bytes 393224 | tf_op jit(solution)/shard_map/ppermute | solution.py:590
  49.7 5.5 %collective-permute-start.7 = (bf16[64,1024]{1,0:T(8,128)(2,1)S(1)}, bf16[64,1024]{1,0:T(8,128)(2,1)S(1)}, u32[]{:S(2)}, u32[]{:S(2)}) collective-permute-start(bf16[64,1024]{1,0:T(8,128)(2,1)S(1)} %get-tuple-element.38), channel_id=1, source_target_pairs={{0,4},{2,6},{4,0},{6,2},{8,12},{10,14},{12,8},{14,10},{1,5},{3,7},... | collective-permute-start | bytes 393224 | tf_op jit(solution)/shard_map/ppermute | solution.py:600
  51.9 6.4 %collective-permute-start.9 = (bf16[64,1024]{1,0:T(8,128)(2,1)S(1)}, bf16[64,1024]{1,0:T(8,128)(2,1)S(1)}, u32[]{:S(2)}, u32[]{:S(2)}) collective-permute-start(bf16[64,1024]{1,0:T(8,128)(2,1)S(1)} %get-tuple-element.45), channel_id=1, source_target_pairs={{0,4},{2,6},{4,0},{6,2},{8,12},{10,14},{12,8},{14,10},{1,5},{3,7},... | collective-permute-start | bytes 393224 | tf_op jit(solution)/shard_map/ppermute | solution.py:604
  55.3 6.1 %collective-permute-start.10 = (bf16[32,1024]{1,0:T(8,128)(2,1)S(1)}, bf16[32,1024]{1,0:T(8,128)(2,1)S(1)}, u32[]{:S(2)}, u32[]{:S(2)}) collective-permute-start(bf16[32,1024]{1,0:T(8,128)(2,1)S(1)} %get-tuple-element.47), channel_id=1, source_target_pairs={{0,8},{2,10},{4,12},{6,14},{8,0},{10,2},{12,4},{14,6},{1,9},{3,11}... | collective-permute-start | bytes 196616 | tf_op jit(solution)/shard_map/ppermute | solution.py:609
  58.3 5.6 %collective-permute-start.11 = (bf16[32,1024]{1,0:T(8,128)(2,1)S(1)}, bf16[32,1024]{1,0:T(8,128)(2,1)S(1)}, u32[]{:S(2)}, u32[]{:S(2)}) collective-permute-start(bf16[32,1024]{1,0:T(8,128)(2,1)S(1)} %get-tuple-element.48), channel_id=1, source_target_pairs={{0,8},{2,10},{4,12},{6,14},{8,0},{10,2},{12,4},{14,6},{1,9},{3,11}... | collective-permute-start | bytes 196616 | tf_op jit(solution)/shard_map/ppermute | solution.py:609
  64.1 4.3 %collective-permute-start.12 = (bf16[16,2048]{1,0:T(8,128)(2,1)S(1)}, bf16[16,2048]{1,0:T(8,128)(2,1)S(1)}, u32[]{:S(2)}, u32[]{:S(2)}) collective-permute-start(bf16[16,2048]{1,0:T(8,128)(2,1)S(1)} %get-tuple-element.50), channel_id=1, source_target_pairs={{0,2},{2,0},{4,6},{6,4},{8,10},{10,8},{12,14},{14,12},{1,3},{3,1},... | collective-permute-start | bytes 196616 | tf_op jit(solution)/shard_map/ppermute | solution.py:611

commit v10 on v9

--- a/solution.py
+++ b/solution.py
@@ -303,13 +303,9 @@
     return (slot == row * capacity + rank).astype(F32).astype(BF16)
 
 
-def prepare_kernel(
-    devices, capacity, first, after_ref, row_ref, w_hbm, far_ref, near_ref, chosen_ref, far_sems, sems
-):
+def prepare_kernel(devices, capacity, first, after_ref, row_ref, w_hbm, far_ref, chosen_ref, sems):
     base = half_base(devices, False, far_ref.shape[1])
-    copies = down_copies(w_hbm, base, far_ref, far_sems, first)
-    base = quarter_base(devices, False, 0, near_ref.shape[1])
-    copies += down_copies(w_hbm, base, near_ref, sems, 0)
+    copies = down_copies(w_hbm, base, far_ref, sems, first)
     for c in copies:
         c.start()
     nz, nx = grid_of(devices)
@@ -323,25 +319,21 @@
         c.wait()
 
 
-def prepare(after, row, down_weight, devices, capacity, first, near_rows):
+def prepare(after, row, down_weight, devices, capacity, first):
     columns, features = down_weight.shape
     total = row.shape[1]
-    far_rows = columns - first
+    rows = columns - first
     return pl.pallas_call(
         functools.partial(prepare_kernel, devices, capacity, first),
         out_shape=(
-            pltpu.VMEM((far_rows, features // 2), BF16),
-            pltpu.VMEM((near_rows, features // 4), BF16),
+            pltpu.VMEM((rows, features // 2), BF16),
             jax.ShapeDtypeStruct((devices * 2 * capacity, total), BF16),
         ),
         in_specs=[ANY, VMEM, HBM],
-        out_specs=(VMEM, VMEM, VMEM),
-        scratch_shapes=[
-            pltpu.SemaphoreType.DMA((far_rows // TILE,)),
-            pltpu.SemaphoreType.DMA((near_rows // TILE,)),
-        ],
+        out_specs=(VMEM, VMEM),
+        scratch_shapes=[pltpu.SemaphoreType.DMA((rows // TILE,))],
         compiler_params=params(2),
-        cost_estimate=cost(0, (2 * far_rows + near_rows) * features // 2),
+        cost_estimate=cost(0, rows * features),
         name="prepare",
     )(after, row, in_hbm(down_weight))
 
@@ -562,33 +554,32 @@
     c = lax.ppermute(a, AXIS, swap_z(devices, 1))
     d = lax.ppermute(two, AXIS, swap_x(devices))
     tiles = columns // TILE
-    far_cut = 11 * tiles // 13 * TILE
-    first = 6 * tiles // 13 * TILE
-    cut = 2 * tiles // 13 * TILE, 8 * tiles // 13 * TILE
+    far_cut = 8 * tiles // 13 * TILE
+    cut = 8 * tiles // 13 * TILE, 7 * tiles // 13 * TILE
     part, rows, far_a = gate_up(
         (a, c, d, e), gate_weight, up_weight, down_weight, devices, far_cut
     )
     other = lax.ppermute(part, "ffn", [(0, 1), (1, 0)])
-    far_b, near_a, chosen = prepare(
-        part, target.reshape(1, -1), down_weight, devices, capacity, far_cut, first
+    far_b, chosen = prepare(
+        part, target.reshape(1, -1), down_weight, devices, capacity, far_cut
     )
     held_far = far_a, far_b
 
-    far, near_b, near_c, hidden = down(
-        (part, other),
+    far, near_a, hidden = down(
+        (part, other), held_far, down_weight, devices, True, 0, ((0, 0, cut[0]),)
+    )
+    arrived = [lax.ppermute(far, AXIS, swap_x(devices))]
+    far, near_b, near_c = down(
+        (hidden,),
         held_far,
         down_weight,
         devices,
         True,
-        0,
-        ((0, first, columns - first), (1, 0, cut[0])),
-    )
-    arrived = [lax.ppermute(far, AXIS, swap_x(devices))]
-    far, near_d = down(
-        (hidden,), held_far, down_weight, devices, True, 1, ((1, cut[0], cut[1] - cut[0]),)
+        1,
+        ((0, cut[0], columns - cut[0]), (1, 0, cut[1])),
     )
     arrived.append(lax.ppermute(far, AXIS, swap_x(devices)))
-    keep_a, send_a, near_e = down(
+    keep_a, send_a, near_d = down(
         (hidden, arrived[0], chosen),
         (near_a, near_b),
         down_weight,
@@ -599,7 +590,7 @@
     )
     came_a = lax.ppermute(send_a, AXIS, swap_z(devices, 1))
     keep_b, send_b = down(
-        (hidden, arrived[1], chosen), (near_c, near_d, near_e), down_weight, devices, False, 1
+        (hidden, arrived[1], chosen), (near_c, near_d), down_weight, devices, False, 1
     )
     came_b = lax.ppermute(send_b, AXIS, swap_z(devices, 1))
     own, came = [], []

time: 69.2 us -> 68.9 us (level)
  waiting for transfers between devices: 24.6 us -> 22.8 us
  Pallas kernels: 29.2 us -> 30.2 us
    ppermute x1, waiting for transfers between devices: 2.28 us -> 0.87 us  [local(): arrived = [lax.ppermute(far, AXIS, swap_x(devices))]]
    pallas_call x4, Pallas kernels: 7.57 us -> 8.58 us  [down(): pl.pallas_call(functools.partial(down_kernel, devices, far, quarter, len(...]
    ppermute x1, waiting for transfers between devices: 4 us -> 3.06 us  [local(): return join(keep, lax.ppermute(send, AXIS, swap_x(devices)), devices)]
    ppermute x1, starting transfers between devices: 0.33 us -> 1.28 us  [local(): return join(keep, lax.ppermute(send, AXIS, swap_x(devices)), devices)]
  transfers between devices with their start and end apart: 13 -> 13, of which waited for: 10 -> 10; matrix products, arithmetic and copies ran while one was open for 0% -> 0% of each run, Pallas kernels for 11% -> 13%
where the time goes in v10:
time: 68.9 us; the launch traced here: 68.8 us
  Pallas kernels  30.2 us (44%)
  waiting for transfers between devices  22.8 us (33%)
  starting transfers between devices  15.7 us (23%)
    pallas_call x1, Pallas kernels, gate_up(): pl.pallas_call(functools.partial(gate_up_kernel, devices), out_shape=(jax...  15.1 us
    pallas_call x4, Pallas kernels, down(): pl.pallas_call(functools.partial(down_kernel, devices, far, quarter, len(...  8.58 us
    ppermute x1, waiting for transfers between devices, local(): e = lax.ppermute(mixed_rows, AXIS, swap_x(devices, 3))  5.51 us
    ppermute x2, waiting for transfers between devices, local(): came.append(lax.ppermute(send, AXIS, swap_z(devices, 2)))  4.88 us
    ppermute x1, starting transfers between devices, local(): two = lax.ppermute(mixed_rows, AXIS, swap_z(devices, 2))  4.1 us
    ppermute x1, waiting for transfers between devices, local(): return join(keep, lax.ppermute(send, AXIS, swap_x(devices)), devices)  3.06 us
    pallas_call x1, Pallas kernels, attend(): pl.pallas_call(functools.partial(attend_kernel, kv), out_shape=jax.ShapeD...  3 us
    ppermute x1, waiting for transfers between devices, local(): came_b = lax.ppermute(send_b, AXIS, swap_z(devices, 1))  2.71 us
  transfers between devices with their start and end apart: 13, of which 10 were waited for; matrix products, arithmetic and copies ran while one was open for 0% of the time, Pallas kernels for 13%

profile of v10, /device:TPU:0, one launch (start us, length us, event | category | flops | bytes accessed | tf_op | source)
XLA Modules:
  0.0 68.8 jit_solution(17002713639819469291)
XLA Ops:
  0.0 3.0 %attention.1.refs_0_ = bf16[8,4096]{1,0:T(8,128)(2,1)S(1)} custom-call(s32[8]{0:T(128)} %lengths.1, bf16[8,32,128]{2,1,0:T(8,128)(2,1)} %q_hbm.1, bf16[8,256,128]{2,1,0:T(8,128)(2,1)} %bitcast.4, bf16[8,256,128]{2,1,0:T(8,128)(2,1)} %bitcast.5, bf16[8,4096]{1,0:T(8,128)(2,1)} %res_ref.1, bf16[4096,3328]{1,0:T(8,128)(2,1)} %u_hbm.1), custom_call_target="tpu_custom_call" | custom-call | flops 33554432 | bytes 1048576 | tf_op jit(solution)/shard_map/attention/pallas_call | solution.py:107
  3.0 4.1 %collective-permute-start = (bf16[8,4096]{1,0:T(8,128)(2,1)S(1)}, bf16[8,4096]{1,0:T(8,128)(2,1)S(1)}, u32[]{:S(2)}, u32[]{:S(2)}) collective-permute-start(bf16[8,4096]{1,0:T(8,128)(2,1)S(1)} %attention.1.refs_0_), channel_id=1, source_target_pairs={{0,8},{2,10},{4,12},{6,14},{8,0},{10,2},{12,4},{14,6},{1,9},{3,11}... | collective-permute-start | bytes 196616 | tf_op jit(solution)/shard_map/ppermute | solution.py:550
  7.1 1.5 %collective-permute-start.1 = (bf16[8,4096]{1,0:T(8,128)(2,1)S(1)}, bf16[8,4096]{1,0:T(8,128)(2,1)S(1)}, u32[]{:S(2)}, u32[]{:S(2)}) collective-permute-start(bf16[8,4096]{1,0:T(8,128)(2,1)S(1)} %attention.1.refs_0_), channel_id=1, source_target_pairs={{0,2},{2,0},{4,6},{6,4},{8,10},{10,8},{12,14},{14,12},{1,3},{3,1},... | collective-permute-start | bytes 196616 | tf_op jit(solution)/shard_map/ppermute | solution.py:551
  8.6 2.2 %collective-permute-done.refs_1_ = bf16[8,4096]{1,0:T(8,128)(2,1)S(1)} collective-permute-done((bf16[8,4096]{1,0:T(8,128)(2,1)S(1)}, bf16[8,4096]{1,0:T(8,128)(2,1)S(1)}, u32[]{:S(2)}, u32[]{:S(2)}) %collective-permute-start) | collective-permute-done | bytes 65568 | tf_op jit(solution)/shard_map/ppermute | solution.py:550
  11.4 1.6 %collective-permute-start.2 = (bf16[3,8,4096]{2,1,0:T(8,128)(2,1)S(1)}, bf16[3,8,4096]{2,1,0:T(8,128)(2,1)S(1)}, u32[]{:S(2)}, u32[]{:S(2)}) collective-permute-start(bf16[3,8,4096]{2,1,0:T(8,128)(2,1)S(1)} %pack.1.a_ref), channel_id=1, source_target_pairs={{0,4},{2,6},{4,0},{6,2},{8,12},{10,14},{12,8},{14,10},{1,5},{3,7},... | collective-permute-start | bytes 589832 | tf_op jit(solution)/shard_map/ppermute | solution.py:554
  13.0 2.2 %collective-permute-start.4 = (bf16[8,4096]{1,0:T(8,128)(2,1)S(1)}, bf16[8,4096]{1,0:T(8,128)(2,1)S(1)}, u32[]{:S(2)}, u32[]{:S(2)}) collective-permute-start(bf16[8,4096]{1,0:T(8,128)(2,1)S(1)} %attention.1.refs_0_), channel_id=1, source_target_pairs={{0,14},{2,12},{4,10},{6,8},{8,6},{10,4},{12,2},{14,0},{1,15},{3,13... | collective-permute-start | bytes 196616 | tf_op jit(solution)/shard_map/ppermute | solution.py:552
  15.8 5.5 %collective-permute-done.4.e_ref = bf16[8,4096]{1,0:T(8,128)(2,1)S(1)} collective-permute-done((bf16[8,4096]{1,0:T(8,128)(2,1)S(1)}, bf16[8,4096]{1,0:T(8,128)(2,1)S(1)}, u32[]{:S(2)}, u32[]{:S(2)}) %collective-permute-start.4) | collective-permute-done | bytes 65568 | tf_op jit(solution)/shard_map/ppermute | solution.py:552
  21.3 15.1 %gate_up.1 = (bf16[2,64,3328]{2,1,0:T(8,128)(2,1)S(1)}, bf16[64,4096]{1,0:T(8,128)(2,1)S(1)}, bf16[2048,2048]{1,0:T(8,128)(2,1)S(1)}) custom-call(bf16[3,8,4096]{2,1,0:T(8,128)(2,1)S(1)} %pack.1.a_ref, bf16[3,8,4096]{2,1,0:T(8,128)(2,1)S(1)} %collective-permute-done.2.c_ref, bf16[8,4096]{1,0:T(8,128)(2,1)S(1)} %collective-permute-done.3.d_ref, ...), custom_call_target="tpu_custom_call" | custom-call | flops 3489660928 | bytes 54525952 | tf_op jit(solution)/shard_map/gate_up/pallas_call | solution.py:244
  36.5 2.6 %prepare.1 = (bf16[1280,2048]{1,0:T(8,128)(2,1)S(1)}, bf16[128,64]{1,0:T(8,128)(2,1)S(1)}) custom-call(bf16[2,64,3328]{2,1,0:T(8,128)(2,1)S(1)} %get-tuple-element.27.after_ref.refs_0_, s32[1,64]{1,0:T(1,128)S(1)} %bitcast.3, bf16[3328,4096]{1,0:T(8,128)(2,1)} %refs_5_.3), custom_call_target="tpu_custom_call" | custom-call | bytes 5242880 | tf_op jit(solution)/shard_map/prepare/pallas_call | solution.py:326
  39.1 2.2 %down_far.2 = (bf16[64,1024]{1,0:T(8,128)(2,1)S(1)}, bf16[2048,1024]{1,0:T(8,128)(2,1)S(1)}, bf16[64,3328]{1,0:T(8,128)(2,1)S(1)}) custom-call(bf16[2,64,3328]{2,1,0:T(8,128)(2,1)S(1)} %get-tuple-element.27.after_ref.refs_0_, bf16[2,64,3328]{2,1,0:T(8,128)(2,1)S(1)} %collective-permute-done.5.refs_1_, ...), custom_call_target="tpu_custom_call" | custom-call | bytes 1024 | tf_op jit(solution)/shard_map/down_far/pallas_call | solution.py:409
  42.0 2.9 %down_far.3 = (bf16[64,1024]{1,0:T(8,128)(2,1)S(1)}, bf16[1280,1024]{1,0:T(8,128)(2,1)S(1)}, bf16[1792,1024]{1,0:T(8,128)(2,1)S(1)}) custom-call(bf16[64,3328]{1,0:T(8,128)(2,1)S(1)} %get-tuple-element.32.refs_0_, bf16[2048,2048]{1,0:T(8,128)(2,1)S(1)} %get-tuple-element.30.refs_2_.refs_1_, bf16[1280,2048]{1,0:T(8,128)(2,1)S(1)} %get-tuple-element.31.refs_3_.refs_2_, ...), custom_call_target="tpu_custom_call" | custom-call | bytes 1024 | tf_op jit(solution)/shard_map/down_far/pallas_call | solution.py:409
  44.9 1.6 %collective-permute-start.8 = (bf16[64,1024]{1,0:T(8,128)(2,1)S(1)}, bf16[64,1024]{1,0:T(8,128)(2,1)S(1)}, u32[]{:S(2)}, u32[]{:S(2)}) collective-permute-start(bf16[64,1024]{1,0:T(8,128)(2,1)S(1)} %get-tuple-element.39), channel_id=1, source_target_pairs={{0,2},{2,0},{4,6},{6,4},{8,10},{10,8},{12,14},{14,12},{1,3},{3,1},... | collective-permute-start | bytes 393224 | tf_op jit(solution)/shard_map/ppermute | solution.py:581
  46.4 0.9 %collective-permute-done.6.refs_1_ = bf16[64,1024]{1,0:T(8,128)(2,1)S(1)} collective-permute-done((bf16[64,1024]{1,0:T(8,128)(2,1)S(1)}, bf16[64,1024]{1,0:T(8,128)(2,1)S(1)}, u32[]{:S(2)}, u32[]{:S(2)}) %collective-permute-start.6) | collective-permute-done | bytes 131104 | tf_op jit(solution)/shard_map/ppermute | solution.py:571
  47.3 1.9 %down_near.2 = (bf16[64,1024]{1,0:T(8,128)(2,1)S(1)}, bf16[64,1024]{1,0:T(8,128)(2,1)S(1)}, bf16[1536,1024]{1,0:T(8,128)(2,1)S(1)}) custom-call(bf16[64,3328]{1,0:T(8,128)(2,1)S(1)} %get-tuple-element.32.refs_0_, bf16[64,1024]{1,0:T(8,128)(2,1)S(1)} %collective-permute-done.6.refs_1_, bf16[128,64]{1,0:T(8,128)(2,1)S(1)} %get-tuple-element.28.refs_2_.chosen_ref, ...), custom_call_target="tpu_custom_call" | custom-call | bytes 1024 | tf_op jit(solution)/shard_map/down_near/pallas_call | solution.py:409
  49.3 1.3 %collective-permute-done.8.refs_1_ = bf16[64,1024]{1,0:T(8,128)(2,1)S(1)} collective-permute-done((bf16[64,1024]{1,0:T(8,128)(2,1)S(1)}, bf16[64,1024]{1,0:T(8,128)(2,1)S(1)}, u32[]{:S(2)}, u32[]{:S(2)}) %collective-permute-start.8) | collective-permute-done | bytes 131104 | tf_op jit(solution)/shard_map/ppermute | solution.py:581
  50.6 1.5 %down_near.3 = (bf16[64,1024]{1,0:T(8,128)(2,1)S(1)}, bf16[64,1024]{1,0:T(8,128)(2,1)S(1)}) custom-call(bf16[64,3328]{1,0:T(8,128)(2,1)S(1)} %get-tuple-element.32.refs_0_, bf16[64,1024]{1,0:T(8,128)(2,1)S(1)} %collective-permute-done.8.refs_1_, bf16[128,64]{1,0:T(8,128)(2,1)S(1)} %get-tuple-element.28.refs_2_.chosen_ref, ...), custom_call_target="tpu_custom_call" | custom-call | bytes 1024 | tf_op jit(solution)/shard_map/down_near/pallas_call | solution.py:409
  52.1 0.8 %collective-permute-start.9 = (bf16[64,1024]{1,0:T(8,128)(2,1)S(1)}, bf16[64,1024]{1,0:T(8,128)(2,1)S(1)}, u32[]{:S(2)}, u32[]{:S(2)}) collective-permute-start(bf16[64,1024]{1,0:T(8,128)(2,1)S(1)} %get-tuple-element.43), channel_id=1, source_target_pairs={{0,4},{2,6},{4,0},{6,2},{8,12},{10,14},{12,8},{14,10},{1,5},{3,7},... | collective-permute-start | bytes 393224 | tf_op jit(solution)/shard_map/ppermute | solution.py:595
  52.9 1.7 %collective-permute-done.7.came_ref = bf16[64,1024]{1,0:T(8,128)(2,1)S(1)} collective-permute-done((bf16[64,1024]{1,0:T(8,128)(2,1)S(1)}, bf16[64,1024]{1,0:T(8,128)(2,1)S(1)}, u32[]{:S(2)}, u32[]{:S(2)}) %collective-permute-start.7) | collective-permute-done | bytes 131104 | tf_op jit(solution)/shard_map/ppermute | solution.py:591
  54.9 2.7 %collective-permute-done.9.came_ref = bf16[64,1024]{1,0:T(8,128)(2,1)S(1)} collective-permute-done((bf16[64,1024]{1,0:T(8,128)(2,1)S(1)}, bf16[64,1024]{1,0:T(8,128)(2,1)S(1)}, u32[]{:S(2)}, u32[]{:S(2)}) %collective-permute-start.9) | collective-permute-done | bytes 131104 | tf_op jit(solution)/shard_map/ppermute | solution.py:595
  57.7 1.1 %collective-permute-start.11 = (bf16[32,1024]{1,0:T(8,128)(2,1)S(1)}, bf16[32,1024]{1,0:T(8,128)(2,1)S(1)}, u32[]{:S(2)}, u32[]{:S(2)}) collective-permute-start(bf16[32,1024]{1,0:T(8,128)(2,1)S(1)} %get-tuple-element.46), channel_id=1, source_target_pairs={{0,8},{2,10},{4,12},{6,14},{8,0},{10,2},{12,4},{14,6},{1,9},{3,11}... | collective-permute-start | bytes 196616 | tf_op jit(solution)/shard_map/ppermute | solution.py:600
  58.7 2.7 %collective-permute-done.10.refs_2_ = bf16[32,1024]{1,0:T(8,128)(2,1)S(1)} collective-permute-done((bf16[32,1024]{1,0:T(8,128)(2,1)S(1)}, bf16[32,1024]{1,0:T(8,128)(2,1)S(1)}, u32[]{:S(2)}, u32[]{:S(2)}) %collective-permute-start.10) | collective-permute-done | bytes 65568 | tf_op jit(solution)/shard_map/ppermute | solution.py:600
  61.5 2.1 %collective-permute-done.11.refs_3_ = bf16[32,1024]{1,0:T(8,128)(2,1)S(1)} collective-permute-done((bf16[32,1024]{1,0:T(8,128)(2,1)S(1)}, bf16[32,1024]{1,0:T(8,128)(2,1)S(1)}, u32[]{:S(2)}, u32[]{:S(2)}) %collective-permute-start.11) | collective-permute-done | bytes 65568 | tf_op jit(solution)/shard_map/ppermute | solution.py:600
  63.8 1.3 %collective-permute-start.12 = (bf16[16,2048]{1,0:T(8,128)(2,1)S(1)}, bf16[16,2048]{1,0:T(8,128)(2,1)S(1)}, u32[]{:S(2)}, u32[]{:S(2)}) collective-permute-start(bf16[16,2048]{1,0:T(8,128)(2,1)S(1)} %get-tuple-element.48), channel_id=1, source_target_pairs={{0,2},{2,0},{4,6},{6,4},{8,10},{10,8},{12,14},{14,12},{1,3},{3,1},... | collective-permute-start | bytes 196616 | tf_op jit(solution)/shard_map/ppermute | solution.py:602
  65.1 3.1 %collective-permute-done.12.other_ref = bf16[16,2048]{1,0:T(8,128)(2,1)S(1)} collective-permute-done((bf16[16,2048]{1,0:T(8,128)(2,1)S(1)}, bf16[16,2048]{1,0:T(8,128)(2,1)S(1)}, u32[]{:S(2)}, u32[]{:S(2)}) %collective-permute-start.12) | collective-permute-done | bytes 65568 | tf_op jit(solution)/shard_map/ppermute | solution.py:602
  (18 shorter events, 3.1 us)
Async XLA Ops:
  0.0 21.3 %copy-start = (bf16[4096,3328]{1,0:T(8,128)(2,1)S(1)}, bf16[4096,3328]{1,0:T(8,128)(2,1)}, u32[]{:S(2)}) copy-start(bf16[4096,3328]{1,0:T(8,128)(2,1)} %gate_ref.1) | copy-start | bytes 81788928
  3.0 7.7 %collective-permute-start = (bf16[8,4096]{1,0:T(8,128)(2,1)S(1)}, bf16[8,4096]{1,0:T(8,128)(2,1)S(1)}, u32[]{:S(2)}, u32[]{:S(2)}) collective-permute-start(bf16[8,4096]{1,0:T(8,128)(2,1)S(1)} %attention.1.refs_0_), channel_id=1, source_target_pairs={{0,8},{2,10},{4,12},{6,14},{8,0},{10,2},{12,4},{14,6},{1,9},{3,11}... | collective-permute-start | bytes 196616 | tf_op jit(solution)/shard_map/ppermute | solution.py:550
  7.1 4.3 %collective-permute-start.1 = (bf16[8,4096]{1,0:T(8,128)(2,1)S(1)}, bf16[8,4096]{1,0:T(8,128)(2,1)S(1)}, u32[]{:S(2)}, u32[]{:S(2)}) collective-permute-start(bf16[8,4096]{1,0:T(8,128)(2,1)S(1)} %attention.1.refs_0_), channel_id=1, source_target_pairs={{0,2},{2,0},{4,6},{6,4},{8,10},{10,8},{12,14},{14,12},{1,3},{3,1},... | collective-permute-start | bytes 196616 | tf_op jit(solution)/shard_map/ppermute | solution.py:551
  11.4 25.1 %copy-start.1 = (s32[64,1]{0,1:T(1,128)S(1)}, s32[64,1]{0,1:T(1,128)}, u32[]{:S(2)}) copy-start(s32[64,1]{0,1:T(1,128)} %param.14) | copy-start | bytes 772
  11.4 9.9 %collective-permute-start.2 = (bf16[3,8,4096]{2,1,0:T(8,128)(2,1)S(1)}, bf16[3,8,4096]{2,1,0:T(8,128)(2,1)S(1)}, u32[]{:S(2)}, u32[]{:S(2)}) collective-permute-start(bf16[3,8,4096]{2,1,0:T(8,128)(2,1)S(1)} %pack.1.a_ref), channel_id=1, source_target_pairs={{0,4},{2,6},{4,0},{6,2},{8,12},{10,14},{12,8},{14,10},{1,5},{3,7},... | collective-permute-start | bytes 589832 | tf_op jit(solution)/shard_map/ppermute | solution.py:554
  13.0 8.3 %collective-permute-start.4 = (bf16[8,4096]{1,0:T(8,128)(2,1)S(1)}, bf16[8,4096]{1,0:T(8,128)(2,1)S(1)}, u32[]{:S(2)}, u32[]{:S(2)}) collective-permute-start(bf16[8,4096]{1,0:T(8,128)(2,1)S(1)} %attention.1.refs_0_), channel_id=1, source_target_pairs={{0,14},{2,12},{4,10},{6,8},{8,6},{10,4},{12,2},{14,0},{1,15},{3,13... | collective-permute-start | bytes 196616 | tf_op jit(solution)/shard_map/ppermute | solution.py:552
  15.2 6.1 %collective-permute-start.3 = (bf16[8,4096]{1,0:T(8,128)(2,1)S(1)}, bf16[8,4096]{1,0:T(8,128)(2,1)S(1)}, u32[]{:S(2)}, u32[]{:S(2)}) collective-permute-start(bf16[8,4096]{1,0:T(8,128)(2,1)S(1)} %collective-permute-done.refs_1_), channel_id=1, source_target_pairs={{0,2},{2,0},{4,6},{6,4},{8,10},{10,8},{12,14},{14,12},{1,3},{3,1},... | collective-permute-start | bytes 196616 | tf_op jit(solution)/shard_map/ppermute | solution.py:555
  36.5 2.7 %collective-permute-start.5 = (bf16[2,64,3328]{2,1,0:T(8,128)(2,1)S(1)}, bf16[2,64,3328]{2,1,0:T(8,128)(2,1)S(1)}, u32[]{:S(2)}, u32[]{:S(2)}) collective-permute-start(bf16[2,64,3328]{2,1,0:T(8,128)(2,1)S(1)} %get-tuple-element.27.after_ref.refs_0_), channel_id=1, source_target_pairs={{0,1},{1,0},{2,3},{3,2},{4,5},{5,4},{6,7},{7,6},{8,9},{9,8},{10,11... | collective-permute-start | bytes 2555912 | tf_op jit(solution)/shard_map/ppermute | solution.py:562
  41.4 6.0 %collective-permute-start.6 = (bf16[64,1024]{1,0:T(8,128)(2,1)S(1)}, bf16[64,1024]{1,0:T(8,128)(2,1)S(1)}, u32[]{:S(2)}, u32[]{:S(2)}) collective-permute-start(bf16[64,1024]{1,0:T(8,128)(2,1)S(1)} %get-tuple-element.33), channel_id=1, source_target_pairs={{0,2},{2,0},{4,6},{6,4},{8,10},{10,8},{12,14},{14,12},{1,3},{3,1},... | collective-permute-start | bytes 393224 | tf_op jit(solution)/shard_map/ppermute | solution.py:571
  44.9 5.7 %collective-permute-start.8 = (bf16[64,1024]{1,0:T(8,128)(2,1)S(1)}, bf16[64,1024]{1,0:T(8,128)(2,1)S(1)}, u32[]{:S(2)}, u32[]{:S(2)}) collective-permute-start(bf16[64,1024]{1,0:T(8,128)(2,1)S(1)} %get-tuple-element.39), channel_id=1, source_target_pairs={{0,2},{2,0},{4,6},{6,4},{8,10},{10,8},{12,14},{14,12},{1,3},{3,1},... | collective-permute-start | bytes 393224 | tf_op jit(solution)/shard_map/ppermute | solution.py:581
  49.2 5.4 %collective-permute-start.7 = (bf16[64,1024]{1,0:T(8,128)(2,1)S(1)}, bf16[64,1024]{1,0:T(8,128)(2,1)S(1)}, u32[]{:S(2)}, u32[]{:S(2)}) collective-permute-start(bf16[64,1024]{1,0:T(8,128)(2,1)S(1)} %get-tuple-element.37), channel_id=1, source_target_pairs={{0,4},{2,6},{4,0},{6,2},{8,12},{10,14},{12,8},{14,10},{1,5},{3,7},... | collective-permute-start | bytes 393224 | tf_op jit(solution)/shard_map/ppermute | solution.py:591
  52.1 5.5 %collective-permute-start.9 = (bf16[64,1024]{1,0:T(8,128)(2,1)S(1)}, bf16[64,1024]{1,0:T(8,128)(2,1)S(1)}, u32[]{:S(2)}, u32[]{:S(2)}) collective-permute-start(bf16[64,1024]{1,0:T(8,128)(2,1)S(1)} %get-tuple-element.43), channel_id=1, source_target_pairs={{0,4},{2,6},{4,0},{6,2},{8,12},{10,14},{12,8},{14,10},{1,5},{3,7},... | collective-permute-start | bytes 393224 | tf_op jit(solution)/shard_map/ppermute | solution.py:595
  54.7 6.8 %collective-permute-start.10 = (bf16[32,1024]{1,0:T(8,128)(2,1)S(1)}, bf16[32,1024]{1,0:T(8,128)(2,1)S(1)}, u32[]{:S(2)}, u32[]{:S(2)}) collective-permute-start(bf16[32,1024]{1,0:T(8,128)(2,1)S(1)} %get-tuple-element.45), channel_id=1, source_target_pairs={{0,8},{2,10},{4,12},{6,14},{8,0},{10,2},{12,4},{14,6},{1,9},{3,11}... | collective-permute-start | bytes 196616 | tf_op jit(solution)/shard_map/ppermute | solution.py:600
  57.7 5.9 %collective-permute-start.11 = (bf16[32,1024]{1,0:T(8,128)(2,1)S(1)}, bf16[32,1024]{1,0:T(8,128)(2,1)S(1)}, u32[]{:S(2)}, u32[]{:S(2)}) collective-permute-start(bf16[32,1024]{1,0:T(8,128)(2,1)S(1)} %get-tuple-element.46), channel_id=1, source_target_pairs={{0,8},{2,10},{4,12},{6,14},{8,0},{10,2},{12,4},{14,6},{1,9},{3,11}... | collective-permute-start | bytes 196616 | tf_op jit(solution)/shard_map/ppermute | solution.py:600
  63.8 4.3 %collective-permute-start.12 = (bf16[16,2048]{1,0:T(8,128)(2,1)S(1)}, bf16[16,2048]{1,0:T(8,128)(2,1)S(1)}, u32[]{:S(2)}, u32[]{:S(2)}) collective-permute-start(bf16[16,2048]{1,0:T(8,128)(2,1)S(1)} %get-tuple-element.48), channel_id=1, source_target_pairs={{0,2},{2,0},{4,6},{6,4},{8,10},{10,8},{12,14},{14,12},{1,3},{3,1},... | collective-permute-start | bytes 196616 | tf_op jit(solution)/shard_map/ppermute | solution.py:602

commit v11 on v10

--- a/solution.py
+++ b/solution.py
@@ -10,8 +10,8 @@
 
 AXIS = "attn"
 TILE = 256
-BAND = 256
-GATE_MIB = 11
+BAND = 512
+GATE_MIB = 14
 ORDER = (0, 2, 1, 3)
 MIB = 1 << 20
 VMEM = pl.BlockSpec(memory_space=pltpu.VMEM)
@@ -185,7 +185,7 @@
     for j in range(min(slots, left)):
         streamed(j).start()
     far_tiles = far_ref.shape[0] // TILE
-    per_step = -(-far_tiles // left)
+    per_step = -(-far_tiles // (left - 1))
     far_base = half_base(devices, False, far_ref.shape[1])
 
     def far_copy(i):
@@ -213,11 +213,17 @@
 
     total_ref[...] = jnp.zeros_like(total_ref)
 
+    def band(j):
+        return pl.ds(pl.multiple_of(j * BAND, BAND), BAND)
+
+    @pl.when(me >= 0)
+    def _():
+        add(band(0), gate_ref[band(0), :], 0)
+
     def step(j, _):
-        at = pl.ds(pl.multiple_of(j * BAND, BAND), BAND)
-        add(at, gate_ref[at, :], 0)
         streamed(j).wait()
-        add(at, buf[lax.rem(j, slots)], 1)
+        add(band(j), buf[lax.rem(j, slots)], 1)
+        add(band(j + 1), gate_ref[band(j + 1), :], 0)
 
         @pl.when(j + slots < left)
         def _():
@@ -231,7 +237,9 @@
 
         return 0
 
-    lax.fori_loop(0, left, step, 0)
+    lax.fori_loop(0, left - 1, step, 0)
+    streamed(left - 1).wait()
+    add(band(left - 1), buf[(left - 1) % slots], 1)
     part_ref[...] = total_ref[...].astype(BF16)
     for i in range(far_tiles):
         far_copy(i).wait()
@@ -240,7 +248,7 @@
 def gate_up(blocks, gate_weight, up_weight, down_weight, devices, ahead):
     total = devices * blocks[0].shape[1]
     features, columns = gate_weight.shape
-    slots = 4
+    slots = 3
     return pl.pallas_call(
         functools.partial(gate_up_kernel, devices),
         out_shape=(
@@ -542,7 +550,7 @@
     nz, nx = grid_of(devices)
     capacity = cache_keys.shape[0]
     columns, features = down_weight.shape
-    fits = nz == 4 and nx == 2 and columns % TILE == 0 and features == 16 * BAND
+    fits = nz == 4 and nx == 2 and columns % TILE == 0 and features % (8 * BAND) == 0
     mixed_rows = attend(queries, cache_keys, stored_value_cache, lengths, residual, up_weight)
     if not fits:
         return plain(mixed_rows, target, gate_weight, up_weight, down_weight, devices)

time: 68.9 us -> 66.1 us (0.959)
  Pallas kernels: 30.2 us -> 27.4 us
    pallas_call x1, Pallas kernels: 15.1 us -> 12.3 us  [gate_up(): pl.pallas_call(functools.partial(gate_up_kernel, devices), out_shape=(jax...]
  transfers between devices with their start and end apart: 13 -> 13, of which waited for: 10 -> 10; matrix products, arithmetic and copies ran while one was open for 0% -> 0% of each run, Pallas kernels for 13% -> 14%
where the time goes in v11:
time: 66.1 us; the launch traced here: 66 us
  Pallas kernels  27.4 us (41%)
  waiting for transfers between devices  22.8 us (34%)
  starting transfers between devices  15.7 us (24%)
    pallas_call x1, Pallas kernels, gate_up(): pl.pallas_call(functools.partial(gate_up_kernel, devices), out_shape=(jax...  12.3 us
    pallas_call x4, Pallas kernels, down(): pl.pallas_call(functools.partial(down_kernel, devices, far, quarter, len(...  8.58 us
    ppermute x1, waiting for transfers between devices, local(): e = lax.ppermute(mixed_rows, AXIS, swap_x(devices, 3))  5.51 us
    ppermute x2, waiting for transfers between devices, local(): came.append(lax.ppermute(send, AXIS, swap_z(devices, 2)))  4.87 us
    ppermute x1, starting transfers between devices, local(): two = lax.ppermute(mixed_rows, AXIS, swap_z(devices, 2))  4.1 us
    ppermute x1, waiting for transfers between devices, local(): return join(keep, lax.ppermute(send, AXIS, swap_x(devices)), devices)  3.05 us
    pallas_call x1, Pallas kernels, attend(): pl.pallas_call(functools.partial(attend_kernel, kv), out_shape=jax.ShapeD...  3 us
    ppermute x1, waiting for transfers between devices, local(): came_b = lax.ppermute(send_b, AXIS, swap_z(devices, 1))  2.7 us
  transfers between devices with their start and end apart: 13, of which 10 were waited for; matrix products, arithmetic and copies ran while one was open for 0% of the time, Pallas kernels for 14%

profile of v11, /device:TPU:0, one launch (start us, length us, event | category | flops | bytes accessed | tf_op | source)
XLA Modules:
  0.0 66.0 jit_solution(8316377750591439345)
XLA Ops:
  0.0 3.0 %attention.1.refs_0_ = bf16[8,4096]{1,0:T(8,128)(2,1)S(1)} custom-call(s32[8]{0:T(128)} %lengths.1, bf16[8,32,128]{2,1,0:T(8,128)(2,1)} %q_hbm.1, bf16[8,256,128]{2,1,0:T(8,128)(2,1)} %bitcast.4, bf16[8,256,128]{2,1,0:T(8,128)(2,1)} %bitcast.5, bf16[8,4096]{1,0:T(8,128)(2,1)} %res_ref.1, bf16[4096,3328]{1,0:T(8,128)(2,1)} %u_hbm.1), custom_call_target="tpu_custom_call" | custom-call | flops 33554432 | bytes 1048576 | tf_op jit(solution)/shard_map/attention/pallas_call | solution.py:107
  3.0 4.1 %collective-permute-start = (bf16[8,4096]{1,0:T(8,128)(2,1)S(1)}, bf16[8,4096]{1,0:T(8,128)(2,1)S(1)}, u32[]{:S(2)}, u32[]{:S(2)}) collective-permute-start(bf16[8,4096]{1,0:T(8,128)(2,1)S(1)} %attention.1.refs_0_), channel_id=1, source_target_pairs={{0,8},{2,10},{4,12},{6,14},{8,0},{10,2},{12,4},{14,6},{1,9},{3,11}... | collective-permute-start | bytes 196616 | tf_op jit(solution)/shard_map/ppermute | solution.py:558
  7.1 1.5 %collective-permute-start.1 = (bf16[8,4096]{1,0:T(8,128)(2,1)S(1)}, bf16[8,4096]{1,0:T(8,128)(2,1)S(1)}, u32[]{:S(2)}, u32[]{:S(2)}) collective-permute-start(bf16[8,4096]{1,0:T(8,128)(2,1)S(1)} %attention.1.refs_0_), channel_id=1, source_target_pairs={{0,2},{2,0},{4,6},{6,4},{8,10},{10,8},{12,14},{14,12},{1,3},{3,1},... | collective-permute-start | bytes 196616 | tf_op jit(solution)/shard_map/ppermute | solution.py:559
  8.6 2.2 %collective-permute-done.refs_1_ = bf16[8,4096]{1,0:T(8,128)(2,1)S(1)} collective-permute-done((bf16[8,4096]{1,0:T(8,128)(2,1)S(1)}, bf16[8,4096]{1,0:T(8,128)(2,1)S(1)}, u32[]{:S(2)}, u32[]{:S(2)}) %collective-permute-start) | collective-permute-done | bytes 65568 | tf_op jit(solution)/shard_map/ppermute | solution.py:558
  11.4 1.6 %collective-permute-start.2 = (bf16[3,8,4096]{2,1,0:T(8,128)(2,1)S(1)}, bf16[3,8,4096]{2,1,0:T(8,128)(2,1)S(1)}, u32[]{:S(2)}, u32[]{:S(2)}) collective-permute-start(bf16[3,8,4096]{2,1,0:T(8,128)(2,1)S(1)} %pack.1.a_ref), channel_id=1, source_target_pairs={{0,4},{2,6},{4,0},{6,2},{8,12},{10,14},{12,8},{14,10},{1,5},{3,7},... | collective-permute-start | bytes 589832 | tf_op jit(solution)/shard_map/ppermute | solution.py:562
  13.0 2.2 %collective-permute-start.4 = (bf16[8,4096]{1,0:T(8,128)(2,1)S(1)}, bf16[8,4096]{1,0:T(8,128)(2,1)S(1)}, u32[]{:S(2)}, u32[]{:S(2)}) collective-permute-start(bf16[8,4096]{1,0:T(8,128)(2,1)S(1)} %attention.1.refs_0_), channel_id=1, source_target_pairs={{0,14},{2,12},{4,10},{6,8},{8,6},{10,4},{12,2},{14,0},{1,15},{3,13... | collective-permute-start | bytes 196616 | tf_op jit(solution)/shard_map/ppermute | solution.py:560
  15.8 5.5 %collective-permute-done.4.e_ref = bf16[8,4096]{1,0:T(8,128)(2,1)S(1)} collective-permute-done((bf16[8,4096]{1,0:T(8,128)(2,1)S(1)}, bf16[8,4096]{1,0:T(8,128)(2,1)S(1)}, u32[]{:S(2)}, u32[]{:S(2)}) %collective-permute-start.4) | collective-permute-done | bytes 65568 | tf_op jit(solution)/shard_map/ppermute | solution.py:560
  21.3 12.3 %gate_up.1 = (bf16[2,64,3328]{2,1,0:T(8,128)(2,1)S(1)}, bf16[64,4096]{1,0:T(8,128)(2,1)S(1)}, bf16[2048,2048]{1,0:T(8,128)(2,1)S(1)}) custom-call(bf16[3,8,4096]{2,1,0:T(8,128)(2,1)S(1)} %pack.1.a_ref, bf16[3,8,4096]{2,1,0:T(8,128)(2,1)S(1)} %collective-permute-done.2.c_ref, bf16[8,4096]{1,0:T(8,128)(2,1)S(1)} %collective-permute-done.3.d_ref, ...), custom_call_target="tpu_custom_call" | custom-call | flops 3489660928 | bytes 54525952 | tf_op jit(solution)/shard_map/gate_up/pallas_call | solution.py:252
  33.7 2.6 %prepare.1 = (bf16[1280,2048]{1,0:T(8,128)(2,1)S(1)}, bf16[128,64]{1,0:T(8,128)(2,1)S(1)}) custom-call(bf16[2,64,3328]{2,1,0:T(8,128)(2,1)S(1)} %get-tuple-element.27.after_ref.refs_0_, s32[1,64]{1,0:T(1,128)S(1)} %bitcast.3, bf16[3328,4096]{1,0:T(8,128)(2,1)} %refs_5_.3), custom_call_target="tpu_custom_call" | custom-call | bytes 5242880 | tf_op jit(solution)/shard_map/prepare/pallas_call | solution.py:334
  36.3 2.2 %down_far.2 = (bf16[64,1024]{1,0:T(8,128)(2,1)S(1)}, bf16[2048,1024]{1,0:T(8,128)(2,1)S(1)}, bf16[64,3328]{1,0:T(8,128)(2,1)S(1)}) custom-call(bf16[2,64,3328]{2,1,0:T(8,128)(2,1)S(1)} %get-tuple-element.27.after_ref.refs_0_, bf16[2,64,3328]{2,1,0:T(8,128)(2,1)S(1)} %collective-permute-done.5.refs_1_, ...), custom_call_target="tpu_custom_call" | custom-call | bytes 1024 | tf_op jit(solution)/shard_map/down_far/pallas_call | solution.py:417
  39.2 2.9 %down_far.3 = (bf16[64,1024]{1,0:T(8,128)(2,1)S(1)}, bf16[1280,1024]{1,0:T(8,128)(2,1)S(1)}, bf16[1792,1024]{1,0:T(8,128)(2,1)S(1)}) custom-call(bf16[64,3328]{1,0:T(8,128)(2,1)S(1)} %get-tuple-element.32.refs_0_, bf16[2048,2048]{1,0:T(8,128)(2,1)S(1)} %get-tuple-element.30.refs_2_.refs_1_, bf16[1280,2048]{1,0:T(8,128)(2,1)S(1)} %get-tuple-element.31.refs_3_.refs_2_, ...), custom_call_target="tpu_custom_call" | custom-call | bytes 1024 | tf_op jit(solution)/shard_map/down_far/pallas_call | solution.py:417
  42.1 1.5 %collective-permute-start.8 = (bf16[64,1024]{1,0:T(8,128)(2,1)S(1)}, bf16[64,1024]{1,0:T(8,128)(2,1)S(1)}, u32[]{:S(2)}, u32[]{:S(2)}) collective-permute-start(bf16[64,1024]{1,0:T(8,128)(2,1)S(1)} %get-tuple-element.39), channel_id=1, source_target_pairs={{0,2},{2,0},{4,6},{6,4},{8,10},{10,8},{12,14},{14,12},{1,3},{3,1},... | collective-permute-start | bytes 393224 | tf_op jit(solution)/shard_map/ppermute | solution.py:589
  43.6 0.9 %collective-permute-done.6.refs_1_ = bf16[64,1024]{1,0:T(8,128)(2,1)S(1)} collective-permute-done((bf16[64,1024]{1,0:T(8,128)(2,1)S(1)}, bf16[64,1024]{1,0:T(8,128)(2,1)S(1)}, u32[]{:S(2)}, u32[]{:S(2)}) %collective-permute-start.6) | collective-permute-done | bytes 131104 | tf_op jit(solution)/shard_map/ppermute | solution.py:579
  44.5 1.9 %down_near.2 = (bf16[64,1024]{1,0:T(8,128)(2,1)S(1)}, bf16[64,1024]{1,0:T(8,128)(2,1)S(1)}, bf16[1536,1024]{1,0:T(8,128)(2,1)S(1)}) custom-call(bf16[64,3328]{1,0:T(8,128)(2,1)S(1)} %get-tuple-element.32.refs_0_, bf16[64,1024]{1,0:T(8,128)(2,1)S(1)} %collective-permute-done.6.refs_1_, bf16[128,64]{1,0:T(8,128)(2,1)S(1)} %get-tuple-element.28.refs_2_.chosen_ref, ...), custom_call_target="tpu_custom_call" | custom-call | bytes 1024 | tf_op jit(solution)/shard_map/down_near/pallas_call | solution.py:417
  46.5 1.3 %collective-permute-done.8.refs_1_ = bf16[64,1024]{1,0:T(8,128)(2,1)S(1)} collective-permute-done((bf16[64,1024]{1,0:T(8,128)(2,1)S(1)}, bf16[64,1024]{1,0:T(8,128)(2,1)S(1)}, u32[]{:S(2)}, u32[]{:S(2)}) %collective-permute-start.8) | collective-permute-done | bytes 131104 | tf_op jit(solution)/shard_map/ppermute | solution.py:589
  47.8 1.5 %down_near.3 = (bf16[64,1024]{1,0:T(8,128)(2,1)S(1)}, bf16[64,1024]{1,0:T(8,128)(2,1)S(1)}) custom-call(bf16[64,3328]{1,0:T(8,128)(2,1)S(1)} %get-tuple-element.32.refs_0_, bf16[64,1024]{1,0:T(8,128)(2,1)S(1)} %collective-permute-done.8.refs_1_, bf16[128,64]{1,0:T(8,128)(2,1)S(1)} %get-tuple-element.28.refs_2_.chosen_ref, ...), custom_call_target="tpu_custom_call" | custom-call | bytes 1024 | tf_op jit(solution)/shard_map/down_near/pallas_call | solution.py:417
  49.3 0.8 %collective-permute-start.9 = (bf16[64,1024]{1,0:T(8,128)(2,1)S(1)}, bf16[64,1024]{1,0:T(8,128)(2,1)S(1)}, u32[]{:S(2)}, u32[]{:S(2)}) collective-permute-start(bf16[64,1024]{1,0:T(8,128)(2,1)S(1)} %get-tuple-element.43), channel_id=1, source_target_pairs={{0,4},{2,6},{4,0},{6,2},{8,12},{10,14},{12,8},{14,10},{1,5},{3,7},... | collective-permute-start | bytes 393224 | tf_op jit(solution)/shard_map/ppermute | solution.py:603
  50.1 1.8 %collective-permute-done.7.came_ref = bf16[64,1024]{1,0:T(8,128)(2,1)S(1)} collective-permute-done((bf16[64,1024]{1,0:T(8,128)(2,1)S(1)}, bf16[64,1024]{1,0:T(8,128)(2,1)S(1)}, u32[]{:S(2)}, u32[]{:S(2)}) %collective-permute-start.7) | collective-permute-done | bytes 131104 | tf_op jit(solution)/shard_map/ppermute | solution.py:599
  52.1 2.7 %collective-permute-done.9.came_ref = bf16[64,1024]{1,0:T(8,128)(2,1)S(1)} collective-permute-done((bf16[64,1024]{1,0:T(8,128)(2,1)S(1)}, bf16[64,1024]{1,0:T(8,128)(2,1)S(1)}, u32[]{:S(2)}, u32[]{:S(2)}) %collective-permute-start.9) | collective-permute-done | bytes 131104 | tf_op jit(solution)/shard_map/ppermute | solution.py:603
  54.9 1.1 %collective-permute-start.11 = (bf16[32,1024]{1,0:T(8,128)(2,1)S(1)}, bf16[32,1024]{1,0:T(8,128)(2,1)S(1)}, u32[]{:S(2)}, u32[]{:S(2)}) collective-permute-start(bf16[32,1024]{1,0:T(8,128)(2,1)S(1)} %get-tuple-element.46), channel_id=1, source_target_pairs={{0,8},{2,10},{4,12},{6,14},{8,0},{10,2},{12,4},{14,6},{1,9},{3,11}... | collective-permute-start | bytes 196616 | tf_op jit(solution)/shard_map/ppermute | solution.py:608
  55.9 2.8 %collective-permute-done.10.refs_2_ = bf16[32,1024]{1,0:T(8,128)(2,1)S(1)} collective-permute-done((bf16[32,1024]{1,0:T(8,128)(2,1)S(1)}, bf16[32,1024]{1,0:T(8,128)(2,1)S(1)}, u32[]{:S(2)}, u32[]{:S(2)}) %collective-permute-start.10) | collective-permute-done | bytes 65568 | tf_op jit(solution)/shard_map/ppermute | solution.py:608
  58.7 2.1 %collective-permute-done.11.refs_3_ = bf16[32,1024]{1,0:T(8,128)(2,1)S(1)} collective-permute-done((bf16[32,1024]{1,0:T(8,128)(2,1)S(1)}, bf16[32,1024]{1,0:T(8,128)(2,1)S(1)}, u32[]{:S(2)}, u32[]{:S(2)}) %collective-permute-start.11) | collective-permute-done | bytes 65568 | tf_op jit(solution)/shard_map/ppermute | solution.py:608
  61.0 1.3 %collective-permute-start.12 = (bf16[16,2048]{1,0:T(8,128)(2,1)S(1)}, bf16[16,2048]{1,0:T(8,128)(2,1)S(1)}, u32[]{:S(2)}, u32[]{:S(2)}) collective-permute-start(bf16[16,2048]{1,0:T(8,128)(2,1)S(1)} %get-tuple-element.48), channel_id=1, source_target_pairs={{0,2},{2,0},{4,6},{6,4},{8,10},{10,8},{12,14},{14,12},{1,3},{3,1},... | collective-permute-start | bytes 196616 | tf_op jit(solution)/shard_map/ppermute | solution.py:610
  62.2 3.1 %collective-permute-done.12.other_ref = bf16[16,2048]{1,0:T(8,128)(2,1)S(1)} collective-permute-done((bf16[16,2048]{1,0:T(8,128)(2,1)S(1)}, bf16[16,2048]{1,0:T(8,128)(2,1)S(1)}, u32[]{:S(2)}, u32[]{:S(2)}) %collective-permute-start.12) | collective-permute-done | bytes 65568 | tf_op jit(solution)/shard_map/ppermute | solution.py:610
  (18 shorter events, 3.1 us)
Async XLA Ops:
  0.0 21.3 %copy-start = (bf16[4096,3328]{1,0:T(8,128)(2,1)S(1)}, bf16[4096,3328]{1,0:T(8,128)(2,1)}, u32[]{:S(2)}) copy-start(bf16[4096,3328]{1,0:T(8,128)(2,1)} %gate_ref.1) | copy-start | bytes 81788928
  3.0 7.7 %collective-permute-start = (bf16[8,4096]{1,0:T(8,128)(2,1)S(1)}, bf16[8,4096]{1,0:T(8,128)(2,1)S(1)}, u32[]{:S(2)}, u32[]{:S(2)}) collective-permute-start(bf16[8,4096]{1,0:T(8,128)(2,1)S(1)} %attention.1.refs_0_), channel_id=1, source_target_pairs={{0,8},{2,10},{4,12},{6,14},{8,0},{10,2},{12,4},{14,6},{1,9},{3,11}... | collective-permute-start | bytes 196616 | tf_op jit(solution)/shard_map/ppermute | solution.py:558
  7.1 4.3 %collective-permute-start.1 = (bf16[8,4096]{1,0:T(8,128)(2,1)S(1)}, bf16[8,4096]{1,0:T(8,128)(2,1)S(1)}, u32[]{:S(2)}, u32[]{:S(2)}) collective-permute-start(bf16[8,4096]{1,0:T(8,128)(2,1)S(1)} %attention.1.refs_0_), channel_id=1, source_target_pairs={{0,2},{2,0},{4,6},{6,4},{8,10},{10,8},{12,14},{14,12},{1,3},{3,1},... | collective-permute-start | bytes 196616 | tf_op jit(solution)/shard_map/ppermute | solution.py:559
  11.4 22.3 %copy-start.1 = (s32[64,1]{0,1:T(1,128)S(1)}, s32[64,1]{0,1:T(1,128)}, u32[]{:S(2)}) copy-start(s32[64,1]{0,1:T(1,128)} %param.14) | copy-start | bytes 772
  11.4 9.9 %collective-permute-start.2 = (bf16[3,8,4096]{2,1,0:T(8,128)(2,1)S(1)}, bf16[3,8,4096]{2,1,0:T(8,128)(2,1)S(1)}, u32[]{:S(2)}, u32[]{:S(2)}) collective-permute-start(bf16[3,8,4096]{2,1,0:T(8,128)(2,1)S(1)} %pack.1.a_ref), channel_id=1, source_target_pairs={{0,4},{2,6},{4,0},{6,2},{8,12},{10,14},{12,8},{14,10},{1,5},{3,7},... | collective-permute-start | bytes 589832 | tf_op jit(solution)/shard_map/ppermute | solution.py:562
  13.0 8.3 %collective-permute-start.4 = (bf16[8,4096]{1,0:T(8,128)(2,1)S(1)}, bf16[8,4096]{1,0:T(8,128)(2,1)S(1)}, u32[]{:S(2)}, u32[]{:S(2)}) collective-permute-start(bf16[8,4096]{1,0:T(8,128)(2,1)S(1)} %attention.1.refs_0_), channel_id=1, source_target_pairs={{0,14},{2,12},{4,10},{6,8},{8,6},{10,4},{12,2},{14,0},{1,15},{3,13... | collective-permute-start | bytes 196616 | tf_op jit(solution)/shard_map/ppermute | solution.py:560
  15.2 6.1 %collective-permute-start.3 = (bf16[8,4096]{1,0:T(8,128)(2,1)S(1)}, bf16[8,4096]{1,0:T(8,128)(2,1)S(1)}, u32[]{:S(2)}, u32[]{:S(2)}) collective-permute-start(bf16[8,4096]{1,0:T(8,128)(2,1)S(1)} %collective-permute-done.refs_1_), channel_id=1, source_target_pairs={{0,2},{2,0},{4,6},{6,4},{8,10},{10,8},{12,14},{14,12},{1,3},{3,1},... | collective-permute-start | bytes 196616 | tf_op jit(solution)/shard_map/ppermute | solution.py:563
  33.6 2.6 %collective-permute-start.5 = (bf16[2,64,3328]{2,1,0:T(8,128)(2,1)S(1)}, bf16[2,64,3328]{2,1,0:T(8,128)(2,1)S(1)}, u32[]{:S(2)}, u32[]{:S(2)}) collective-permute-start(bf16[2,64,3328]{2,1,0:T(8,128)(2,1)S(1)} %get-tuple-element.27.after_ref.refs_0_), channel_id=1, source_target_pairs={{0,1},{1,0},{2,3},{3,2},{4,5},{5,4},{6,7},{7,6},{8,9},{9,8},{10,11... | collective-permute-start | bytes 2555912 | tf_op jit(solution)/shard_map/ppermute | solution.py:570
  38.6 6.0 %collective-permute-start.6 = (bf16[64,1024]{1,0:T(8,128)(2,1)S(1)}, bf16[64,1024]{1,0:T(8,128)(2,1)S(1)}, u32[]{:S(2)}, u32[]{:S(2)}) collective-permute-start(bf16[64,1024]{1,0:T(8,128)(2,1)S(1)} %get-tuple-element.33), channel_id=1, source_target_pairs={{0,2},{2,0},{4,6},{6,4},{8,10},{10,8},{12,14},{14,12},{1,3},{3,1},... | collective-permute-start | bytes 393224 | tf_op jit(solution)/shard_map/ppermute | solution.py:579
  42.1 5.7 %collective-permute-start.8 = (bf16[64,1024]{1,0:T(8,128)(2,1)S(1)}, bf16[64,1024]{1,0:T(8,128)(2,1)S(1)}, u32[]{:S(2)}, u32[]{:S(2)}) collective-permute-start(bf16[64,1024]{1,0:T(8,128)(2,1)S(1)} %get-tuple-element.39), channel_id=1, source_target_pairs={{0,2},{2,0},{4,6},{6,4},{8,10},{10,8},{12,14},{14,12},{1,3},{3,1},... | collective-permute-start | bytes 393224 | tf_op jit(solution)/shard_map/ppermute | solution.py:589
  46.4 5.4 %collective-permute-start.7 = (bf16[64,1024]{1,0:T(8,128)(2,1)S(1)}, bf16[64,1024]{1,0:T(8,128)(2,1)S(1)}, u32[]{:S(2)}, u32[]{:S(2)}) collective-permute-start(bf16[64,1024]{1,0:T(8,128)(2,1)S(1)} %get-tuple-element.37), channel_id=1, source_target_pairs={{0,4},{2,6},{4,0},{6,2},{8,12},{10,14},{12,8},{14,10},{1,5},{3,7},... | collective-permute-start | bytes 393224 | tf_op jit(solution)/shard_map/ppermute | solution.py:599
  49.3 5.5 %collective-permute-start.9 = (bf16[64,1024]{1,0:T(8,128)(2,1)S(1)}, bf16[64,1024]{1,0:T(8,128)(2,1)S(1)}, u32[]{:S(2)}, u32[]{:S(2)}) collective-permute-start(bf16[64,1024]{1,0:T(8,128)(2,1)S(1)} %get-tuple-element.43), channel_id=1, source_target_pairs={{0,4},{2,6},{4,0},{6,2},{8,12},{10,14},{12,8},{14,10},{1,5},{3,7},... | collective-permute-start | bytes 393224 | tf_op jit(solution)/shard_map/ppermute | solution.py:603
  51.9 6.8 %collective-permute-start.10 = (bf16[32,1024]{1,0:T(8,128)(2,1)S(1)}, bf16[32,1024]{1,0:T(8,128)(2,1)S(1)}, u32[]{:S(2)}, u32[]{:S(2)}) collective-permute-start(bf16[32,1024]{1,0:T(8,128)(2,1)S(1)} %get-tuple-element.45), channel_id=1, source_target_pairs={{0,8},{2,10},{4,12},{6,14},{8,0},{10,2},{12,4},{14,6},{1,9},{3,11}... | collective-permute-start | bytes 196616 | tf_op jit(solution)/shard_map/ppermute | solution.py:608
  54.9 5.9 %collective-permute-start.11 = (bf16[32,1024]{1,0:T(8,128)(2,1)S(1)}, bf16[32,1024]{1,0:T(8,128)(2,1)S(1)}, u32[]{:S(2)}, u32[]{:S(2)}) collective-permute-start(bf16[32,1024]{1,0:T(8,128)(2,1)S(1)} %get-tuple-element.46), channel_id=1, source_target_pairs={{0,8},{2,10},{4,12},{6,14},{8,0},{10,2},{12,4},{14,6},{1,9},{3,11}... | collective-permute-start | bytes 196616 | tf_op jit(solution)/shard_map/ppermute | solution.py:608
  61.0 4.3 %collective-permute-start.12 = (bf16[16,2048]{1,0:T(8,128)(2,1)S(1)}, bf16[16,2048]{1,0:T(8,128)(2,1)S(1)}, u32[]{:S(2)}, u32[]{:S(2)}) collective-permute-start(bf16[16,2048]{1,0:T(8,128)(2,1)S(1)} %get-tuple-element.48), channel_id=1, source_target_pairs={{0,2},{2,0},{4,6},{6,4},{8,10},{10,8},{12,14},{14,12},{1,3},{3,1},... | collective-permute-start | bytes 196616 | tf_op jit(solution)/shard_map/ppermute | solution.py:610

commit v12 on v11

--- a/solution.py
+++ b/solution.py
@@ -562,7 +562,7 @@
     c = lax.ppermute(a, AXIS, swap_z(devices, 1))
     d = lax.ppermute(two, AXIS, swap_x(devices))
     tiles = columns // TILE
-    far_cut = 8 * tiles // 13 * TILE
+    far_cut = 10 * tiles // 13 * TILE
     cut = 8 * tiles // 13 * TILE, 7 * tiles // 13 * TILE
     part, rows, far_a = gate_up(
         (a, c, d, e), gate_weight, up_weight, down_weight, devices, far_cut

time: 66.1 us -> 65.4 us (0.989)
  Pallas kernels: 27.4 us -> 26.7 us
  transfers between devices with their start and end apart: 13 -> 13, of which waited for: 10 -> 11; matrix products, arithmetic and copies ran while one was open for 0% -> 0% of each run, Pallas kernels for 14% -> 13%
where the time goes in v12:
time: 65.4 us; the launch traced here: 65.3 us
  Pallas kernels  26.7 us (41%)
  waiting for transfers between devices  23.1 us (35%)
  starting transfers between devices  15.3 us (23%)
    pallas_call x1, Pallas kernels, gate_up(): pl.pallas_call(functools.partial(gate_up_kernel, devices), out_shape=(jax...  12.4 us
    pallas_call x4, Pallas kernels, down(): pl.pallas_call(functools.partial(down_kernel, devices, far, quarter, len(...  8.56 us
    ppermute x1, waiting for transfers between devices, local(): e = lax.ppermute(mixed_rows, AXIS, swap_x(devices, 3))  5.51 us
    ppermute x2, waiting for transfers between devices, local(): came.append(lax.ppermute(send, AXIS, swap_z(devices, 2)))  4.77 us
    ppermute x1, starting transfers between devices, local(): two = lax.ppermute(mixed_rows, AXIS, swap_z(devices, 2))  4.1 us
    ppermute x1, waiting for transfers between devices, local(): return join(keep, lax.ppermute(send, AXIS, swap_x(devices)), devices)  3.03 us
    pallas_call x1, Pallas kernels, attend(): pl.pallas_call(functools.partial(attend_kernel, kv), out_shape=jax.ShapeD...  3 us
    ppermute x1, waiting for transfers between devices, local(): came_b = lax.ppermute(send_b, AXIS, swap_z(devices, 1))  2.88 us
  transfers between devices with their start and end apart: 13, of which 11 were waited for; matrix products, arithmetic and copies ran while one was open for 0% of the time, Pallas kernels for 13%

profile of v12, /device:TPU:0, one launch (start us, length us, event | category | flops | bytes accessed | tf_op | source)
XLA Modules:
  0.0 65.3 jit_solution(15333609923454018144)
XLA Ops:
  0.0 3.0 %attention.1.refs_0_ = bf16[8,4096]{1,0:T(8,128)(2,1)S(1)} custom-call(s32[8]{0:T(128)} %lengths.1, bf16[8,32,128]{2,1,0:T(8,128)(2,1)} %q_hbm.1, bf16[8,256,128]{2,1,0:T(8,128)(2,1)} %bitcast.4, bf16[8,256,128]{2,1,0:T(8,128)(2,1)} %bitcast.5, bf16[8,4096]{1,0:T(8,128)(2,1)} %res_ref.1, bf16[4096,3328]{1,0:T(8,128)(2,1)} %u_hbm.1), custom_call_target="tpu_custom_call" | custom-call | flops 33554432 | bytes 1048576 | tf_op jit(solution)/shard_map/attention/pallas_call | solution.py:107
  3.0 4.1 %collective-permute-start = (bf16[8,4096]{1,0:T(8,128)(2,1)S(1)}, bf16[8,4096]{1,0:T(8,128)(2,1)S(1)}, u32[]{:S(2)}, u32[]{:S(2)}) collective-permute-start(bf16[8,4096]{1,0:T(8,128)(2,1)S(1)} %attention.1.refs_0_), channel_id=1, source_target_pairs={{0,8},{2,10},{4,12},{6,14},{8,0},{10,2},{12,4},{14,6},{1,9},{3,11}... | collective-permute-start | bytes 196616 | tf_op jit(solution)/shard_map/ppermute | solution.py:558
  7.1 1.5 %collective-permute-start.1 = (bf16[8,4096]{1,0:T(8,128)(2,1)S(1)}, bf16[8,4096]{1,0:T(8,128)(2,1)S(1)}, u32[]{:S(2)}, u32[]{:S(2)}) collective-permute-start(bf16[8,4096]{1,0:T(8,128)(2,1)S(1)} %attention.1.refs_0_), channel_id=1, source_target_pairs={{0,2},{2,0},{4,6},{6,4},{8,10},{10,8},{12,14},{14,12},{1,3},{3,1},... | collective-permute-start | bytes 196616 | tf_op jit(solution)/shard_map/ppermute | solution.py:559
  8.6 2.2 %collective-permute-done.refs_1_ = bf16[8,4096]{1,0:T(8,128)(2,1)S(1)} collective-permute-done((bf16[8,4096]{1,0:T(8,128)(2,1)S(1)}, bf16[8,4096]{1,0:T(8,128)(2,1)S(1)}, u32[]{:S(2)}, u32[]{:S(2)}) %collective-permute-start) | collective-permute-done | bytes 65568 | tf_op jit(solution)/shard_map/ppermute | solution.py:558
  11.4 1.6 %collective-permute-start.2 = (bf16[3,8,4096]{2,1,0:T(8,128)(2,1)S(1)}, bf16[3,8,4096]{2,1,0:T(8,128)(2,1)S(1)}, u32[]{:S(2)}, u32[]{:S(2)}) collective-permute-start(bf16[3,8,4096]{2,1,0:T(8,128)(2,1)S(1)} %pack.1.a_ref), channel_id=1, source_target_pairs={{0,4},{2,6},{4,0},{6,2},{8,12},{10,14},{12,8},{14,10},{1,5},{3,7},... | collective-permute-start | bytes 589832 | tf_op jit(solution)/shard_map/ppermute | solution.py:562
  13.0 2.2 %collective-permute-start.4 = (bf16[8,4096]{1,0:T(8,128)(2,1)S(1)}, bf16[8,4096]{1,0:T(8,128)(2,1)S(1)}, u32[]{:S(2)}, u32[]{:S(2)}) collective-permute-start(bf16[8,4096]{1,0:T(8,128)(2,1)S(1)} %attention.1.refs_0_), channel_id=1, source_target_pairs={{0,14},{2,12},{4,10},{6,8},{8,6},{10,4},{12,2},{14,0},{1,15},{3,13... | collective-permute-start | bytes 196616 | tf_op jit(solution)/shard_map/ppermute | solution.py:560
  15.8 5.5 %collective-permute-done.4.e_ref = bf16[8,4096]{1,0:T(8,128)(2,1)S(1)} collective-permute-done((bf16[8,4096]{1,0:T(8,128)(2,1)S(1)}, bf16[8,4096]{1,0:T(8,128)(2,1)S(1)}, u32[]{:S(2)}, u32[]{:S(2)}) %collective-permute-start.4) | collective-permute-done | bytes 65568 | tf_op jit(solution)/shard_map/ppermute | solution.py:560
  21.3 12.4 %gate_up.1 = (bf16[2,64,3328]{2,1,0:T(8,128)(2,1)S(1)}, bf16[64,4096]{1,0:T(8,128)(2,1)S(1)}, bf16[2560,2048]{1,0:T(8,128)(2,1)S(1)}) custom-call(bf16[3,8,4096]{2,1,0:T(8,128)(2,1)S(1)} %pack.1.a_ref, bf16[3,8,4096]{2,1,0:T(8,128)(2,1)S(1)} %collective-permute-done.2.c_ref, bf16[8,4096]{1,0:T(8,128)(2,1)S(1)} %collective-permute-done.3.d_ref, ...), custom_call_target="tpu_custom_call" | custom-call | flops 3489660928 | bytes 54525952 | tf_op jit(solution)/shard_map/gate_up/pallas_call | solution.py:252
  33.8 1.9 %prepare.1 = (bf16[768,2048]{1,0:T(8,128)(2,1)S(1)}, bf16[128,64]{1,0:T(8,128)(2,1)S(1)}) custom-call(bf16[2,64,3328]{2,1,0:T(8,128)(2,1)S(1)} %get-tuple-element.27.after_ref.refs_0_, s32[1,64]{1,0:T(1,128)S(1)} %bitcast.3, bf16[3328,4096]{1,0:T(8,128)(2,1)} %refs_5_.3), custom_call_target="tpu_custom_call" | custom-call | bytes 3145728 | tf_op jit(solution)/shard_map/prepare/pallas_call | solution.py:334
  36.1 2.2 %down_far.2 = (bf16[64,1024]{1,0:T(8,128)(2,1)S(1)}, bf16[2048,1024]{1,0:T(8,128)(2,1)S(1)}, bf16[64,3328]{1,0:T(8,128)(2,1)S(1)}) custom-call(bf16[2,64,3328]{2,1,0:T(8,128)(2,1)S(1)} %get-tuple-element.27.after_ref.refs_0_, bf16[2,64,3328]{2,1,0:T(8,128)(2,1)S(1)} %collective-permute-done.5.refs_1_, ...), custom_call_target="tpu_custom_call" | custom-call | bytes 1024 | tf_op jit(solution)/shard_map/down_far/pallas_call | solution.py:417
  39.0 2.9 %down_far.3 = (bf16[64,1024]{1,0:T(8,128)(2,1)S(1)}, bf16[1280,1024]{1,0:T(8,128)(2,1)S(1)}, bf16[1792,1024]{1,0:T(8,128)(2,1)S(1)}) custom-call(bf16[64,3328]{1,0:T(8,128)(2,1)S(1)} %get-tuple-element.32.refs_0_, bf16[2560,2048]{1,0:T(8,128)(2,1)S(1)} %get-tuple-element.30.refs_2_.refs_1_, bf16[768,2048]{1,0:T(8,128)(2,1)S(1)} %get-tuple-element.31.refs_3_.refs_2_, ...), custom_call_target="tpu_custom_call" | custom-call | bytes 1024 | tf_op jit(solution)/shard_map/down_far/pallas_call | solution.py:417
  41.9 1.6 %collective-permute-start.8 = (bf16[64,1024]{1,0:T(8,128)(2,1)S(1)}, bf16[64,1024]{1,0:T(8,128)(2,1)S(1)}, u32[]{:S(2)}, u32[]{:S(2)}) collective-permute-start(bf16[64,1024]{1,0:T(8,128)(2,1)S(1)} %get-tuple-element.39), channel_id=1, source_target_pairs={{0,2},{2,0},{4,6},{6,4},{8,10},{10,8},{12,14},{14,12},{1,3},{3,1},... | collective-permute-start | bytes 393224 | tf_op jit(solution)/shard_map/ppermute | solution.py:589
  44.0 1.9 %down_near.2 = (bf16[64,1024]{1,0:T(8,128)(2,1)S(1)}, bf16[64,1024]{1,0:T(8,128)(2,1)S(1)}, bf16[1536,1024]{1,0:T(8,128)(2,1)S(1)}) custom-call(bf16[64,3328]{1,0:T(8,128)(2,1)S(1)} %get-tuple-element.32.refs_0_, bf16[64,1024]{1,0:T(8,128)(2,1)S(1)} %collective-permute-done.6.refs_1_, bf16[128,64]{1,0:T(8,128)(2,1)S(1)} %get-tuple-element.28.refs_2_.chosen_ref, ...), custom_call_target="tpu_custom_call" | custom-call | bytes 1024 | tf_op jit(solution)/shard_map/down_near/pallas_call | solution.py:417
  46.0 1.3 %collective-permute-done.8.refs_1_ = bf16[64,1024]{1,0:T(8,128)(2,1)S(1)} collective-permute-done((bf16[64,1024]{1,0:T(8,128)(2,1)S(1)}, bf16[64,1024]{1,0:T(8,128)(2,1)S(1)}, u32[]{:S(2)}, u32[]{:S(2)}) %collective-permute-start.8) | collective-permute-done | bytes 131104 | tf_op jit(solution)/shard_map/ppermute | solution.py:589
  47.2 1.5 %down_near.3 = (bf16[64,1024]{1,0:T(8,128)(2,1)S(1)}, bf16[64,1024]{1,0:T(8,128)(2,1)S(1)}) custom-call(bf16[64,3328]{1,0:T(8,128)(2,1)S(1)} %get-tuple-element.32.refs_0_, bf16[64,1024]{1,0:T(8,128)(2,1)S(1)} %collective-permute-done.8.refs_1_, bf16[128,64]{1,0:T(8,128)(2,1)S(1)} %get-tuple-element.28.refs_2_.chosen_ref, ...), custom_call_target="tpu_custom_call" | custom-call | bytes 1024 | tf_op jit(solution)/shard_map/down_near/pallas_call | solution.py:417
  48.7 0.8 %collective-permute-start.9 = (bf16[64,1024]{1,0:T(8,128)(2,1)S(1)}, bf16[64,1024]{1,0:T(8,128)(2,1)S(1)}, u32[]{:S(2)}, u32[]{:S(2)}) collective-permute-start(bf16[64,1024]{1,0:T(8,128)(2,1)S(1)} %get-tuple-element.43), channel_id=1, source_target_pairs={{0,4},{2,6},{4,0},{6,2},{8,12},{10,14},{12,8},{14,10},{1,5},{3,7},... | collective-permute-start | bytes 393224 | tf_op jit(solution)/shard_map/ppermute | solution.py:603
  49.6 1.9 %collective-permute-done.7.came_ref = bf16[64,1024]{1,0:T(8,128)(2,1)S(1)} collective-permute-done((bf16[64,1024]{1,0:T(8,128)(2,1)S(1)}, bf16[64,1024]{1,0:T(8,128)(2,1)S(1)}, u32[]{:S(2)}, u32[]{:S(2)}) %collective-permute-start.7) | collective-permute-done | bytes 131104 | tf_op jit(solution)/shard_map/ppermute | solution.py:599
  51.6 2.9 %collective-permute-done.9.came_ref = bf16[64,1024]{1,0:T(8,128)(2,1)S(1)} collective-permute-done((bf16[64,1024]{1,0:T(8,128)(2,1)S(1)}, bf16[64,1024]{1,0:T(8,128)(2,1)S(1)}, u32[]{:S(2)}, u32[]{:S(2)}) %collective-permute-start.9) | collective-permute-done | bytes 131104 | tf_op jit(solution)/shard_map/ppermute | solution.py:603
  54.5 0.8 %collective-permute-start.11 = (bf16[32,1024]{1,0:T(8,128)(2,1)S(1)}, bf16[32,1024]{1,0:T(8,128)(2,1)S(1)}, u32[]{:S(2)}, u32[]{:S(2)}) collective-permute-start(bf16[32,1024]{1,0:T(8,128)(2,1)S(1)} %get-tuple-element.46), channel_id=1, source_target_pairs={{0,8},{2,10},{4,12},{6,14},{8,0},{10,2},{12,4},{14,6},{1,9},{3,11}... | collective-permute-start | bytes 196616 | tf_op jit(solution)/shard_map/ppermute | solution.py:608
  55.3 2.5 %collective-permute-done.10.refs_2_ = bf16[32,1024]{1,0:T(8,128)(2,1)S(1)} collective-permute-done((bf16[32,1024]{1,0:T(8,128)(2,1)S(1)}, bf16[32,1024]{1,0:T(8,128)(2,1)S(1)}, u32[]{:S(2)}, u32[]{:S(2)}) %collective-permute-start.10) | collective-permute-done | bytes 65568 | tf_op jit(solution)/shard_map/ppermute | solution.py:608
  57.8 2.3 %collective-permute-done.11.refs_3_ = bf16[32,1024]{1,0:T(8,128)(2,1)S(1)} collective-permute-done((bf16[32,1024]{1,0:T(8,128)(2,1)S(1)}, bf16[32,1024]{1,0:T(8,128)(2,1)S(1)}, u32[]{:S(2)}, u32[]{:S(2)}) %collective-permute-start.11) | collective-permute-done | bytes 65568 | tf_op jit(solution)/shard_map/ppermute | solution.py:608
  60.3 1.3 %collective-permute-start.12 = (bf16[16,2048]{1,0:T(8,128)(2,1)S(1)}, bf16[16,2048]{1,0:T(8,128)(2,1)S(1)}, u32[]{:S(2)}, u32[]{:S(2)}) collective-permute-start(bf16[16,2048]{1,0:T(8,128)(2,1)S(1)} %get-tuple-element.48), channel_id=1, source_target_pairs={{0,2},{2,0},{4,6},{6,4},{8,10},{10,8},{12,14},{14,12},{1,3},{3,1},... | collective-permute-start | bytes 196616 | tf_op jit(solution)/shard_map/ppermute | solution.py:610
  61.6 3.0 %collective-permute-done.12.other_ref = bf16[16,2048]{1,0:T(8,128)(2,1)S(1)} collective-permute-done((bf16[16,2048]{1,0:T(8,128)(2,1)S(1)}, bf16[16,2048]{1,0:T(8,128)(2,1)S(1)}, u32[]{:S(2)}, u32[]{:S(2)}) %collective-permute-start.12) | collective-permute-done | bytes 65568 | tf_op jit(solution)/shard_map/ppermute | solution.py:610
  64.6 0.7 %join_halves.1 = bf16[16,4096]{1,0:T(8,128)(2,1)} custom-call(bf16[16,2048]{1,0:T(8,128)(2,1)S(1)} %get-tuple-element.47.keep_ref, bf16[16,2048]{1,0:T(8,128)(2,1)S(1)} %collective-permute-done.12.other_ref), custom_call_target="tpu_custom_call" | custom-call | tf_op jit(solution)/shard_map/join_halves/pallas_call | solution.py:489
  (18 shorter events, 3.2 us)
Async XLA Ops:
  0.0 21.3 %copy-start = (bf16[4096,3328]{1,0:T(8,128)(2,1)S(1)}, bf16[4096,3328]{1,0:T(8,128)(2,1)}, u32[]{:S(2)}) copy-start(bf16[4096,3328]{1,0:T(8,128)(2,1)} %gate_ref.1) | copy-start | bytes 81788928
  3.0 7.7 %collective-permute-start = (bf16[8,4096]{1,0:T(8,128)(2,1)S(1)}, bf16[8,4096]{1,0:T(8,128)(2,1)S(1)}, u32[]{:S(2)}, u32[]{:S(2)}) collective-permute-start(bf16[8,4096]{1,0:T(8,128)(2,1)S(1)} %attention.1.refs_0_), channel_id=1, source_target_pairs={{0,8},{2,10},{4,12},{6,14},{8,0},{10,2},{12,4},{14,6},{1,9},{3,11}... | collective-permute-start | bytes 196616 | tf_op jit(solution)/shard_map/ppermute | solution.py:558
  7.1 4.3 %collective-permute-start.1 = (bf16[8,4096]{1,0:T(8,128)(2,1)S(1)}, bf16[8,4096]{1,0:T(8,128)(2,1)S(1)}, u32[]{:S(2)}, u32[]{:S(2)}) collective-permute-start(bf16[8,4096]{1,0:T(8,128)(2,1)S(1)} %attention.1.refs_0_), channel_id=1, source_target_pairs={{0,2},{2,0},{4,6},{6,4},{8,10},{10,8},{12,14},{14,12},{1,3},{3,1},... | collective-permute-start | bytes 196616 | tf_op jit(solution)/shard_map/ppermute | solution.py:559
  11.4 22.4 %copy-start.1 = (s32[64,1]{0,1:T(1,128)S(1)}, s32[64,1]{0,1:T(1,128)}, u32[]{:S(2)}) copy-start(s32[64,1]{0,1:T(1,128)} %param.14) | copy-start | bytes 772
  11.4 9.9 %collective-permute-start.2 = (bf16[3,8,4096]{2,1,0:T(8,128)(2,1)S(1)}, bf16[3,8,4096]{2,1,0:T(8,128)(2,1)S(1)}, u32[]{:S(2)}, u32[]{:S(2)}) collective-permute-start(bf16[3,8,4096]{2,1,0:T(8,128)(2,1)S(1)} %pack.1.a_ref), channel_id=1, source_target_pairs={{0,4},{2,6},{4,0},{6,2},{8,12},{10,14},{12,8},{14,10},{1,5},{3,7},... | collective-permute-start | bytes 589832 | tf_op jit(solution)/shard_map/ppermute | solution.py:562
  13.0 8.3 %collective-permute-start.4 = (bf16[8,4096]{1,0:T(8,128)(2,1)S(1)}, bf16[8,4096]{1,0:T(8,128)(2,1)S(1)}, u32[]{:S(2)}, u32[]{:S(2)}) collective-permute-start(bf16[8,4096]{1,0:T(8,128)(2,1)S(1)} %attention.1.refs_0_), channel_id=1, source_target_pairs={{0,14},{2,12},{4,10},{6,8},{8,6},{10,4},{12,2},{14,0},{1,15},{3,13... | collective-permute-start | bytes 196616 | tf_op jit(solution)/shard_map/ppermute | solution.py:560
  15.2 6.1 %collective-permute-start.3 = (bf16[8,4096]{1,0:T(8,128)(2,1)S(1)}, bf16[8,4096]{1,0:T(8,128)(2,1)S(1)}, u32[]{:S(2)}, u32[]{:S(2)}) collective-permute-start(bf16[8,4096]{1,0:T(8,128)(2,1)S(1)} %collective-permute-done.refs_1_), channel_id=1, source_target_pairs={{0,2},{2,0},{4,6},{6,4},{8,10},{10,8},{12,14},{14,12},{1,3},{3,1},... | collective-permute-start | bytes 196616 | tf_op jit(solution)/shard_map/ppermute | solution.py:563
  33.7 2.4 %collective-permute-start.5 = (bf16[2,64,3328]{2,1,0:T(8,128)(2,1)S(1)}, bf16[2,64,3328]{2,1,0:T(8,128)(2,1)S(1)}, u32[]{:S(2)}, u32[]{:S(2)}) collective-permute-start(bf16[2,64,3328]{2,1,0:T(8,128)(2,1)S(1)} %get-tuple-element.27.after_ref.refs_0_), channel_id=1, source_target_pairs={{0,1},{1,0},{2,3},{3,2},{4,5},{5,4},{6,7},{7,6},{8,9},{9,8},{10,11... | collective-permute-start | bytes 2555912 | tf_op jit(solution)/shard_map/ppermute | solution.py:570
  38.4 5.6 %collective-permute-start.6 = (bf16[64,1024]{1,0:T(8,128)(2,1)S(1)}, bf16[64,1024]{1,0:T(8,128)(2,1)S(1)}, u32[]{:S(2)}, u32[]{:S(2)}) collective-permute-start(bf16[64,1024]{1,0:T(8,128)(2,1)S(1)} %get-tuple-element.33), channel_id=1, source_target_pairs={{0,2},{2,0},{4,6},{6,4},{8,10},{10,8},{12,14},{14,12},{1,3},{3,1},... | collective-permute-start | bytes 393224 | tf_op jit(solution)/shard_map/ppermute | solution.py:579
  41.9 5.3 %collective-permute-start.8 = (bf16[64,1024]{1,0:T(8,128)(2,1)S(1)}, bf16[64,1024]{1,0:T(8,128)(2,1)S(1)}, u32[]{:S(2)}, u32[]{:S(2)}) collective-permute-start(bf16[64,1024]{1,0:T(8,128)(2,1)S(1)} %get-tuple-element.39), channel_id=1, source_target_pairs={{0,2},{2,0},{4,6},{6,4},{8,10},{10,8},{12,14},{14,12},{1,3},{3,1},... | collective-permute-start | bytes 393224 | tf_op jit(solution)/shard_map/ppermute | solution.py:589
  45.9 5.6 %collective-permute-start.7 = (bf16[64,1024]{1,0:T(8,128)(2,1)S(1)}, bf16[64,1024]{1,0:T(8,128)(2,1)S(1)}, u32[]{:S(2)}, u32[]{:S(2)}) collective-permute-start(bf16[64,1024]{1,0:T(8,128)(2,1)S(1)} %get-tuple-element.37), channel_id=1, source_target_pairs={{0,4},{2,6},{4,0},{6,2},{8,12},{10,14},{12,8},{14,10},{1,5},{3,7},... | collective-permute-start | bytes 393224 | tf_op jit(solution)/shard_map/ppermute | solution.py:599
  48.7 5.7 %collective-permute-start.9 = (bf16[64,1024]{1,0:T(8,128)(2,1)S(1)}, bf16[64,1024]{1,0:T(8,128)(2,1)S(1)}, u32[]{:S(2)}, u32[]{:S(2)}) collective-permute-start(bf16[64,1024]{1,0:T(8,128)(2,1)S(1)} %get-tuple-element.43), channel_id=1, source_target_pairs={{0,4},{2,6},{4,0},{6,2},{8,12},{10,14},{12,8},{14,10},{1,5},{3,7},... | collective-permute-start | bytes 393224 | tf_op jit(solution)/shard_map/ppermute | solution.py:603
  51.5 6.3 %collective-permute-start.10 = (bf16[32,1024]{1,0:T(8,128)(2,1)S(1)}, bf16[32,1024]{1,0:T(8,128)(2,1)S(1)}, u32[]{:S(2)}, u32[]{:S(2)}) collective-permute-start(bf16[32,1024]{1,0:T(8,128)(2,1)S(1)} %get-tuple-element.45), channel_id=1, source_target_pairs={{0,8},{2,10},{4,12},{6,14},{8,0},{10,2},{12,4},{14,6},{1,9},{3,11}... | collective-permute-start | bytes 196616 | tf_op jit(solution)/shard_map/ppermute | solution.py:608
  54.5 5.6 %collective-permute-start.11 = (bf16[32,1024]{1,0:T(8,128)(2,1)S(1)}, bf16[32,1024]{1,0:T(8,128)(2,1)S(1)}, u32[]{:S(2)}, u32[]{:S(2)}) collective-permute-start(bf16[32,1024]{1,0:T(8,128)(2,1)S(1)} %get-tuple-element.46), channel_id=1, source_target_pairs={{0,8},{2,10},{4,12},{6,14},{8,0},{10,2},{12,4},{14,6},{1,9},{3,11}... | collective-permute-start | bytes 196616 | tf_op jit(solution)/shard_map/ppermute | solution.py:608
  60.3 4.3 %collective-permute-start.12 = (bf16[16,2048]{1,0:T(8,128)(2,1)S(1)}, bf16[16,2048]{1,0:T(8,128)(2,1)S(1)}, u32[]{:S(2)}, u32[]{:S(2)}) collective-permute-start(bf16[16,2048]{1,0:T(8,128)(2,1)S(1)} %get-tuple-element.48), channel_id=1, source_target_pairs={{0,2},{2,0},{4,6},{6,4},{8,10},{10,8},{12,14},{14,12},{1,3},{3,1},... | collective-permute-start | bytes 196616 | tf_op jit(solution)/shard_map/ppermute | solution.py:610
